TPU v7x, 32 devices: a whole 2x2x4 slice. The times are simulated.
32 devices in a mesh: dp: 2 (over y), fsdp: 4 (over z), ctx: 4 (over x, core).
Axes of the slice: x: 2, y: 2, z: 4, core: 2. Of those that a mesh axis runs over, the one named last changes fastest.
Arguments:
- inputs: bfloat16 [32, 1024, 1088], P(('dp', 'fsdp'), 'ctx'), may hold values from -6 to 6
- cotangent: bfloat16 [32, 1024, 1088], P(('dp', 'fsdp'), 'ctx'), may hold values from -6 to 6
- first_gain: bfloat16 [1088], P('fsdp'), may hold values from 0.099609375 to 1.8984375
- first_shift: bfloat16 [1088], P('fsdp'), may hold values from -3 to 3
- project_in: bfloat16 [1088, 3264], P('fsdp'), may hold values from -0.1875 to 0.1875
- query_bias: bfloat16 [1088], P('fsdp'), may hold values from -3 to 3
- value_bias: bfloat16 [1088], P('fsdp'), may hold values from -3 to 3
- project_out: bfloat16 [1088, 1088], P('fsdp'), may hold values from -1 to 1
- output_bias: bfloat16 [1088], P('fsdp'), may hold values from -3 to 3
- second_gain: bfloat16 [1088], P('fsdp'), may hold values from 0.099609375 to 1.8984375
- second_shift: bfloat16 [1088], P('fsdp'), may hold values from -3 to 3
- up_weight: bfloat16 [1088, 4352], P('fsdp'), may hold values from -0.1875 to 0.1875
- up_bias: bfloat16 [4352], P('fsdp'), may hold values from -3 to 3
- down_weight: bfloat16 [4352, 1088], P('fsdp'), may hold values from -0.09375 to 0.09375
- down_bias: bfloat16 [1088], P('fsdp'), may hold values from -3 to 3
Outputs:
- outputs: bfloat16 [32, 1024, 1088], P(('dp', 'fsdp'), 'ctx')
- input_gradient: float32 [32, 1024, 1088], P(('dp', 'fsdp'), 'ctx')
- first_gain_gradient: float32 [1088], P('fsdp')
- first_shift_gradient: float32 [1088], P('fsdp')
- project_in_gradient: float32 [1088, 3264], P('fsdp')
- query_bias_gradient: float32 [1088], P('fsdp')
- value_bias_gradient: float32 [1088], P('fsdp')
- project_out_gradient: float32 [1088, 1088], P('fsdp')
- output_bias_gradient: float32 [1088], P('fsdp')
- second_gain_gradient: float32 [1088], P('fsdp')
- second_shift_gradient: float32 [1088], P('fsdp')
- up_weight_gradient: float32 [1088, 4352], P('fsdp')
- up_bias_gradient: float32 [4352], P('fsdp')
- down_weight_gradient: float32 [4352, 1088], P('fsdp')
- down_bias_gradient: float32 [1088], P('fsdp')
All inputs are finite; a program needn't handle non-finite values.
Results may differ from a plain program's by a relative error of at most 0.017.
Values may be sent and summed in bfloat16 or wider, within the bound.
No kernel may reach another device: no remote copies, remote signals or barrier semaphores. Data moves between devices by JAX's collectives and lax.ppermute only.
A program may use at most 320 MiB of HBM per device.

v0:
```python
import jax
import jax.numpy as jnp
from jax import lax
from jax.sharding import PartitionSpec as P

HEADS = 17
HEAD_DIM = 64


epsilon = 1e-05


def layer_norm(values, gain, shift):
    centred = values - jnp.mean(values, axis=-1, keepdims=True)
    spread = jnp.mean(centred * centred, axis=-1, keepdims=True)
    return centred * lax.rsqrt(spread + epsilon) * gain + shift


def gelu_tanh(values):
    return jax.nn.gelu(values, approximate=True)


def score_grads(
    query_heads, key_heads, value_heads, grad_heads, log_total, row_delta, query_at, key_at
):
    score_scale = HEAD_DIM ** (-0.5)
    scores = (
        jnp.einsum("sqhd,skhd->shqk", query_heads, key_heads, preferred_element_type=jnp.float32)
        * score_scale
    )
    visible = query_at[:, None] >= key_at[None, :]
    shifted = jnp.where(visible, scores - log_total[..., None], -1e30)
    weights = jnp.where(visible, jnp.exp(shifted), 0.0)
    pressure = jnp.einsum(
        "sqhd,skhd->shqk", grad_heads, value_heads, preferred_element_type=jnp.float32
    )
    score_low = (weights * (pressure - row_delta[..., None])).astype(jnp.bfloat16)
    return (weights.astype(jnp.bfloat16), score_low)


def per_device(
    inputs,
    cotangent,
    first_gain,
    first_shift,
    project_in,
    query_bias,
    value_bias,
    project_out,
    output_bias,
    second_gain,
    second_shift,
    up_weight,
    up_bias,
    down_weight,
    down_bias,
):
    seq_count, block_len, model_width = inputs.shape
    flat_rows = seq_count * block_len
    cycle_size = lax.axis_size("ctx")
    my_block = lax.axis_index("ctx")
    score_scale = HEAD_DIM ** (-0.5)
    head_shape = (seq_count, block_len, HEADS, HEAD_DIM)
    offsets = jnp.arange(block_len, dtype=jnp.int32)
    query_at = my_block * block_len + offsets
    gain_first, shift_first, full_in, qbias_full, vbias_full, full_out, obias_full = (
        lax.all_gather(first_gain, "fsdp", axis=0, tiled=True),
        lax.all_gather(first_shift, "fsdp", axis=0, tiled=True),
        lax.all_gather(project_in, "fsdp", axis=0, tiled=True),
        lax.all_gather(query_bias, "fsdp", axis=0, tiled=True),
        lax.all_gather(value_bias, "fsdp", axis=0, tiled=True),
        lax.all_gather(project_out, "fsdp", axis=0, tiled=True),
        lax.all_gather(output_bias, "fsdp", axis=0, tiled=True),
    )
    rows_in = inputs.astype(jnp.float32).reshape(flat_rows, model_width)
    normed, norm_first_back = jax.vjp(
        layer_norm, rows_in, gain_first.astype(jnp.float32), shift_first.astype(jnp.float32)
    )
    normed_low = normed.astype(jnp.bfloat16)
    projected = jnp.dot(normed_low, full_in, preferred_element_type=jnp.float32)
    queries = (projected[:, :model_width] + qbias_full).astype(jnp.bfloat16)
    key_rows = projected[:, model_width : 2 * model_width].astype(jnp.bfloat16)
    value_rows = (projected[:, 2 * model_width :] + vbias_full).astype(jnp.bfloat16)
    query_heads = queries.reshape(head_shape)
    running_top = jnp.full((seq_count, HEADS, block_len), -1e30, jnp.float32)
    accumulated = jnp.zeros(head_shape, jnp.float32)
    piece_keys = lax.all_gather(
        key_rows.reshape(seq_count, block_len, model_width), "ctx", axis=1, tiled=True
    )
    piece_values = lax.all_gather(
        value_rows.reshape(seq_count, block_len, model_width), "ctx", axis=1, tiled=True
    )
    piece_len = piece_keys.shape[1]
    key_heads = piece_keys.reshape(seq_count, piece_len, HEADS, HEAD_DIM)
    value_heads = piece_values.reshape(seq_count, piece_len, HEADS, HEAD_DIM)
    scores = (
        jnp.einsum("sqhd,skhd->shqk", query_heads, key_heads, preferred_element_type=jnp.float32)
        * score_scale
    )
    key_at = jnp.arange(piece_len, dtype=jnp.int32)
    visible = query_at[:, None] >= key_at[None, :]
    masked = jnp.where(visible, scores, -1e30)
    new_top = jnp.maximum(running_top, jnp.max(masked, axis=-1))
    factor = jnp.exp(running_top - new_top)
    weights = jnp.where(visible, jnp.exp(masked - new_top[..., None]), 0.0)
    row_total = jnp.sum(weights, axis=-1)
    added = jnp.einsum(
        "shqk,skhd->sqhd",
        weights.astype(jnp.bfloat16),
        value_heads,
        preferred_element_type=jnp.float32,
    )
    accumulated = accumulated * jnp.swapaxes(factor, 1, 2)[..., None] + added
    running_top, row_total, accumulated = (new_top, row_total, accumulated)
    attended = accumulated / jnp.swapaxes(row_total, 1, 2)[..., None]
    log_total = running_top + jnp.log(row_total)
    attended_low = attended.reshape(flat_rows, model_width).astype(jnp.bfloat16)
    middle = (
        rows_in + jnp.dot(attended_low, full_out, preferred_element_type=jnp.float32) + obias_full
    )
    gain_second, shift_second, full_up, ubias_full, full_down, dbias_full = (
        lax.all_gather(second_gain, "fsdp", axis=0, tiled=True),
        lax.all_gather(second_shift, "fsdp", axis=0, tiled=True),
        lax.all_gather(up_weight, "fsdp", axis=0, tiled=True),
        lax.all_gather(up_bias, "fsdp", axis=0, tiled=True),
        lax.all_gather(down_weight, "fsdp", axis=0, tiled=True),
        lax.all_gather(down_bias, "fsdp", axis=0, tiled=True),
    )
    normed_two, norm_second_back = jax.vjp(
        layer_norm, middle, gain_second.astype(jnp.float32), shift_second.astype(jnp.float32)
    )
    normed_two_low = normed_two.astype(jnp.bfloat16)
    hidden = jnp.dot(normed_two_low, full_up, preferred_element_type=jnp.float32) + ubias_full
    active, gelu_back = jax.vjp(gelu_tanh, hidden)
    active_low = active.astype(jnp.bfloat16)
    result = (
        middle + jnp.dot(active_low, full_down, preferred_element_type=jnp.float32) + dbias_full
    )
    outputs = result.astype(jnp.bfloat16).reshape(seq_count, block_len, model_width)
    upstream = cotangent.astype(jnp.float32).reshape(flat_rows, model_width)
    upstream_low = upstream.astype(jnp.bfloat16)
    down_grad = jnp.einsum(
        "rf,rd->fd", active_low, upstream_low, preferred_element_type=jnp.float32
    )
    down_bias_grad = jnp.sum(upstream_low.astype(jnp.float32), axis=0)
    active_grad = jnp.einsum(
        "rd,fd->rf", upstream_low, full_down, preferred_element_type=jnp.float32
    )
    (hidden_grad,) = gelu_back(active_grad)
    hidden_low = hidden_grad.astype(jnp.bfloat16)
    up_grad = jnp.einsum(
        "rd,rf->df", normed_two_low, hidden_low, preferred_element_type=jnp.float32
    )
    up_bias_grad = jnp.sum(hidden_low.astype(jnp.float32), axis=0)
    normed_two_grad = jnp.einsum(
        "rf,df->rd", hidden_low, full_up, preferred_element_type=jnp.float32
    )
    middle_part, gain_two_grad, shift_two_grad = norm_second_back(normed_two_grad)
    middle_grad = upstream + middle_part
    middle_low = middle_grad.astype(jnp.bfloat16)
    out_grad = jnp.einsum("rd,re->de", attended_low, middle_low, preferred_element_type=jnp.float32)
    out_bias_grad = jnp.sum(middle_low.astype(jnp.float32), axis=0)
    attended_grad = jnp.einsum(
        "re,de->rd", middle_low, full_out, preferred_element_type=jnp.float32
    )
    grad_low = attended_grad.astype(jnp.bfloat16).reshape(head_shape)
    row_delta = jnp.swapaxes(jnp.sum(grad_low.astype(jnp.float32) * attended, axis=-1), 1, 2)
    gathered_keys, gathered_values = (
        lax.all_gather(
            key_rows.reshape(1, seq_count, block_len, model_width), "ctx", axis=0, tiled=True
        ),
        lax.all_gather(
            value_rows.reshape(1, seq_count, block_len, model_width), "ctx", axis=0, tiled=True
        ),
    )
    block_ids = jnp.arange(cycle_size, dtype=jnp.int32)

    def key_step(carry, inputs_here):
        key_block, value_block, block_index = inputs_here
        key_heads = key_block.reshape(head_shape)
        value_heads = value_block.reshape(head_shape)
        weights_low, score_low = score_grads(
            query_heads,
            key_heads,
            value_heads,
            grad_low,
            log_total,
            row_delta,
            query_at,
            block_index * block_len + offsets,
        )
        carry = (
            carry
            + jnp.einsum(
                "shqk,skhd->sqhd", score_low, key_heads, preferred_element_type=jnp.float32
            )
            * score_scale
        )
        key_term = (
            jnp.einsum(
                "shqk,sqhd->skhd", score_low, query_heads, preferred_element_type=jnp.float32
            )
            * score_scale
        )
        value_term = jnp.einsum(
            "shqk,sqhd->skhd", weights_low, grad_low, preferred_element_type=jnp.float32
        )
        return (
            carry,
            (
                key_term.reshape(seq_count, block_len, model_width),
                value_term.reshape(seq_count, block_len, model_width),
            ),
        )

    query_grad, (key_terms, value_terms) = lax.scan(
        key_step, jnp.zeros(head_shape, jnp.float32), (gathered_keys, gathered_values, block_ids)
    )
    key_sum, value_sum = (
        lax.psum_scatter(
            key_terms.astype(jnp.bfloat16), "ctx", scatter_dimension=0, tiled=True
        ).astype(jnp.float32),
        lax.psum_scatter(
            value_terms.astype(jnp.bfloat16), "ctx", scatter_dimension=0, tiled=True
        ).astype(jnp.float32),
    )
    key_grad = key_sum.reshape(flat_rows, model_width)
    value_grad = value_sum.reshape(flat_rows, model_width)
    query_low = query_grad.reshape(flat_rows, model_width).astype(jnp.bfloat16)
    key_low = key_grad.astype(jnp.bfloat16)
    value_low = value_grad.astype(jnp.bfloat16)
    stacked = jnp.concatenate([query_low, key_low, value_low], axis=1)
    in_grad = jnp.einsum("rd,re->de", normed_low, stacked, preferred_element_type=jnp.float32)
    query_bias_grad = jnp.sum(query_low.astype(jnp.float32), axis=0)
    value_bias_grad = jnp.sum(value_low.astype(jnp.float32), axis=0)
    normed_grad = jnp.einsum("re,de->rd", stacked, full_in, preferred_element_type=jnp.float32)
    input_part, gain_one_grad, shift_one_grad = norm_first_back(normed_grad)
    input_gradient = (middle_grad + input_part).reshape(seq_count, block_len, model_width)
    (
        gain_one_part,
        shift_one_part,
        in_part,
        qbias_part,
        vbias_part,
        out_part,
        obias_part,
        gain_two_part,
        shift_two_part,
        up_part,
        ubias_part,
        down_part,
        dbias_part,
    ) = (
        lax.psum_scatter(
            gain_one_grad.astype(jnp.bfloat16), "fsdp", scatter_dimension=0, tiled=True
        ).astype(jnp.float32),
        lax.psum_scatter(
            shift_one_grad.astype(jnp.bfloat16), "fsdp", scatter_dimension=0, tiled=True
        ).astype(jnp.float32),
        lax.psum_scatter(
            in_grad.astype(jnp.bfloat16), "fsdp", scatter_dimension=0, tiled=True
        ).astype(jnp.float32),
        lax.psum_scatter(
            query_bias_grad.astype(jnp.bfloat16), "fsdp", scatter_dimension=0, tiled=True
        ).astype(jnp.float32),
        lax.psum_scatter(
            value_bias_grad.astype(jnp.bfloat16), "fsdp", scatter_dimension=0, tiled=True
        ).astype(jnp.float32),
        lax.psum_scatter(
            out_grad.astype(jnp.bfloat16), "fsdp", scatter_dimension=0, tiled=True
        ).astype(jnp.float32),
        lax.psum_scatter(
            out_bias_grad.astype(jnp.bfloat16), "fsdp", scatter_dimension=0, tiled=True
        ).astype(jnp.float32),
        lax.psum_scatter(
            gain_two_grad.astype(jnp.bfloat16), "fsdp", scatter_dimension=0, tiled=True
        ).astype(jnp.float32),
        lax.psum_scatter(
            shift_two_grad.astype(jnp.bfloat16), "fsdp", scatter_dimension=0, tiled=True
        ).astype(jnp.float32),
        lax.psum_scatter(
            up_grad.astype(jnp.bfloat16), "fsdp", scatter_dimension=0, tiled=True
        ).astype(jnp.float32),
        lax.psum_scatter(
            up_bias_grad.astype(jnp.bfloat16), "fsdp", scatter_dimension=0, tiled=True
        ).astype(jnp.float32),
        lax.psum_scatter(
            down_grad.astype(jnp.bfloat16), "fsdp", scatter_dimension=0, tiled=True
        ).astype(jnp.float32),
        lax.psum_scatter(
            down_bias_grad.astype(jnp.bfloat16), "fsdp", scatter_dimension=0, tiled=True
        ).astype(jnp.float32),
    )
    (
        gain_one_sum,
        shift_one_sum,
        in_sum,
        qbias_sum,
        vbias_sum,
        out_sum,
        obias_sum,
        gain_two_sum,
        shift_two_sum,
        up_sum,
        ubias_sum,
        down_sum,
        dbias_sum,
    ) = lax.psum(
        (
            gain_one_part,
            shift_one_part,
            in_part,
            qbias_part,
            vbias_part,
            out_part,
            obias_part,
            gain_two_part,
            shift_two_part,
            up_part,
            ubias_part,
            down_part,
            dbias_part,
        ),
        ("dp", "ctx"),
    )
    return (
        outputs,
        input_gradient,
        gain_one_sum,
        shift_one_sum,
        in_sum,
        qbias_sum,
        vbias_sum,
        out_sum,
        obias_sum,
        gain_two_sum,
        shift_two_sum,
        up_sum,
        ubias_sum,
        down_sum,
        dbias_sum,
    )


def solution(mesh):
    return jax.shard_map(
        per_device,
        mesh=mesh,
        in_specs=(
            P(("dp", "fsdp"), "ctx", None),
            P(("dp", "fsdp"), "ctx", None),
            P("fsdp"),
            P("fsdp"),
            P("fsdp", None),
            P("fsdp"),
            P("fsdp"),
            P("fsdp", None),
            P("fsdp"),
            P("fsdp"),
            P("fsdp"),
            P("fsdp", None),
            P("fsdp"),
            P("fsdp", None),
            P("fsdp"),
        ),
        out_specs=(
            P(("dp", "fsdp"), "ctx", None),
            P(("dp", "fsdp"), "ctx", None),
            P("fsdp"),
            P("fsdp"),
            P("fsdp", None),
            P("fsdp"),
            P("fsdp"),
            P("fsdp", None),
            P("fsdp"),
            P("fsdp"),
            P("fsdp"),
            P("fsdp", None),
            P("fsdp"),
            P("fsdp", None),
            P("fsdp"),
        ),
        check_vma=False,
    )
```

profile of v0, /device:TPU:8, one launch (start us, length us, event | category | flops | bytes accessed | tf_op | source)
XLA Modules:
  0.0 1996.9 jit_solution(2306782960087242432)
XLA Ops:
  17.6 23.5 %all-reduce.20 = (bf16[1088]{0:T(1024)(128)(2,1)S(1)}, bf16[1088]{0:T(1024)(128)(2,1)S(1)}, bf16[1088]{0:T(1024)(128)(2,1)S(1)}, bf16[1088]{0:T(1024)(128)(2,1)S...) all-reduce(bf16[1088]{0:T(1024)(128)(2,1)S(1)} %dynamic-update-slic, ...), channel_id=1, replica_groups=mesh['dp'=2,'fsdp'=4,'ctx'=4] {'fsdp'}, use_global_device_ids=true, to_apply=%add.1 | all-reduce | flops 11968 | bytes 47872
  47.5 92.8 %all-gather.9.cloned.1.call-done = bf16[1088,3264]{1,0:T(8,128)(2,1)} async-done(((bf16[272,3264]{1,0:T(8,128)(2,1)}), bf16[1088,3264]{1,0:T(8,128)(2,1)}) %all-gather.9.cloned.1.call-update) | async-done | bytes 7102480 | tf_op jit(solution)/shard_map/all_gather | solution.py:69
  140.3 15.9 fusion.49
  195.3 30.3 %all-gather.11.cloned.1.call-done = bf16[4,1024,1088]{1,0,2:T(4,128)(2,1)} async-done(((bf16[4,256,1088]{1,0,2:T(4,128)(2,1)}), bf16[4,1024,1088]{1,0,2:T(4,128)(2,1)}) %all-gather.11.cloned.1.call-update) | async-done | bytes 8912912 | tf_op jit(solution)/shard_map/all_gather | solution.py:87
  225.6 10.5 copy.68
  236.1 30.4 %fusion.14 = (f32[4,17,256]{2,1,0:T(8,128)S(1)}, f32[4,17,256,1024]{3,2,1,0:T(8,128)}) fusion(pred[256,1024]{1,0:T(8,128)(4,1)S(1)} %iota_compare_fusion, bf16[4,1024,17,64]{1,3,2,0:T(8,128)(2,1)} %bitcast.156, bf16[4,256,17,64]{1,0,3,2:T(4,128)(2,1)S(1)} %reshape.196), kind=kOutput, calls=%fused_computation.24 | convolution fusion | flops 2335161344 | bytes 82776064 | tf_op jit(solution)/shard_map/sqhd,skhd->shqk/dot_general | solution.py:97
  266.5 26.5 %fusion.15 = f32[4,17,256]{2,1,0:T(8,128)S(1)} fusion(f32[4,17,256,1024]{3,2,1,0:T(8,128)} %get-tuple-element.293, f32[4,17,256]{2,1,0:T(8,128)S(1)} %broadcast_maximum_fusion, pred[256,1024]{1,0:T(8,128)(4,1)S(1)} %iota_compare_fusion), kind=kLoop, calls=%fused_computation.25 | loop fusion | flops 89111552 | bytes 71704576 | tf_op jit(solution)/shard_map/reduce_sum | solution.py:106
  293.7 10.1 copy.70
  303.7 32.5 %fusion.59 = (bf16[4,256,17,64]{1,3,2,0:T(8,128)(2,1)S(1)}, f32[4,256,17,64]{1,3,2,0:T(8,128)}) fusion(f32[4,256,17]{1,2,0:T(8,128)S(1)} %bitcast.175, bf16[4,1024,17,64]{1,3,2,0:T(8,128)(2,1)} %bitcast.164, f32[4,17,256,1024]{3,2,1,0:T(8,128)} %get-tuple-element.293, f32[4,17,256]{2,1,0:T(8,128)S(1)} %broadcast_maximum_fusion, ...), kind=kOutput, calls=%fused_computation.118 | convolution fusion | flops 2374172672 | bytes 87371776 | tf_op jit(solution)/shard_map/shqk,skhd->sqhd/dot_general | solution.py:107
  351.3 157.9 %all-gather.17.cloned.1.call-done = bf16[1088,4352]{1,0:T(8,128)(2,1)} async-done(((bf16[272,4352]{1,0:T(8,128)(2,1)}), bf16[1088,4352]{1,0:T(8,128)(2,1)}) %all-gather.17.cloned.1.call-update) | async-done | bytes 9469968 | tf_op jit(solution)/shard_map/all_gather | solution.py:124
  509.2 20.3 %fusion.50 = f32[1024,4352]{1,0:T(8,128)} fusion(bf16[1088,4352]{1,0:T(8,128)(2,1)} %all-gather.17.cloned.1.call-done, f32[1024,1088]{0,1:T(8,128)} %copy-done.9, f32[1088]{0:T(1024)S(1)} %copy-done.40, f32[1088]{0:T(1024)S(1)} %copy-done.30, f32[1024]{0:T(1024)S(1)} %fusion.39, f32[1024]{0:T(1024)S(1)} %broadcast_multiply_fusion.1), kind=kOutput, calls=%fused_computation.111 | convolution fusion | flops 9702801408 | bytes 31769088 | tf_op jit(solution)/shard_map/dot_general | solution.py:133
  529.5 155.8 %all-gather.19.cloned.1.call-done = bf16[4352,1088]{1,0:T(8,128)(2,1)} async-done(((bf16[1088,1088]{1,0:T(8,128)(2,1)}), bf16[4352,1088]{1,0:T(8,128)(2,1)}) %all-gather.19.cloned.1.call-update) | async-done | bytes 9469968 | tf_op jit(solution)/shard_map/all_gather | solution.py:126
  685.3 27.0 %fusion.52 = (bf16[4352]{0:T(1024)(128)(2,1)}, bf16[1024,4352]{1,0:T(8,128)(2,1)}) fusion(f32[1024,4352]{1,0:T(8,128)} %fusion.50, f32[4352]{0:T(1024)S(1)} %copy-done.32, bf16[1024,1088]{0,1:T(8,128)(2,1)S(1)} %bitcast.157, bf16[4352,1088]{1,0:T(8,128)(2,1)} %all-gather.19.cloned.1.call-done), kind=kOutput, calls=%fused_computation.113 | convolution fusion | flops 9795268608 | bytes 38462976 | tf_op jit(solution)/shard_map/rd,fd->rf/dot_general | solution.py:146
  712.2 18.9 multiply_reduce_fusion
  749.6 63.1 %all-gather.21.cloned.1.call-done = bf16[4,4,256,1088]{2,3,1,0:T(8,128)(2,1)} async-done(((bf16[1,4,256,1088]{2,3,1,0:T(8,128)(2,1)}), bf16[4,4,256,1088]{2,3,1,0:T(8,128)(2,1)}) %all-gather.21.cloned.1.call-update) | async-done | bytes 8912912 | tf_op jit(solution)/shard_map/all_gather | solution.py:169
  812.7 213.4 %while.15 = (s32[]{:T(128)}, f32[4,256,17,64]{1,3,2,0:T(8,128)}, bf16[4,4,256,1088]{2,3,1,0:T(8,128)(2,1)}, bf16[4,4,256,1088]{2,3,1,0:T(8,128)(2,1)}, bf16[4,4,...) while((s32[]{:T(128)}, f32[4,256,17,64]{1,3,2,0:T(8,128)}, ...), condition=%wide.region_10.11_spmd.clone, body=%wide.region_9.10_spmd.clone.sunk | while | flops 2911240704 | bytes 180896560 | solution.py:216
  815.0 8.6 fusion.112
  828.1 10.7 fusion.113
  838.8 7.5 broadcast_multiply_fusion.4
  846.3 9.3 fusion.114
  867.4 8.6 fusion.112
  880.6 10.7 fusion.113
  891.3 7.5 broadcast_multiply_fusion.4
  898.7 9.3 fusion.114
  910.4 8.4 bitcast_add_fusion.3
  921.1 8.6 fusion.112
  934.2 10.7 fusion.113
  944.9 7.5 broadcast_multiply_fusion.4
  952.4 9.3 fusion.114
  964.1 8.4 bitcast_add_fusion.3
  974.8 8.6 fusion.112
  987.9 10.7 fusion.113
  998.6 7.5 broadcast_multiply_fusion.4
  1006.0 9.3 fusion.114
  1017.7 8.4 bitcast_add_fusion.3
  1034.3 19.6 convolution_convert_fusion.1
  1055.5 22.1 %convolution_convert_fusion = bf16[4352,1088]{1,0:T(8,128)(2,1)} fusion(bf16[1024,1088]{0,1:T(8,128)(2,1)S(1)} %bitcast.159, f32[1024,4352]{1,0:T(8,128)} %fusion.50, f32[4352]{0:T(1024)S(1)} %copy-done.33), kind=kOutput, calls=%fused_computation.31 | convolution fusion | flops 9746530304 | bytes 29541376 | tf_op jit(solution)/shard_map/rf,rd->fd/dot_general | solution.py:142
  1084.2 17.2 reduce-scatter.7.cloned.1.call-done
  1109.9 69.0 %reduce-scatter.9.cloned.1.call-done = bf16[1,4,256,1088]{2,3,1,0:T(8,128)(2,1)} async-done(((bf16[4,4,256,1088]{2,3,1,0:T(8,128)(2,1)}), bf16[1,4,256,1088]{2,3,1,0:T(8,128)(2,1)}) %reduce-scatter.9.cloned.1.call-update) | async-done | bytes 2228240 | tf_op jit(solution)/shard_map/reduce_scatter | solution.py:223
  1187.3 15.6 convolution_convert_fusion.2
  1206.6 24.8 %reduce-scatter.13.cloned.1.call-done = bf16[272,1088]{1,0:T(8,128)(2,1)} async-done(((bf16[1088,1088]{1,0:T(8,128)(2,1)}), bf16[272,1088]{1,0:T(8,128)(2,1)}) %reduce-scatter.13.cloned.1.call-update) | async-done | bytes 591888 | tf_op jit(solution)/shard_map/reduce_scatter | solution.py:269
  1231.4 13.9 fusion.51
  1257.6 22.6 %all-reduce.19 = (bf16[1088]{0:T(1024)(128)(2,1)S(1)}, bf16[1088]{0:T(1024)(128)(2,1)S(1)}, bf16[1088]{0:T(1024)(128)(2,1)S(1)}, bf16[1088]{0:T(1024)(128)(2,1)S...) all-reduce(bf16[1088]{0:T(1024)(128)(2,1)S(1)} %dynamic-update-slic, ...), channel_id=1, replica_groups=mesh['dp'=2,'fsdp'=4,'ctx'=4] {'fsdp'}, use_global_device_ids=true, to_apply=%add.8 | all-reduce | flops 14144 | bytes 56576
  1280.2 23.1 %fusion.34 = bf16[1024,1088]{0,1:T(8,128)(2,1)S(1)} fusion(f32[1024,1088]{0,1:T(8,128)} %copy-done.9, bf16[4352,1088]{1,0:T(8,128)(2,1)} %all-gather.19.cloned.1.call-done, f32[1088]{0:T(1024)S(1)} %convert_element_type.193, f32[1024,4352]{1,0:T(8,128)} %fusion.50, f32[4352]{0:T(1024)S(1)} %copy-done.33), kind=kOutput, calls=%fused_computation.73 | convolution fusion | flops 9745137664 | bytes 34002176 | tf_op jit(solution)/shard_map/dot_general | solution.py:137
  1305.2 92.6 %reduce-scatter.15.cloned.1.call-done = bf16[272,4352]{1,0:T(8,128)(2,1)} async-done(((bf16[1088,4352]{1,0:T(8,128)(2,1)}), bf16[272,4352]{1,0:T(8,128)(2,1)}) %reduce-scatter.15.cloned.1.call-update) | async-done | bytes 2367504 | tf_op jit(solution)/shard_map/reduce_scatter | solution.py:281
  1397.8 174.1 %reduce-scatter.17.cloned.1.call-done = bf16[1088,1088]{1,0:T(8,128)(2,1)} async-done(((bf16[4352,1088]{1,0:T(8,128)(2,1)}), bf16[1088,1088]{1,0:T(8,128)(2,1)}) %reduce-scatter.17.cloned.1.call-update) | async-done | bytes 2367504 | tf_op jit(solution)/shard_map/reduce_scatter | solution.py:287
  1571.9 129.5 %reduce-scatter.11.cloned.1.call-done = bf16[272,3264]{1,0:T(8,128)(2,1)} async-done(((bf16[1088,3264]{1,0:T(8,128)(2,1)}), bf16[272,3264]{1,0:T(8,128)(2,1)}) %reduce-scatter.11.cloned.1.call-update) | async-done | bytes 1775632 | tf_op jit(solution)/shard_map/reduce_scatter | solution.py:260
  1701.4 288.8 %all-reduce.22 = (f32[272]{0:T(512)}, f32[272]{0:T(512)}, f32[272,3264]{1,0:T(8,128)}, f32[272]{0:T(512)}, f32[272]{0:T(512)}, /*index=5*/f32[272,1088]{1,0:T(8,...) all-reduce(f32[272]{0:T(512)S(1)} %get-tuple-element.307, ...), channel_id=1, replica_groups=mesh['dp'=2,'fsdp'=4,'ctx'=4] {'dp','ctx'}, use_global_device_ids=true, to_apply=%region_17.18 | all-reduce | flops 3554496 | bytes 21333504 | tf_op jit(solution)/shard_map/psum | solution.py:308
  (262 shorter events, 179.3 us)
Async XLA Ops:
  7.2 133.1 %all-gather.9.cloned.1.call-start = ((), (), s32[]{:S(2)}) async-start(), calls=%async_computation.6 | async-start | bytes 9052160 | tf_op jit(solution)/shard_map/all_gather | solution.py:69
  7.9 217.7 %all-gather.11.cloned.1.call-start = ((), (), s32[]{:S(2)}) async-start(), calls=%async_computation.7 | async-start | bytes 11141120 | tf_op jit(solution)/shard_map/all_gather | solution.py:87
  41.1 99.2 %copy-start.18 = (f32[1088]{0:T(1024)}, f32[1088]{0:T(1024)S(1)}, u32[]{:S(2)}) copy-start(f32[1088]{0:T(1024)S(1)} %convert_element_type.177) | copy-start | bytes 13060
  41.1 99.2 %copy-start.38 = (f32[1088]{0:T(1024)}, f32[1088]{0:T(1024)S(1)}, u32[]{:S(2)}) copy-start(f32[1088]{0:T(1024)S(1)} %convert_element_type.178) | copy-start | bytes 13060
  47.5 92.8 %copy-start.22 = (f32[1024]{0:T(1024)}, f32[1024]{0:T(1024)S(1)}, u32[]{:S(2)}) copy-start(f32[1024]{0:T(1024)S(1)} %rsqrt.20) | copy-start | bytes 12292
  47.5 92.8 %copy-start.24 = (f32[1,2,4,128]{3,1,2,0:T(2,128)}, f32[1,2,4,128]{3,1,2,0:T(2,128)S(1)}, u32[]{:S(2)}) copy-start(f32[1,2,4,128]{3,1,2,0:T(2,128)S(1)} %copy.92) | copy-start | bytes 12292
  162.0 131.7 %all-gather.13.cloned.1.call-start = ((), (), s32[]{:S(2)}) async-start(), calls=%async_computation.8 | async-start | bytes 11141120 | tf_op jit(solution)/shard_map/all_gather | solution.py:90
  170.0 172.9 %all-gather.15.cloned.1.call-start = ((), (), s32[]{:S(2)}) async-start(), calls=%async_computation.9 | async-start | bytes 3133440 | tf_op jit(solution)/shard_map/all_gather | solution.py:72
  170.6 338.6 %all-gather.17.cloned.1.call-start = ((), (), s32[]{:S(2)}) async-start(), calls=%async_computation.10 | async-start | bytes 11837440 | tf_op jit(solution)/shard_map/all_gather | solution.py:124
  171.2 514.1 %all-gather.19.cloned.1.call-start = ((), (), s32[]{:S(2)}) async-start(), calls=%async_computation.11 | async-start | bytes 12533760 | tf_op jit(solution)/shard_map/all_gather | solution.py:126
  171.7 577.9 %all-gather.23.cloned.1.call-start = ((), (), s32[]{:S(2)}) async-start(), calls=%async_computation.13 | async-start | bytes 11141120 | tf_op jit(solution)/shard_map/all_gather | solution.py:172
  178.2 5.9 copy-start.8
  178.2 634.5 %all-gather.21.cloned.1.call-start = ((), (), s32[]{:S(2)}) async-start(), calls=%async_computation.12 | async-start | bytes 11141120 | tf_op jit(solution)/shard_map/all_gather | solution.py:169
  195.3 906.1 %reduce-scatter.7.cloned.1.call-start = ((), (), s32[]{:S(2)}) async-start(), calls=%async_computation.14 | async-start | bytes 11141120 | tf_op jit(solution)/shard_map/reduce_scatter | solution.py:220
  338.7 10.4 copy-start.13
  349.2 160.0 %copy-start.30 = (f32[1088]{0:T(1024)S(1)}, f32[1088]{0:T(1024)}, u32[]{:S(2)}) copy-start(f32[1088]{0:T(1024)} %convert_element_type.188) | copy-start | bytes 13060
  349.2 160.0 %copy-start.40 = (f32[1088]{0:T(1024)S(1)}, f32[1088]{0:T(1024)}, u32[]{:S(2)}) copy-start(f32[1088]{0:T(1024)} %convert_element_type.189) | copy-start | bytes 13060
  349.2 381.9 %copy-start.28 = (f32[1024]{0:T(1024)}, f32[1024]{0:T(1024)S(1)}, u32[]{:S(2)}) copy-start(f32[1024]{0:T(1024)S(1)} %broadcast_multiply_fusion.1) | copy-start | bytes 12292
  351.3 379.9 %copy-start.35 = (f32[1024]{0:T(1024)}, f32[1024]{0:T(1024)S(1)}, u32[]{:S(2)}) copy-start(f32[1024]{0:T(1024)S(1)} %fusion.39) | copy-start | bytes 12292
  351.3 334.0 %copy-start.4 = (bf16[4,136,8,256]{3,2,0,1:T(8,128)(2,1)S(1)}, bf16[4,136,8,256]{3,2,0,1:T(8,128)(2,1)}, u32[]{:S(2)}) copy-start(bf16[4,136,8,256]{3,2,0,1:T(8,128)(2,1)} %copy.91) | copy-start | bytes 6684676
  351.3 334.0 %copy-start.32 = (f32[4352]{0:T(1024)S(1)}, f32[4352]{0:T(1024)}, u32[]{:S(2)}) copy-start(f32[4352]{0:T(1024)} %convert_element_type.191) | copy-start | bytes 52228
  712.2 18.9 copy-start.10
  732.3 3.6 copy-start.45
  746.4 66.3 %copy-start.17 = (f32[4,17,256]{2,1,0:T(8,128)S(1)}, f32[4,17,256]{2,1,0:T(8,128)}, u32[]{:S(2)}) copy-start(f32[4,17,256]{2,1,0:T(8,128)} %get-tuple-element.392) | copy-start | bytes 208900
  838.8 7.5 copy-start
  846.3 9.3 copy-start.2
  891.2 7.5 copy-start
  898.7 9.3 copy-start.2
  944.9 7.5 copy-start
  952.4 9.3 copy-start.2
  998.6 7.5 copy-start
  1006.0 9.3 copy-start.2
  1026.1 152.8 %reduce-scatter.9.cloned.1.call-start = ((), (), s32[]{:S(2)}) async-start(), calls=%async_computation.15 | async-start | bytes 11141120 | tf_op jit(solution)/shard_map/reduce_scatter | solution.py:223
  1026.7 7.5 copy-start.29
  1026.7 7.5 copy-start.31
  1026.7 7.5 copy-start.36
  1026.7 7.5 copy-start.41
  1026.8 204.7 %reduce-scatter.13.cloned.1.call-start = ((), (), s32[]{:S(2)}) async-start(), calls=%async_computation.17 | async-start | bytes 3133440 | tf_op jit(solution)/shard_map/reduce_scatter | solution.py:269
  1034.2 363.6 %reduce-scatter.15.cloned.1.call-start = ((), (), s32[]{:S(2)}) async-start(), calls=%async_computation.18 | async-start | bytes 11837440 | tf_op jit(solution)/shard_map/reduce_scatter | solution.py:281
  1053.9 518.0 %reduce-scatter.17.cloned.1.call-start = ((), (), s32[]{:S(2)}) async-start(), calls=%async_computation.19 | async-start | bytes 12533760 | tf_op jit(solution)/shard_map/reduce_scatter | solution.py:287
  1077.7 623.8 %reduce-scatter.11.cloned.1.call-start = ((), (), s32[]{:S(2)}) async-start(), calls=%async_computation.16 | async-start | bytes 9052160 | tf_op jit(solution)/shard_map/reduce_scatter | solution.py:260
  1109.9 77.4 %copy-start.19 = (f32[1088]{0:T(1024)S(1)}, f32[1088]{0:T(1024)}, u32[]{:S(2)}) copy-start(f32[1088]{0:T(1024)} %copy-done.18) | copy-start | bytes 13060
  1109.9 77.4 %copy-start.23 = (f32[1024]{0:T(1024)S(1)}, f32[1024]{0:T(1024)}, u32[]{:S(2)}) copy-start(f32[1024]{0:T(1024)} %copy-done.22) | copy-start | bytes 12292
  1109.9 77.4 %copy-start.25 = (f32[1,2,4,128]{3,1,2,0:T(2,128)S(1)}, f32[1,2,4,128]{3,1,2,0:T(2,128)}, u32[]{:S(2)}) copy-start(f32[1,2,4,128]{3,1,2,0:T(2,128)} %copy-done.24) | copy-start | bytes 12292
  1109.9 77.4 %copy-start.39 = (f32[1088]{0:T(1024)S(1)}, f32[1088]{0:T(1024)}, u32[]{:S(2)}) copy-start(f32[1088]{0:T(1024)} %copy-done.38) | copy-start | bytes 13060
  1206.6 38.7 %copy-start.27 = (f32[1,2,4,128]{3,1,2,0:T(2,128)S(1)}, f32[1,2,4,128]{3,1,2,0:T(2,128)}, u32[]{:S(2)}) copy-start(f32[1,2,4,128]{3,1,2,0:T(2,128)} %copy-done.26) | copy-start | bytes 12292
  1245.3 4.2 copy-start.21
  1303.3 398.1 %copy-start.16 = (bf16[272,1088]{1,0:T(8,128)(2,1)S(1)}, bf16[272,1088]{1,0:T(8,128)(2,1)}, u32[]{:S(2)}) copy-start(bf16[272,1088]{1,0:T(8,128)(2,1)} %reduce-scatter.13.cloned.1.call-done) | copy-start | bytes 1775620
  (21 other events, 48.7 us)
Sparse Core Ops, SparseCore 0:
  9.6 130.6 all-gather.8
  162.1 63.4 all-gather.10
  227.7 62.4 all-gather.12
  291.7 51.1 all-gather.14
  344.3 164.8 all-gather.16
  510.6 174.6 all-gather.18
  686.8 62.4 all-gather.22
  751.4 61.2 all-gather.20
  1026.2 75.0 reduce-scatter.6
  1103.8 75.0 reduce-scatter.8
  1181.8 49.5 reduce-scatter.12
  1233.7 164.0 reduce-scatter.14
  1400.3 171.5 reduce-scatter.16
  1574.2 127.1 reduce-scatter.10
where the time goes:
time: 2010 us; the launch traced here: 2000 us
  waiting for transfers between devices  1010 us (50%)
  matrix products  433 us (22%)
  blocking collectives  335 us (17%)
  local copies, waits for them, and re-layouts  136 us (7%)
  other arithmetic  58.5 us (3%)
    psum x1, blocking collectives, per_device(): lax.psum((gain_one_part, shift_one_part, in_part, qbias_part, vbias_part,...  289 us
    reduce_scatter x1, waiting for transfers between devices, per_device(): lax.psum_scatter(down_grad.astype(jnp.bfloat16), 'fsdp', scatter_dimensio...  174 us
    all_gather x1, waiting for transfers between devices, per_device(): lax.all_gather(up_weight, 'fsdp', axis=0, tiled=True)  158 us
    all_gather x1, waiting for transfers between devices, per_device(): lax.all_gather(down_weight, 'fsdp', axis=0, tiled=True)  156 us
    reduce_scatter x1, waiting for transfers between devices, per_device(): lax.psum_scatter(in_grad.astype(jnp.bfloat16), 'fsdp', scatter_dimension=...  130 us
    all_gather x1, waiting for transfers between devices, per_device(): lax.all_gather(project_in, 'fsdp', axis=0, tiled=True)  92.8 us
    reduce_scatter x1, waiting for transfers between devices, per_device(): lax.psum_scatter(up_grad.astype(jnp.bfloat16), 'fsdp', scatter_dimension=...  92.6 us
    reduce_scatter x1, waiting for transfers between devices, per_device(): lax.psum_scatter(value_terms.astype(jnp.bfloat16), 'ctx', scatter_dimensi...  69 us
  transfers between devices with their start and end apart: 14, of which 12 were waited for; matrix products, arithmetic and copies ran while one was open for 19% of the time, Pallas kernels for 0%

commit v1 on v0

--- a/solution.py
+++ b/solution.py
@@ -1,6 +1,10 @@
+import functools
+
 import jax
 import jax.numpy as jnp
 from jax import lax
+from jax.experimental import pallas as pl
+from jax.experimental.pallas import tpu as pltpu
 from jax.sharding import PartitionSpec as P
 
 HEADS = 17
@@ -38,7 +42,7 @@
     return (weights.astype(jnp.bfloat16), score_low)
 
 
-def per_device(
+def per_device_gathered(
     inputs,
     cotangent,
     first_gain,
@@ -342,7 +346,584 @@
     )
 
 
+NT = (((1,), (1,)), ((), ()))
+PAIR = 2 * HEAD_DIM
+
+
+def attend_kernel(place_ref, q_ref, k_ref, v_ref, o_ref, log_ref, keys, values, *, count, width):
+    pair = pl.program_id(0)
+    shift = place_ref[0]
+    block_len = q_ref.shape[0] // count
+    lane = lax.broadcasted_iota(jnp.int32, (1, PAIR), 1)
+    valid = lane + pair * PAIR < width
+    first = lane < HEAD_DIM
+
+    def rows(block):
+        return pl.ds(pl.multiple_of((block ^ shift) * block_len, block_len), block_len)
+
+    for block in range(count):
+        here = pl.ds(block * block_len, block_len)
+        keys[here, :] = jnp.where(valid, k_ref[rows(block), :], 0)
+        values[here, :] = jnp.where(valid, v_ref[rows(block), :], 0)
+    diagonal = lax.broadcasted_iota(jnp.int32, (block_len, block_len), 0) >= (
+        lax.broadcasted_iota(jnp.int32, (block_len, block_len), 1)
+    )
+    for block in range(count):
+        seen = (block + 1) * block_len
+        before = block * block_len
+        queries = q_ref[rows(block), :] * jnp.bfloat16(HEAD_DIM**-0.5)
+        parts = []
+        logs = log_ref[rows(block), :]
+        for half in range(2):
+            pick = jnp.logical_and(first if half == 0 else jnp.logical_not(first), valid)
+            scores = lax.dot_general(
+                jnp.where(pick, queries, 0),
+                keys[pl.ds(0, seen), :],
+                NT,
+                preferred_element_type=jnp.float32,
+            )
+            last = jnp.where(diagonal, scores[:, before:], -1e30)
+            scores = last if block == 0 else jnp.concatenate([scores[:, :before], last], axis=1)
+            top = jnp.max(scores, axis=1, keepdims=True)
+            weights = jnp.exp(scores - top)
+            total = jnp.sum(weights, axis=1, keepdims=True)
+            added = jnp.dot(
+                weights.astype(jnp.bfloat16),
+                values[pl.ds(0, seen), :],
+                preferred_element_type=jnp.float32,
+            )
+            parts.append(added / total)
+            logs = jnp.where(lane == 2 * pair + half, top + jnp.log(total), logs)
+        o_ref[rows(block), :] = jnp.where(first, parts[0], parts[1]).astype(jnp.bfloat16)
+        log_ref[rows(block), :] = logs
+
+
+def attend_back_kernel(
+    place_ref,
+    q_ref,
+    k_ref,
+    v_ref,
+    g_ref,
+    o_ref,
+    log_ref,
+    dq_ref,
+    dk_ref,
+    dv_ref,
+    queries,
+    grads,
+    keys,
+    values,
+    keys_turned,
+    logs,
+    deltas,
+    turned,
+    *,
+    count,
+    width,
+):
+    pair = pl.program_id(0)
+    shift = place_ref[0]
+    length = q_ref.shape[0]
+    block_len = length // count
+    lane = lax.broadcasted_iota(jnp.int32, (1, PAIR), 1)
+    valid = lane + pair * PAIR < width
+    first = lane < HEAD_DIM
+    picks = (jnp.logical_and(first, valid), jnp.logical_and(jnp.logical_not(first), valid))
+    half_of = (lax.broadcasted_iota(jnp.int32, (8, PAIR), 1) // HEAD_DIM) == (
+        lax.broadcasted_iota(jnp.int32, (8, PAIR), 0)
+    )
+    ones_of = jnp.where(half_of, 1.0, 0.0)
+
+    def rows(block):
+        return pl.ds(pl.multiple_of((block ^ shift) * block_len, block_len), block_len)
+
+    for block in range(count):
+        here = pl.ds(block * block_len, block_len)
+        key_block = jnp.where(valid, k_ref[rows(block), :], 0)
+        keys[here, :] = key_block
+        keys_turned[:, here] = key_block.astype(jnp.float32).T.astype(jnp.bfloat16)
+        values[here, :] = jnp.where(valid, v_ref[rows(block), :], 0)
+        query_block = q_ref[rows(block), :] * jnp.bfloat16(HEAD_DIM**-0.5)
+        grad_block = jnp.where(valid, g_ref[rows(block), :], 0)
+        for half in range(2):
+            queries[half, here, :] = jnp.where(picks[half], query_block, 0)
+            grads[half, here, :] = jnp.where(picks[half], grad_block, 0)
+        mixed = grad_block.astype(jnp.float32) * jnp.where(
+            valid, o_ref[rows(block), :], 0
+        ).astype(jnp.float32)
+        deltas[:, here] = lax.dot_general(
+            ones_of,
+            mixed,
+            NT,
+            preferred_element_type=jnp.float32,
+            precision=lax.Precision.HIGHEST,
+        )
+        logs[:, here] = log_ref[
+            0, :, pl.ds(pl.multiple_of((block ^ shift) * block_len, block_len), block_len)
+        ]
+    diagonal = lax.broadcasted_iota(jnp.int32, (block_len, block_len), 0) <= (
+        lax.broadcasted_iota(jnp.int32, (block_len, block_len), 1)
+    )
+    for block in range(count):
+        here = pl.ds(block * block_len, block_len)
+        after = pl.ds(block * block_len, length - block * block_len)
+        key_total = jnp.zeros((block_len, PAIR), jnp.float32)
+        value_total = jnp.zeros((block_len, PAIR), jnp.float32)
+        for half in range(2):
+            scores = lax.dot_general(
+                keys[here, :], queries[half, after, :], NT, preferred_element_type=jnp.float32
+            )
+            shifted = scores - logs[half : half + 1, after]
+            own = jnp.where(diagonal, shifted[:, :block_len], -1e30)
+            if block < count - 1:
+                own = jnp.concatenate([own, shifted[:, block_len:]], axis=1)
+            weights = jnp.exp(own)
+            pressure = lax.dot_general(
+                values[here, :], grads[half, after, :], NT, preferred_element_type=jnp.float32
+            )
+            score_low = (weights * (pressure - deltas[half : half + 1, after])).astype(
+                jnp.bfloat16
+            )
+            value_total += jnp.dot(
+                weights.astype(jnp.bfloat16),
+                grads[half, after, :],
+                preferred_element_type=jnp.float32,
+            )
+            key_total += jnp.dot(
+                score_low, queries[half, after, :], preferred_element_type=jnp.float32
+            )
+            part = pl.ds(half * HEAD_DIM, HEAD_DIM)
+            term = jnp.dot(
+                keys_turned[part, here], score_low, preferred_element_type=jnp.float32
+            )
+            if block == 0:
+                turned[part, after] = term
+            else:
+                turned[part, after] += term
+        dk_ref[rows(block), :] = key_total.astype(jnp.bfloat16)
+        dv_ref[rows(block), :] = value_total.astype(jnp.bfloat16)
+    for block in range(count):
+        here = pl.ds(block * block_len, block_len)
+        dq_ref[rows(block), :] = (turned[:, here].T * HEAD_DIM**-0.5).astype(jnp.bfloat16)
+
+
+def attend(place, queries, key_rows, value_rows, count):
+    length, width = queries.shape
+    pairs = pl.cdiv(width, PAIR)
+    heads_block = pl.BlockSpec((length, PAIR), lambda pair, place_ref: (0, pair))
+    return pl.pallas_call(
+        functools.partial(attend_kernel, count=count, width=width),
+        grid_spec=pltpu.PrefetchScalarGridSpec(
+            num_scalar_prefetch=1,
+            grid=(pairs,),
+            in_specs=[heads_block] * 3,
+            out_specs=[
+                heads_block,
+                pl.BlockSpec((length, 128), lambda pair, place_ref: (0, 0)),
+            ],
+            scratch_shapes=[pltpu.VMEM((length, PAIR), jnp.bfloat16)] * 2,
+        ),
+        out_shape=[
+            jax.ShapeDtypeStruct((length, width), jnp.bfloat16),
+            jax.ShapeDtypeStruct((length, 128), jnp.float32),
+        ],
+        compiler_params=pltpu.CompilerParams(vmem_limit_bytes=48 * 2**20),
+        cost_estimate=pl.CostEstimate(
+            flops=4 * length * length * width,
+            bytes_accessed=8 * length * width,
+            transcendentals=HEADS * length * length // 2,
+        ),
+        name="attend",
+    )(place, queries, key_rows, value_rows)
+
+
+def attend_back(place, queries, key_rows, value_rows, grads, attended, logs, count):
+    length, width = queries.shape
+    pairs = pl.cdiv(width, PAIR)
+    heads_block = pl.BlockSpec((length, PAIR), lambda pair, place_ref: (0, pair))
+    low_rows = pltpu.VMEM((length, PAIR), jnp.bfloat16)
+    low_pair = pltpu.VMEM((2, length, PAIR), jnp.bfloat16)
+    return pl.pallas_call(
+        functools.partial(attend_back_kernel, count=count, width=width),
+        grid_spec=pltpu.PrefetchScalarGridSpec(
+            num_scalar_prefetch=1,
+            grid=(pairs,),
+            in_specs=[heads_block] * 5
+            + [pl.BlockSpec((1, 2, length), lambda pair, place_ref: (pair, 0, 0))],
+            out_specs=[heads_block] * 3,
+            scratch_shapes=[
+                low_pair,
+                low_pair,
+                low_rows,
+                low_rows,
+                pltpu.VMEM((PAIR, length), jnp.bfloat16),
+                pltpu.VMEM((2, length), jnp.float32),
+                pltpu.VMEM((8, length), jnp.float32),
+                pltpu.VMEM((PAIR, length), jnp.float32),
+            ],
+        ),
+        out_shape=[jax.ShapeDtypeStruct((length, width), jnp.bfloat16)] * 3,
+        compiler_params=pltpu.CompilerParams(vmem_limit_bytes=48 * 2**20),
+        cost_estimate=pl.CostEstimate(
+            flops=10 * length * length * width,
+            bytes_accessed=16 * length * width,
+            transcendentals=HEADS * length * length // 2,
+        ),
+        name="attend_back",
+    )(place, queries, key_rows, value_rows, grads, attended, logs)
+
+
+def settle_kernel(place_ref, *refs):
+    pieces, out_ref = refs[:-1], refs[-1]
+    for at, piece in enumerate(pieces):
+        out_ref[place_ref[at]] = piece[...].astype(out_ref.dtype)
+
+
+def settle(places, pieces, dtype):
+    return pl.pallas_call(
+        settle_kernel,
+        in_specs=[pl.BlockSpec(memory_space=pltpu.SMEM)]
+        + [pl.BlockSpec(memory_space=pltpu.VMEM)] * len(pieces),
+        out_specs=pl.BlockSpec(memory_space=pltpu.VMEM),
+        out_shape=jax.ShapeDtypeStruct((len(pieces),) + pieces[0].shape, dtype),
+        compiler_params=pltpu.CompilerParams(vmem_limit_bytes=48 * 2**20),
+        name="settle",
+    )(places, *pieces)
+
+
+def plane_partner(device, kind):
+    core = device & 1
+    if kind == "core":
+        return device ^ 1
+    if kind == "near":
+        return device ^ (2 if core else 4)
+    return device ^ (4 if core else 2)
+
+
+def plane_swap(values, kind):
+    return lax.ppermute(
+        values, ("dp", "ctx"), [(device, plane_partner(device, kind)) for device in range(8)]
+    )
+
+
+def ctx_swap(values, bits):
+    return lax.ppermute(values, "ctx", [(device, device ^ bits) for device in range(4)])
+
+
+def gather_piece(piece):
+    own = lax.all_gather(piece, "fsdp", axis=0, tiled=True)
+    near = plane_swap(own, "near")
+    return [own, near, plane_swap(own, "core"), plane_swap(near, "core")]
+
+
+def reduce_pieces(pieces):
+    far_two = plane_swap(pieces[3], "core")
+    far = plane_swap(pieces[2], "core")
+    second = (pieces[1].astype(jnp.float32) + far_two.astype(jnp.float32)).astype(jnp.bfloat16)
+    near = plane_swap(second, "near")
+    first = (
+        pieces[0].astype(jnp.float32) + far.astype(jnp.float32) + near.astype(jnp.float32)
+    ).astype(jnp.bfloat16)
+    shard = lax.psum_scatter(first, "fsdp", scatter_dimension=0, tiled=True)
+    whole = (shard.astype(jnp.float32) + plane_swap(shard, "other").astype(jnp.float32)).astype(
+        jnp.bfloat16
+    )
+    beside = plane_swap(whole, "near")
+    return [whole, beside, plane_swap(whole, "core"), plane_swap(beside, "core")]
+
+
+def chosen(index, options):
+    result = options[-1]
+    for at in range(len(options) - 2, -1, -1):
+        result = jnp.where(index == at, options[at], result)
+    return result
+
+
+def gather_vector(values, z):
+    around = [values] + [
+        lax.ppermute(values, "fsdp", [(device, (device + step) % 4) for device in range(4)])
+        for step in range(1, 4)
+    ]
+    return jnp.stack([chosen((z - at) % 4, around) for at in range(4)])
+
+
+def reduce_vector(values, z):
+    rows = [values[at] for at in range(4)]
+    total = chosen(z, rows)
+    for step in range(1, 4):
+        total = total + lax.ppermute(
+            chosen((z + step) % 4, rows),
+            "fsdp",
+            [(device, (device + step) % 4) for device in range(4)],
+        )
+    for bits in (1, 2, 4):
+        total = total + lax.ppermute(
+            total, ("dp", "ctx"), [(device, device ^ bits) for device in range(8)]
+        )
+    return total
+
+
+def normalised(values):
+    centred = values - jnp.mean(values, axis=-1, keepdims=True)
+    scale = lax.rsqrt(jnp.mean(centred * centred, axis=-1, keepdims=True) + epsilon)
+    return centred * scale, scale
+
+
+def norm_back(values, gain, grad):
+    unit, scale = normalised(values)
+    turned = grad * gain
+    inner = (
+        turned
+        - jnp.mean(turned, axis=-1, keepdims=True)
+        - unit * jnp.mean(turned * unit, axis=-1, keepdims=True)
+    )
+    return scale * inner, jnp.sum(grad * unit, axis=0), jnp.sum(grad, axis=0)
+
+
+def product(left, right, dims):
+    return lax.dot_general(left, right, ((dims[:1], dims[1:]), ((), ())),
+                           preferred_element_type=jnp.float32)
+
+
+def gelu_pair(values):
+    inner = 0.7978845608028654
+    squared = values * values
+    curve = jnp.tanh(inner * (values + 0.044715 * values * squared))
+    active = 0.5 * values * (1.0 + curve)
+    slope = 0.5 * (1.0 + curve) + 0.5 * values * (1.0 - curve * curve) * inner * (
+        1.0 + 3.0 * 0.044715 * squared
+    )
+    return active, slope
+
+
+def per_device_exchanged(
+    inputs,
+    cotangent,
+    first_gain,
+    first_shift,
+    project_in,
+    query_bias,
+    value_bias,
+    project_out,
+    output_bias,
+    second_gain,
+    second_shift,
+    up_weight,
+    up_bias,
+    down_weight,
+    down_bias,
+):
+    seq_count, block_len, width = inputs.shape
+    low = jnp.bfloat16
+    wide = jnp.float32
+    c = lax.axis_index("ctx")
+    y = lax.axis_index("dp")
+    z = lax.axis_index("fsdp")
+    core = c & 1
+    x = c >> 1
+    mine = core * 2 + jnp.where(core == 0, y, x)
+    across = (1 - core) * 2 + jnp.where(core == 0, x, y)
+    classes = [mine, mine ^ 1, across, across ^ 1]
+    slot_of = [
+        chosen(0, [sum(at * (classes[at] == kind).astype(jnp.int32) for at in range(4))])
+        for kind in range(4)
+    ]
+    quarter = width // 4
+    place = jnp.stack([c])
+    places = jnp.stack([c ^ at for at in range(4)])
+    class_places = jnp.stack(classes)
+
+    def spread(values):
+        return jnp.concatenate(
+            [lax.dynamic_index_in_dim(values, c, 0, keepdims=False)]
+            + [
+                ctx_swap(lax.dynamic_index_in_dim(values, c ^ bits, 0, keepdims=False), bits)
+                for bits in range(1, 4)
+            ],
+            axis=0,
+        )
+
+    def collect(rows, dtype):
+        pieces = [rows[at * block_len : (at + 1) * block_len].astype(low) for at in range(4)]
+        moved = [pieces[0]] + [ctx_swap(pieces[bits], bits) for bits in range(1, 4)]
+        return settle(places, moved, dtype)
+
+    sections = [
+        project_in[:, :width],
+        project_in[:, width : 2 * width],
+        project_in[:, 2 * width :],
+        project_out,
+    ]
+    attend_slots = gather_piece(chosen(mine, sections))
+    up_piece = jnp.concatenate(
+        [
+            lax.dynamic_slice_in_dim(up_weight, at * width + mine * quarter, quarter, 1)
+            for at in range(4)
+        ],
+        axis=1,
+    )
+    up_slots = gather_piece(up_piece)
+    down_slots = gather_piece(lax.dynamic_slice_in_dim(down_weight, mine * quarter, quarter, 0))
+    vectors = gather_vector(
+        jnp.concatenate(
+            [
+                first_gain,
+                first_shift,
+                query_bias,
+                value_bias,
+                output_bias,
+                second_gain,
+                second_shift,
+                down_bias,
+                up_bias,
+            ]
+        ),
+        z,
+    ).astype(wide)
+    gain_first, shift_first, qbias, vbias, obias, gain_second, shift_second, dbias = (
+        vectors[:, at * quarter : (at + 1) * quarter].reshape(width) for at in range(8)
+    )
+    ubias = vectors[:, 8 * quarter :].reshape(4, 4, quarter)
+
+    rows_in = spread(inputs)
+    wide_in = rows_in.astype(wide)
+    unit, _ = normalised(wide_in)
+    normed_low = (unit * gain_first + shift_first).astype(low)
+    weights = settle(class_places, attend_slots, low)
+    queries = (product(normed_low, weights[0], (1, 0)) + qbias).astype(low)
+    key_rows = product(normed_low, weights[1], (1, 0)).astype(low)
+    value_rows = (product(normed_low, weights[2], (1, 0)) + vbias).astype(low)
+    attended, logs = attend(place, queries, key_rows, value_rows, seq_count)
+    logs = logs.T.reshape(64, 2, seq_count * block_len)
+    middle = wide_in + product(attended, weights[3], (1, 0)) + obias
+    unit_two, _ = normalised(middle)
+    normed_two_low = (unit_two * gain_second + shift_second).astype(low)
+    active, slopes = [], []
+    for slot in range(4):
+        bias = chosen(classes[slot], [ubias[:, kind] for kind in range(4)]).reshape(width)
+        hidden = product(normed_two_low, up_slots[slot], (1, 0)) + bias
+        value, slope = gelu_pair(hidden)
+        active.append(value.astype(low))
+        slopes.append(slope.astype(low))
+    result = middle + dbias
+    for slot in range(4):
+        result = result + product(active[slot], down_slots[slot], (1, 0))
+    outputs = collect(result, low)
+
+    upstream_low = spread(cotangent)
+    upstream = upstream_low.astype(wide)
+    down_parts = reduce_pieces(
+        [product(active[slot], upstream_low, (0, 0)).astype(low) for slot in range(4)]
+    )
+    hidden_low = [
+        (product(upstream_low, down_slots[slot], (1, 1)) * slopes[slot].astype(wide)).astype(low)
+        for slot in range(4)
+    ]
+    up_parts = reduce_pieces(
+        [product(normed_two_low, hidden_low[slot], (0, 0)).astype(low) for slot in range(4)]
+    )
+    normed_two_grad = sum(product(hidden_low[slot], up_slots[slot], (1, 1)) for slot in range(4))
+    middle_part, gain_two_grad, shift_two_grad = norm_back(middle, gain_second, normed_two_grad)
+    middle_grad = upstream + middle_part
+    middle_low = middle_grad.astype(low)
+    grad_low = product(middle_low, weights[3], (1, 1)).astype(low)
+    query_low, key_low, value_low = attend_back(
+        place, queries, key_rows, value_rows, grad_low, attended, logs, seq_count
+    )
+    section_grads = [
+        product(normed_low, query_low, (0, 0)).astype(low),
+        product(normed_low, key_low, (0, 0)).astype(low),
+        product(normed_low, value_low, (0, 0)).astype(low),
+        product(attended, middle_low, (0, 0)).astype(low),
+    ]
+    section_parts = reduce_pieces([chosen(kind, section_grads) for kind in classes])
+    normed_grad = (
+        product(query_low, weights[0], (1, 1))
+        + product(key_low, weights[1], (1, 1))
+        + product(value_low, weights[2], (1, 1))
+    )
+    input_part, gain_one_grad, shift_one_grad = norm_back(wide_in, gain_first, normed_grad)
+    input_gradient = collect(middle_grad + input_part, wide)
+
+    def column_sum(values):
+        return jnp.sum(values.astype(wide), axis=0)
+
+    hidden_sums = [column_sum(hidden_low[slot]).reshape(4, quarter) for slot in range(4)]
+    hidden_sums = jnp.stack(
+        [chosen(slot_of[kind], hidden_sums) for kind in range(4)], axis=1
+    ).reshape(4, 4 * quarter)
+    early = reduce_vector(
+        jnp.concatenate(
+            [
+                values.reshape(4, quarter)
+                for values in (
+                    column_sum(middle_low),
+                    gain_two_grad,
+                    shift_two_grad,
+                    column_sum(upstream_low),
+                )
+            ]
+            + [hidden_sums],
+            axis=1,
+        ),
+        z,
+    )
+    late = reduce_vector(
+        jnp.concatenate(
+            [
+                values.reshape(4, quarter)
+                for values in (
+                    gain_one_grad,
+                    shift_one_grad,
+                    column_sum(query_low),
+                    column_sum(value_low),
+                )
+            ],
+            axis=1,
+        ),
+        z,
+    )
+    obias_sum, gain_two_sum, shift_two_sum, dbias_sum = (
+        early[at * quarter : (at + 1) * quarter] for at in range(4)
+    )
+    ubias_sum = early[4 * quarter :]
+    gain_one_sum, shift_one_sum, qbias_sum, vbias_sum = (
+        late[at * quarter : (at + 1) * quarter] for at in range(4)
+    )
+    in_parts = [chosen(slot_of[kind], section_parts).astype(wide) for kind in range(4)]
+    up_parts = [chosen(slot_of[kind], up_parts) for kind in range(4)]
+    up_sum = jnp.concatenate(
+        [
+            up_parts[kind][:, at * quarter : (at + 1) * quarter]
+            for at in range(4)
+            for kind in range(4)
+        ],
+        axis=1,
+    ).astype(wide)
+    down_sum = settle(class_places, down_parts, wide).reshape(down_weight.shape)
+    return (
+        outputs,
+        input_gradient,
+        gain_one_sum,
+        shift_one_sum,
+        jnp.concatenate(in_parts[:3], axis=1),
+        qbias_sum,
+        vbias_sum,
+        in_parts[3],
+        obias_sum,
+        gain_two_sum,
+        shift_two_sum,
+        up_sum,
+        ubias_sum,
+        down_sum,
+        dbias_sum,
+    )
+
+
 def solution(mesh):
+    sizes = dict(mesh.shape)
+    exchanged = sizes["dp"] == 2 and sizes["fsdp"] == 4 and sizes["ctx"] == 4
+    per_device = per_device_exchanged if exchanged else per_device_gathered
     return jax.shard_map(
         per_device,
         mesh=mesh,

time: 2010 us -> 787 us (0.39)
  waiting for transfers between devices: 1010 us -> 216 us
  blocking collectives: 335 us -> 0 us
  matrix products: 433 us -> 261 us
  Pallas kernels: 0 us -> 94 us
  local copies, waits for them, and re-layouts: 136 us -> 80.8 us
  starting transfers between devices: 0.97 us -> 51.4 us
    reduce_scatter x6 -> x3, waiting for transfers between devices: 507 us -> 27.2 us  [reduce_pieces(): shard = lax.psum_scatter(first, 'fsdp', scatter_dimension=0, tiled=True)]
    all_gather x8 -> x3, waiting for transfers between devices: 504 us -> 83.5 us  [gather_piece(): own = lax.all_gather(piece, 'fsdp', axis=0, tiled=True)]
    psum x1 -> x0, blocking collectives: 289 us -> none  [per_device(): lax.psum((gain_one_part, shift_one_part, in_part, qbias_part, vbias_part,...]
    dot_general x34 -> x36, matrix products: 433 us -> 261 us  [product(): lax.dot_general(left, right, ((dims[:1], dims[1:]), ((), ())), preferred_...]
    ppermute x0 -> x57, waiting for transfers between devices: none -> 105 us  [the longest x12 85.3 us: ctx_swap(): lax.ppermute(values, 'ctx', [(device, device ^ bits) for device in range(...]
    pallas_call x0 -> x6, Pallas kernels: none -> 94 us  [the longest x1 45.9 us: attend_back(): pl.pallas_call(functools.partial(attend_back_kernel, count=count, width=w...]
    ppermute x0 -> x57, starting transfers between devices: none -> 50.7 us  [the longest x30 20.3 us: plane_swap(): lax.ppermute(values, ('dp', 'ctx'), [(device, plane_partner(device, kind)...]
    unnamed x2 -> x0, blocking collectives: 46 us -> none
  transfers between devices with their start and end apart: 14 -> 63, of which waited for: 12 -> 15; matrix products, arithmetic and copies ran while one was open for 19% -> 43% of each run, Pallas kernels for 0% -> 6%
where the time goes in v1:
time: 787 us; the launch traced here: 777 us
  matrix products  261 us (33%)
  waiting for transfers between devices  216 us (27%)
  Pallas kernels  94 us (12%)
  local copies, waits for them, and re-layouts  80.8 us (10%)
  other arithmetic  58 us (7%)
  starting transfers between devices  51.4 us (7%)
  between operations  16 us (2%)
    dot_general x36, matrix products, product(): lax.dot_general(left, right, ((dims[:1], dims[1:]), ((), ())), preferred_...  261 us
    ppermute x12, waiting for transfers between devices, ctx_swap(): lax.ppermute(values, 'ctx', [(device, device ^ bits) for device in range(...  85.3 us
    all_gather x3, waiting for transfers between devices, gather_piece(): own = lax.all_gather(piece, 'fsdp', axis=0, tiled=True)  83.5 us
    pallas_call x1, Pallas kernels, attend_back(): pl.pallas_call(functools.partial(attend_back_kernel, count=count, width=w...  45.9 us
    pallas_call x1, Pallas kernels, attend(): pl.pallas_call(functools.partial(attend_kernel, count=count, width=width)...  32.5 us
    reduce_scatter x3, waiting for transfers between devices, reduce_pieces(): shard = lax.psum_scatter(first, 'fsdp', scatter_dimension=0, tiled=True)  27.2 us
    ppermute x12, local copies, waits for them, and re-layouts, ctx_swap(): lax.ppermute(values, 'ctx', [(device, device ^ bits) for device in range(...  22 us
    ppermute x30, starting transfers between devices, plane_swap(): lax.ppermute(values, ('dp', 'ctx'), [(device, plane_partner(device, kind)...  20.3 us
  transfers between devices with their start and end apart: 63, of which 15 were waited for; matrix products, arithmetic and copies ran while one was open for 43% of the time, Pallas kernels for 6%

profile of v1, /device:TPU:8, one launch (start us, length us, event | category | flops | bytes accessed | tf_op | source)
XLA Modules:
  0.0 777.4 jit_solution(2862407436053730028)
XLA Ops:
  14.4 48.4 %all-gather.4.cloned.1.call-done.refs_0_ = bf16[1088,1088]{1,0:T(8,128)(2,1)} async-done(((bf16[272,1088]{1,0:T(8,128)(2,1)}), bf16[1088,1088]{1,0:T(8,128)(2,1)}) %all-gather.4.cloned.1.call-update) | async-done | bytes 2367504 | tf_op jit(solution)/shard_map/all_gather | solution.py:614
  76.0 39.9 %collective-permute-done.2 = bf16[256,1088]{0,1:T(8,128)(2,1)S(1)} collective-permute-done((bf16[256,1088]{0,1:T(8,128)(2,1)}, bf16[256,1088]{0,1:T(8,128)(2,1)S(1)}, u32[]{:S(2)}, u32[]{:S(2)}) %collective-permute-start.2) | collective-permute-done | bytes 557088 | tf_op jit(solution)/shard_map/ppermute | solution.py:610
  124.3 9.6 %collective-permute-done.20 = bf16[256,1088]{0,1:T(8,128)(2,1)} collective-permute-done((bf16[256,1088]{0,1:T(8,128)(2,1)}, bf16[256,1088]{0,1:T(8,128)(2,1)}, u32[]{:S(2)}, u32[]{:S(2)}) %collective-permute-start.20) | collective-permute-done | bytes 557088 | tf_op jit(solution)/shard_map/ppermute | solution.py:610
  135.4 35.1 %all-gather.6.cloned.1.call-done = bf16[1088,1088]{1,0:T(8,128)(2,1)} async-done(((bf16[272,1088]{1,0:T(8,128)(2,1)}), bf16[1088,1088]{1,0:T(8,128)(2,1)}) %all-gather.6.cloned.1.call-update) | async-done | bytes 2367504 | tf_op jit(solution)/shard_map/all_gather | solution.py:614
  195.9 5.3 collective-permute-done.9
  201.3 7.8 %settle.4 = bf16[4,1088,1088]{2,1,0:T(8,128)(2,1)} custom-call(s32[4]{0:T(128)S(1)} %pad_add_fusion.1.place_ref, bf16[1088,1088]{1,0:T(8,128)(2,1)S(1)} %copy-done.3, bf16[1088,1088]{1,0:T(8,128)(2,1)} %collective-permute-done.6.refs_1_, bf16[1088,1088]{1,0:T(8,128)(2,1)} %collective-permute-done.7.refs_2_, bf16[1088,1088]{1,0:T(8,128)(2,1)} %collective-permute-done.8.refs_3_), custom_call_target="tpu_custom_call" | custom-call | tf_op jit(solution)/shard_map/settle/pallas_call | solution.py:583
  209.1 6.6 convolution_convert_fusion.13.k_ref
  219.4 4.8 add_convert_fusion.6.v_ref
  224.2 32.5 %attend.1 = (bf16[1024,1088]{1,0:T(8,128)(2,1)S(1)}, f32[1024,128]{1,0:T(8,128)S(1)}) custom-call(s32[1]{0:T(128)} %bitcast.place_ref, bf16[1024,1088]{1,0:T(8,128)(2,1)S(1)} %add_convert_fusion.7.q_ref, bf16[1024,1088]{1,0:T(8,128)(2,1)} %convolution_convert_fusion.13.k_ref, bf16[1024,1088]{1,0:T(8,128)(2,1)} %add_convert_fusion.6.v_ref), custom_call_target="tpu_custom_call" | custom-call | flops 4563402752 | bytes 8912896 | tf_op jit(solution)/shard_map/attend/pallas_call | solution.py:514
  256.7 6.2 fusion.58
  264.3 5.8 convolution_add_fusion.2
  270.1 6.5 convolution_add_fusion.3
  276.7 6.7 convolution_add_fusion.1
  283.5 11.0 %convert_reduce_fusion.8 = (f32[1088]{0:T(1024)}, bf16[1024,1088]{0,1:T(8,128)(2,1)S(1)}) fusion(f32[1024,1088]{0,1:T(8,128)S(1)} %convolution_add_fusion.3, bf16[1088,1088]{1,0:T(8,128)(2,1)} %all-gather.8.cloned.1.call-done, bf16[256,1088]{1,0:T(8,128)(2,1)S(1)} %copy-done.38, bf16[256,1088]{1,0:T(8,128)(2,1)S(1)} %copy-done.41, ...), kind=kOutput, calls=%fused_computation.69 | convolution fusion | flops 2457730048 | bytes 11284736 | tf_op jit(solution)/shard_map/dot_general | solution.py:684
  294.6 10.3 %convert_reduce_fusion.7 = (f32[1088]{0:T(1024)}, bf16[1024,1088]{0,1:T(8,128)(2,1)S(1)}) fusion(f32[1024,1088]{0,1:T(8,128)S(1)} %convolution_add_fusion.2, bf16[1088,1088]{1,0:T(8,128)(2,1)} %collective-permute-done.10, bf16[256,1088]{1,0:T(8,128)(2,1)S(1)} %copy-done.38, bf16[256,1088]{1,0:T(8,128)(2,1)S(1)} %copy-done.41, ...), kind=kOutput, calls=%fused_computation.68 | convolution fusion | flops 2457730048 | bytes 11284736 | tf_op jit(solution)/shard_map/dot_general | solution.py:684
  304.9 10.3 %convert_reduce_fusion.6 = (f32[1088]{0:T(1024)}, bf16[1024,1088]{0,1:T(8,128)(2,1)S(1)}) fusion(f32[1024,1088]{0,1:T(8,128)S(1)} %convolution_add_fusion.1, bf16[1088,1088]{1,0:T(8,128)(2,1)} %collective-permute-done.12, bf16[256,1088]{1,0:T(8,128)(2,1)S(1)} %copy-done.38, bf16[256,1088]{1,0:T(8,128)(2,1)S(1)} %copy-done.41, ...), kind=kOutput, calls=%fused_computation.67 | convolution fusion | flops 2457730048 | bytes 11284736 | tf_op jit(solution)/shard_map/dot_general | solution.py:684
  315.2 7.7 fusion.61
  322.9 7.0 fusion.59
  329.9 7.0 fusion.60
  340.1 11.4 %convert_reduce_fusion.5 = (f32[1088]{0:T(1024)}, bf16[1024,1088]{0,1:T(8,128)(2,1)S(1)}) fusion(f32[1024,1088]{0,1:T(8,128)S(1)} %convolution_add_fusion, bf16[1088,1088]{1,0:T(8,128)(2,1)} %collective-permute-done.14, bf16[256,1088]{1,0:T(8,128)(2,1)S(1)} %copy-done.38, bf16[256,1088]{1,0:T(8,128)(2,1)S(1)} %copy-done.41, ...), kind=kOutput, calls=%fused_computation.66 | convolution fusion | flops 2457730048 | bytes 11284736 | tf_op jit(solution)/shard_map/dot_general | solution.py:684
  351.5 9.9 %multiply_reduce_fusion = (f32[1088]{0:T(1024)}, f32[1024]{0:T(1024)S(1)}, f32[1024]{0:T(1024)S(1)}, f32[1088]{0:T(1024)}, f32[1024,1088]{1,0:T(8,128)S(1)}) fusion(f32[1024,1088]{1,0:T(8,128)S(1)} %get-tuple-element.164, f32[1024]{0:T(1024)S(1)} %add_rsqrt_fusion, f32[1024]{0:T(1024)S(1)} %broadcast_multiply_fusion.4, f32[1088]{0:T(1024)S(1)} %mul.312, ...), kind=kOutput, calls=%fused_computation.50 | convolution fusion | flops 2437672960 | bytes 26907392 | tf_op jit(solution)/shard_map/dot_general | solution.py:684
  366.1 7.7 convolution_convert_fusion.12
  383.1 45.9 %attend_back.1 = (bf16[1024,1088]{1,0:T(8,128)(2,1)S(1)}, bf16[1024,1088]{1,0:T(8,128)(2,1)S(1)}, bf16[1024,1088]{1,0:T(8,128)(2,1)}) custom-call(s32[1]{0:T(128)} %bitcast.place_ref, bf16[1024,1088]{1,0:T(8,128)(2,1)} %copy-done.12, bf16[1024,1088]{1,0:T(8,128)(2,1)} %convolution_convert_fusion.13.k_ref, bf16[1024,1088]{1,0:T(8,128)(2,1)} %add_convert_fusion.6.v_ref, ...), custom_call_target="tpu_custom_call" | custom-call | flops 11408506880 | bytes 17825792 | tf_op jit(solution)/shard_map/attend_back/pallas_call | solution.py:546
  435.4 6.9 select_select_fusion.1
  443.0 7.4 convolution_convert_fusion.4
  460.9 7.6 convolution_convert_fusion
  468.7 8.0 %convolution_convert_fusion.2 = bf16[1088,1088]{1,0:T(8,128)(2,1)} fusion(f32[1024,1088]{0,1:T(8,128)} %copy-done.90, bf16[256,1088]{1,0:T(8,128)(2,1)S(1)} %copy-done.39, bf16[256,1088]{1,0:T(8,128)(2,1)S(1)} %copy-done.42, bf16[256,1088]{1,0:T(8,128)(2,1)S(1)} %copy-done.45, bf16[256,1088]{1,0:T(8,128)(2,1)S(1)} %bitcast.106), kind=kOutput, calls=%fused_computation.4 | convolution fusion | flops 2444431360 | bytes 9052160 | tf_op jit(solution)/shard_map/dot_general | solution.py:684
  477.0 6.5 add_convert_fusion.1
  484.7 5.2 collective-permute-done.32
  489.9 5.1 add_convert_fusion.2
  495.3 9.1 %fusion.48 = f32[1024,1088]{1,0:T(8,128)} fusion(bf16[1088,1088]{1,0:T(8,128)(2,1)} %collective-permute-done.12, f32[1024,1088]{0,1:T(8,128)} %copy-done.90), kind=kOutput, calls=%fused_computation.201 | convolution fusion | flops 2434334720 | bytes 11280384 | tf_op jit(solution)/shard_map/dot_general | solution.py:684
  504.4 9.0 %fusion.47 = f32[1024,1088]{1,0:T(8,128)} fusion(bf16[1088,1088]{1,0:T(8,128)(2,1)} %collective-permute-done.10, f32[1024,1088]{0,1:T(8,128)} %copy-done.89), kind=kOutput, calls=%fused_computation.200 | convolution fusion | flops 2434334720 | bytes 11280384 | tf_op jit(solution)/shard_map/dot_general | solution.py:684
  513.5 7.9 %fusion.46 = f32[1024,1088]{1,0:T(8,128)} fusion(bf16[1088,1088]{1,0:T(8,128)(2,1)} %all-gather.8.cloned.1.call-done, f32[1024,1088]{0,1:T(8,128)S(1)} %bitcast.110), kind=kOutput, calls=%fused_computation.199 | convolution fusion | flops 2434334720 | bytes 11280384 | tf_op jit(solution)/shard_map/dot_general | solution.py:684
  529.6 8.5 %fusion.8 = bf16[1088,1088]{1,0:T(8,128)(2,1)} fusion(bf16[1088,1088]{1,0:T(8,128)(2,1)} %collective-permute-done.51, f32[1024,1088]{0,1:T(8,128)} %copy-done.89, bf16[256,1088]{1,0:T(8,128)(2,1)} %copy.117, bf16[256,1088]{1,0:T(8,128)(2,1)} %copy.116, bf16[256,1088]{1,0:T(8,128)(2,1)} %copy.115, bf16[256,1088]{1,0:T(8,128)(2,1)S(1)} %bitcast.107), kind=kOutput, calls=%fused_computation.20 | convolution fusion | flops 2449166336 | bytes 11419648 | tf_op jit(solution)/shard_map/dot_general | solution.py:684
  539.6 12.9 %add_convert_fusion.4 = bf16[1024,1088]{1,0:T(8,128)(2,1)S(1)} fusion(f32[1024,1088]{1,0:T(8,128)} %fusion.48, f32[1024,1088]{1,0:T(8,128)} %fusion.47, f32[1024,1088]{1,0:T(8,128)} %fusion.46, f32[1024,1088]{1,0:T(8,128)} %copy-done.15, bf16[1088,1088]{1,0:T(8,128)(2,1)} %collective-permute-done.14, f32[1088]{0:T(1024)S(1)} %add.409, ...), kind=kOutput, calls=%fused_computation.57 | convolution fusion | flops 2441019392 | bytes 26882304 | tf_op jit(solution)/shard_map/dot_general | solution.py:684
  554.8 7.4 fusion.29
  562.1 7.0 fusion.30
  569.3 7.6 fusion.5
  577.0 10.7 %fusion.22 = (f32[1088]{0:T(1024)S(1)}, f32[1024]{0:T(1024)S(1)}, f32[1024]{0:T(1024)S(1)}, f32[1088]{0:T(1024)S(1)}, f32[1024,1088]{1,0:T(8,128)}) fusion(f32[1024]{0:T(1024)S(1)} %copy-done.68, f32[1024]{0:T(1024)S(1)} %copy-done.66, bf16[256,1088]{1,0:T(8,128)(2,1)} %copy.99, bf16[256,1088]{1,0:T(8,128)(2,1)} %copy.98, bf16[256,1088]{1,0:T(8,128)(2,1)} %copy.97, ...), kind=kOutput, calls=%fused_computation.47 | convolution fusion | flops 2445471744 | bytes 21115648 | tf_op jit(solution)/shard_map/dot_general | solution.py:684
  604.4 6.3 fusion.21
  624.0 27.2 %reduce-scatter.8.cloned.1.call-done = bf16[272,1088]{1,0:T(8,128)(2,1)} async-done(((bf16[1088,1088]{1,0:T(8,128)(2,1)}), bf16[272,1088]{1,0:T(8,128)(2,1)}) %reduce-scatter.8.cloned.1.call-update) | async-done | bytes 591888 | tf_op jit(solution)/shard_map/reduce_scatter | solution.py:627
  660.3 7.3 collective-permute-done.53
  670.4 9.2 %collective-permute-done.16 = bf16[256,1088]{0,1:T(8,128)(2,1)S(1)} collective-permute-done((bf16[256,1088]{0,1:T(8,128)(2,1)}, bf16[256,1088]{0,1:T(8,128)(2,1)S(1)}, u32[]{:S(2)}, u32[]{:S(2)}) %collective-permute-start.16) | collective-permute-done | bytes 557088 | tf_op jit(solution)/shard_map/ppermute | solution.py:610
  679.6 11.0 %collective-permute-done.17 = bf16[256,1088]{0,1:T(8,128)(2,1)S(1)} collective-permute-done((bf16[256,1088]{0,1:T(8,128)(2,1)}, bf16[256,1088]{0,1:T(8,128)(2,1)S(1)}, u32[]{:S(2)}, u32[]{:S(2)}) %collective-permute-start.17) | collective-permute-done | bytes 557088 | tf_op jit(solution)/shard_map/ppermute | solution.py:610
  694.6 8.9 %collective-permute-done.22 = bf16[256,1088]{0,1:T(8,128)(2,1)S(1)} collective-permute-done((bf16[256,1088]{0,1:T(8,128)(2,1)}, bf16[256,1088]{0,1:T(8,128)(2,1)S(1)}, u32[]{:S(2)}, u32[]{:S(2)}) %collective-permute-start.22) | collective-permute-done | bytes 557088 | tf_op jit(solution)/shard_map/ppermute | solution.py:610
  723.0 6.7 collective-permute-done.23
  735.1 6.0 copy.134
  755.9 5.8 concatenate.35
  (451 shorter events, 202.9 us)
Async XLA Ops:
  7.2 55.5 %all-gather.4.cloned.1.call-start = ((), (), s32[]{:S(2)}) async-start(), calls=%async_computation.3 | async-start | bytes 3133440 | tf_op jit(solution)/shard_map/all_gather | solution.py:614
  10.2 123.7 %all-gather.8.cloned.1.call-start = ((), (), s32[]{:S(2)}) async-start(), calls=%async_computation.5 | async-start | bytes 3133440 | tf_op jit(solution)/shard_map/all_gather | solution.py:614
  11.3 159.2 %all-gather.6.cloned.1.call-start = ((), (), s32[]{:S(2)}) async-start(), calls=%async_computation.4 | async-start | bytes 3133440 | tf_op jit(solution)/shard_map/all_gather | solution.py:614
  14.3 588.6 %reduce-scatter.4.cloned.1.call-start = ((), (), s32[]{:S(2)}) async-start(), calls=%async_computation.6 | async-start | bytes 3133440 | tf_op jit(solution)/shard_map/reduce_scatter | solution.py:627
  62.7 109.2 %collective-permute-start.6 = (bf16[1088,1088]{1,0:T(8,128)(2,1)}, bf16[1088,1088]{1,0:T(8,128)(2,1)}, u32[]{:S(2)}, u32[]{:S(2)}) collective-permute-start(bf16[1088,1088]{1,0:T(8,128)(2,1)} %all-gather.4.cloned.1.call-done.refs_0_), channel_id=1, source_target_pairs={{0,16},{1,3},{2,18},{3,1},{16,0},{17,19},{18,2},{19,17},{4,20},{5,... | collective-permute-start | bytes 7102472 | tf_op jit(solution)/shard_map/ppermute | solution.py:604
  65.6 50.3 %collective-permute-start.2 = (bf16[256,1088]{0,1:T(8,128)(2,1)}, bf16[256,1088]{0,1:T(8,128)(2,1)S(1)}, u32[]{:S(2)}, u32[]{:S(2)}) collective-permute-start(bf16[256,1088]{0,1:T(8,128)(2,1)} %get-tuple-element.121), channel_id=1, source_target_pairs={{0,3},{1,2},{2,1},{3,0},{4,7},{5,6},{6,5},{7,4},{8,11},{9,10},{10,... | collective-permute-start | bytes 1671176 | tf_op jit(solution)/shard_map/ppermute | solution.py:610
  73.4 47.8 %collective-permute-start.1 = (bf16[256,1088]{0,1:T(8,128)(2,1)}, bf16[256,1088]{0,1:T(8,128)(2,1)}, u32[]{:S(2)}, u32[]{:S(2)}) collective-permute-start(bf16[256,1088]{0,1:T(8,128)(2,1)} %get-tuple-element.122), channel_id=1, source_target_pairs={{0,2},{1,3},{2,0},{3,1},{4,6},{5,7},{6,4},{7,5},{8,10},{9,11},{10,... | collective-permute-start | bytes 1671176 | tf_op jit(solution)/shard_map/ppermute | solution.py:610
  74.9 49.3 %collective-permute-start = (bf16[256,1088]{0,1:T(8,128)(2,1)}, bf16[256,1088]{0,1:T(8,128)(2,1)}, u32[]{:S(2)}, u32[]{:S(2)}) collective-permute-start(bf16[256,1088]{0,1:T(8,128)(2,1)} %get-tuple-element.120), channel_id=1, source_target_pairs={{0,1},{1,0},{2,3},{3,2},{4,5},{5,4},{6,7},{7,6},{8,9},{9,8},{10,11... | collective-permute-start | bytes 1671176 | tf_op jit(solution)/shard_map/ppermute | solution.py:610
  74.9 59.0 %collective-permute-start.20 = (bf16[256,1088]{0,1:T(8,128)(2,1)}, bf16[256,1088]{0,1:T(8,128)(2,1)}, u32[]{:S(2)}, u32[]{:S(2)}) collective-permute-start(bf16[256,1088]{0,1:T(8,128)(2,1)} %get-tuple-element.117), channel_id=1, source_target_pairs={{0,3},{1,2},{2,1},{3,0},{4,7},{5,6},{6,5},{7,4},{8,11},{9,10},{10,... | collective-permute-start | bytes 1671176 | tf_op jit(solution)/shard_map/ppermute | solution.py:610
  115.9 19.5 %collective-permute-start.19 = (bf16[256,1088]{0,1:T(8,128)(2,1)}, bf16[256,1088]{0,1:T(8,128)(2,1)}, u32[]{:S(2)}, u32[]{:S(2)}) collective-permute-start(bf16[256,1088]{0,1:T(8,128)(2,1)} %get-tuple-element.118), channel_id=1, source_target_pairs={{0,2},{1,3},{2,0},{3,1},{4,6},{5,7},{6,4},{7,5},{8,10},{9,11},{10,... | collective-permute-start | bytes 1671176 | tf_op jit(solution)/shard_map/ppermute | solution.py:610
  121.2 63.2 %collective-permute-start.18 = (bf16[256,1088]{0,1:T(8,128)(2,1)}, bf16[256,1088]{0,1:T(8,128)(2,1)}, u32[]{:S(2)}, u32[]{:S(2)}) collective-permute-start(bf16[256,1088]{0,1:T(8,128)(2,1)} %get-tuple-element.116), channel_id=1, source_target_pairs={{0,1},{1,0},{2,3},{3,2},{4,5},{5,4},{6,7},{7,6},{8,9},{9,8},{10,11... | collective-permute-start | bytes 1671176 | tf_op jit(solution)/shard_map/ppermute | solution.py:610
  124.2 71.2 %collective-permute-start.7 = (bf16[1088,1088]{1,0:T(8,128)(2,1)S(1)}, bf16[1088,1088]{1,0:T(8,128)(2,1)}, u32[]{:S(2)}, u32[]{:S(2)}) collective-permute-start(bf16[1088,1088]{1,0:T(8,128)(2,1)S(1)} %copy-done.2), channel_id=1, source_target_pairs={{0,1},{1,0},{2,3},{3,2},{16,17},{17,16},{18,19},{19,18},{4,5},{5,4... | collective-permute-start | bytes 7102472 | tf_op jit(solution)/shard_map/ppermute | solution.py:604
  133.9 61.6 %collective-permute-start.10 = (bf16[1088,1088]{1,0:T(8,128)(2,1)}, bf16[1088,1088]{1,0:T(8,128)(2,1)}, u32[]{:S(2)}, u32[]{:S(2)}) collective-permute-start(bf16[1088,1088]{1,0:T(8,128)(2,1)} %all-gather.8.cloned.1.call-done), channel_id=1, source_target_pairs={{0,16},{1,3},{2,18},{3,1},{16,0},{17,19},{18,2},{19,17},{4,20},{5,... | collective-permute-start | bytes 7102472 | tf_op jit(solution)/shard_map/ppermute | solution.py:604
  170.5 30.7 %collective-permute-start.9 = (bf16[1088,1088]{1,0:T(8,128)(2,1)}, bf16[1088,1088]{1,0:T(8,128)(2,1)}, u32[]{:S(2)}, u32[]{:S(2)}) collective-permute-start(bf16[1088,1088]{1,0:T(8,128)(2,1)} %all-gather.6.cloned.1.call-done), channel_id=1, source_target_pairs={{0,16},{1,3},{2,18},{3,1},{16,0},{17,19},{18,2},{19,17},{4,20},{5,... | collective-permute-start | bytes 7102472 | tf_op jit(solution)/shard_map/ppermute | solution.py:604
  172.0 29.3 %collective-permute-start.8 = (bf16[1088,1088]{1,0:T(8,128)(2,1)}, bf16[1088,1088]{1,0:T(8,128)(2,1)}, u32[]{:S(2)}, u32[]{:S(2)}) collective-permute-start(bf16[1088,1088]{1,0:T(8,128)(2,1)} %collective-permute-done.6.refs_1_), channel_id=1, source_target_pairs={{0,1},{1,0},{2,3},{3,2},{16,17},{17,16},{18,19},{19,18},{4,5},{5,4... | collective-permute-start | bytes 7102472 | tf_op jit(solution)/shard_map/ppermute | solution.py:604
  194.8 110.0 %collective-permute-start.12 = (bf16[1088,1088]{1,0:T(8,128)(2,1)}, bf16[1088,1088]{1,0:T(8,128)(2,1)}, u32[]{:S(2)}, u32[]{:S(2)}) collective-permute-start(bf16[1088,1088]{1,0:T(8,128)(2,1)} %all-gather.8.cloned.1.call-done), channel_id=1, source_target_pairs={{0,1},{1,0},{2,3},{3,2},{16,17},{17,16},{18,19},{19,18},{4,5},{5,4... | collective-permute-start | bytes 7102472 | tf_op jit(solution)/shard_map/ppermute | solution.py:604
  195.4 81.3 %collective-permute-start.11 = (bf16[1088,1088]{1,0:T(8,128)(2,1)}, bf16[1088,1088]{1,0:T(8,128)(2,1)}, u32[]{:S(2)}, u32[]{:S(2)}) collective-permute-start(bf16[1088,1088]{1,0:T(8,128)(2,1)} %all-gather.6.cloned.1.call-done), channel_id=1, source_target_pairs={{0,1},{1,0},{2,3},{3,2},{16,17},{17,16},{18,19},{19,18},{4,5},{5,4... | collective-permute-start | bytes 7102472 | tf_op jit(solution)/shard_map/ppermute | solution.py:604
  195.5 144.6 %collective-permute-start.14 = (bf16[1088,1088]{1,0:T(8,128)(2,1)}, bf16[1088,1088]{1,0:T(8,128)(2,1)}, u32[]{:S(2)}, u32[]{:S(2)}) collective-permute-start(bf16[1088,1088]{1,0:T(8,128)(2,1)} %collective-permute-done.10), channel_id=1, source_target_pairs={{0,1},{1,0},{2,3},{3,2},{16,17},{17,16},{18,19},{19,18},{4,5},{5,4... | collective-permute-start | bytes 7102472 | tf_op jit(solution)/shard_map/ppermute | solution.py:604
  201.2 135.6 %collective-permute-start.13 = (bf16[1088,1088]{1,0:T(8,128)(2,1)}, bf16[1088,1088]{1,0:T(8,128)(2,1)S(1)}, u32[]{:S(2)}, u32[]{:S(2)}) collective-permute-start(bf16[1088,1088]{1,0:T(8,128)(2,1)} %collective-permute-done.9), channel_id=1, source_target_pairs={{0,1},{1,0},{2,3},{3,2},{16,17},{17,16},{18,19},{19,18},{4,5},{5,4... | collective-permute-start | bytes 7102472 | tf_op jit(solution)/shard_map/ppermute | solution.py:604
  442.3 13.5 %collective-permute-start.31 = (bf16[1088,1088]{1,0:T(8,128)(2,1)}, bf16[1088,1088]{1,0:T(8,128)(2,1)}, u32[]{:S(2)}, u32[]{:S(2)}) collective-permute-start(bf16[1088,1088]{1,0:T(8,128)(2,1)} %get-tuple-element.93), channel_id=1, source_target_pairs={{0,1},{1,0},{2,3},{3,2},{16,17},{17,16},{18,19},{19,18},{4,5},{5,4... | collective-permute-start | bytes 7102472 | tf_op jit(solution)/shard_map/ppermute | solution.py:604
  442.9 40.6 %collective-permute-start.30 = (bf16[1088,1088]{1,0:T(8,128)(2,1)}, bf16[1088,1088]{1,0:T(8,128)(2,1)S(1)}, u32[]{:S(2)}, u32[]{:S(2)}) collective-permute-start(bf16[1088,1088]{1,0:T(8,128)(2,1)} %get-tuple-element.92), channel_id=1, source_target_pairs={{0,1},{1,0},{2,3},{3,2},{16,17},{17,16},{18,19},{19,18},{4,5},{5,4... | collective-permute-start | bytes 7102472 | tf_op jit(solution)/shard_map/ppermute | solution.py:604
  450.4 26.2 %collective-permute-start.44 = (bf16[1088,1088]{1,0:T(8,128)(2,1)}, bf16[1088,1088]{1,0:T(8,128)(2,1)}, u32[]{:S(2)}, u32[]{:S(2)}) collective-permute-start(bf16[1088,1088]{1,0:T(8,128)(2,1)} %convolution_convert_fusion.4), channel_id=1, source_target_pairs={{0,1},{1,0},{2,3},{3,2},{16,17},{17,16},{18,19},{19,18},{4,5},{5,4... | collective-permute-start | bytes 7102472 | tf_op jit(solution)/shard_map/ppermute | solution.py:604
  455.8 68.9 %collective-permute-start.43 = (bf16[1088,1088]{1,0:T(8,128)(2,1)}, bf16[1088,1088]{1,0:T(8,128)(2,1)}, u32[]{:S(2)}, u32[]{:S(2)}) collective-permute-start(bf16[1088,1088]{1,0:T(8,128)(2,1)} %convolution_convert_fusion.6), channel_id=1, source_target_pairs={{0,1},{1,0},{2,3},{3,2},{16,17},{17,16},{18,19},{19,18},{4,5},{5,4... | collective-permute-start | bytes 7102472 | tf_op jit(solution)/shard_map/ppermute | solution.py:604
  459.3 30.6 %collective-permute-start.32 = (bf16[1088,1088]{1,0:T(8,128)(2,1)S(1)}, bf16[1088,1088]{1,0:T(8,128)(2,1)}, u32[]{:S(2)}, u32[]{:S(2)}) collective-permute-start(bf16[1088,1088]{1,0:T(8,128)(2,1)S(1)} %add_convert_fusion.3), channel_id=1, source_target_pairs={{0,16},{1,3},{2,18},{3,1},{16,0},{17,19},{18,2},{19,17},{4,20},{5,... | collective-permute-start | bytes 7102472 | tf_op jit(solution)/shard_map/ppermute | solution.py:604
  468.5 61.1 %collective-permute-start.51 = (bf16[1088,1088]{1,0:T(8,128)(2,1)}, bf16[1088,1088]{1,0:T(8,128)(2,1)}, u32[]{:S(2)}, u32[]{:S(2)}) collective-permute-start(bf16[1088,1088]{1,0:T(8,128)(2,1)} %convolution_convert_fusion), channel_id=1, source_target_pairs={{0,1},{1,0},{2,3},{3,2},{16,17},{17,16},{18,19},{19,18},{4,5},{5,4... | collective-permute-start | bytes 7102472 | tf_op jit(solution)/shard_map/ppermute | solution.py:604
  476.6 92.6 %collective-permute-start.50 = (bf16[1088,1088]{1,0:T(8,128)(2,1)}, bf16[1088,1088]{1,0:T(8,128)(2,1)}, u32[]{:S(2)}, u32[]{:S(2)}) collective-permute-start(bf16[1088,1088]{1,0:T(8,128)(2,1)} %convolution_convert_fusion.2), channel_id=1, source_target_pairs={{0,1},{1,0},{2,3},{3,2},{16,17},{17,16},{18,19},{19,18},{4,5},{5,4... | collective-permute-start | bytes 7102472 | tf_op jit(solution)/shard_map/ppermute | solution.py:604
  483.5 41.2 %collective-permute-start.45 = (bf16[1088,1088]{1,0:T(8,128)(2,1)}, bf16[1088,1088]{1,0:T(8,128)(2,1)}, u32[]{:S(2)}, u32[]{:S(2)}) collective-permute-start(bf16[1088,1088]{1,0:T(8,128)(2,1)} %add_convert_fusion.1), channel_id=1, source_target_pairs={{0,16},{1,3},{2,18},{3,1},{16,0},{17,19},{18,2},{19,17},{4,20},{5,... | collective-permute-start | bytes 7102472 | tf_op jit(solution)/shard_map/ppermute | solution.py:604
  495.0 117.9 %reduce-scatter.6.cloned.1.call-start = ((), (), s32[]{:S(2)}) async-start(), calls=%async_computation.7 | async-start | bytes 3133440 | tf_op jit(solution)/shard_map/reduce_scatter | solution.py:627
  529.4 121.8 %reduce-scatter.8.cloned.1.call-start = ((), (), s32[]{:S(2)}) async-start(), calls=%async_computation.8 | async-start | bytes 3133440 | tf_op jit(solution)/shard_map/reduce_scatter | solution.py:627
  538.1 31.1 %collective-permute-start.52 = (bf16[1088,1088]{1,0:T(8,128)(2,1)}, bf16[1088,1088]{1,0:T(8,128)(2,1)}, u32[]{:S(2)}, u32[]{:S(2)}) collective-permute-start(bf16[1088,1088]{1,0:T(8,128)(2,1)} %fusion.8), channel_id=1, source_target_pairs={{0,16},{1,3},{2,18},{3,1},{16,0},{17,19},{18,2},{19,17},{4,20},{5,... | collective-permute-start | bytes 7102472 | tf_op jit(solution)/shard_map/ppermute | solution.py:604
  554.8 100.5 %collective-permute-start.15 = (bf16[256,1088]{0,1:T(8,128)(2,1)}, bf16[256,1088]{0,1:T(8,128)(2,1)}, u32[]{:S(2)}, u32[]{:S(2)}) collective-permute-start(bf16[256,1088]{0,1:T(8,128)(2,1)} %copy.108), channel_id=1, source_target_pairs={{0,1},{1,0},{2,3},{3,2},{4,5},{5,4},{6,7},{7,6},{8,9},{9,8},{10,11... | collective-permute-start | bytes 1671176 | tf_op jit(solution)/shard_map/ppermute | solution.py:610
  602.9 48.2 %collective-permute-start.33 = (bf16[272,1088]{1,0:T(8,128)(2,1)}, bf16[272,1088]{1,0:T(8,128)(2,1)}, u32[]{:S(2)}, u32[]{:S(2)}) collective-permute-start(bf16[272,1088]{1,0:T(8,128)(2,1)} %reduce-scatter.4.cloned.1.call-done), channel_id=1, source_target_pairs={{0,2},{1,17},{2,0},{3,19},{16,18},{17,1},{18,16},{19,3},{4,6},{5,2... | collective-permute-start | bytes 1775624 | tf_op jit(solution)/shard_map/ppermute | solution.py:604
  612.9 43.9 %collective-permute-start.46 = (bf16[272,1088]{1,0:T(8,128)(2,1)}, bf16[272,1088]{1,0:T(8,128)(2,1)}, u32[]{:S(2)}, u32[]{:S(2)}) collective-permute-start(bf16[272,1088]{1,0:T(8,128)(2,1)} %reduce-scatter.6.cloned.1.call-done), channel_id=1, source_target_pairs={{0,2},{1,17},{2,0},{3,19},{16,18},{17,1},{18,16},{19,3},{4,6},{5,2... | collective-permute-start | bytes 1775624 | tf_op jit(solution)/shard_map/ppermute | solution.py:604
  622.0 32.7 %collective-permute-start.29 = (f32[1088]{0:T(1024)S(1)}, f32[1088]{0:T(1024)S(1)}, u32[]{:S(2)}, u32[]{:S(2)}) collective-permute-start(f32[1088]{0:T(1024)S(1)} %add.466), channel_id=1, source_target_pairs={{0,16},{1,17},{2,18},{3,19},{16,0},{17,1},{18,2},{19,3},{4,20},{5,... | collective-permute-start | bytes 13064 | tf_op jit(solution)/shard_map/ppermute | solution.py:660
  623.0 32.2 %collective-permute-start.42 = (f32[2176]{0:T(1024)S(1)}, f32[2176]{0:T(1024)S(1)}, u32[]{:S(2)}, u32[]{:S(2)}) collective-permute-start(f32[2176]{0:T(1024)S(1)} %add.484), channel_id=1, source_target_pairs={{0,16},{1,17},{2,18},{3,19},{16,0},{17,1},{18,2},{19,3},{4,20},{5,... | collective-permute-start | bytes 26120 | tf_op jit(solution)/shard_map/ppermute | solution.py:660
  651.1 16.5 %collective-permute-start.53 = (bf16[272,1088]{1,0:T(8,128)(2,1)}, bf16[272,1088]{1,0:T(8,128)(2,1)S(1)}, u32[]{:S(2)}, u32[]{:S(2)}) collective-permute-start(bf16[272,1088]{1,0:T(8,128)(2,1)} %reduce-scatter.8.cloned.1.call-done), channel_id=1, source_target_pairs={{0,2},{1,17},{2,0},{3,19},{16,18},{17,1},{18,16},{19,3},{4,6},{5,2... | collective-permute-start | bytes 1775624 | tf_op jit(solution)/shard_map/ppermute | solution.py:604
  654.7 25.0 %collective-permute-start.16 = (bf16[256,1088]{0,1:T(8,128)(2,1)}, bf16[256,1088]{0,1:T(8,128)(2,1)S(1)}, u32[]{:S(2)}, u32[]{:S(2)}) collective-permute-start(bf16[256,1088]{0,1:T(8,128)(2,1)} %copy.109), channel_id=1, source_target_pairs={{0,2},{1,3},{2,0},{3,1},{4,6},{5,7},{6,4},{7,5},{8,10},{9,11},{10,... | collective-permute-start | bytes 1671176 | tf_op jit(solution)/shard_map/ppermute | solution.py:610
  655.2 35.4 %collective-permute-start.17 = (bf16[256,1088]{0,1:T(8,128)(2,1)}, bf16[256,1088]{0,1:T(8,128)(2,1)S(1)}, u32[]{:S(2)}, u32[]{:S(2)}) collective-permute-start(bf16[256,1088]{0,1:T(8,128)(2,1)} %copy.110), channel_id=1, source_target_pairs={{0,3},{1,2},{2,1},{3,0},{4,7},{5,6},{6,5},{7,4},{8,11},{9,10},{10,... | collective-permute-start | bytes 1671176 | tf_op jit(solution)/shard_map/ppermute | solution.py:610
  655.2 37.5 %collective-permute-start.21 = (bf16[256,1088]{0,1:T(8,128)(2,1)}, bf16[256,1088]{0,1:T(8,128)(2,1)}, u32[]{:S(2)}, u32[]{:S(2)}) collective-permute-start(bf16[256,1088]{0,1:T(8,128)(2,1)} %copy.127), channel_id=1, source_target_pairs={{0,1},{1,0},{2,3},{3,2},{4,5},{5,4},{6,7},{7,6},{8,9},{9,8},{10,11... | collective-permute-start | bytes 1671176 | tf_op jit(solution)/shard_map/ppermute | solution.py:610
  656.8 36.8 %collective-permute-start.34 = (bf16[272,1088]{1,0:T(8,128)(2,1)}, bf16[272,1088]{1,0:T(8,128)(2,1)}, u32[]{:S(2)}, u32[]{:S(2)}) collective-permute-start(bf16[272,1088]{1,0:T(8,128)(2,1)} %add_convert_fusion.14), channel_id=1, source_target_pairs={{0,16},{1,3},{2,18},{3,1},{16,0},{17,19},{18,2},{19,17},{4,20},{5,... | collective-permute-start | bytes 1775624 | tf_op jit(solution)/shard_map/ppermute | solution.py:604
  667.7 35.8 %collective-permute-start.22 = (bf16[256,1088]{0,1:T(8,128)(2,1)}, bf16[256,1088]{0,1:T(8,128)(2,1)S(1)}, u32[]{:S(2)}, u32[]{:S(2)}) collective-permute-start(bf16[256,1088]{0,1:T(8,128)(2,1)} %copy.128), channel_id=1, source_target_pairs={{0,2},{1,3},{2,0},{3,1},{4,6},{5,7},{6,4},{7,5},{8,10},{9,11},{10,... | collective-permute-start | bytes 1671176 | tf_op jit(solution)/shard_map/ppermute | solution.py:610
  679.6 61.4 %collective-permute-start.35 = (bf16[272,1088]{1,0:T(8,128)(2,1)}, bf16[272,1088]{1,0:T(8,128)(2,1)}, u32[]{:S(2)}, u32[]{:S(2)}) collective-permute-start(bf16[272,1088]{1,0:T(8,128)(2,1)} %add_convert_fusion.14), channel_id=1, source_target_pairs={{0,1},{1,0},{2,3},{3,2},{16,17},{17,16},{18,19},{19,18},{4,5},{5,4... | collective-permute-start | bytes 1775624 | tf_op jit(solution)/shard_map/ppermute | solution.py:604
  690.6 50.9 %collective-permute-start.47 = (bf16[272,1088]{1,0:T(8,128)(2,1)}, bf16[272,1088]{1,0:T(8,128)(2,1)}, u32[]{:S(2)}, u32[]{:S(2)}) collective-permute-start(bf16[272,1088]{1,0:T(8,128)(2,1)} %add_convert_fusion.13), channel_id=1, source_target_pairs={{0,16},{1,3},{2,18},{3,1},{16,0},{17,19},{18,2},{19,17},{4,20},{5,... | collective-permute-start | bytes 1775624 | tf_op jit(solution)/shard_map/ppermute | solution.py:604
  692.8 48.9 %collective-permute-start.54 = (bf16[272,1088]{1,0:T(8,128)(2,1)S(1)}, bf16[272,1088]{1,0:T(8,128)(2,1)}, u32[]{:S(2)}, u32[]{:S(2)}) collective-permute-start(bf16[272,1088]{1,0:T(8,128)(2,1)S(1)} %add_convert_fusion.12.refs_0_), channel_id=1, source_target_pairs={{0,16},{1,3},{2,18},{3,1},{16,0},{17,19},{18,2},{19,17},{4,20},{5,... | collective-permute-start | bytes 1775624 | tf_op jit(solution)/shard_map/ppermute | solution.py:604
  693.6 48.5 %collective-permute-start.36 = (bf16[272,1088]{1,0:T(8,128)(2,1)}, bf16[272,1088]{1,0:T(8,128)(2,1)}, u32[]{:S(2)}, u32[]{:S(2)}) collective-permute-start(bf16[272,1088]{1,0:T(8,128)(2,1)} %collective-permute-done.34), channel_id=1, source_target_pairs={{0,1},{1,0},{2,3},{3,2},{16,17},{17,16},{18,19},{19,18},{4,5},{5,4... | collective-permute-start | bytes 1775624 | tf_op jit(solution)/shard_map/ppermute | solution.py:604
  703.5 26.1 %collective-permute-start.23 = (bf16[256,1088]{0,1:T(8,128)(2,1)}, bf16[256,1088]{0,1:T(8,128)(2,1)}, u32[]{:S(2)}, u32[]{:S(2)}) collective-permute-start(bf16[256,1088]{0,1:T(8,128)(2,1)} %copy.129), channel_id=1, source_target_pairs={{0,3},{1,2},{2,1},{3,0},{4,7},{5,6},{6,5},{7,4},{8,11},{9,10},{10,... | collective-permute-start | bytes 1671176 | tf_op jit(solution)/shard_map/ppermute | solution.py:610
  741.1 25.0 %collective-permute-start.55 = (bf16[272,1088]{1,0:T(8,128)(2,1)S(1)}, bf16[272,1088]{1,0:T(8,128)(2,1)}, u32[]{:S(2)}, u32[]{:S(2)}) collective-permute-start(bf16[272,1088]{1,0:T(8,128)(2,1)S(1)} %add_convert_fusion.12.refs_0_), channel_id=1, source_target_pairs={{0,1},{1,0},{2,3},{3,2},{16,17},{17,16},{18,19},{19,18},{4,5},{5,4... | collective-permute-start | bytes 1775624 | tf_op jit(solution)/shard_map/ppermute | solution.py:604
  741.6 24.4 %collective-permute-start.56 = (bf16[272,1088]{1,0:T(8,128)(2,1)}, bf16[272,1088]{1,0:T(8,128)(2,1)}, u32[]{:S(2)}, u32[]{:S(2)}) collective-permute-start(bf16[272,1088]{1,0:T(8,128)(2,1)} %collective-permute-done.54.refs_1_), channel_id=1, source_target_pairs={{0,1},{1,0},{2,3},{3,2},{16,17},{17,16},{18,19},{19,18},{4,5},{5,4... | collective-permute-start | bytes 1775624 | tf_op jit(solution)/shard_map/ppermute | solution.py:604
  (116 other events, 2071.3 us)
Sparse Core Ops, SparseCore 0:
  10.3 52.3 all-gather.3
  64.9 51.6 all-gather.7
  118.8 51.6 all-gather.5
  495.1 50.1 reduce-scatter.3
  548.1 50.5 reduce-scatter.5
  600.8 50.2 reduce-scatter.7

commit v2 on v1

--- a/solution.py
+++ b/solution.py
@@ -610,12 +610,6 @@
     return lax.ppermute(values, "ctx", [(device, device ^ bits) for device in range(4)])
 
 
-def gather_piece(piece):
-    own = lax.all_gather(piece, "fsdp", axis=0, tiled=True)
-    near = plane_swap(own, "near")
-    return [own, near, plane_swap(own, "core"), plane_swap(near, "core")]
-
-
 def reduce_pieces(pieces):
     far_two = plane_swap(pieces[3], "core")
     far = plane_swap(pieces[2], "core")
@@ -663,23 +657,6 @@
     return total
 
 
-def normalised(values):
-    centred = values - jnp.mean(values, axis=-1, keepdims=True)
-    scale = lax.rsqrt(jnp.mean(centred * centred, axis=-1, keepdims=True) + epsilon)
-    return centred * scale, scale
-
-
-def norm_back(values, gain, grad):
-    unit, scale = normalised(values)
-    turned = grad * gain
-    inner = (
-        turned
-        - jnp.mean(turned, axis=-1, keepdims=True)
-        - unit * jnp.mean(turned * unit, axis=-1, keepdims=True)
-    )
-    return scale * inner, jnp.sum(grad * unit, axis=0), jnp.sum(grad, axis=0)
-
-
 def product(left, right, dims):
     return lax.dot_general(left, right, ((dims[:1], dims[1:]), ((), ())),
                            preferred_element_type=jnp.float32)
@@ -694,6 +671,297 @@
         1.0 + 3.0 * 0.044715 * squared
     )
     return active, slope
+
+
+def block_flops(rows, width, count):
+    return pl.CostEstimate(
+        flops=2 * rows * width * width * count,
+        bytes_accessed=2 * width * width * count + 4 * rows * width * count,
+        transcendentals=0,
+    )
+
+
+def unit_of(values):
+    centred = values - jnp.mean(values, axis=-1, keepdims=True)
+    scale = lax.rsqrt(jnp.mean(centred * centred, axis=-1, keepdims=True) + epsilon)
+    return centred * scale, scale
+
+
+def fold(values):
+    rows, width = values.shape
+    return jnp.sum(values.reshape(rows // 8, 8, width), axis=0)
+
+
+def front_kernel(places_ref, x_ref, vectors_ref, *refs):
+    pieces = refs[:16]
+    h_ref, q_ref, k_ref, v_ref, all_ref, weights, arrived, left = refs[16:]
+    copies = [
+        pltpu.make_async_copy(piece, weights.at[places_ref[at]], arrived.at[at])
+        for at, piece in enumerate(pieces)
+    ]
+    for copy in copies:
+        copy.start()
+    rows, width = x_ref.shape
+    step = 256
+
+    def norm(at, carry):
+        here = pl.ds(pl.multiple_of(at * step, step), step)
+        unit, _ = unit_of(x_ref[here, :].astype(jnp.float32))
+        h_ref[here, :] = (unit * vectors_ref[0:1, :] + vectors_ref[1:2, :]).astype(jnp.bfloat16)
+        return carry
+
+    lax.fori_loop(0, rows // step, norm, 0)
+    for copy in copies:
+        copy.wait()
+    leave = pltpu.make_async_copy(weights, all_ref, left)
+    leave.start()
+    for section, out_ref in enumerate((q_ref, k_ref, v_ref)):
+
+        def multiply(at, carry, section=section, out_ref=out_ref):
+            here = pl.ds(pl.multiple_of(at * step, step), step)
+            matrix = weights[4 * section : 4 * section + 4].reshape(width, width)
+            total = jnp.dot(h_ref[here, :], matrix, preferred_element_type=jnp.float32)
+            if section != 1:
+                row = 2 if section == 0 else 3
+                total = total + vectors_ref[row : row + 1, :]
+            out_ref[here, :] = total.astype(jnp.bfloat16)
+            return carry
+
+        lax.fori_loop(0, rows // step, multiply, 0)
+    leave.wait()
+
+
+def front(places, rows_in, vectors, pieces):
+    rows, width = rows_in.shape
+    vmem = pl.BlockSpec(memory_space=pltpu.VMEM)
+    hbm = pl.BlockSpec(memory_space=pl.ANY)
+    shape = jax.ShapeDtypeStruct((rows, width), jnp.bfloat16)
+    whole = (16,) + pieces[0].shape
+    return pl.pallas_call(
+        front_kernel,
+        in_specs=[pl.BlockSpec(memory_space=pltpu.SMEM), vmem, vmem] + [hbm] * 16,
+        out_specs=[vmem] * 4 + [hbm],
+        out_shape=[shape] * 4 + [jax.ShapeDtypeStruct(whole, jnp.bfloat16)],
+        scratch_shapes=[
+            pltpu.VMEM(whole, jnp.bfloat16),
+            pltpu.SemaphoreType.DMA((16,)),
+            pltpu.SemaphoreType.DMA,
+        ],
+        compiler_params=pltpu.CompilerParams(vmem_limit_bytes=56 * 2**20),
+        cost_estimate=block_flops(rows, width, 3),
+        name="front",
+    )(places, rows_in, vectors, *pieces)
+
+
+def fetch(step, copies):
+    @pl.when(step == 0)
+    def _():
+        for copy in copies:
+            copy.start()
+
+
+def arrive(step, copy):
+    @pl.when(step == 0)
+    def _():
+        copy.wait()
+
+
+def add_sums(step, sums_ref, terms):
+    @pl.when(step == 0)
+    def _():
+        sums_ref[...] = jnp.zeros_like(sums_ref)
+
+    for at, term in enumerate(terms):
+        sums_ref[at] += fold(term)
+
+
+def middle_kernel(x_ref, o_ref, vectors_ref, all_ref, middle_ref, h_ref, weights, arrived):
+    step = pl.program_id(0)
+    width = x_ref.shape[1]
+    copy = pltpu.make_async_copy(all_ref.at[pl.ds(12, 4)], weights, arrived)
+    fetch(step, [copy])
+    arrive(step, copy)
+    middle = (
+        x_ref[...].astype(jnp.float32)
+        + jnp.dot(
+            o_ref[...], weights[...].reshape(width, width), preferred_element_type=jnp.float32
+        )
+        + vectors_ref[0:1, :]
+    )
+    middle_ref[...] = middle
+    unit, _ = unit_of(middle)
+    h_ref[...] = (unit * vectors_ref[1:2, :] + vectors_ref[2:3, :]).astype(jnp.bfloat16)
+
+
+def up_kernel(h_ref, biases_ref, *refs):
+    sources = refs[:4]
+    active_refs, slope_refs = refs[4:8], refs[8:12]
+    weights, arrived = refs[12:]
+    step = pl.program_id(0)
+    copies = [
+        pltpu.make_async_copy(source, weights.at[at], arrived.at[at])
+        for at, source in enumerate(sources)
+    ]
+    fetch(step, copies)
+    for at in range(4):
+        arrive(step, copies[at])
+        hidden = (
+            jnp.dot(h_ref[...], weights[at], preferred_element_type=jnp.float32)
+            + biases_ref[at : at + 1, :]
+        )
+        active, slope = gelu_pair(hidden)
+        active_refs[at][...] = active.astype(jnp.bfloat16)
+        slope_refs[at][...] = slope.astype(jnp.bfloat16)
+
+
+def down_kernel(middle_ref, vectors_ref, *refs):
+    actives, sources = refs[:4], refs[4:8]
+    out_ref, weights, arrived = refs[8:]
+    step = pl.program_id(0)
+    copies = [
+        pltpu.make_async_copy(source, weights.at[at], arrived.at[at])
+        for at, source in enumerate(sources)
+    ]
+    fetch(step, copies)
+    total = middle_ref[...] + vectors_ref[0:1, :]
+    for at in range(4):
+        arrive(step, copies[at])
+        total = total + jnp.dot(
+            actives[at][...], weights[at], preferred_element_type=jnp.float32
+        )
+    out_ref[...] = total.astype(jnp.bfloat16)
+
+
+def norm_back(values, gain, grad):
+    unit, scale = unit_of(values)
+    turned = grad * gain
+    inner = (
+        turned
+        - jnp.mean(turned, axis=-1, keepdims=True)
+        - unit * jnp.mean(turned * unit, axis=-1, keepdims=True)
+    )
+    return scale * inner, grad * unit
+
+
+def back_kernel(g_ref, middle_ref, vectors_ref, *refs):
+    slopes, downs, ups, all_ref = refs[:4], refs[4:8], refs[8:12], refs[12]
+    hidden_refs = refs[13:17]
+    grad_ref, low_ref, out_ref, sums_ref = refs[17:21]
+    down_weights, up_weights, out_weights, arrived = refs[21:]
+    step = pl.program_id(0)
+    width = middle_ref.shape[1]
+    copies = []
+    for at in range(4):
+        copies.append(
+            pltpu.make_async_copy(downs[at], down_weights.at[at], arrived.at[2 * at])
+        )
+        copies.append(
+            pltpu.make_async_copy(ups[at], up_weights.at[at], arrived.at[2 * at + 1])
+        )
+    copies.append(
+        pltpu.make_async_copy(all_ref.at[pl.ds(12, 4)], out_weights, arrived.at[8])
+    )
+    fetch(step, copies)
+    upstream = g_ref[...]
+    sums = []
+    total = jnp.zeros(middle_ref.shape, jnp.float32)
+    for at in range(4):
+        arrive(step, copies[2 * at])
+        hidden = lax.dot_general(
+            upstream, down_weights[at], NT, preferred_element_type=jnp.float32
+        )
+        hidden = (hidden * slopes[at][...].astype(jnp.float32)).astype(jnp.bfloat16)
+        hidden_refs[at][...] = hidden
+        sums.append(fold(hidden.astype(jnp.float32)))
+        arrive(step, copies[2 * at + 1])
+        total = total + lax.dot_general(
+            hidden, up_weights[at], NT, preferred_element_type=jnp.float32
+        )
+    part, gain_term = norm_back(middle_ref[...], vectors_ref[0:1, :], total)
+    upstream = upstream.astype(jnp.float32)
+    grad = upstream + part
+    grad_ref[...] = grad
+    grad_low = grad.astype(jnp.bfloat16)
+    low_ref[...] = grad_low
+    sums += [
+        fold(gain_term), fold(total), fold(upstream), fold(grad_low.astype(jnp.float32))
+    ]
+    arrive(step, copies[8])
+    out_ref[...] = lax.dot_general(
+        grad_low,
+        out_weights[...].reshape(width, width),
+        NT,
+        preferred_element_type=jnp.float32,
+    ).astype(jnp.bfloat16)
+
+    @pl.when(step == 0)
+    def _():
+        sums_ref[...] = jnp.zeros_like(sums_ref)
+
+    for at, term in enumerate(sums):
+        sums_ref[at] += term
+
+
+def last_kernel(q_ref, k_ref, v_ref, x_ref, grad_ref, vectors_ref, all_ref, *refs):
+    out_ref, sums_ref, weights, arrived = refs
+    step = pl.program_id(0)
+    width = x_ref.shape[1]
+    copies = [
+        pltpu.make_async_copy(
+            all_ref.at[pl.ds(4 * at, 4)], weights.at[pl.ds(4 * at, 4)], arrived.at[at]
+        )
+        for at in range(3)
+    ]
+    fetch(step, copies)
+    total = jnp.zeros(x_ref.shape, jnp.float32)
+    for at, ref in enumerate((q_ref, k_ref, v_ref)):
+        arrive(step, copies[at])
+        total = total + lax.dot_general(
+            ref[...],
+            weights[4 * at : 4 * at + 4].reshape(width, width),
+            NT,
+            preferred_element_type=jnp.float32,
+        )
+    part, gain_term = norm_back(x_ref[...].astype(jnp.float32), vectors_ref[0:1, :], total)
+    out_ref[...] = (grad_ref[...] + part).astype(jnp.bfloat16)
+
+    @pl.when(step == 0)
+    def _():
+        sums_ref[...] = jnp.zeros_like(sums_ref)
+
+    terms = (
+        gain_term,
+        total,
+        q_ref[...].astype(jnp.float32),
+        v_ref[...].astype(jnp.float32),
+    )
+    for at, term in enumerate(terms):
+        sums_ref[at] += fold(term)
+
+
+def by_rows(kernel, name, rows, width, tiled, whole, remote, outs, sums, scratch, sems, blocks):
+    step = 256
+    tile = pl.BlockSpec((step, width), lambda at: (at, 0))
+    out_specs = [tile] * len(outs)
+    out_shape = [jax.ShapeDtypeStruct((rows, width), dtype) for dtype in outs]
+    if sums:
+        out_specs.append(pl.BlockSpec((sums, 8, width), lambda at: (0, 0, 0)))
+        out_shape.append(jax.ShapeDtypeStruct((sums, 8, width), jnp.float32))
+    return pl.pallas_call(
+        kernel,
+        grid=(rows // step,),
+        in_specs=[tile] * len(tiled[0])
+        + [pl.BlockSpec(value.shape, lambda at: (0, 0)) for value in whole]
+        + [tile] * len(tiled[1])
+        + [pl.BlockSpec(memory_space=pl.ANY)] * len(remote),
+        out_specs=out_specs,
+        out_shape=out_shape,
+        scratch_shapes=[pltpu.VMEM(shape, jnp.bfloat16) for shape in scratch]
+        + [pltpu.SemaphoreType.DMA((sems,)) if sems > 1 else pltpu.SemaphoreType.DMA],
+        compiler_params=pltpu.CompilerParams(vmem_limit_bytes=60 * 2**20),
+        cost_estimate=block_flops(rows, width, blocks),
+        name=name,
+    )(*tiled[0], *whole, *tiled[1], *remote)
 
 
 def per_device_exchanged(
@@ -729,6 +997,8 @@
         for kind in range(4)
     ]
     quarter = width // 4
+    rows, area = seq_count * block_len, (width, width)
+    pin = lax.optimization_barrier
     place = jnp.stack([c])
     places = jnp.stack([c ^ at for at in range(4)])
     class_places = jnp.stack(classes)
@@ -743,8 +1013,8 @@
             axis=0,
         )
 
-    def collect(rows, dtype):
-        pieces = [rows[at * block_len : (at + 1) * block_len].astype(low) for at in range(4)]
+    def collect(values, dtype):
+        pieces = [values[at * block_len : (at + 1) * block_len] for at in range(4)]
         moved = [pieces[0]] + [ctx_swap(pieces[bits], bits) for bits in range(1, 4)]
         return settle(places, moved, dtype)
 
@@ -754,7 +1024,11 @@
         project_in[:, 2 * width :],
         project_out,
     ]
-    attend_slots = gather_piece(chosen(mine, sections))
+    section = chosen(mine, sections)
+    shards = [
+        lax.ppermute(section, "fsdp", [(device, (device + step) % 4) for device in range(4)])
+        for step in range(1, 4)
+    ]
     up_piece = jnp.concatenate(
         [
             lax.dynamic_slice_in_dim(up_weight, at * width + mine * quarter, quarter, 1)
@@ -762,8 +1036,28 @@
         ],
         axis=1,
     )
-    up_slots = gather_piece(up_piece)
-    down_slots = gather_piece(lax.dynamic_slice_in_dim(down_weight, mine * quarter, quarter, 0))
+    up_piece, *shards = pin((up_piece, *shards))
+    near_shards = [plane_swap(shard, "near") for shard in shards]
+    around = (
+        sections
+        + shards
+        + near_shards
+        + [plane_swap(shard, "core") for shard in shards]
+        + [plane_swap(shard, "core") for shard in near_shards]
+    )
+    around_places = jnp.stack(
+        [kind * 4 + z for kind in range(4)]
+        + [kind * 4 + (z - step) % 4 for kind in classes for step in range(1, 4)]
+    )
+    up_own = lax.all_gather(up_piece, "fsdp", axis=0, tiled=True)
+    down_piece = lax.dynamic_slice_in_dim(down_weight, mine * quarter, quarter, 0)
+    down_piece, up_own = pin((down_piece, up_own))
+    down_own = lax.all_gather(down_piece, "fsdp", axis=0, tiled=True)
+
+    def exchange(own):
+        near = plane_swap(own, "near")
+        return [own, near, plane_swap(own, "core"), plane_swap(near, "core")]
+
     vectors = gather_vector(
         jnp.concatenate(
             [
@@ -781,109 +1075,152 @@
         z,
     ).astype(wide)
     gain_first, shift_first, qbias, vbias, obias, gain_second, shift_second, dbias = (
-        vectors[:, at * quarter : (at + 1) * quarter].reshape(width) for at in range(8)
+        vectors[:, at * quarter : (at + 1) * quarter].reshape(1, width) for at in range(8)
     )
     ubias = vectors[:, 8 * quarter :].reshape(4, 4, quarter)
+    ubias = jnp.concatenate(
+        [
+            chosen(kind, [ubias[:, at] for at in range(4)]).reshape(1, width)
+            for kind in classes
+        ],
+        axis=0,
+    )
 
     rows_in = spread(inputs)
-    wide_in = rows_in.astype(wide)
-    unit, _ = normalised(wide_in)
-    normed_low = (unit * gain_first + shift_first).astype(low)
-    weights = settle(class_places, attend_slots, low)
-    queries = (product(normed_low, weights[0], (1, 0)) + qbias).astype(low)
-    key_rows = product(normed_low, weights[1], (1, 0)).astype(low)
-    value_rows = (product(normed_low, weights[2], (1, 0)) + vbias).astype(low)
+    normed_low, queries, key_rows, value_rows, weights = front(
+        around_places,
+        rows_in,
+        jnp.concatenate([gain_first, shift_first, qbias, vbias], axis=0),
+        around,
+    )
+    up_own, late_queries = pin((up_own, queries))
+    up_slots = exchange(up_own)
+    cotangent, late_queries = pin((cotangent, late_queries))
+    upstream_low = spread(cotangent)
     attended, logs = attend(place, queries, key_rows, value_rows, seq_count)
-    logs = logs.T.reshape(64, 2, seq_count * block_len)
-    middle = wide_in + product(attended, weights[3], (1, 0)) + obias
-    unit_two, _ = normalised(middle)
-    normed_two_low = (unit_two * gain_second + shift_second).astype(low)
-    active, slopes = [], []
-    for slot in range(4):
-        bias = chosen(classes[slot], [ubias[:, kind] for kind in range(4)]).reshape(width)
-        hidden = product(normed_two_low, up_slots[slot], (1, 0)) + bias
-        value, slope = gelu_pair(hidden)
-        active.append(value.astype(low))
-        slopes.append(slope.astype(low))
-    result = middle + dbias
-    for slot in range(4):
-        result = result + product(active[slot], down_slots[slot], (1, 0))
+    down_own, late_attended = pin((down_own, attended))
+    down_slots = exchange(down_own)
+    turned_logs = logs.T.reshape(64, 2, rows)
+    middle, normed_two_low = by_rows(
+        middle_kernel,
+        "middle",
+        rows,
+        width,
+        ([rows_in, attended], []),
+        [jnp.concatenate([obias, gain_second, shift_second], axis=0)],
+        [weights],
+        [wide, low],
+        0,
+        [(4,) + section.shape],
+        1,
+        1,
+    )
+    up_outs = by_rows(
+        up_kernel,
+        "up",
+        rows,
+        width,
+        ([normed_two_low], []),
+        [ubias],
+        up_slots,
+        [low] * 8,
+        0,
+        [(4,) + area],
+        4,
+        4,
+    )
+    active, slopes = up_outs[:4], up_outs[4:]
+    (result,) = by_rows(
+        down_kernel,
+        "down",
+        rows,
+        width,
+        ([middle], active),
+        [dbias],
+        down_slots,
+        [low],
+        0,
+        [(4,) + area],
+        4,
+        4,
+    )
     outputs = collect(result, low)
 
-    upstream_low = spread(cotangent)
-    upstream = upstream_low.astype(wide)
-    down_parts = reduce_pieces(
-        [product(active[slot], upstream_low, (0, 0)).astype(low) for slot in range(4)]
-    )
-    hidden_low = [
-        (product(upstream_low, down_slots[slot], (1, 1)) * slopes[slot].astype(wide)).astype(low)
-        for slot in range(4)
+    down_terms = [product(active[slot], upstream_low, (0, 0)).astype(low) for slot in range(4)]
+    upstream_low, *down_terms = pin((upstream_low, *down_terms))
+    down_parts = reduce_pieces(down_terms)
+    back_outs = by_rows(
+        back_kernel,
+        "back",
+        rows,
+        width,
+        ([upstream_low, middle], slopes),
+        [gain_second],
+        down_slots + up_slots + [weights],
+        [low] * 4 + [wide, low, low],
+        8,
+        [(4,) + area, (4,) + area, (4,) + section.shape],
+        9,
+        9,
+    )
+    hidden_low = back_outs[:4]
+    middle_grad, middle_low, grad_low, back_sums = back_outs[4:]
+    up_terms = [
+        product(normed_two_low, hidden_low[slot], (0, 0)).astype(low) for slot in range(4)
     ]
-    up_parts = reduce_pieces(
-        [product(normed_two_low, hidden_low[slot], (0, 0)).astype(low) for slot in range(4)]
-    )
-    normed_two_grad = sum(product(hidden_low[slot], up_slots[slot], (1, 1)) for slot in range(4))
-    middle_part, gain_two_grad, shift_two_grad = norm_back(middle, gain_second, normed_two_grad)
-    middle_grad = upstream + middle_part
-    middle_low = middle_grad.astype(low)
-    grad_low = product(middle_low, weights[3], (1, 1)).astype(low)
+    out_term = product(attended, middle_low, (0, 0)).astype(low)
+    grad_low, out_term, *up_terms = pin((grad_low, out_term, *up_terms))
+    up_parts = reduce_pieces(up_terms)
     query_low, key_low, value_low = attend_back(
-        place, queries, key_rows, value_rows, grad_low, attended, logs, seq_count
-    )
-    section_grads = [
-        product(normed_low, query_low, (0, 0)).astype(low),
-        product(normed_low, key_low, (0, 0)).astype(low),
-        product(normed_low, value_low, (0, 0)).astype(low),
-        product(attended, middle_low, (0, 0)).astype(low),
+        place,
+        late_queries,
+        key_rows,
+        value_rows,
+        grad_low,
+        late_attended,
+        turned_logs,
+        seq_count,
+    )
+    in_terms = [
+        product(normed_low, grad, (0, 0)).astype(low) for grad in (query_low, key_low, value_low)
     ]
+    query_low, key_low, value_low, *in_terms = pin(
+        (query_low, key_low, value_low, *in_terms)
+    )
+    section_grads = in_terms + [out_term]
     section_parts = reduce_pieces([chosen(kind, section_grads) for kind in classes])
-    normed_grad = (
-        product(query_low, weights[0], (1, 1))
-        + product(key_low, weights[1], (1, 1))
-        + product(value_low, weights[2], (1, 1))
-    )
-    input_part, gain_one_grad, shift_one_grad = norm_back(wide_in, gain_first, normed_grad)
-    input_gradient = collect(middle_grad + input_part, wide)
-
-    def column_sum(values):
-        return jnp.sum(values.astype(wide), axis=0)
-
-    hidden_sums = [column_sum(hidden_low[slot]).reshape(4, quarter) for slot in range(4)]
+    input_low, last_sums = by_rows(
+        last_kernel,
+        "last",
+        rows,
+        width,
+        ([query_low, key_low, value_low, rows_in, middle_grad], []),
+        [gain_first],
+        [weights],
+        [low],
+        4,
+        [(12,) + section.shape],
+        3,
+        3,
+    )
+    input_gradient = collect(input_low, wide)
+
+    back_sums = jnp.sum(back_sums, axis=1)
+    last_sums = jnp.sum(last_sums, axis=1)
+    hidden_sums = [back_sums[slot].reshape(4, quarter) for slot in range(4)]
     hidden_sums = jnp.stack(
         [chosen(slot_of[kind], hidden_sums) for kind in range(4)], axis=1
     ).reshape(4, 4 * quarter)
     early = reduce_vector(
         jnp.concatenate(
-            [
-                values.reshape(4, quarter)
-                for values in (
-                    column_sum(middle_low),
-                    gain_two_grad,
-                    shift_two_grad,
-                    column_sum(upstream_low),
-                )
-            ]
-            + [hidden_sums],
-            axis=1,
+            [back_sums[at].reshape(4, quarter) for at in range(4, 8)] + [hidden_sums], axis=1
         ),
         z,
     )
     late = reduce_vector(
-        jnp.concatenate(
-            [
-                values.reshape(4, quarter)
-                for values in (
-                    gain_one_grad,
-                    shift_one_grad,
-                    column_sum(query_low),
-                    column_sum(value_low),
-                )
-            ],
-            axis=1,
-        ),
-        z,
-    )
-    obias_sum, gain_two_sum, shift_two_sum, dbias_sum = (
+        jnp.concatenate([last_sums[at].reshape(4, quarter) for at in range(4)], axis=1), z
+    )
+    gain_two_sum, shift_two_sum, dbias_sum, obias_sum = (
         early[at * quarter : (at + 1) * quarter] for at in range(4)
     )
     ubias_sum = early[4 * quarter :]

time: 787 us -> 768 us (0.976)
  matrix products: 261 us -> 52.9 us
  Pallas kernels: 94 us -> 240 us
  starting transfers between devices: 51.4 us -> 104 us
  local copies, waits for them, and re-layouts: 80.8 us -> 72.8 us
    dot_general x36 -> x12, matrix products: 261 us -> 52.9 us  [product(): lax.dot_general(left, right, ((dims[:1], dims[1:]), ((), ())), preferred_...]
    pallas_call x0 -> x6, Pallas kernels: none -> 154 us  [the longest x5 133 us: by_rows(): pl.pallas_call(kernel, grid=(rows // step,), in_specs=[tile] * len(tiled[...]
    ppermute x30 -> x36, waiting for transfers between devices: 18.3 us -> 105 us  [plane_swap(): lax.ppermute(values, ('dp', 'ctx'), [(device, plane_partner(device, kind)...]
    all_gather x3 -> x2, waiting for transfers between devices: 83.5 us -> 0.01 us  [the longest x1 0.01 us: per_device_exchanged(): up_own = lax.all_gather(up_piece, 'fsdp', axis=0, tiled=True)]
    ppermute x30 -> x36, starting transfers between devices: 20.3 us -> 75.3 us  [plane_swap(): lax.ppermute(values, ('dp', 'ctx'), [(device, plane_partner(device, kind)...]
    ppermute x0 -> x3, waiting for transfers between devices: none -> 49.7 us  [per_device_exchanged(): lax.ppermute(section, 'fsdp', [(device, (device + step) % 4) for device i...]
    ppermute x12, waiting for transfers between devices: 85.3 us -> 51.2 us  [ctx_swap(): lax.ppermute(values, 'ctx', [(device, device ^ bits) for device in range(...]
    reduce_scatter x3, waiting for transfers between devices: 27.2 us -> 13.4 us  [reduce_pieces(): shard = lax.psum_scatter(first, 'fsdp', scatter_dimension=0, tiled=True)]
  transfers between devices with their start and end apart: 63 -> 71, of which waited for: 15 -> 16; matrix products, arithmetic and copies ran while one was open for 43% -> 20% of each run, Pallas kernels for 6% -> 32%
where the time goes in v2:
time: 768 us; the launch traced here: 760 us
  Pallas kernels  240 us (31%)
  waiting for transfers between devices  221 us (29%)
  starting transfers between devices  104 us (14%)
  local copies, waits for them, and re-layouts  72.8 us (9%)
  other arithmetic  54.7 us (7%)
  matrix products  52.9 us (7%)
  between operations  15.7 us (2%)
    pallas_call x5, Pallas kernels, by_rows(): pl.pallas_call(kernel, grid=(rows // step,), in_specs=[tile] * len(tiled[...  133 us
    ppermute x36, waiting for transfers between devices, plane_swap(): lax.ppermute(values, ('dp', 'ctx'), [(device, plane_partner(device, kind)...  105 us
    ppermute x36, starting transfers between devices, plane_swap(): lax.ppermute(values, ('dp', 'ctx'), [(device, plane_partner(device, kind)...  75.3 us
    dot_general x12, matrix products, product(): lax.dot_general(left, right, ((dims[:1], dims[1:]), ((), ())), preferred_...  52.9 us
    ppermute x12, waiting for transfers between devices, ctx_swap(): lax.ppermute(values, 'ctx', [(device, device ^ bits) for device in range(...  51.2 us
    ppermute x3, waiting for transfers between devices, per_device_exchanged(): lax.ppermute(section, 'fsdp', [(device, (device + step) % 4) for device i...  49.7 us
    pallas_call x1, Pallas kernels, attend_back(): pl.pallas_call(functools.partial(attend_back_kernel, count=count, width=w...  45.9 us
    pallas_call x1, Pallas kernels, attend(): pl.pallas_call(functools.partial(attend_kernel, count=count, width=width)...  32 us
  transfers between devices with their start and end apart: 71, of which 16 were waited for; matrix products, arithmetic and copies ran while one was open for 20% of the time, Pallas kernels for 32%

profile of v2, /device:TPU:8, one launch (start us, length us, event | category | flops | bytes accessed | tf_op | source)
XLA Modules:
  0.0 760.0 jit_solution(15248470379019223177)
XLA Ops:
  7.3 3.6 select_select_fusion.9
  18.3 35.8 %collective-permute-done.6.refs_4_ = bf16[272,1088]{1,0:T(8,128)(2,1)} collective-permute-done((bf16[272,1088]{1,0:T(8,128)(2,1)}, bf16[272,1088]{1,0:T(8,128)(2,1)}, u32[]{:S(2)}, u32[]{:S(2)}) %collective-permute-start.6) | collective-permute-done | bytes 591904 | tf_op jit(solution)/shard_map/ppermute | solution.py:1029
  54.1 12.1 %collective-permute-done.7.refs_5_ = bf16[272,1088]{1,0:T(8,128)(2,1)} collective-permute-done((bf16[272,1088]{1,0:T(8,128)(2,1)}, bf16[272,1088]{1,0:T(8,128)(2,1)}, u32[]{:S(2)}, u32[]{:S(2)}) %collective-permute-start.7) | collective-permute-done | bytes 591904 | tf_op jit(solution)/shard_map/ppermute | solution.py:1029
  80.0 5.9 collective-permute-done.2
  87.4 10.9 %collective-permute-done.1 = bf16[256,1088]{0,1:T(8,128)(2,1)} collective-permute-done((bf16[256,1088]{0,1:T(8,128)(2,1)}, bf16[256,1088]{0,1:T(8,128)(2,1)}, u32[]{:S(2)}, u32[]{:S(2)}) %collective-permute-start.1) | collective-permute-done | bytes 557088 | tf_op jit(solution)/shard_map/ppermute | solution.py:610
  101.0 3.9 collective-permute-start.14
  104.9 6.7 collective-permute-start.15
  111.6 6.7 collective-permute-start.16
  124.7 21.2 %front.1 = (bf16[1024,1088]{1,0:T(8,128)(2,1)}, bf16[1024,1088]{1,0:T(8,128)(2,1)}, bf16[1024,1088]{1,0:T(8,128)(2,1)}, bf16[1024,1088]{1,0:T(8,128)(2,1)}, bf16[16,272,1088]{2,1,0:T(8,128)(2,1)}) custom-call(s32[16]{0:T(128)} %stack.125.places_ref, bf16[1024,1088]{1,0:T(8,128)(2,1)} %pad_maximum_fusion.x_ref, f32[4,1088]{1,0:T(4,128)} %pad_maximum_fusion.3.vectors_ref, ...), custom_call_target="tpu_custom_call" | custom-call | flops 7272923136 | bytes 20471808 | tf_op jit(solution)/shard_map/front/pallas_call | solution.py:740
  147.5 29.2 %collective-permute-done.18.refs_1_.refs_9_ = bf16[1088,1088]{1,0:T(8,128)(2,1)} collective-permute-done((bf16[1088,1088]{1,0:T(8,128)(2,1)}, bf16[1088,1088]{1,0:T(8,128)(2,1)}, u32[]{:S(2)}, u32[]{:S(2)}) %collective-permute-start.18) | collective-permute-done | bytes 2367520 | tf_op jit(solution)/shard_map/ppermute | solution.py:604
  181.7 32.0 %attend.1 = (bf16[1024,1088]{1,0:T(8,128)(2,1)S(1)}, f32[1024,128]{1,0:T(8,128)S(1)}) custom-call(s32[1]{0:T(128)} %bitcast.place_ref, bf16[1024,1088]{1,0:T(8,128)(2,1)S(1)} %copy-done.11, bf16[1024,1088]{1,0:T(8,128)(2,1)} %get-tuple-element.78.k_ref, bf16[1024,1088]{1,0:T(8,128)(2,1)} %get-tuple-element.79.v_ref), custom_call_target="tpu_custom_call" | custom-call | flops 4563402752 | bytes 8912896 | tf_op jit(solution)/shard_map/attend/pallas_call | solution.py:514
  219.3 9.5 %middle.1 = (f32[1024,1088]{1,0:T(8,128)}, bf16[1024,1088]{1,0:T(8,128)(2,1)}) custom-call(bf16[1024,1088]{1,0:T(8,128)(2,1)} %pad_maximum_fusion.x_ref, bf16[1024,1088]{1,0:T(8,128)(2,1)} %copy-done.7, f32[3,1088]{1,0:T(4,128)} %pad_maximum_fusion.4.vectors_ref, bf16[16,272,1088]{2,1,0:T(8,128)(2,1)} %get-tuple-element.81.all_ref.refs_12_), custom_call_target="tpu_custom_call" | custom-call | flops 2424307712 | bytes 6823936 | tf_op jit(solution)/shard_map/middle/pallas_call | solution.py:950
  237.0 24.0 %collective-permute-start.22 = (bf16[1088,1088]{1,0:T(8,128)(2,1)}, bf16[1088,1088]{1,0:T(8,128)(2,1)}, u32[]{:S(2)}, u32[]{:S(2)}) collective-permute-start(bf16[1088,1088]{1,0:T(8,128)(2,1)} %all-gather.5.cloned.1.call-done.refs_4_), channel_id=1, source_target_pairs={{0,1},{1,0},{2,3},{3,2},{16,17},{17,16},{18,19},{19,18},{4,5},{5,4... | collective-permute-start | bytes 7102472 | tf_op jit(solution)/shard_map/ppermute | solution.py:604
  261.0 29.7 %up.1 = (bf16[1024,1088]{1,0:T(8,128)(2,1)}, bf16[1024,1088]{1,0:T(8,128)(2,1)}, bf16[1024,1088]{1,0:T(8,128)(2,1)}, bf16[1024,1088]{1,0:T(8,128)(2,1)}, bf16[10...) custom-call(bf16[1024,1088]{1,0:T(8,128)(2,1)} %get-tuple-element.83., ...), custom_call_target="tpu_custom_call" | custom-call | flops 9697230848 | bytes 27295744 | tf_op jit(solution)/shard_map/up/pallas_call | solution.py:950
  290.8 6.4 convolution_convert_fusion.11
  297.2 4.5 convolution_convert_fusion.10
  301.7 4.6 convolution_convert_fusion.9
  306.3 4.5 convolution_convert_fusion.8
  313.2 50.7 %back.1 = (bf16[1024,1088]{1,0:T(8,128)(2,1)}, bf16[1024,1088]{1,0:T(8,128)(2,1)}, bf16[1024,1088]{1,0:T(8,128)(2,1)}, bf16[1024,1088]{1,0:T(8,128)(2,1)}, f32[1...) custom-call(bf16[1024,1088]{1,0:T(8,128)(2,1)} %pad_maximum_fusion.1.g_ref, ...), custom_call_target="tpu_custom_call" | custom-call | flops 21818769408 | bytes 61415424 | tf_op jit(solution)/shard_map/back/pallas_call | solution.py:950
  363.9 4.9 convolution_convert_fusion.7
  368.9 4.6 convolution_convert_fusion.6
  373.5 4.6 convolution_convert_fusion.5
  378.0 4.6 convolution_convert_fusion.4
  382.6 4.8 convolution_convert_fusion.3
  387.5 45.9 %attend_back.1 = (bf16[1024,1088]{1,0:T(8,128)(2,1)S(1)}, bf16[1024,1088]{1,0:T(8,128)(2,1)S(1)}, bf16[1024,1088]{1,0:T(8,128)(2,1)}) custom-call(s32[1]{0:T(128)} %bitcast.place_ref, bf16[1024,1088]{1,0:T(8,128)(2,1)} %get-tuple-element.94.q_ref, bf16[1024,1088]{1,0:T(8,128)(2,1)} %get-tuple-element.78.k_ref, bf16[1024,1088]{1,0:T(8,128)(2,1)} %get-tuple-element.79.v_ref, ...), custom_call_target="tpu_custom_call" | custom-call | flops 11408506880 | bytes 17825792 | tf_op jit(solution)/shard_map/attend_back/pallas_call | solution.py:546
  433.4 3.1 convolution_convert_fusion.2
  436.6 3.1 convolution_convert_fusion.1
  439.7 3.1 convolution_convert_fusion
  446.4 3.8 add_convert_fusion.1
  452.8 4.8 add_convert_fusion.5
  459.1 21.8 %collective-permute-done.61 = bf16[1088,1088]{1,0:T(8,128)(2,1)S(1)} collective-permute-done((bf16[1088,1088]{1,0:T(8,128)(2,1)}, bf16[1088,1088]{1,0:T(8,128)(2,1)S(1)}, u32[]{:S(2)}, u32[]{:S(2)}) %collective-permute-start.61) | collective-permute-done | bytes 2367520 | tf_op jit(solution)/shard_map/ppermute | solution.py:604
  483.9 23.9 %collective-permute-done.41 = bf16[1088,1088]{1,0:T(8,128)(2,1)} collective-permute-done((bf16[1088,1088]{1,0:T(8,128)(2,1)}, bf16[1088,1088]{1,0:T(8,128)(2,1)}, u32[]{:S(2)}, u32[]{:S(2)}) %collective-permute-start.41) | collective-permute-done | bytes 2367520 | tf_op jit(solution)/shard_map/ppermute | solution.py:604
  507.9 6.6 add_convert_fusion.4
  514.5 3.3 add_convert_fusion.3
  519.4 28.9 %collective-permute-done.54 = bf16[1088,1088]{1,0:T(8,128)(2,1)S(1)} collective-permute-done((bf16[1088,1088]{1,0:T(8,128)(2,1)S(1)}, bf16[1088,1088]{1,0:T(8,128)(2,1)S(1)}, u32[]{:S(2)}, u32[]{:S(2)}) %collective-permute-start.54) | collective-permute-done | bytes 2367520 | tf_op jit(solution)/shard_map/ppermute | solution.py:604
  548.3 4.1 add_convert_fusion.2
  553.7 21.7 %last.1 = (bf16[1024,1088]{1,0:T(8,128)(2,1)}, f32[4,8,1088]{2,1,0:T(8,128)}) custom-call(bf16[1024,1088]{1,0:T(8,128)(2,1)} %copy-done.9, bf16[1024,1088]{1,0:T(8,128)(2,1)} %copy-done.10, bf16[1024,1088]{1,0:T(8,128)(2,1)} %get-tuple-element.116.v_ref, bf16[1024,1088]{1,0:T(8,128)(2,1)} %pad_maximum_fusion.x_ref, ...), custom_call_target="tpu_custom_call" | custom-call | flops 7272923136 | bytes 20471808 | tf_op jit(solution)/shard_map/last/pallas_call | solution.py:950
  589.4 21.2 %down.1 = bf16[1024,1088]{1,0:T(8,128)(2,1)} custom-call(f32[1024,1088]{1,0:T(8,128)} %get-tuple-element.82.middle_ref, f32[1,1088]{1,0:T(1,128)} %reshape.469.vectors_ref, bf16[1024,1088]{1,0:T(8,128)(2,1)} %get-tuple-element.87.refs_0_, bf16[1024,1088]{1,0:T(8,128)(2,1)} %get-tuple-element.88.refs_1_, bf16[1024,1088]{1,0:T(8,128)(2,1)} %get-tuple-element.89.refs_2_, ...), custom_call_target="tpu_custom_call" | custom-call | flops 9697230848 | bytes 27295744 | tf_op jit(solution)/shard_map/down/pallas_call | solution.py:950
  624.9 13.4 %reduce-scatter.6.cloned.1.call-done = bf16[272,1088]{1,0:T(8,128)(2,1)} async-done(((bf16[1088,1088]{1,0:T(8,128)(2,1)}), bf16[272,1088]{1,0:T(8,128)(2,1)}) %reduce-scatter.6.cloned.1.call-update) | async-done | bytes 591888 | tf_op jit(solution)/shard_map/reduce_scatter | solution.py:621
  649.7 14.8 %collective-permute-done.26 = bf16[256,1088]{0,1:T(8,128)(2,1)S(1)} collective-permute-done((bf16[256,1088]{0,1:T(8,128)(2,1)}, bf16[256,1088]{0,1:T(8,128)(2,1)S(1)}, u32[]{:S(2)}, u32[]{:S(2)}) %collective-permute-start.26) | collective-permute-done | bytes 557088 | tf_op jit(solution)/shard_map/ppermute | solution.py:610
  669.1 11.2 %collective-permute-done.31 = bf16[256,1088]{0,1:T(8,128)(2,1)S(1)} collective-permute-done((bf16[256,1088]{0,1:T(8,128)(2,1)}, bf16[256,1088]{0,1:T(8,128)(2,1)S(1)}, u32[]{:S(2)}, u32[]{:S(2)}) %collective-permute-start.31) | collective-permute-done | bytes 557088 | tf_op jit(solution)/shard_map/ppermute | solution.py:610
  680.3 11.5 %collective-permute-start.44 = (bf16[272,1088]{1,0:T(8,128)(2,1)}, bf16[272,1088]{1,0:T(8,128)(2,1)}, u32[]{:S(2)}, u32[]{:S(2)}) collective-permute-start(bf16[272,1088]{1,0:T(8,128)(2,1)} %add_convert_fusion.8), channel_id=1, source_target_pairs={{0,1},{1,0},{2,3},{3,2},{16,17},{17,16},{18,19},{19,18},{4,5},{5,4... | collective-permute-start | bytes 1775624 | tf_op jit(solution)/shard_map/ppermute | solution.py:604
  691.8 6.3 collective-permute-done.32
  719.5 6.0 copy.71
  725.4 4.1 settle.5
  730.1 3.3 select_convert_fusion
  743.4 5.7 concatenate.47
  749.0 4.2 convert_element_type.196
  (358 shorter events, 143.3 us)
Async XLA Ops:
  7.2 117.2 %all-gather.3.cloned.1.call-start = ((), (), s32[]{:S(2)}) async-start(), calls=%async_computation.3 | async-start | bytes 3133440 | tf_op jit(solution)/shard_map/all_gather | solution.py:1052
  10.8 43.3 %collective-permute-start.6 = (bf16[272,1088]{1,0:T(8,128)(2,1)}, bf16[272,1088]{1,0:T(8,128)(2,1)}, u32[]{:S(2)}, u32[]{:S(2)}) collective-permute-start(bf16[272,1088]{1,0:T(8,128)(2,1)} %get-tuple-element.213), channel_id=1, source_target_pairs={{0,4},{4,8},{8,12},{12,0},{1,5},{5,9},{9,13},{13,1},{2,6},{6,10},{... | collective-permute-start | bytes 1775624 | tf_op jit(solution)/shard_map/ppermute | solution.py:1029
  12.4 53.8 %collective-permute-start.7 = (bf16[272,1088]{1,0:T(8,128)(2,1)}, bf16[272,1088]{1,0:T(8,128)(2,1)}, u32[]{:S(2)}, u32[]{:S(2)}) collective-permute-start(bf16[272,1088]{1,0:T(8,128)(2,1)} %get-tuple-element.213), channel_id=1, source_target_pairs={{0,8},{4,12},{8,0},{12,4},{1,9},{5,13},{9,1},{13,5},{2,10},{6,14},... | collective-permute-start | bytes 1775624 | tf_op jit(solution)/shard_map/ppermute | solution.py:1029
  13.4 54.6 %collective-permute-start.8 = (bf16[272,1088]{1,0:T(8,128)(2,1)}, bf16[272,1088]{1,0:T(8,128)(2,1)}, u32[]{:S(2)}, u32[]{:S(2)}) collective-permute-start(bf16[272,1088]{1,0:T(8,128)(2,1)} %get-tuple-element.213), channel_id=1, source_target_pairs={{0,12},{4,0},{8,4},{12,8},{1,13},{5,1},{9,5},{13,9},{2,14},{6,2},{... | collective-permute-start | bytes 1775624 | tf_op jit(solution)/shard_map/ppermute | solution.py:1029
  68.0 147.1 %all-gather.5.cloned.1.call-start = ((), (), s32[]{:S(2)}) async-start(), calls=%async_computation.4 | async-start | bytes 3133440 | tf_op jit(solution)/shard_map/all_gather | solution.py:1055
  72.2 26.1 %collective-permute-start.1 = (bf16[256,1088]{0,1:T(8,128)(2,1)}, bf16[256,1088]{0,1:T(8,128)(2,1)}, u32[]{:S(2)}, u32[]{:S(2)}) collective-permute-start(bf16[256,1088]{0,1:T(8,128)(2,1)} %get-tuple-element.212), channel_id=1, source_target_pairs={{0,2},{1,3},{2,0},{3,1},{4,6},{5,7},{6,4},{7,5},{8,10},{9,11},{10,... | collective-permute-start | bytes 1671176 | tf_op jit(solution)/shard_map/ppermute | solution.py:610
  78.3 22.6 %collective-permute-start = (bf16[256,1088]{0,1:T(8,128)(2,1)}, bf16[256,1088]{0,1:T(8,128)(2,1)S(1)}, u32[]{:S(2)}, u32[]{:S(2)}) collective-permute-start(bf16[256,1088]{0,1:T(8,128)(2,1)} %get-tuple-element.210), channel_id=1, source_target_pairs={{0,1},{1,0},{2,3},{3,2},{4,5},{5,4},{6,7},{7,6},{8,9},{9,8},{10,11... | collective-permute-start | bytes 1671176 | tf_op jit(solution)/shard_map/ppermute | solution.py:610
  78.4 22.6 %collective-permute-start.9 = (bf16[272,1088]{1,0:T(8,128)(2,1)}, bf16[272,1088]{1,0:T(8,128)(2,1)}, u32[]{:S(2)}, u32[]{:S(2)}) collective-permute-start(bf16[272,1088]{1,0:T(8,128)(2,1)} %collective-permute-done.6.refs_4_), channel_id=1, source_target_pairs={{0,16},{1,3},{2,18},{3,1},{16,0},{17,19},{18,2},{19,17},{4,20},{5,... | collective-permute-start | bytes 1775624 | tf_op jit(solution)/shard_map/ppermute | solution.py:604
  80.0 38.3 %collective-permute-start.12 = (bf16[272,1088]{1,0:T(8,128)(2,1)}, bf16[272,1088]{1,0:T(8,128)(2,1)S(1)}, u32[]{:S(2)}, u32[]{:S(2)}) collective-permute-start(bf16[272,1088]{1,0:T(8,128)(2,1)} %collective-permute-done.6.refs_4_), channel_id=1, source_target_pairs={{0,1},{1,0},{2,3},{3,2},{16,17},{17,16},{18,19},{19,18},{4,5},{5,4... | collective-permute-start | bytes 1775624 | tf_op jit(solution)/shard_map/ppermute | solution.py:604
  85.9 19.0 %collective-permute-start.10 = (bf16[272,1088]{1,0:T(8,128)(2,1)}, bf16[272,1088]{1,0:T(8,128)(2,1)}, u32[]{:S(2)}, u32[]{:S(2)}) collective-permute-start(bf16[272,1088]{1,0:T(8,128)(2,1)} %collective-permute-done.7.refs_5_), channel_id=1, source_target_pairs={{0,16},{1,3},{2,18},{3,1},{16,0},{17,19},{18,2},{19,17},{4,20},{5,... | collective-permute-start | bytes 1775624 | tf_op jit(solution)/shard_map/ppermute | solution.py:604
  100.9 23.7 %collective-permute-start.13 = (bf16[272,1088]{1,0:T(8,128)(2,1)}, bf16[272,1088]{1,0:T(8,128)(2,1)}, u32[]{:S(2)}, u32[]{:S(2)}) collective-permute-start(bf16[272,1088]{1,0:T(8,128)(2,1)} %collective-permute-done.7.refs_5_), channel_id=1, source_target_pairs={{0,1},{1,0},{2,3},{3,2},{16,17},{17,16},{18,19},{19,18},{4,5},{5,4... | collective-permute-start | bytes 1775624 | tf_op jit(solution)/shard_map/ppermute | solution.py:604
  101.0 23.6 %collective-permute-start.14 = (bf16[272,1088]{1,0:T(8,128)(2,1)}, bf16[272,1088]{1,0:T(8,128)(2,1)}, u32[]{:S(2)}, u32[]{:S(2)}) collective-permute-start(bf16[272,1088]{1,0:T(8,128)(2,1)} %collective-permute-done.8.refs_6_), channel_id=1, source_target_pairs={{0,1},{1,0},{2,3},{3,2},{16,17},{17,16},{18,19},{19,18},{4,5},{5,4... | collective-permute-start | bytes 1775624 | tf_op jit(solution)/shard_map/ppermute | solution.py:604
  104.9 19.8 %collective-permute-start.15 = (bf16[272,1088]{1,0:T(8,128)(2,1)}, bf16[272,1088]{1,0:T(8,128)(2,1)}, u32[]{:S(2)}, u32[]{:S(2)}) collective-permute-start(bf16[272,1088]{1,0:T(8,128)(2,1)} %collective-permute-done.9.refs_7_), channel_id=1, source_target_pairs={{0,1},{1,0},{2,3},{3,2},{16,17},{17,16},{18,19},{19,18},{4,5},{5,4... | collective-permute-start | bytes 1775624 | tf_op jit(solution)/shard_map/ppermute | solution.py:604
  124.4 464.5 %reduce-scatter.8.cloned.1.call-start = ((), (), s32[]{:S(2)}) async-start(), calls=%async_computation.7 | async-start | bytes 3133440 | tf_op jit(solution)/shard_map/reduce_scatter | solution.py:621
  145.9 30.8 %collective-permute-start.18 = (bf16[1088,1088]{1,0:T(8,128)(2,1)}, bf16[1088,1088]{1,0:T(8,128)(2,1)}, u32[]{:S(2)}, u32[]{:S(2)}) collective-permute-start(bf16[1088,1088]{1,0:T(8,128)(2,1)} %all-gather.3.cloned.1.call-done.refs_0_.refs_8_), channel_id=1, source_target_pairs={{0,16},{1,3},{2,18},{3,1},{16,0},{17,19},{18,2},{19,17},{4,20},{5,... | collective-permute-start | bytes 7102472 | tf_op jit(solution)/shard_map/ppermute | solution.py:604
  147.5 113.5 %collective-permute-start.19 = (bf16[1088,1088]{1,0:T(8,128)(2,1)}, bf16[1088,1088]{1,0:T(8,128)(2,1)}, u32[]{:S(2)}, u32[]{:S(2)}) collective-permute-start(bf16[1088,1088]{1,0:T(8,128)(2,1)} %all-gather.3.cloned.1.call-done.refs_0_.refs_8_), channel_id=1, source_target_pairs={{0,1},{1,0},{2,3},{3,2},{16,17},{17,16},{18,19},{19,18},{4,5},{5,4... | collective-permute-start | bytes 7102472 | tf_op jit(solution)/shard_map/ppermute | solution.py:604
  176.7 84.3 %collective-permute-start.20 = (bf16[1088,1088]{1,0:T(8,128)(2,1)}, bf16[1088,1088]{1,0:T(8,128)(2,1)}, u32[]{:S(2)}, u32[]{:S(2)}) collective-permute-start(bf16[1088,1088]{1,0:T(8,128)(2,1)} %collective-permute-done.18.refs_1_.refs_9_), channel_id=1, source_target_pairs={{0,1},{1,0},{2,3},{3,2},{16,17},{17,16},{18,19},{19,18},{4,5},{5,4... | collective-permute-start | bytes 7102472 | tf_op jit(solution)/shard_map/ppermute | solution.py:604
  179.9 37.3 %collective-permute-start.29 = (bf16[256,1088]{0,1:T(8,128)(2,1)}, bf16[256,1088]{0,1:T(8,128)(2,1)}, u32[]{:S(2)}, u32[]{:S(2)}) collective-permute-start(bf16[256,1088]{0,1:T(8,128)(2,1)} %get-tuple-element.206), channel_id=1, source_target_pairs={{0,3},{1,2},{2,1},{3,0},{4,7},{5,6},{6,5},{7,4},{8,11},{9,10},{10,... | collective-permute-start | bytes 1671176 | tf_op jit(solution)/shard_map/ppermute | solution.py:610
  215.2 75.5 %collective-permute-start.21 = (bf16[1088,1088]{1,0:T(8,128)(2,1)}, bf16[1088,1088]{1,0:T(8,128)(2,1)}, u32[]{:S(2)}, u32[]{:S(2)}) collective-permute-start(bf16[1088,1088]{1,0:T(8,128)(2,1)} %all-gather.5.cloned.1.call-done.refs_4_), channel_id=1, source_target_pairs={{0,16},{1,3},{2,18},{3,1},{16,0},{17,19},{18,2},{19,17},{4,20},{5,... | collective-permute-start | bytes 7102472 | tf_op jit(solution)/shard_map/ppermute | solution.py:604
  237.0 74.3 %collective-permute-start.22 = (bf16[1088,1088]{1,0:T(8,128)(2,1)}, bf16[1088,1088]{1,0:T(8,128)(2,1)}, u32[]{:S(2)}, u32[]{:S(2)}) collective-permute-start(bf16[1088,1088]{1,0:T(8,128)(2,1)} %all-gather.5.cloned.1.call-done.refs_4_), channel_id=1, source_target_pairs={{0,1},{1,0},{2,3},{3,2},{16,17},{17,16},{18,19},{19,18},{4,5},{5,4... | collective-permute-start | bytes 7102472 | tf_op jit(solution)/shard_map/ppermute | solution.py:604
  290.7 21.1 %collective-permute-start.23 = (bf16[1088,1088]{1,0:T(8,128)(2,1)}, bf16[1088,1088]{1,0:T(8,128)(2,1)S(1)}, u32[]{:S(2)}, u32[]{:S(2)}) collective-permute-start(bf16[1088,1088]{1,0:T(8,128)(2,1)} %collective-permute-done.21.refs_5_), channel_id=1, source_target_pairs={{0,1},{1,0},{2,3},{3,2},{16,17},{17,16},{18,19},{19,18},{4,5},{5,4... | collective-permute-start | bytes 7102472 | tf_op jit(solution)/shard_map/ppermute | solution.py:604
  310.8 134.8 %collective-permute-start.60 = (bf16[1088,1088]{1,0:T(8,128)(2,1)}, bf16[1088,1088]{1,0:T(8,128)(2,1)}, u32[]{:S(2)}, u32[]{:S(2)}) collective-permute-start(bf16[1088,1088]{1,0:T(8,128)(2,1)} %convolution_convert_fusion.8), channel_id=1, source_target_pairs={{0,1},{1,0},{2,3},{3,2},{16,17},{17,16},{18,19},{19,18},{4,5},{5,4... | collective-permute-start | bytes 7102472 | tf_op jit(solution)/shard_map/ppermute | solution.py:604
  450.2 30.6 %collective-permute-start.61 = (bf16[1088,1088]{1,0:T(8,128)(2,1)}, bf16[1088,1088]{1,0:T(8,128)(2,1)S(1)}, u32[]{:S(2)}, u32[]{:S(2)}) collective-permute-start(bf16[1088,1088]{1,0:T(8,128)(2,1)} %add_convert_fusion.1), channel_id=1, source_target_pairs={{0,16},{1,3},{2,18},{3,1},{16,0},{17,19},{18,2},{19,17},{4,20},{5,... | collective-permute-start | bytes 7102472 | tf_op jit(solution)/shard_map/ppermute | solution.py:604
  451.8 32.1 %collective-permute-start.39 = (bf16[1088,1088]{1,0:T(8,128)(2,1)}, bf16[1088,1088]{1,0:T(8,128)(2,1)}, u32[]{:S(2)}, u32[]{:S(2)}) collective-permute-start(bf16[1088,1088]{1,0:T(8,128)(2,1)} %get-tuple-element.183), channel_id=1, source_target_pairs={{0,1},{1,0},{2,3},{3,2},{16,17},{17,16},{18,19},{19,18},{4,5},{5,4... | collective-permute-start | bytes 7102472 | tf_op jit(solution)/shard_map/ppermute | solution.py:604
  457.6 50.2 %collective-permute-start.41 = (bf16[1088,1088]{1,0:T(8,128)(2,1)}, bf16[1088,1088]{1,0:T(8,128)(2,1)}, u32[]{:S(2)}, u32[]{:S(2)}) collective-permute-start(bf16[1088,1088]{1,0:T(8,128)(2,1)} %add_convert_fusion.5), channel_id=1, source_target_pairs={{0,16},{1,3},{2,18},{3,1},{16,0},{17,19},{18,2},{19,17},{4,20},{5,... | collective-permute-start | bytes 7102472 | tf_op jit(solution)/shard_map/ppermute | solution.py:604
  483.3 129.5 %reduce-scatter.4.cloned.1.call-start = ((), (), s32[]{:S(2)}) async-start(), calls=%async_computation.5 | async-start | bytes 3133440 | tf_op jit(solution)/shard_map/reduce_scatter | solution.py:621
  483.3 31.2 %collective-permute-start.53 = (bf16[1088,1088]{1,0:T(8,128)(2,1)}, bf16[1088,1088]{1,0:T(8,128)(2,1)}, u32[]{:S(2)}, u32[]{:S(2)}) collective-permute-start(bf16[1088,1088]{1,0:T(8,128)(2,1)} %convolution_convert_fusion.3), channel_id=1, source_target_pairs={{0,1},{1,0},{2,3},{3,2},{16,17},{17,16},{18,19},{19,18},{4,5},{5,4... | collective-permute-start | bytes 7102472 | tf_op jit(solution)/shard_map/ppermute | solution.py:604
  483.4 36.0 %collective-permute-start.52 = (bf16[1088,1088]{1,0:T(8,128)(2,1)}, bf16[1088,1088]{1,0:T(8,128)(2,1)}, u32[]{:S(2)}, u32[]{:S(2)}) collective-permute-start(bf16[1088,1088]{1,0:T(8,128)(2,1)} %convolution_convert_fusion.4), channel_id=1, source_target_pairs={{0,1},{1,0},{2,3},{3,2},{16,17},{17,16},{18,19},{19,18},{4,5},{5,4... | collective-permute-start | bytes 7102472 | tf_op jit(solution)/shard_map/ppermute | solution.py:604
  514.5 123.8 %reduce-scatter.6.cloned.1.call-start = ((), (), s32[]{:S(2)}) async-start(), calls=%async_computation.6 | async-start | bytes 3133440 | tf_op jit(solution)/shard_map/reduce_scatter | solution.py:621
  517.8 30.5 %collective-permute-start.54 = (bf16[1088,1088]{1,0:T(8,128)(2,1)S(1)}, bf16[1088,1088]{1,0:T(8,128)(2,1)S(1)}, u32[]{:S(2)}, u32[]{:S(2)}) collective-permute-start(bf16[1088,1088]{1,0:T(8,128)(2,1)S(1)} %add_convert_fusion.3), channel_id=1, source_target_pairs={{0,16},{1,3},{2,18},{3,1},{16,0},{17,19},{18,2},{19,17},{4,20},{5,... | collective-permute-start | bytes 7102472 | tf_op jit(solution)/shard_map/ppermute | solution.py:604
  587.5 23.2 %collective-permute-start.36 = (f32[1088]{0:T(1024)S(1)}, f32[1088]{0:T(1024)S(1)}, u32[]{:S(2)}, u32[]{:S(2)}) collective-permute-start(f32[1088]{0:T(1024)S(1)} %add_add_fusion.1), channel_id=1, source_target_pairs={{0,1},{1,0},{2,3},{3,2},{16,17},{17,16},{18,19},{19,18},{4,5},{5,4... | collective-permute-start | bytes 13064 | tf_op jit(solution)/shard_map/ppermute | solution.py:654
  588.9 23.4 %collective-permute-start.49 = (f32[2176]{0:T(1024)S(1)}, f32[2176]{0:T(1024)S(1)}, u32[]{:S(2)}, u32[]{:S(2)}) collective-permute-start(f32[2176]{0:T(1024)S(1)} %add_add_fusion), channel_id=1, source_target_pairs={{0,1},{1,0},{2,3},{3,2},{16,17},{17,16},{18,19},{19,18},{4,5},{5,4... | collective-permute-start | bytes 26120 | tf_op jit(solution)/shard_map/ppermute | solution.py:654
  588.9 33.3 %collective-permute-start.62 = (bf16[272,1088]{1,0:T(8,128)(2,1)}, bf16[272,1088]{1,0:T(8,128)(2,1)S(1)}, u32[]{:S(2)}, u32[]{:S(2)}) collective-permute-start(bf16[272,1088]{1,0:T(8,128)(2,1)} %reduce-scatter.8.cloned.1.call-done), channel_id=1, source_target_pairs={{0,2},{1,17},{2,0},{3,19},{16,18},{17,1},{18,16},{19,3},{4,6},{5,2... | collective-permute-start | bytes 1775624 | tf_op jit(solution)/shard_map/ppermute | solution.py:604
  612.8 25.5 %collective-permute-start.42 = (bf16[272,1088]{1,0:T(8,128)(2,1)}, bf16[272,1088]{1,0:T(8,128)(2,1)}, u32[]{:S(2)}, u32[]{:S(2)}) collective-permute-start(bf16[272,1088]{1,0:T(8,128)(2,1)} %reduce-scatter.4.cloned.1.call-done), channel_id=1, source_target_pairs={{0,2},{1,17},{2,0},{3,19},{16,18},{17,1},{18,16},{19,3},{4,6},{5,2... | collective-permute-start | bytes 1775624 | tf_op jit(solution)/shard_map/ppermute | solution.py:604
  618.0 25.4 %collective-permute-start.24 = (bf16[256,1088]{0,1:T(8,128)(2,1)}, bf16[256,1088]{0,1:T(8,128)(2,1)S(1)}, u32[]{:S(2)}, u32[]{:S(2)}) collective-permute-start(bf16[256,1088]{0,1:T(8,128)(2,1)} %copy.53), channel_id=1, source_target_pairs={{0,1},{1,0},{2,3},{3,2},{4,5},{5,4},{6,7},{7,6},{8,9},{9,8},{10,11... | collective-permute-start | bytes 1671176 | tf_op jit(solution)/shard_map/ppermute | solution.py:610
  620.1 28.6 %collective-permute-start.25 = (bf16[256,1088]{0,1:T(8,128)(2,1)}, bf16[256,1088]{0,1:T(8,128)(2,1)}, u32[]{:S(2)}, u32[]{:S(2)}) collective-permute-start(bf16[256,1088]{0,1:T(8,128)(2,1)} %copy.54), channel_id=1, source_target_pairs={{0,2},{1,3},{2,0},{3,1},{4,6},{5,7},{6,4},{7,5},{8,10},{9,11},{10,... | collective-permute-start | bytes 1671176 | tf_op jit(solution)/shard_map/ppermute | solution.py:610
  620.6 21.3 %collective-permute-start.38 = (f32[1088]{0:T(1024)S(1)}, f32[1088]{0:T(1024)S(1)}, u32[]{:S(2)}, u32[]{:S(2)}) collective-permute-start(f32[1088]{0:T(1024)S(1)} %add.276), channel_id=1, source_target_pairs={{0,16},{1,17},{2,18},{3,19},{16,0},{17,1},{18,2},{19,3},{4,20},{5,... | collective-permute-start | bytes 13064 | tf_op jit(solution)/shard_map/ppermute | solution.py:654
  638.3 26.2 %collective-permute-start.55 = (bf16[272,1088]{1,0:T(8,128)(2,1)}, bf16[272,1088]{1,0:T(8,128)(2,1)}, u32[]{:S(2)}, u32[]{:S(2)}) collective-permute-start(bf16[272,1088]{1,0:T(8,128)(2,1)} %reduce-scatter.6.cloned.1.call-done), channel_id=1, source_target_pairs={{0,2},{1,17},{2,0},{3,19},{16,18},{17,1},{18,16},{19,3},{4,6},{5,2... | collective-permute-start | bytes 1775624 | tf_op jit(solution)/shard_map/ppermute | solution.py:604
  641.9 22.6 %collective-permute-start.26 = (bf16[256,1088]{0,1:T(8,128)(2,1)}, bf16[256,1088]{0,1:T(8,128)(2,1)S(1)}, u32[]{:S(2)}, u32[]{:S(2)}) collective-permute-start(bf16[256,1088]{0,1:T(8,128)(2,1)} %copy.55), channel_id=1, source_target_pairs={{0,3},{1,2},{2,1},{3,0},{4,7},{5,6},{6,5},{7,4},{8,11},{9,10},{10,... | collective-permute-start | bytes 1671176 | tf_op jit(solution)/shard_map/ppermute | solution.py:610
  641.9 27.0 %collective-permute-start.63 = (bf16[272,1088]{1,0:T(8,128)(2,1)S(1)}, bf16[272,1088]{1,0:T(8,128)(2,1)}, u32[]{:S(2)}, u32[]{:S(2)}) collective-permute-start(bf16[272,1088]{1,0:T(8,128)(2,1)S(1)} %add_convert_fusion.6.refs_0_), channel_id=1, source_target_pairs={{0,16},{1,3},{2,18},{3,1},{16,0},{17,19},{18,2},{19,17},{4,20},{5,... | collective-permute-start | bytes 1775624 | tf_op jit(solution)/shard_map/ppermute | solution.py:604
  643.4 56.1 %collective-permute-start.43 = (bf16[272,1088]{1,0:T(8,128)(2,1)}, bf16[272,1088]{1,0:T(8,128)(2,1)}, u32[]{:S(2)}, u32[]{:S(2)}) collective-permute-start(bf16[272,1088]{1,0:T(8,128)(2,1)} %add_convert_fusion.8), channel_id=1, source_target_pairs={{0,16},{1,3},{2,18},{3,1},{16,0},{17,19},{18,2},{19,17},{4,20},{5,... | collective-permute-start | bytes 1775624 | tf_op jit(solution)/shard_map/ppermute | solution.py:604
  648.7 19.9 %collective-permute-start.30 = (bf16[256,1088]{0,1:T(8,128)(2,1)}, bf16[256,1088]{0,1:T(8,128)(2,1)S(1)}, u32[]{:S(2)}, u32[]{:S(2)}) collective-permute-start(bf16[256,1088]{0,1:T(8,128)(2,1)} %copy.64), channel_id=1, source_target_pairs={{0,1},{1,0},{2,3},{3,2},{4,5},{5,4},{6,7},{7,6},{8,9},{9,8},{10,11... | collective-permute-start | bytes 1671176 | tf_op jit(solution)/shard_map/ppermute | solution.py:610
  664.5 33.6 %collective-permute-start.32 = (bf16[256,1088]{0,1:T(8,128)(2,1)}, bf16[256,1088]{0,1:T(8,128)(2,1)S(1)}, u32[]{:S(2)}, u32[]{:S(2)}) collective-permute-start(bf16[256,1088]{0,1:T(8,128)(2,1)} %copy.66), channel_id=1, source_target_pairs={{0,3},{1,2},{2,1},{3,0},{4,7},{5,6},{6,5},{7,4},{8,11},{9,10},{10,... | collective-permute-start | bytes 1671176 | tf_op jit(solution)/shard_map/ppermute | solution.py:610
  668.6 56.8 %collective-permute-start.64 = (bf16[272,1088]{1,0:T(8,128)(2,1)S(1)}, bf16[272,1088]{1,0:T(8,128)(2,1)}, u32[]{:S(2)}, u32[]{:S(2)}) collective-permute-start(bf16[272,1088]{1,0:T(8,128)(2,1)S(1)} %add_convert_fusion.6.refs_0_), channel_id=1, source_target_pairs={{0,1},{1,0},{2,3},{3,2},{16,17},{17,16},{18,19},{19,18},{4,5},{5,4... | collective-permute-start | bytes 1775624 | tf_op jit(solution)/shard_map/ppermute | solution.py:604
  668.9 56.5 %collective-permute-start.65 = (bf16[272,1088]{1,0:T(8,128)(2,1)}, bf16[272,1088]{1,0:T(8,128)(2,1)}, u32[]{:S(2)}, u32[]{:S(2)}) collective-permute-start(bf16[272,1088]{1,0:T(8,128)(2,1)} %collective-permute-done.63.refs_1_), channel_id=1, source_target_pairs={{0,1},{1,0},{2,3},{3,2},{16,17},{17,16},{18,19},{19,18},{4,5},{5,4... | collective-permute-start | bytes 1775624 | tf_op jit(solution)/shard_map/ppermute | solution.py:604
  680.3 49.8 %collective-permute-start.44 = (bf16[272,1088]{1,0:T(8,128)(2,1)}, bf16[272,1088]{1,0:T(8,128)(2,1)}, u32[]{:S(2)}, u32[]{:S(2)}) collective-permute-start(bf16[272,1088]{1,0:T(8,128)(2,1)} %add_convert_fusion.8), channel_id=1, source_target_pairs={{0,1},{1,0},{2,3},{3,2},{16,17},{17,16},{18,19},{19,18},{4,5},{5,4... | collective-permute-start | bytes 1775624 | tf_op jit(solution)/shard_map/ppermute | solution.py:604
  698.1 32.0 %collective-permute-start.56 = (bf16[272,1088]{1,0:T(8,128)(2,1)}, bf16[272,1088]{1,0:T(8,128)(2,1)}, u32[]{:S(2)}, u32[]{:S(2)}) collective-permute-start(bf16[272,1088]{1,0:T(8,128)(2,1)} %add_convert_fusion.7), channel_id=1, source_target_pairs={{0,16},{1,3},{2,18},{3,1},{16,0},{17,19},{18,2},{19,17},{4,20},{5,... | collective-permute-start | bytes 1775624 | tf_op jit(solution)/shard_map/ppermute | solution.py:604
  699.6 30.5 %collective-permute-start.45 = (bf16[272,1088]{1,0:T(8,128)(2,1)}, bf16[272,1088]{1,0:T(8,128)(2,1)}, u32[]{:S(2)}, u32[]{:S(2)}) collective-permute-start(bf16[272,1088]{1,0:T(8,128)(2,1)} %collective-permute-done.43), channel_id=1, source_target_pairs={{0,1},{1,0},{2,3},{3,2},{16,17},{17,16},{18,19},{19,18},{4,5},{5,4... | collective-permute-start | bytes 1775624 | tf_op jit(solution)/shard_map/ppermute | solution.py:604
  (82 other events, 1642.3 us)
Sparse Core Ops, SparseCore 0:
  68.1 51.5 all-gather.2
  124.5 50.6 all-gather.4
  483.4 48.5 reduce-scatter.7
  534.9 50.9 reduce-scatter.3
  588.1 50.1 reduce-scatter.5

commit v3 on v2

--- a/solution.py
+++ b/solution.py
@@ -350,8 +350,10 @@
 PAIR = 2 * HEAD_DIM
 
 
-def attend_kernel(place_ref, q_ref, k_ref, v_ref, o_ref, log_ref, keys, values, *, count, width):
-    pair = pl.program_id(0)
+def attend_kernel(place_ref, q_ref, k_ref, v_ref, *refs, count, width, start):
+    o_ref, log_ref, keys, values = refs[-4:]
+    own_pair = pl.program_id(0)
+    pair = own_pair + start
     shift = place_ref[0]
     block_len = q_ref.shape[0] // count
     lane = lax.broadcasted_iota(jnp.int32, (1, PAIR), 1)
@@ -393,7 +395,7 @@
                 preferred_element_type=jnp.float32,
             )
             parts.append(added / total)
-            logs = jnp.where(lane == 2 * pair + half, top + jnp.log(total), logs)
+            logs = jnp.where(lane == 2 * own_pair + half, top + jnp.log(total), logs)
         o_ref[rows(block), :] = jnp.where(first, parts[0], parts[1]).astype(jnp.bfloat16)
         log_ref[rows(block), :] = logs
 
@@ -406,22 +408,14 @@
     g_ref,
     o_ref,
     log_ref,
-    dq_ref,
-    dk_ref,
-    dv_ref,
-    queries,
-    grads,
-    keys,
-    values,
-    keys_turned,
-    logs,
-    deltas,
-    turned,
-    *,
+    *refs,
     count,
     width,
+    start,
 ):
-    pair = pl.program_id(0)
+    dq_ref, dk_ref, dv_ref, queries, grads, keys, values = refs[-11:-4]
+    keys_turned, logs, deltas, turned = refs[-4:]
+    pair = pl.program_id(0) + start
     shift = place_ref[0]
     length = q_ref.shape[0]
     block_len = length // count
@@ -507,16 +501,15 @@
         dq_ref[rows(block), :] = (turned[:, here].T * HEAD_DIM**-0.5).astype(jnp.bfloat16)
 
 
-def attend(place, queries, key_rows, value_rows, count):
+def attend(place, queries, key_rows, value_rows, count, start, pairs, before):
     length, width = queries.shape
-    pairs = pl.cdiv(width, PAIR)
-    heads_block = pl.BlockSpec((length, PAIR), lambda pair, place_ref: (0, pair))
+    heads_block = pl.BlockSpec((length, PAIR), lambda pair, place_ref: (0, pair + start))
     return pl.pallas_call(
-        functools.partial(attend_kernel, count=count, width=width),
+        functools.partial(attend_kernel, count=count, width=width, start=start),
         grid_spec=pltpu.PrefetchScalarGridSpec(
             num_scalar_prefetch=1,
             grid=(pairs,),
-            in_specs=[heads_block] * 3,
+            in_specs=[heads_block] * 3 + [pl.BlockSpec(memory_space=pl.ANY)] * len(before),
             out_specs=[
                 heads_block,
                 pl.BlockSpec((length, 128), lambda pair, place_ref: (0, 0)),
@@ -527,29 +520,32 @@
             jax.ShapeDtypeStruct((length, width), jnp.bfloat16),
             jax.ShapeDtypeStruct((length, 128), jnp.float32),
         ],
+        input_output_aliases={4 + at: at for at in range(len(before))},
         compiler_params=pltpu.CompilerParams(vmem_limit_bytes=48 * 2**20),
         cost_estimate=pl.CostEstimate(
-            flops=4 * length * length * width,
-            bytes_accessed=8 * length * width,
-            transcendentals=HEADS * length * length // 2,
+            flops=4 * length * length * PAIR * pairs * 4,
+            bytes_accessed=8 * length * PAIR * pairs,
+            transcendentals=length * length * pairs,
         ),
         name="attend",
-    )(place, queries, key_rows, value_rows)
-
-
-def attend_back(place, queries, key_rows, value_rows, grads, attended, logs, count):
+    )(place, queries, key_rows, value_rows, *before)
+
+
+def attend_back(
+    place, queries, key_rows, value_rows, grads, attended, logs, count, start, pairs, before
+):
     length, width = queries.shape
-    pairs = pl.cdiv(width, PAIR)
-    heads_block = pl.BlockSpec((length, PAIR), lambda pair, place_ref: (0, pair))
+    heads_block = pl.BlockSpec((length, PAIR), lambda pair, place_ref: (0, pair + start))
     low_rows = pltpu.VMEM((length, PAIR), jnp.bfloat16)
     low_pair = pltpu.VMEM((2, length, PAIR), jnp.bfloat16)
     return pl.pallas_call(
-        functools.partial(attend_back_kernel, count=count, width=width),
+        functools.partial(attend_back_kernel, count=count, width=width, start=start),
         grid_spec=pltpu.PrefetchScalarGridSpec(
             num_scalar_prefetch=1,
             grid=(pairs,),
             in_specs=[heads_block] * 5
-            + [pl.BlockSpec((1, 2, length), lambda pair, place_ref: (pair, 0, 0))],
+            + [pl.BlockSpec((1, 2, length), lambda pair, place_ref: (pair, 0, 0))]
+            + [pl.BlockSpec(memory_space=pl.ANY)] * len(before),
             out_specs=[heads_block] * 3,
             scratch_shapes=[
                 low_pair,
@@ -563,14 +559,15 @@
             ],
         ),
         out_shape=[jax.ShapeDtypeStruct((length, width), jnp.bfloat16)] * 3,
+        input_output_aliases={7 + at: at for at in range(len(before))},
         compiler_params=pltpu.CompilerParams(vmem_limit_bytes=48 * 2**20),
         cost_estimate=pl.CostEstimate(
-            flops=10 * length * length * width,
-            bytes_accessed=16 * length * width,
-            transcendentals=HEADS * length * length // 2,
+            flops=10 * length * length * PAIR * pairs * 3,
+            bytes_accessed=16 * length * PAIR * pairs,
+            transcendentals=length * length * pairs,
         ),
         name="attend_back",
-    )(place, queries, key_rows, value_rows, grads, attended, logs)
+    )(place, queries, key_rows, value_rows, grads, attended, logs, *before)
 
 
 def settle_kernel(place_ref, *refs):
@@ -595,6 +592,8 @@
     core = device & 1
     if kind == "core":
         return device ^ 1
+    if kind == "far":
+        return device ^ (3 if core else 5)
     if kind == "near":
         return device ^ (2 if core else 4)
     return device ^ (4 if core else 2)
@@ -610,20 +609,21 @@
     return lax.ppermute(values, "ctx", [(device, device ^ bits) for device in range(4)])
 
 
-def reduce_pieces(pieces):
-    far_two = plane_swap(pieces[3], "core")
-    far = plane_swap(pieces[2], "core")
-    second = (pieces[1].astype(jnp.float32) + far_two.astype(jnp.float32)).astype(jnp.bfloat16)
-    near = plane_swap(second, "near")
-    first = (
-        pieces[0].astype(jnp.float32) + far.astype(jnp.float32) + near.astype(jnp.float32)
-    ).astype(jnp.bfloat16)
-    shard = lax.psum_scatter(first, "fsdp", scatter_dimension=0, tiled=True)
-    whole = (shard.astype(jnp.float32) + plane_swap(shard, "other").astype(jnp.float32)).astype(
-        jnp.bfloat16
-    )
-    beside = plane_swap(whole, "near")
-    return [whole, beside, plane_swap(whole, "core"), plane_swap(beside, "core")]
+def low_sum(*terms):
+    return sum(term.astype(jnp.float32) for term in terms).astype(jnp.bfloat16)
+
+
+def reduce_core(pieces):
+    return plane_swap(pieces[2], "core"), plane_swap(pieces[3], "core")
+
+
+def reduce_last(shard):
+    whole = low_sum(shard, plane_swap(shard, "other"))
+    return [whole] + [plane_swap(whole, kind) for kind in ("near", "core", "far")]
+
+
+def scatter_rows(values):
+    return lax.psum_scatter(values, "fsdp", scatter_dimension=0, tiled=True)
 
 
 def chosen(index, options):
@@ -664,12 +664,12 @@
 
 def gelu_pair(values):
     inner = 0.7978845608028654
+    cubic = inner * 0.044715
     squared = values * values
-    curve = jnp.tanh(inner * (values + 0.044715 * values * squared))
-    active = 0.5 * values * (1.0 + curve)
-    slope = 0.5 * (1.0 + curve) + 0.5 * values * (1.0 - curve * curve) * inner * (
-        1.0 + 3.0 * 0.044715 * squared
-    )
+    curve = jnp.tanh(values * (inner + cubic * squared))
+    half = 0.5 * values
+    active = half + half * curve
+    slope = 0.5 + 0.5 * curve + half * (1.0 - curve * curve) * (inner + 3.0 * cubic * squared)
     return active, slope
 
 
@@ -766,15 +766,6 @@
         copy.wait()
 
 
-def add_sums(step, sums_ref, terms):
-    @pl.when(step == 0)
-    def _():
-        sums_ref[...] = jnp.zeros_like(sums_ref)
-
-    for at, term in enumerate(terms):
-        sums_ref[at] += fold(term)
-
-
 def middle_kernel(x_ref, o_ref, vectors_ref, all_ref, middle_ref, h_ref, weights, arrived):
     step = pl.program_id(0)
     width = x_ref.shape[1]
@@ -794,16 +785,16 @@
 
 
 def up_kernel(h_ref, biases_ref, *refs):
-    sources = refs[:4]
-    active_refs, slope_refs = refs[4:8], refs[8:12]
-    weights, arrived = refs[12:]
+    sources = refs[:2]
+    active_refs, slope_refs = refs[2:4], refs[4:6]
+    weights, arrived = refs[6:]
     step = pl.program_id(0)
     copies = [
         pltpu.make_async_copy(source, weights.at[at], arrived.at[at])
         for at, source in enumerate(sources)
     ]
     fetch(step, copies)
-    for at in range(4):
+    for at in range(2):
         arrive(step, copies[at])
         hidden = (
             jnp.dot(h_ref[...], weights[at], preferred_element_type=jnp.float32)
@@ -843,63 +834,70 @@
     return scale * inner, grad * unit
 
 
+def hidden_kernel(g_ref, *refs):
+    slopes, sources = refs[:2], refs[2:4]
+    hidden_refs, sums_ref = refs[4:6], refs[6]
+    weights, arrived = refs[7:]
+    step = pl.program_id(0)
+    copies = [
+        pltpu.make_async_copy(source, weights.at[at], arrived.at[at])
+        for at, source in enumerate(sources)
+    ]
+    fetch(step, copies)
+
+    @pl.when(step == 0)
+    def _():
+        sums_ref[...] = jnp.zeros_like(sums_ref)
+
+    upstream = g_ref[...]
+    for at in range(2):
+        arrive(step, copies[at])
+        hidden = lax.dot_general(
+            upstream, weights[at], NT, preferred_element_type=jnp.float32
+        )
+        hidden = (hidden * slopes[at][...].astype(jnp.float32)).astype(jnp.bfloat16)
+        hidden_refs[at][...] = hidden
+        sums_ref[at] += fold(hidden.astype(jnp.float32))
+    sums_ref[2] += fold(upstream.astype(jnp.float32))
+
+
 def back_kernel(g_ref, middle_ref, vectors_ref, *refs):
-    slopes, downs, ups, all_ref = refs[:4], refs[4:8], refs[8:12], refs[12]
-    hidden_refs = refs[13:17]
-    grad_ref, low_ref, out_ref, sums_ref = refs[17:21]
-    down_weights, up_weights, out_weights, arrived = refs[21:]
+    hiddens, sources, all_ref = refs[:4], refs[4:8], refs[8]
+    grad_ref, low_ref, out_ref, sums_ref = refs[9:13]
+    weights, out_weights, arrived = refs[13:]
     step = pl.program_id(0)
     width = middle_ref.shape[1]
-    copies = []
-    for at in range(4):
-        copies.append(
-            pltpu.make_async_copy(downs[at], down_weights.at[at], arrived.at[2 * at])
-        )
-        copies.append(
-            pltpu.make_async_copy(ups[at], up_weights.at[at], arrived.at[2 * at + 1])
-        )
-    copies.append(
-        pltpu.make_async_copy(all_ref.at[pl.ds(12, 4)], out_weights, arrived.at[8])
-    )
+    copies = [
+        pltpu.make_async_copy(source, weights.at[at], arrived.at[at])
+        for at, source in enumerate(sources)
+    ] + [pltpu.make_async_copy(all_ref.at[pl.ds(12, 4)], out_weights, arrived.at[4])]
     fetch(step, copies)
-    upstream = g_ref[...]
-    sums = []
+
+    @pl.when(step == 0)
+    def _():
+        sums_ref[...] = jnp.zeros_like(sums_ref)
+
     total = jnp.zeros(middle_ref.shape, jnp.float32)
     for at in range(4):
-        arrive(step, copies[2 * at])
-        hidden = lax.dot_general(
-            upstream, down_weights[at], NT, preferred_element_type=jnp.float32
-        )
-        hidden = (hidden * slopes[at][...].astype(jnp.float32)).astype(jnp.bfloat16)
-        hidden_refs[at][...] = hidden
-        sums.append(fold(hidden.astype(jnp.float32)))
-        arrive(step, copies[2 * at + 1])
+        arrive(step, copies[at])
         total = total + lax.dot_general(
-            hidden, up_weights[at], NT, preferred_element_type=jnp.float32
+            hiddens[at][...], weights[at], NT, preferred_element_type=jnp.float32
         )
     part, gain_term = norm_back(middle_ref[...], vectors_ref[0:1, :], total)
-    upstream = upstream.astype(jnp.float32)
-    grad = upstream + part
+    sums_ref[0] += fold(gain_term)
+    sums_ref[1] += fold(total)
+    grad = g_ref[...].astype(jnp.float32) + part
     grad_ref[...] = grad
     grad_low = grad.astype(jnp.bfloat16)
     low_ref[...] = grad_low
-    sums += [
-        fold(gain_term), fold(total), fold(upstream), fold(grad_low.astype(jnp.float32))
-    ]
-    arrive(step, copies[8])
+    sums_ref[2] += fold(grad_low.astype(jnp.float32))
+    arrive(step, copies[4])
     out_ref[...] = lax.dot_general(
         grad_low,
         out_weights[...].reshape(width, width),
         NT,
         preferred_element_type=jnp.float32,
     ).astype(jnp.bfloat16)
-
-    @pl.when(step == 0)
-    def _():
-        sums_ref[...] = jnp.zeros_like(sums_ref)
-
-    for at, term in enumerate(sums):
-        sums_ref[at] += term
 
 
 def last_kernel(q_ref, k_ref, v_ref, x_ref, grad_ref, vectors_ref, all_ref, *refs):
@@ -940,7 +938,7 @@
 
 
 def by_rows(kernel, name, rows, width, tiled, whole, remote, outs, sums, scratch, sems, blocks):
-    step = 256
+    step = 512
     tile = pl.BlockSpec((step, width), lambda at: (at, 0))
     out_specs = [tile] * len(outs)
     out_shape = [jax.ShapeDtypeStruct((rows, width), dtype) for dtype in outs]
@@ -1036,28 +1034,6 @@
         ],
         axis=1,
     )
-    up_piece, *shards = pin((up_piece, *shards))
-    near_shards = [plane_swap(shard, "near") for shard in shards]
-    around = (
-        sections
-        + shards
-        + near_shards
-        + [plane_swap(shard, "core") for shard in shards]
-        + [plane_swap(shard, "core") for shard in near_shards]
-    )
-    around_places = jnp.stack(
-        [kind * 4 + z for kind in range(4)]
-        + [kind * 4 + (z - step) % 4 for kind in classes for step in range(1, 4)]
-    )
-    up_own = lax.all_gather(up_piece, "fsdp", axis=0, tiled=True)
-    down_piece = lax.dynamic_slice_in_dim(down_weight, mine * quarter, quarter, 0)
-    down_piece, up_own = pin((down_piece, up_own))
-    down_own = lax.all_gather(down_piece, "fsdp", axis=0, tiled=True)
-
-    def exchange(own):
-        near = plane_swap(own, "near")
-        return [own, near, plane_swap(own, "core"), plane_swap(near, "core")]
-
     vectors = gather_vector(
         jnp.concatenate(
             [
@@ -1073,7 +1049,26 @@
             ]
         ),
         z,
-    ).astype(wide)
+    )
+    rows_in, upstream_low = spread(inputs), spread(cotangent)
+    up_piece, vectors, rows_in, upstream_low, *shards = pin(
+        (up_piece, vectors, rows_in, upstream_low, *shards)
+    )
+    vectors = vectors.astype(wide)
+    near_shards = [plane_swap(shard, "near") for shard in shards]
+    around = (
+        sections
+        + shards
+        + near_shards
+        + [plane_swap(shard, "core") for shard in shards]
+        + [plane_swap(shard, "core") for shard in near_shards]
+    )
+    around_places = jnp.stack(
+        [kind * 4 + z for kind in range(4)]
+        + [kind * 4 + (z - step) % 4 for kind in classes for step in range(1, 4)]
+    )
+    up_own = lax.all_gather(up_piece, "fsdp", axis=0, tiled=True)
+    down_piece = lax.dynamic_slice_in_dim(down_weight, mine * quarter, quarter, 0)
     gain_first, shift_first, qbias, vbias, obias, gain_second, shift_second, dbias = (
         vectors[:, at * quarter : (at + 1) * quarter].reshape(1, width) for at in range(8)
     )
@@ -1086,21 +1081,22 @@
         axis=0,
     )
 
-    rows_in = spread(inputs)
     normed_low, queries, key_rows, value_rows, weights = front(
         around_places,
         rows_in,
         jnp.concatenate([gain_first, shift_first, qbias, vbias], axis=0),
         around,
     )
-    up_own, late_queries = pin((up_own, queries))
-    up_slots = exchange(up_own)
-    cotangent, late_queries = pin((cotangent, late_queries))
-    upstream_low = spread(cotangent)
-    attended, logs = attend(place, queries, key_rows, value_rows, seq_count)
-    down_own, late_attended = pin((down_own, attended))
-    down_slots = exchange(down_own)
-    turned_logs = logs.T.reshape(64, 2, rows)
+    down_piece, queries = pin((down_piece, queries))
+    down_own = lax.all_gather(down_piece, "fsdp", axis=0, tiled=True)
+    attended, logs_one = attend(place, queries, key_rows, value_rows, seq_count, 0, 5, [])
+    up_own, late_queries, attended = pin((up_own, queries, attended))
+    up_near, up_core = plane_swap(up_own, "near"), plane_swap(up_own, "core")
+    attended, logs_two = attend(
+        place, late_queries, key_rows, value_rows, seq_count, 5, 4, [attended]
+    )
+    up_core, attended = pin((up_core, attended))
+    logs_one, logs_two = (logs.T.reshape(64, 2, rows) for logs in (logs_one, logs_two))
     middle, normed_two_low = by_rows(
         middle_kernel,
         "middle",
@@ -1115,21 +1111,146 @@
         1,
         1,
     )
-    up_outs = by_rows(
-        up_kernel,
-        "up",
+    up_near, normed_two_low = pin((up_near, normed_two_low))
+    up_slots = [up_own, up_near, up_core, plane_swap(up_near, "core")]
+    active, slopes = [None] * 4, [None] * 4
+
+    def up(first):
+        outs = by_rows(
+            up_kernel,
+            "up",
+            rows,
+            width,
+            ([normed_two_low], []),
+            [jnp.concatenate([ubias[first : first + 1], ubias[first + 2 : first + 3]], axis=0)],
+            [up_slots[first], up_slots[first + 2]],
+            [low] * 4,
+            0,
+            [(2,) + area],
+            2,
+            2,
+        )
+        active[first], active[first + 2], slopes[first], slopes[first + 2] = outs
+
+    up(0)
+    up_slots[3], active[0], active[2] = pin((up_slots[3], active[0], active[2]))
+    up(1)
+    down_own, *active = pin((down_own, *active))
+    down_near, down_core = plane_swap(down_own, "near"), plane_swap(down_own, "core")
+
+    def turned_product(left, right):
+        return product(left, right, (0, 0)).astype(low)
+
+    down_terms = [turned_product(active[slot], upstream_low) for slot in (3, 2)]
+    upstream_low, *down_terms = pin((upstream_low, *down_terms))
+    down_terms += [turned_product(active[slot], upstream_low) for slot in (1, 0)]
+    down_terms = down_terms[::-1]
+    down_far, down_far_two = reduce_core(down_terms)
+    upstream_low, *down_terms = pin((upstream_low, *down_terms))
+    hidden_low = [None] * 4
+
+    def hidden(first, upstream):
+        hidden_low[first], hidden_low[first + 2], sums = by_rows(
+            hidden_kernel,
+            "hidden",
+            rows,
+            width,
+            ([upstream], [slopes[first], slopes[first + 2]]),
+            [],
+            [down_slots[first], down_slots[first + 2]],
+            [low] * 2,
+            3,
+            [(2,) + area],
+            2,
+            2,
+        )
+        return sums
+
+    down_near, upstream_low = pin((down_near, upstream_low))
+    down_slots = [down_own, down_near, down_core, plane_swap(down_near, "core")]
+    sums_even = hidden(0, upstream_low)
+    upstream_late, sums_even = pin((upstream_low, sums_even))
+    sums_odd = hidden(1, upstream_late)
+    hidden_sums = jnp.stack(
+        [sums_even[0], sums_odd[0], sums_even[1], sums_odd[1], sums_even[2]]
+    )
+    down_second = low_sum(down_terms[1], down_far_two)
+    down_second, down_far, *hidden_low = pin((down_second, down_far, *hidden_low))
+    down_close = plane_swap(down_second, "near")
+    middle_grad, middle_low, grad_low, back_sums = by_rows(
+        back_kernel,
+        "back",
         rows,
         width,
-        ([normed_two_low], []),
-        [ubias],
-        up_slots,
-        [low] * 8,
-        0,
-        [(4,) + area],
+        ([upstream_low, middle], hidden_low),
+        [gain_second],
+        up_slots + [weights],
+        [wide, low, low],
+        3,
+        [(4,) + area, (4,) + section.shape],
+        5,
+        5,
+    )
+    down_first = low_sum(down_terms[0], down_far, down_close)
+    down_first, normed_two_low = pin((down_first, pin((normed_two_low, middle_low))[0]))
+    down_shard = scatter_rows(down_first)
+    up_terms = [turned_product(normed_two_low, hidden_low[slot]) for slot in (3, 2)]
+    normed_two_low, *up_terms = pin((normed_two_low, *up_terms))
+    up_terms += [turned_product(normed_two_low, hidden_low[slot]) for slot in (1, 0)]
+    up_terms = up_terms[::-1]
+    up_far, up_far_two = reduce_core(up_terms)
+    out_term = turned_product(attended, middle_low)
+    up_second = low_sum(up_terms[1], up_far_two)
+    grad_low, up_second, up_far, out_term, *up_terms = pin(
+        (grad_low, up_second, up_far, out_term, *up_terms)
+    )
+    up_close = plane_swap(up_second, "near")
+    in_grads = attend_back(
+        place, late_queries, key_rows, value_rows, grad_low, attended, logs_one, seq_count, 0, 5, []
+    )
+    up_first = low_sum(up_terms[0], up_far, up_close)
+    up_first, *in_grads = pin((up_first, *in_grads))
+    in_grads = attend_back(
+        place,
+        late_queries,
+        key_rows,
+        value_rows,
+        grad_low,
+        attended,
+        logs_two,
+        seq_count,
+        5,
         4,
+        in_grads,
+    )
+    up_first, down_shard, *in_grads = pin((up_first, down_shard, *in_grads))
+    up_shard = scatter_rows(up_first)
+    down_parts = reduce_last(down_shard)
+    in_terms = [turned_product(normed_low, grad) for grad in in_grads]
+    section_grads = in_terms + [out_term]
+    sections_mine = [chosen(kind, section_grads) for kind in classes]
+    far, far_two = reduce_core(sections_mine)
+    second = low_sum(sections_mine[1], far_two)
+    second, far, *in_grads = pin((second, far, *in_grads))
+    close = plane_swap(second, "near")
+    query_low, key_low, value_low = in_grads
+    input_low, last_sums = by_rows(
+        last_kernel,
+        "last",
+        rows,
+        width,
+        ([query_low, key_low, value_low, rows_in, middle_grad], []),
+        [gain_first],
+        [weights],
+        [low],
         4,
-    )
-    active, slopes = up_outs[:4], up_outs[4:]
+        [(12,) + section.shape],
+        3,
+        3,
+    )
+    first = low_sum(sections_mine[0], far, close)
+    first, middle, input_low = pin((first, middle, input_low))
+    input_gradient = collect(input_low, wide)
     (result,) = by_rows(
         down_kernel,
         "down",
@@ -1145,66 +1266,10 @@
         4,
     )
     outputs = collect(result, low)
-
-    down_terms = [product(active[slot], upstream_low, (0, 0)).astype(low) for slot in range(4)]
-    upstream_low, *down_terms = pin((upstream_low, *down_terms))
-    down_parts = reduce_pieces(down_terms)
-    back_outs = by_rows(
-        back_kernel,
-        "back",
-        rows,
-        width,
-        ([upstream_low, middle], slopes),
-        [gain_second],
-        down_slots + up_slots + [weights],
-        [low] * 4 + [wide, low, low],
-        8,
-        [(4,) + area, (4,) + area, (4,) + section.shape],
-        9,
-        9,
-    )
-    hidden_low = back_outs[:4]
-    middle_grad, middle_low, grad_low, back_sums = back_outs[4:]
-    up_terms = [
-        product(normed_two_low, hidden_low[slot], (0, 0)).astype(low) for slot in range(4)
-    ]
-    out_term = product(attended, middle_low, (0, 0)).astype(low)
-    grad_low, out_term, *up_terms = pin((grad_low, out_term, *up_terms))
-    up_parts = reduce_pieces(up_terms)
-    query_low, key_low, value_low = attend_back(
-        place,
-        late_queries,
-        key_rows,
-        value_rows,
-        grad_low,
-        late_attended,
-        turned_logs,
-        seq_count,
-    )
-    in_terms = [
-        product(normed_low, grad, (0, 0)).astype(low) for grad in (query_low, key_low, value_low)
-    ]
-    query_low, key_low, value_low, *in_terms = pin(
-        (query_low, key_low, value_low, *in_terms)
-    )
-    section_grads = in_terms + [out_term]
-    section_parts = reduce_pieces([chosen(kind, section_grads) for kind in classes])
-    input_low, last_sums = by_rows(
-        last_kernel,
-        "last",
-        rows,
-        width,
-        ([query_low, key_low, value_low, rows_in, middle_grad], []),
-        [gain_first],
-        [weights],
-        [low],
-        4,
-        [(12,) + section.shape],
-        3,
-        3,
-    )
-    input_gradient = collect(input_low, wide)
-
+    up_parts = reduce_last(up_shard)
+    section_parts = reduce_last(scatter_rows(first))
+
+    back_sums = jnp.concatenate([hidden_sums, back_sums], axis=0)
     back_sums = jnp.sum(back_sums, axis=1)
     last_sums = jnp.sum(last_sums, axis=1)
     hidden_sums = [back_sums[slot].reshape(4, quarter) for slot in range(4)]
@@ -1220,7 +1285,7 @@
     late = reduce_vector(
         jnp.concatenate([last_sums[at].reshape(4, quarter) for at in range(4)], axis=1), z
     )
-    gain_two_sum, shift_two_sum, dbias_sum, obias_sum = (
+    dbias_sum, gain_two_sum, shift_two_sum, obias_sum = (
         early[at * quarter : (at + 1) * quarter] for at in range(4)
     )
     ubias_sum = early[4 * quarter :]

time: 768 us -> 663 us (0.86)
  waiting for transfers between devices: 221 us -> 113 us
  starting transfers between devices: 104 us -> 52 us
  local copies, waits for them, and re-layouts: 72.8 us -> 102 us
  Pallas kernels: 240 us -> 261 us
    ppermute x36, waiting for transfers between devices: 105 us -> 44.9 us  [plane_swap(): lax.ppermute(values, ('dp', 'ctx'), [(device, plane_partner(device, kind)...]
    ppermute x36, starting transfers between devices: 75.3 us -> 22.7 us  [plane_swap(): lax.ppermute(values, ('dp', 'ctx'), [(device, plane_partner(device, kind)...]
    ppermute x3, waiting for transfers between devices: 49.7 us -> 25.4 us  [per_device_exchanged(): lax.ppermute(section, 'fsdp', [(device, (device + step) % 4) for device i...]
    pallas_call x5 -> x8, Pallas kernels: 133 us -> 152 us  [by_rows(): pl.pallas_call(kernel, grid=(rows // step,), in_specs=[tile] * len(tiled[...]
    ppermute x12, waiting for transfers between devices: 51.2 us -> 35.7 us  [ctx_swap(): lax.ppermute(values, 'ctx', [(device, device ^ bits) for device in range(...]
    reduce_scatter x3, waiting for transfers between devices: 13.4 us -> 0.01 us  [scatter_rows(): return lax.psum_scatter(values, 'fsdp', scatter_dimension=0, tiled=True)]
    ppermute x12, local copies, waits for them, and re-layouts: 14.3 us -> 23.1 us  [ctx_swap(): lax.ppermute(values, 'ctx', [(device, device ^ bits) for device in range(...]
    unnamed x120 -> x93, local copies, waits for them, and re-layouts: 18.6 us -> 21.9 us
  transfers between devices with their start and end apart: 71 -> 71, of which waited for: 16 -> 25; matrix products, arithmetic and copies ran while one was open for 20% -> 23% of each run, Pallas kernels for 32% -> 40%
where the time goes in v3:
time: 663 us; the launch traced here: 653 us
  Pallas kernels  261 us (39%)
  waiting for transfers between devices  113 us (17%)
  local copies, waits for them, and re-layouts  102 us (15%)
  matrix products  57.7 us (9%)
  other arithmetic  53 us (8%)
  starting transfers between devices  52 us (8%)
  between operations  14.9 us (2%)
    pallas_call x8, Pallas kernels, by_rows(): pl.pallas_call(kernel, grid=(rows // step,), in_specs=[tile] * len(tiled[...  152 us
    dot_general x12, matrix products, product(): lax.dot_general(left, right, ((dims[:1], dims[1:]), ((), ())), preferred_...  57.7 us
    pallas_call x2, Pallas kernels, attend_back(): pl.pallas_call(functools.partial(attend_back_kernel, count=count, width=w...  47.7 us
    ppermute x36, waiting for transfers between devices, plane_swap(): lax.ppermute(values, ('dp', 'ctx'), [(device, plane_partner(device, kind)...  44.9 us
    ppermute x12, waiting for transfers between devices, ctx_swap(): lax.ppermute(values, 'ctx', [(device, device ^ bits) for device in range(...  35.7 us
    pallas_call x2, Pallas kernels, attend(): pl.pallas_call(functools.partial(attend_kernel, count=count, width=width,...  33 us
    convert_element_type x8, other arithmetic, low_sum(): sum((term.astype(jnp.float32) for term in terms)).astype(jnp.bfloat16)  29.9 us
    ppermute x3, waiting for transfers between devices, per_device_exchanged(): lax.ppermute(section, 'fsdp', [(device, (device + step) % 4) for device i...  25.4 us
  transfers between devices with their start and end apart: 71, of which 25 were waited for; matrix products, arithmetic and copies ran while one was open for 23% of the time, Pallas kernels for 40%

profile of v3, /device:TPU:8, one launch (start us, length us, event | category | flops | bytes accessed | tf_op | source)
XLA Modules:
  0.0 653.4 jit_solution(6537574201729302352)
XLA Ops:
  7.2 6.5 concatenate.43
  40.3 8.1 %collective-permute-done.4 = bf16[256,1088]{0,1:T(8,128)(2,1)} collective-permute-done((bf16[256,1088]{0,1:T(8,128)(2,1)}, bf16[256,1088]{0,1:T(8,128)(2,1)}, u32[]{:S(2)}, u32[]{:S(2)}) %collective-permute-start.4) | collective-permute-done | bytes 557088 | tf_op jit(solution)/shard_map/ppermute | solution.py:609
  50.7 3.5 collective-permute-start.10
  56.4 3.8 collective-permute-done.8
  63.7 8.5 %collective-permute-done.7 = bf16[256,1088]{0,1:T(8,128)(2,1)} collective-permute-done((bf16[256,1088]{0,1:T(8,128)(2,1)}, bf16[256,1088]{0,1:T(8,128)(2,1)}, u32[]{:S(2)}, u32[]{:S(2)}) %collective-permute-start.7) | collective-permute-done | bytes 557088 | tf_op jit(solution)/shard_map/ppermute | solution.py:609
  81.4 21.4 %collective-permute-done.10.refs_5_ = bf16[272,1088]{1,0:T(8,128)(2,1)} collective-permute-done((bf16[272,1088]{1,0:T(8,128)(2,1)}, bf16[272,1088]{1,0:T(8,128)(2,1)}, u32[]{:S(2)}, u32[]{:S(2)}) %collective-permute-start.10) | collective-permute-done | bytes 591904 | tf_op jit(solution)/shard_map/ppermute | solution.py:1027
  102.8 3.9 collective-permute-done.11.refs_6_
  111.9 5.8 collective-permute-done.12.refs_7_
  117.8 6.7 %collective-permute-done.13.refs_8_ = bf16[272,1088]{1,0:T(8,128)(2,1)} collective-permute-done((bf16[272,1088]{1,0:T(8,128)(2,1)}, bf16[272,1088]{1,0:T(8,128)(2,1)}, u32[]{:S(2)}, u32[]{:S(2)}) %collective-permute-start.13) | collective-permute-done | bytes 591904 | tf_op jit(solution)/shard_map/ppermute | solution.py:603
  124.5 6.7 %collective-permute-done.14.refs_9_ = bf16[272,1088]{1,0:T(8,128)(2,1)} collective-permute-done((bf16[272,1088]{1,0:T(8,128)(2,1)}, bf16[272,1088]{1,0:T(8,128)(2,1)}, u32[]{:S(2)}, u32[]{:S(2)}) %collective-permute-start.14) | collective-permute-done | bytes 591904 | tf_op jit(solution)/shard_map/ppermute | solution.py:603
  134.5 21.2 %front.1 = (bf16[1024,1088]{1,0:T(8,128)(2,1)}, bf16[1024,1088]{1,0:T(8,128)(2,1)}, bf16[1024,1088]{1,0:T(8,128)(2,1)}, bf16[1024,1088]{1,0:T(8,128)(2,1)}, bf16[16,272,1088]{2,1,0:T(8,128)(2,1)}) custom-call(s32[16]{0:T(128)} %stack.125.places_ref, bf16[1024,1088]{1,0:T(8,128)(2,1)} %pad_maximum_fusion.x_ref, f32[4,1088]{1,0:T(4,128)} %pad_maximum_fusion.4.vectors_ref, ...), custom_call_target="tpu_custom_call" | custom-call | flops 7272923136 | bytes 20471808 | tf_op jit(solution)/shard_map/front/pallas_call | solution.py:740
  157.4 18.2 %attend.2 = (bf16[1024,1088]{1,0:T(8,128)(2,1)S(1)}, f32[1024,128]{1,0:T(8,128)S(1)}) custom-call(s32[1]{0:T(128)} %bitcast.place_ref, bf16[1024,1088]{1,0:T(8,128)(2,1)S(1)} %copy-done.11, bf16[1024,1088]{1,0:T(8,128)(2,1)} %get-tuple-element.130.k_ref, bf16[1024,1088]{1,0:T(8,128)(2,1)} %get-tuple-element.131.v_ref), custom_call_target="tpu_custom_call" | custom-call | flops 10737418240 | bytes 5242880 | tf_op jit(solution)/shard_map/attend/pallas_call | solution.py:507
  180.5 14.8 %attend.3 = (bf16[1024,1088]{1,0:T(8,128)(2,1)S(1)}, f32[1024,128]{1,0:T(8,128)S(1)}) custom-call(s32[1]{0:T(128)} %bitcast.place_ref, bf16[1024,1088]{1,0:T(8,128)(2,1)S(1)} %copy-done.12, bf16[1024,1088]{1,0:T(8,128)(2,1)} %get-tuple-element.130.k_ref, bf16[1024,1088]{1,0:T(8,128)(2,1)} %get-tuple-element.131.v_ref, ...), custom_call_target="tpu_custom_call", output_to_operand_aliasing={{0}: (4, {})} | custom-call | flops 8589934592 | bytes 4194304 | tf_op jit(solution)/shard_map/attend/pallas_call | solution.py:507
  196.8 9.8 %middle.1 = (f32[1024,1088]{1,0:T(8,128)}, bf16[1024,1088]{1,0:T(8,128)(2,1)}) custom-call(bf16[1024,1088]{1,0:T(8,128)(2,1)} %pad_maximum_fusion.x_ref, bf16[1024,1088]{1,0:T(8,128)(2,1)} %copy-done.5, f32[3,1088]{1,0:T(4,128)} %pad_maximum_fusion.5.vectors_ref, bf16[16,272,1088]{2,1,0:T(8,128)(2,1)} %get-tuple-element.138.all_ref.refs_8_), custom_call_target="tpu_custom_call" | custom-call | flops 2424307712 | bytes 6823936 | tf_op jit(solution)/shard_map/middle/pallas_call | solution.py:948
  208.4 17.4 %up.2 = (bf16[1024,1088]{1,0:T(8,128)(2,1)}, bf16[1024,1088]{1,0:T(8,128)(2,1)}, bf16[1024,1088]{1,0:T(8,128)(2,1)}, bf16[1024,1088]{1,0:T(8,128)(2,1)}) custom-call(bf16[1024,1088]{1,0:T(8,128)(2,1)} %get-tuple-element.185.h_ref, f32[2,1088]{1,0:T(2,128)} %pad_maximum_fusion.6.biases_ref, bf16[1088,1088]{1,0:T(8,128)(2,1)} %all-gather.5.cloned.1.call-done.refs_0_.refs_4_, ...), custom_call_target="tpu_custom_call" | custom-call | flops 4848615424 | bytes 13647872 | tf_op jit(solution)/shard_map/up/pallas_call | solution.py:948
  225.8 17.8 %up.3 = (bf16[1024,1088]{1,0:T(8,128)(2,1)}, bf16[1024,1088]{1,0:T(8,128)(2,1)}, bf16[1024,1088]{1,0:T(8,128)(2,1)}, bf16[1024,1088]{1,0:T(8,128)(2,1)}) custom-call(bf16[1024,1088]{1,0:T(8,128)(2,1)} %get-tuple-element.185.h_ref, f32[2,1088]{1,0:T(2,128)} %pad_maximum_fusion.7.biases_ref, bf16[1088,1088]{1,0:T(8,128)(2,1)} %collective-permute-done.21.refs_0_.refs_5_, ...), custom_call_target="tpu_custom_call" | custom-call | flops 4848615424 | bytes 13647872 | tf_op jit(solution)/shard_map/up/pallas_call | solution.py:948
  245.2 6.2 convolution_convert_fusion.11
  251.5 4.6 convolution_convert_fusion.10
  259.7 4.6 convolution_convert_fusion.8
  264.3 10.2 %collective-permute-done.24.refs_2_.refs_5_ = bf16[1088,1088]{1,0:T(8,128)(2,1)} collective-permute-done((bf16[1088,1088]{1,0:T(8,128)(2,1)}, bf16[1088,1088]{1,0:T(8,128)(2,1)}, u32[]{:S(2)}, u32[]{:S(2)}) %collective-permute-start.24) | collective-permute-done | bytes 2367520 | tf_op jit(solution)/shard_map/ppermute | solution.py:603
  275.5 14.0 %hidden.2 = (bf16[1024,1088]{1,0:T(8,128)(2,1)}, bf16[1024,1088]{1,0:T(8,128)(2,1)}, f32[3,8,1088]{2,1,0:T(8,128)}) custom-call(bf16[1024,1088]{1,0:T(8,128)(2,1)} %pad_maximum_fusion.1.g_ref, bf16[1024,1088]{1,0:T(8,128)(2,1)} %get-tuple-element.163.refs_0_, bf16[1024,1088]{1,0:T(8,128)(2,1)} %get-tuple-element.164.refs_1_, ...), custom_call_target="tpu_custom_call" | custom-call | flops 4848615424 | bytes 13647872 | tf_op jit(solution)/shard_map/hidden/pallas_call | solution.py:948
  289.5 4.5 add_convert_fusion.5
  294.0 14.0 %hidden.3 = (bf16[1024,1088]{1,0:T(8,128)(2,1)}, bf16[1024,1088]{1,0:T(8,128)(2,1)}, f32[3,8,1088]{2,1,0:T(8,128)}) custom-call(bf16[1024,1088]{1,0:T(8,128)(2,1)} %pad_maximum_fusion.1.g_ref, bf16[1024,1088]{1,0:T(8,128)(2,1)} %get-tuple-element.168.refs_0_, bf16[1024,1088]{1,0:T(8,128)(2,1)} %get-tuple-element.169.refs_1_, ...), custom_call_target="tpu_custom_call" | custom-call | flops 4848615424 | bytes 13647872 | tf_op jit(solution)/shard_map/hidden/pallas_call | solution.py:948
  309.5 31.5 %back.1 = (f32[1024,1088]{1,0:T(8,128)}, bf16[1024,1088]{1,0:T(8,128)(2,1)}, bf16[1024,1088]{1,0:T(8,128)(2,1)}, f32[3,8,1088]{2,1,0:T(8,128)}) custom-call(bf16[1024,1088]{1,0:T(8,128)(2,1)} %pad_maximum_fusion.1.g_ref, f32[1024,1088]{1,0:T(8,128)} %get-tuple-element.216.middle_ref, f32[1,1088]{1,0:T(1,128)} %copy-done.31, ...), custom_call_target="tpu_custom_call" | custom-call | flops 12121538560 | bytes 34119680 | tf_op jit(solution)/shard_map/back/pallas_call | solution.py:948
  341.0 4.9 add_convert_fusion.4
  345.9 5.6 convolution_convert_fusion.7
  355.2 4.6 convolution_convert_fusion.4
  359.8 5.0 convolution_convert_fusion.3
  364.8 4.5 add_convert_fusion.3
  371.0 26.2 %attend_back.2 = (bf16[1024,1088]{1,0:T(8,128)(2,1)S(1)}, bf16[1024,1088]{1,0:T(8,128)(2,1)S(1)}, bf16[1024,1088]{1,0:T(8,128)(2,1)}) custom-call(s32[1]{0:T(128)} %bitcast.place_ref, bf16[1024,1088]{1,0:T(8,128)(2,1)} %get-tuple-element.134.q_ref, bf16[1024,1088]{1,0:T(8,128)(2,1)} %get-tuple-element.130.k_ref, ...), custom_call_target="tpu_custom_call" | custom-call | flops 20132659200 | bytes 10485760 | tf_op jit(solution)/shard_map/attend_back/pallas_call | solution.py:541
  400.1 4.8 add_convert_fusion.2
  406.6 21.4 %attend_back.3 = (bf16[1024,1088]{1,0:T(8,128)(2,1)S(1)}, bf16[1024,1088]{1,0:T(8,128)(2,1)S(1)}, bf16[1024,1088]{1,0:T(8,128)(2,1)}) custom-call(s32[1]{0:T(128)} %bitcast.place_ref, bf16[1024,1088]{1,0:T(8,128)(2,1)} %get-tuple-element.134.q_ref, ...), custom_call_target="tpu_custom_call", output_to_operand_aliasing={{0}: (7, {}), {1}: (8, {}), {2}: (9, {})} | custom-call | flops 16106127360 | bytes 8388608 | tf_op jit(solution)/shard_map/attend_back/pallas_call | solution.py:541
  429.5 6.4 convolution_convert_fusion.1
  439.1 6.9 %select_select_fusion = (bf16[1088,1088]{1,0:T(8,128)(2,1)}, bf16[1088,1088]{1,0:T(8,128)(2,1)}, bf16[1088,1088]{1,0:T(8,128)(2,1)}) fusion(bf16[1088,1088]{1,0:T(8,128)(2,1)S(1)} %convolution_convert_fusion.1, bf16[1088,1088]{1,0:T(8,128)(2,1)S(1)} %convolution_convert_fusion, bf16[1088,1088]{1,0:T(8,128)(2,1)S(1)} %copy-done.13, pred[]{:T(512)S(6)} %eq.258, ...), kind=kOutput, calls=%fused_computation.18 | convolution fusion | flops 2432593920 | bytes 18661382 | tf_op jit(solution)/shard_map/dot_general | solution.py:661
  446.6 4.5 collective-permute-done.33
  451.1 5.5 add_convert_fusion.1
  457.4 23.1 %last.1 = (bf16[1024,1088]{1,0:T(8,128)(2,1)}, f32[4,8,1088]{2,1,0:T(8,128)}) custom-call(bf16[1024,1088]{1,0:T(8,128)(2,1)} %copy-done.7, bf16[1024,1088]{1,0:T(8,128)(2,1)} %copy-done.10, bf16[1024,1088]{1,0:T(8,128)(2,1)} %get-tuple-element.213.v_ref, bf16[1024,1088]{1,0:T(8,128)(2,1)} %pad_maximum_fusion.x_ref, ...), custom_call_target="tpu_custom_call" | custom-call | flops 7272923136 | bytes 20471808 | tf_op jit(solution)/shard_map/last/pallas_call | solution.py:948
  480.5 6.9 %collective-permute-done.35 = bf16[1088,1088]{1,0:T(8,128)(2,1)} collective-permute-done((bf16[1088,1088]{1,0:T(8,128)(2,1)}, bf16[1088,1088]{1,0:T(8,128)(2,1)}, u32[]{:S(2)}, u32[]{:S(2)}) %collective-permute-start.35) | collective-permute-done | bytes 2367520 | tf_op jit(solution)/shard_map/ppermute | solution.py:603
  487.3 6.5 %add_convert_fusion = bf16[1088,1088]{1,0:T(8,128)(2,1)} fusion(bf16[1088,1088]{1,0:T(8,128)(2,1)} %collective-permute-done.35, bf16[1088,1088]{1,0:T(8,128)(2,1)} %collective-permute-done.34, bf16[1088,1088]{1,0:T(8,128)(2,1)} %get-tuple-element.355, bf16[1088,1088]{1,0:T(8,128)(2,1)} %copy-done.15, bf16[1088,1088]{1,0:T(8,128)(2,1)} %copy-done.16, ...), kind=kLoop, calls=%fused_computation.12 | loop fusion | flops 10653696 | bytes 16572419 | tf_op jit(solution)/shard_map/convert_element_type | solution.py:613
  505.4 3.7 collective-permute-start.44
  520.6 24.3 %down.1 = bf16[1024,1088]{1,0:T(8,128)(2,1)} custom-call(f32[1024,1088]{1,0:T(8,128)} %get-tuple-element.216.middle_ref, f32[1,1088]{1,0:T(1,128)} %reshape.475.vectors_ref, bf16[1024,1088]{1,0:T(8,128)(2,1)} %get-tuple-element.155.refs_0_, bf16[1024,1088]{1,0:T(8,128)(2,1)} %get-tuple-element.156.refs_1_, bf16[1024,1088]{1,0:T(8,128)(2,1)} %get-tuple-element.153.refs_2_, ...), custom_call_target="tpu_custom_call" | custom-call | flops 9697230848 | bytes 27295744 | tf_op jit(solution)/shard_map/down/pallas_call | solution.py:948
  564.4 3.7 settle.5
  574.0 3.7 collective-permute-done.38
  579.0 11.5 %collective-permute-done.40 = bf16[256,1088]{0,1:T(8,128)(2,1)} collective-permute-done((bf16[256,1088]{0,1:T(8,128)(2,1)}, bf16[256,1088]{0,1:T(8,128)(2,1)}, u32[]{:S(2)}, u32[]{:S(2)}) %collective-permute-start.40) | collective-permute-done | bytes 557088 | tf_op jit(solution)/shard_map/ppermute | solution.py:609
  611.0 6.0 copy.77
  627.5 4.5 concatenate.55
  639.0 4.2 concatenate.51
  643.2 3.5 concatenate.52
  (338 shorter events, 172.7 us)
Async XLA Ops:
  7.2 168.5 %all-gather.5.cloned.1.call-start = ((), (), s32[]{:S(2)}) async-start(), calls=%async_computation.4 | async-start | bytes 3133440 | tf_op jit(solution)/shard_map/all_gather | solution.py:1070
  13.7 22.1 %collective-permute-start = (bf16[3264]{0:T(1024)(128)(2,1)S(1)}, bf16[3264]{0:T(1024)(128)(2,1)S(1)}, u32[]{:S(2)}, u32[]{:S(2)}) collective-permute-start(bf16[3264]{0:T(1024)(128)(2,1)S(1)} %concatenate.43), channel_id=1, source_target_pairs={{0,4},{4,8},{8,12},{12,0},{1,5},{5,9},{9,13},{13,1},{2,6},{6,10},{... | collective-permute-start | bytes 19592 | tf_op jit(solution)/shard_map/ppermute | solution.py:638
  15.3 20.7 %collective-permute-start.1 = (bf16[3264]{0:T(1024)(128)(2,1)S(1)}, bf16[3264]{0:T(1024)(128)(2,1)S(1)}, u32[]{:S(2)}, u32[]{:S(2)}) collective-permute-start(bf16[3264]{0:T(1024)(128)(2,1)S(1)} %concatenate.43), channel_id=1, source_target_pairs={{0,8},{4,12},{8,0},{12,4},{1,9},{5,13},{9,1},{13,5},{2,10},{6,14},... | collective-permute-start | bytes 19592 | tf_op jit(solution)/shard_map/ppermute | solution.py:638
  16.4 21.0 %collective-permute-start.2 = (bf16[3264]{0:T(1024)(128)(2,1)S(1)}, bf16[3264]{0:T(1024)(128)(2,1)S(1)}, u32[]{:S(2)}, u32[]{:S(2)}) collective-permute-start(bf16[3264]{0:T(1024)(128)(2,1)S(1)} %concatenate.43), channel_id=1, source_target_pairs={{0,12},{4,0},{8,4},{12,8},{1,13},{5,1},{9,5},{13,9},{2,14},{6,2},{... | collective-permute-start | bytes 19592 | tf_op jit(solution)/shard_map/ppermute | solution.py:638
  21.1 16.9 %collective-permute-start.5 = (bf16[256,1088]{0,1:T(8,128)(2,1)}, bf16[256,1088]{0,1:T(8,128)(2,1)}, u32[]{:S(2)}, u32[]{:S(2)}) collective-permute-start(bf16[256,1088]{0,1:T(8,128)(2,1)} %get-tuple-element.303), channel_id=1, source_target_pairs={{0,3},{1,2},{2,1},{3,0},{4,7},{5,6},{6,5},{7,4},{8,11},{9,10},{10,... | collective-permute-start | bytes 1671176 | tf_op jit(solution)/shard_map/ppermute | solution.py:609
  21.2 27.1 %collective-permute-start.4 = (bf16[256,1088]{0,1:T(8,128)(2,1)}, bf16[256,1088]{0,1:T(8,128)(2,1)}, u32[]{:S(2)}, u32[]{:S(2)}) collective-permute-start(bf16[256,1088]{0,1:T(8,128)(2,1)} %get-tuple-element.304), channel_id=1, source_target_pairs={{0,2},{1,3},{2,0},{3,1},{4,6},{5,7},{6,4},{7,5},{8,10},{9,11},{10,... | collective-permute-start | bytes 1671176 | tf_op jit(solution)/shard_map/ppermute | solution.py:609
  36.0 24.2 %collective-permute-start.8 = (bf16[256,1088]{0,1:T(8,128)(2,1)}, bf16[256,1088]{0,1:T(8,128)(2,1)}, u32[]{:S(2)}, u32[]{:S(2)}) collective-permute-start(bf16[256,1088]{0,1:T(8,128)(2,1)} %get-tuple-element.299), channel_id=1, source_target_pairs={{0,3},{1,2},{2,1},{3,0},{4,7},{5,6},{6,5},{7,4},{8,11},{9,10},{10,... | collective-permute-start | bytes 1671176 | tf_op jit(solution)/shard_map/ppermute | solution.py:609
  37.4 34.8 %collective-permute-start.7 = (bf16[256,1088]{0,1:T(8,128)(2,1)}, bf16[256,1088]{0,1:T(8,128)(2,1)}, u32[]{:S(2)}, u32[]{:S(2)}) collective-permute-start(bf16[256,1088]{0,1:T(8,128)(2,1)} %get-tuple-element.300), channel_id=1, source_target_pairs={{0,2},{1,3},{2,0},{3,1},{4,6},{5,7},{6,4},{7,5},{8,10},{9,11},{10,... | collective-permute-start | bytes 1671176 | tf_op jit(solution)/shard_map/ppermute | solution.py:609
  38.0 36.3 %collective-permute-start.6 = (bf16[256,1088]{0,1:T(8,128)(2,1)}, bf16[256,1088]{0,1:T(8,128)(2,1)}, u32[]{:S(2)}, u32[]{:S(2)}) collective-permute-start(bf16[256,1088]{0,1:T(8,128)(2,1)} %get-tuple-element.298), channel_id=1, source_target_pairs={{0,1},{1,0},{2,3},{3,2},{4,5},{5,4},{6,7},{7,6},{8,9},{9,8},{10,11... | collective-permute-start | bytes 1671176 | tf_op jit(solution)/shard_map/ppermute | solution.py:609
  48.4 33.0 %collective-permute-start.9 = (bf16[272,1088]{1,0:T(8,128)(2,1)}, bf16[272,1088]{1,0:T(8,128)(2,1)}, u32[]{:S(2)}, u32[]{:S(2)}) collective-permute-start(bf16[272,1088]{1,0:T(8,128)(2,1)} %get-tuple-element.306), channel_id=1, source_target_pairs={{0,4},{4,8},{8,12},{12,0},{1,5},{5,9},{9,13},{13,1},{2,6},{6,10},{... | collective-permute-start | bytes 1775624 | tf_op jit(solution)/shard_map/ppermute | solution.py:1027
  50.7 52.1 %collective-permute-start.10 = (bf16[272,1088]{1,0:T(8,128)(2,1)}, bf16[272,1088]{1,0:T(8,128)(2,1)}, u32[]{:S(2)}, u32[]{:S(2)}) collective-permute-start(bf16[272,1088]{1,0:T(8,128)(2,1)} %get-tuple-element.306), channel_id=1, source_target_pairs={{0,8},{4,12},{8,0},{12,4},{1,9},{5,13},{9,1},{13,5},{2,10},{6,14},... | collective-permute-start | bytes 1775624 | tf_op jit(solution)/shard_map/ppermute | solution.py:1027
  60.2 46.5 %collective-permute-start.11 = (bf16[272,1088]{1,0:T(8,128)(2,1)}, bf16[272,1088]{1,0:T(8,128)(2,1)}, u32[]{:S(2)}, u32[]{:S(2)}) collective-permute-start(bf16[272,1088]{1,0:T(8,128)(2,1)} %get-tuple-element.306), channel_id=1, source_target_pairs={{0,12},{4,0},{8,4},{12,8},{1,13},{5,1},{9,5},{13,9},{2,14},{6,2},{... | collective-permute-start | bytes 1775624 | tf_op jit(solution)/shard_map/ppermute | solution.py:1027
  106.8 137.0 %all-gather.3.cloned.1.call-start = ((), (), s32[]{:S(2)}) async-start(), calls=%async_computation.3 | async-start | bytes 3133440 | tf_op jit(solution)/shard_map/all_gather | solution.py:1091
  108.7 15.8 %collective-permute-start.13 = (bf16[272,1088]{1,0:T(8,128)(2,1)}, bf16[272,1088]{1,0:T(8,128)(2,1)}, u32[]{:S(2)}, u32[]{:S(2)}) collective-permute-start(bf16[272,1088]{1,0:T(8,128)(2,1)} %collective-permute-done.10.refs_5_), channel_id=1, source_target_pairs={{0,16},{1,3},{2,18},{3,1},{16,0},{17,19},{18,2},{19,17},{4,20},{5,... | collective-permute-start | bytes 1775624 | tf_op jit(solution)/shard_map/ppermute | solution.py:603
  109.2 22.0 %collective-permute-start.14 = (bf16[272,1088]{1,0:T(8,128)(2,1)}, bf16[272,1088]{1,0:T(8,128)(2,1)}, u32[]{:S(2)}, u32[]{:S(2)}) collective-permute-start(bf16[272,1088]{1,0:T(8,128)(2,1)} %collective-permute-done.11.refs_6_), channel_id=1, source_target_pairs={{0,16},{1,3},{2,18},{3,1},{16,0},{17,19},{18,2},{19,17},{4,20},{5,... | collective-permute-start | bytes 1775624 | tf_op jit(solution)/shard_map/ppermute | solution.py:603
  110.7 20.5 %collective-permute-start.15 = (bf16[272,1088]{1,0:T(8,128)(2,1)}, bf16[272,1088]{1,0:T(8,128)(2,1)S(1)}, u32[]{:S(2)}, u32[]{:S(2)}) collective-permute-start(bf16[272,1088]{1,0:T(8,128)(2,1)} %collective-permute-done.9.refs_4_), channel_id=1, source_target_pairs={{0,1},{1,0},{2,3},{3,2},{16,17},{17,16},{18,19},{19,18},{4,5},{5,4... | collective-permute-start | bytes 1775624 | tf_op jit(solution)/shard_map/ppermute | solution.py:603
  111.4 22.9 %collective-permute-start.16 = (bf16[272,1088]{1,0:T(8,128)(2,1)}, bf16[272,1088]{1,0:T(8,128)(2,1)}, u32[]{:S(2)}, u32[]{:S(2)}) collective-permute-start(bf16[272,1088]{1,0:T(8,128)(2,1)} %collective-permute-done.10.refs_5_), channel_id=1, source_target_pairs={{0,1},{1,0},{2,3},{3,2},{16,17},{17,16},{18,19},{19,18},{4,5},{5,4... | collective-permute-start | bytes 1775624 | tf_op jit(solution)/shard_map/ppermute | solution.py:603
  117.8 16.5 %collective-permute-start.17 = (bf16[272,1088]{1,0:T(8,128)(2,1)}, bf16[272,1088]{1,0:T(8,128)(2,1)}, u32[]{:S(2)}, u32[]{:S(2)}) collective-permute-start(bf16[272,1088]{1,0:T(8,128)(2,1)} %collective-permute-done.11.refs_6_), channel_id=1, source_target_pairs={{0,1},{1,0},{2,3},{3,2},{16,17},{17,16},{18,19},{19,18},{4,5},{5,4... | collective-permute-start | bytes 1775624 | tf_op jit(solution)/shard_map/ppermute | solution.py:603
  175.7 21.1 %collective-permute-start.22 = (bf16[1088,1088]{1,0:T(8,128)(2,1)}, bf16[1088,1088]{1,0:T(8,128)(2,1)}, u32[]{:S(2)}, u32[]{:S(2)}) collective-permute-start(bf16[1088,1088]{1,0:T(8,128)(2,1)} %all-gather.5.cloned.1.call-done.refs_0_.refs_4_), channel_id=1, source_target_pairs={{0,1},{1,0},{2,3},{3,2},{16,17},{17,16},{18,19},{19,18},{4,5},{5,4... | collective-permute-start | bytes 7102472 | tf_op jit(solution)/shard_map/ppermute | solution.py:603
  175.9 30.7 %collective-permute-start.21 = (bf16[1088,1088]{1,0:T(8,128)(2,1)}, bf16[1088,1088]{1,0:T(8,128)(2,1)}, u32[]{:S(2)}, u32[]{:S(2)}) collective-permute-start(bf16[1088,1088]{1,0:T(8,128)(2,1)} %all-gather.5.cloned.1.call-done.refs_0_.refs_4_), channel_id=1, source_target_pairs={{0,16},{1,3},{2,18},{3,1},{16,0},{17,19},{18,2},{19,17},{4,20},{5,... | collective-permute-start | bytes 7102472 | tf_op jit(solution)/shard_map/ppermute | solution.py:603
  178.3 251.2 %reduce-scatter.4.cloned.1.call-start = ((), (), s32[]{:S(2)}) async-start(), calls=%async_computation.5 | async-start | bytes 3133440 | tf_op jit(solution)/shard_map/reduce_scatter | solution.py:626
  206.6 19.2 %collective-permute-start.23 = (bf16[1088,1088]{1,0:T(8,128)(2,1)}, bf16[1088,1088]{1,0:T(8,128)(2,1)}, u32[]{:S(2)}, u32[]{:S(2)}) collective-permute-start(bf16[1088,1088]{1,0:T(8,128)(2,1)} %collective-permute-done.21.refs_0_.refs_5_), channel_id=1, source_target_pairs={{0,1},{1,0},{2,3},{3,2},{16,17},{17,16},{18,19},{19,18},{4,5},{5,4... | collective-permute-start | bytes 7102472 | tf_op jit(solution)/shard_map/ppermute | solution.py:603
  243.7 30.8 %collective-permute-start.24 = (bf16[1088,1088]{1,0:T(8,128)(2,1)}, bf16[1088,1088]{1,0:T(8,128)(2,1)}, u32[]{:S(2)}, u32[]{:S(2)}) collective-permute-start(bf16[1088,1088]{1,0:T(8,128)(2,1)} %all-gather.3.cloned.1.call-done.refs_2_.refs_4_), channel_id=1, source_target_pairs={{0,16},{1,3},{2,18},{3,1},{16,0},{17,19},{18,2},{19,17},{4,20},{5,... | collective-permute-start | bytes 7102472 | tf_op jit(solution)/shard_map/ppermute | solution.py:603
  245.2 30.2 %collective-permute-start.27 = (bf16[1088,1088]{1,0:T(8,128)(2,1)}, bf16[1088,1088]{1,0:T(8,128)(2,1)}, u32[]{:S(2)}, u32[]{:S(2)}) collective-permute-start(bf16[1088,1088]{1,0:T(8,128)(2,1)} %all-gather.3.cloned.1.call-done.refs_2_.refs_4_), channel_id=1, source_target_pairs={{0,1},{1,0},{2,3},{3,2},{16,17},{17,16},{18,19},{19,18},{4,5},{5,4... | collective-permute-start | bytes 7102472 | tf_op jit(solution)/shard_map/ppermute | solution.py:603
  256.1 33.4 %collective-permute-start.25 = (bf16[1088,1088]{1,0:T(8,128)(2,1)}, bf16[1088,1088]{1,0:T(8,128)(2,1)}, u32[]{:S(2)}, u32[]{:S(2)}) collective-permute-start(bf16[1088,1088]{1,0:T(8,128)(2,1)} %convolution_convert_fusion.11), channel_id=1, source_target_pairs={{0,1},{1,0},{2,3},{3,2},{16,17},{17,16},{18,19},{19,18},{4,5},{5,4... | collective-permute-start | bytes 7102472 | tf_op jit(solution)/shard_map/ppermute | solution.py:603
  274.5 19.5 %collective-permute-start.28 = (bf16[1088,1088]{1,0:T(8,128)(2,1)}, bf16[1088,1088]{1,0:T(8,128)(2,1)}, u32[]{:S(2)}, u32[]{:S(2)}) collective-permute-start(bf16[1088,1088]{1,0:T(8,128)(2,1)} %collective-permute-done.24.refs_2_.refs_5_), channel_id=1, source_target_pairs={{0,1},{1,0},{2,3},{3,2},{16,17},{17,16},{18,19},{19,18},{4,5},{5,4... | collective-permute-start | bytes 7102472 | tf_op jit(solution)/shard_map/ppermute | solution.py:603
  275.0 33.0 %collective-permute-start.26 = (bf16[1088,1088]{1,0:T(8,128)(2,1)}, bf16[1088,1088]{1,0:T(8,128)(2,1)}, u32[]{:S(2)}, u32[]{:S(2)}) collective-permute-start(bf16[1088,1088]{1,0:T(8,128)(2,1)} %convolution_convert_fusion.10), channel_id=1, source_target_pairs={{0,1},{1,0},{2,3},{3,2},{16,17},{17,16},{18,19},{19,18},{4,5},{5,4... | collective-permute-start | bytes 7102472 | tf_op jit(solution)/shard_map/ppermute | solution.py:603
  308.0 33.0 %collective-permute-start.29 = (bf16[1088,1088]{1,0:T(8,128)(2,1)}, bf16[1088,1088]{1,0:T(8,128)(2,1)}, u32[]{:S(2)}, u32[]{:S(2)}) collective-permute-start(bf16[1088,1088]{1,0:T(8,128)(2,1)} %add_convert_fusion.5), channel_id=1, source_target_pairs={{0,16},{1,3},{2,18},{3,1},{16,0},{17,19},{18,2},{19,17},{4,20},{5,... | collective-permute-start | bytes 7102472 | tf_op jit(solution)/shard_map/ppermute | solution.py:603
  369.3 30.7 %collective-permute-start.32 = (bf16[1088,1088]{1,0:T(8,128)(2,1)}, bf16[1088,1088]{1,0:T(8,128)(2,1)}, u32[]{:S(2)}, u32[]{:S(2)}) collective-permute-start(bf16[1088,1088]{1,0:T(8,128)(2,1)} %add_convert_fusion.3), channel_id=1, source_target_pairs={{0,16},{1,3},{2,18},{3,1},{16,0},{17,19},{18,2},{19,17},{4,20},{5,... | collective-permute-start | bytes 7102472 | tf_op jit(solution)/shard_map/ppermute | solution.py:603
  371.0 148.5 %reduce-scatter.8.cloned.1.call-start = ((), (), s32[]{:S(2)}) async-start(), calls=%async_computation.7 | async-start | bytes 3133440 | tf_op jit(solution)/shard_map/reduce_scatter | solution.py:626
  446.5 124.4 %reduce-scatter.6.cloned.1.call-start = ((), (), s32[]{:S(2)}) async-start(), calls=%async_computation.6 | async-start | bytes 3133440 | tf_op jit(solution)/shard_map/reduce_scatter | solution.py:626
  456.6 30.7 %collective-permute-start.35 = (bf16[1088,1088]{1,0:T(8,128)(2,1)}, bf16[1088,1088]{1,0:T(8,128)(2,1)}, u32[]{:S(2)}, u32[]{:S(2)}) collective-permute-start(bf16[1088,1088]{1,0:T(8,128)(2,1)} %add_convert_fusion.1), channel_id=1, source_target_pairs={{0,16},{1,3},{2,18},{3,1},{16,0},{17,19},{18,2},{19,17},{4,20},{5,... | collective-permute-start | bytes 7102472 | tf_op jit(solution)/shard_map/ppermute | solution.py:603
  516.1 34.7 %collective-permute-start.63 = (bf16[272,1088]{1,0:T(8,128)(2,1)S(1)}, bf16[272,1088]{1,0:T(8,128)(2,1)S(1)}, u32[]{:S(2)}, u32[]{:S(2)}) collective-permute-start(bf16[272,1088]{1,0:T(8,128)(2,1)S(1)} %add_convert_fusion.6.refs_0_), channel_id=1, source_target_pairs={{0,16},{1,3},{2,18},{3,1},{16,0},{17,19},{18,2},{19,17},{4,20},{5,... | collective-permute-start | bytes 1775624 | tf_op jit(solution)/shard_map/ppermute | solution.py:603
  517.2 33.7 %collective-permute-start.64 = (bf16[272,1088]{1,0:T(8,128)(2,1)S(1)}, bf16[272,1088]{1,0:T(8,128)(2,1)S(1)}, u32[]{:S(2)}, u32[]{:S(2)}) collective-permute-start(bf16[272,1088]{1,0:T(8,128)(2,1)S(1)} %add_convert_fusion.6.refs_0_), channel_id=1, source_target_pairs={{0,1},{1,0},{2,3},{3,2},{16,17},{17,16},{18,19},{19,18},{4,5},{5,4... | collective-permute-start | bytes 1775624 | tf_op jit(solution)/shard_map/ppermute | solution.py:603
  517.2 43.8 %collective-permute-start.65 = (bf16[272,1088]{1,0:T(8,128)(2,1)S(1)}, bf16[272,1088]{1,0:T(8,128)(2,1)}, u32[]{:S(2)}, u32[]{:S(2)}) collective-permute-start(bf16[272,1088]{1,0:T(8,128)(2,1)S(1)} %add_convert_fusion.6.refs_0_), channel_id=1, source_target_pairs={{0,17},{1,2},{2,19},{3,0},{16,1},{17,18},{18,3},{19,16},{4,21},{5,... | collective-permute-start | bytes 1775624 | tf_op jit(solution)/shard_map/ppermute | solution.py:603
  518.8 43.1 %collective-permute-start.47 = (f32[1088]{0:T(1024)S(1)}, f32[1088]{0:T(1024)S(1)}, u32[]{:S(2)}, u32[]{:S(2)}) collective-permute-start(f32[1088]{0:T(1024)S(1)} %add.285), channel_id=1, source_target_pairs={{0,16},{1,17},{2,18},{3,19},{16,0},{17,1},{18,2},{19,3},{4,20},{5,... | collective-permute-start | bytes 13064 | tf_op jit(solution)/shard_map/ppermute | solution.py:654
  519.4 51.4 %collective-permute-start.58 = (bf16[272,1088]{1,0:T(8,128)(2,1)}, bf16[272,1088]{1,0:T(8,128)(2,1)}, u32[]{:S(2)}, u32[]{:S(2)}) collective-permute-start(bf16[272,1088]{1,0:T(8,128)(2,1)} %reduce-scatter.8.cloned.1.call-done), channel_id=1, source_target_pairs={{0,2},{1,17},{2,0},{3,19},{16,18},{17,1},{18,16},{19,3},{4,6},{5,2... | collective-permute-start | bytes 1775624 | tf_op jit(solution)/shard_map/ppermute | solution.py:603
  550.9 19.3 %collective-permute-start.37 = (bf16[256,1088]{0,1:T(8,128)(2,1)}, bf16[256,1088]{0,1:T(8,128)(2,1)}, u32[]{:S(2)}, u32[]{:S(2)}) collective-permute-start(bf16[256,1088]{0,1:T(8,128)(2,1)} %copy.65), channel_id=1, source_target_pairs={{0,2},{1,3},{2,0},{3,1},{4,6},{5,7},{6,4},{7,5},{8,10},{9,11},{10,... | collective-permute-start | bytes 1671176 | tf_op jit(solution)/shard_map/ppermute | solution.py:609
  560.9 16.8 %collective-permute-start.38 = (bf16[256,1088]{0,1:T(8,128)(2,1)}, bf16[256,1088]{0,1:T(8,128)(2,1)}, u32[]{:S(2)}, u32[]{:S(2)}) collective-permute-start(bf16[256,1088]{0,1:T(8,128)(2,1)} %copy.66), channel_id=1, source_target_pairs={{0,3},{1,2},{2,1},{3,0},{4,7},{5,6},{6,5},{7,4},{8,11},{9,10},{10,... | collective-permute-start | bytes 1671176 | tf_op jit(solution)/shard_map/ppermute | solution.py:609
  561.9 16.8 %collective-permute-start.39 = (bf16[256,1088]{0,1:T(8,128)(2,1)}, bf16[256,1088]{0,1:T(8,128)(2,1)}, u32[]{:S(2)}, u32[]{:S(2)}) collective-permute-start(bf16[256,1088]{0,1:T(8,128)(2,1)} %copy.70), channel_id=1, source_target_pairs={{0,1},{1,0},{2,3},{3,2},{4,5},{5,4},{6,7},{7,6},{8,9},{9,8},{10,11... | collective-permute-start | bytes 1671176 | tf_op jit(solution)/shard_map/ppermute | solution.py:609
  562.2 28.3 %collective-permute-start.40 = (bf16[256,1088]{0,1:T(8,128)(2,1)}, bf16[256,1088]{0,1:T(8,128)(2,1)}, u32[]{:S(2)}, u32[]{:S(2)}) collective-permute-start(bf16[256,1088]{0,1:T(8,128)(2,1)} %copy.71), channel_id=1, source_target_pairs={{0,2},{1,3},{2,0},{3,1},{4,6},{5,7},{6,4},{7,5},{8,10},{9,11},{10,... | collective-permute-start | bytes 1671176 | tf_op jit(solution)/shard_map/ppermute | solution.py:609
  570.2 36.4 %collective-permute-start.41 = (bf16[256,1088]{0,1:T(8,128)(2,1)}, bf16[256,1088]{0,1:T(8,128)(2,1)}, u32[]{:S(2)}, u32[]{:S(2)}) collective-permute-start(bf16[256,1088]{0,1:T(8,128)(2,1)} %copy.72), channel_id=1, source_target_pairs={{0,3},{1,2},{2,1},{3,0},{4,7},{5,6},{6,5},{7,4},{8,11},{9,10},{10,... | collective-permute-start | bytes 1671176 | tf_op jit(solution)/shard_map/ppermute | solution.py:609
  570.9 46.2 %collective-permute-start.48 = (bf16[272,1088]{1,0:T(8,128)(2,1)}, bf16[272,1088]{1,0:T(8,128)(2,1)}, u32[]{:S(2)}, u32[]{:S(2)}) collective-permute-start(bf16[272,1088]{1,0:T(8,128)(2,1)} %reduce-scatter.6.cloned.1.call-done), channel_id=1, source_target_pairs={{0,2},{1,17},{2,0},{3,19},{16,18},{17,1},{18,16},{19,3},{4,6},{5,2... | collective-permute-start | bytes 1775624 | tf_op jit(solution)/shard_map/ppermute | solution.py:603
  577.7 42.5 %collective-permute-start.59 = (bf16[272,1088]{1,0:T(8,128)(2,1)}, bf16[272,1088]{1,0:T(8,128)(2,1)}, u32[]{:S(2)}, u32[]{:S(2)}) collective-permute-start(bf16[272,1088]{1,0:T(8,128)(2,1)} %add_convert_fusion.7), channel_id=1, source_target_pairs={{0,16},{1,3},{2,18},{3,1},{16,0},{17,19},{18,2},{19,17},{4,20},{5,... | collective-permute-start | bytes 1775624 | tf_op jit(solution)/shard_map/ppermute | solution.py:603
  578.7 42.3 %collective-permute-start.60 = (bf16[272,1088]{1,0:T(8,128)(2,1)}, bf16[272,1088]{1,0:T(8,128)(2,1)}, u32[]{:S(2)}, u32[]{:S(2)}) collective-permute-start(bf16[272,1088]{1,0:T(8,128)(2,1)} %add_convert_fusion.7), channel_id=1, source_target_pairs={{0,1},{1,0},{2,3},{3,2},{16,17},{17,16},{18,19},{19,18},{4,5},{5,4... | collective-permute-start | bytes 1775624 | tf_op jit(solution)/shard_map/ppermute | solution.py:603
  590.6 31.6 %collective-permute-start.61 = (bf16[272,1088]{1,0:T(8,128)(2,1)}, bf16[272,1088]{1,0:T(8,128)(2,1)}, u32[]{:S(2)}, u32[]{:S(2)}) collective-permute-start(bf16[272,1088]{1,0:T(8,128)(2,1)} %add_convert_fusion.7), channel_id=1, source_target_pairs={{0,17},{1,2},{2,19},{3,0},{16,1},{17,18},{18,3},{19,16},{4,21},{5,... | collective-permute-start | bytes 1775624 | tf_op jit(solution)/shard_map/ppermute | solution.py:603
  618.3 16.2 %collective-permute-start.49 = (bf16[272,1088]{1,0:T(8,128)(2,1)S(1)}, bf16[272,1088]{1,0:T(8,128)(2,1)}, u32[]{:S(2)}, u32[]{:S(2)}) collective-permute-start(bf16[272,1088]{1,0:T(8,128)(2,1)S(1)} %add_convert_fusion.8), channel_id=1, source_target_pairs={{0,16},{1,3},{2,18},{3,1},{16,0},{17,19},{18,2},{19,17},{4,20},{5,... | collective-permute-start | bytes 1775624 | tf_op jit(solution)/shard_map/ppermute | solution.py:603
  620.2 15.4 %collective-permute-start.51 = (bf16[272,1088]{1,0:T(8,128)(2,1)S(1)}, bf16[272,1088]{1,0:T(8,128)(2,1)}, u32[]{:S(2)}, u32[]{:S(2)}) collective-permute-start(bf16[272,1088]{1,0:T(8,128)(2,1)S(1)} %add_convert_fusion.8), channel_id=1, source_target_pairs={{0,17},{1,2},{2,19},{3,0},{16,1},{17,18},{18,3},{19,16},{4,21},{5,... | collective-permute-start | bytes 1775624 | tf_op jit(solution)/shard_map/ppermute | solution.py:603
  (66 other events, 563.0 us)
Sparse Core Ops, SparseCore 0:
  106.9 49.5 all-gather.4
  178.4 49.0 all-gather.2
  371.1 47.9 reduce-scatter.3
  446.6 47.1 reduce-scatter.7
  496.6 50.8 reduce-scatter.5

commit v4 on v3

--- a/solution.py
+++ b/solution.py
@@ -692,9 +692,9 @@
     return jnp.sum(values.reshape(rows // 8, 8, width), axis=0)
 
 
-def front_kernel(places_ref, x_ref, vectors_ref, *refs):
-    pieces = refs[:16]
-    h_ref, q_ref, k_ref, v_ref, all_ref, weights, arrived, left = refs[16:]
+def front_kernel(places_ref, vectors_ref, *refs):
+    slots, pieces = refs[:4], refs[4:20]
+    x_ref, h_ref, q_ref, k_ref, v_ref, all_ref, weights, arrived, left = refs[20:]
     copies = [
         pltpu.make_async_copy(piece, weights.at[places_ref[at]], arrived.at[at])
         for at, piece in enumerate(pieces)
@@ -702,15 +702,13 @@
     for copy in copies:
         copy.start()
     rows, width = x_ref.shape
-    step = 256
-
-    def norm(at, carry):
-        here = pl.ds(pl.multiple_of(at * step, step), step)
-        unit, _ = unit_of(x_ref[here, :].astype(jnp.float32))
+    step = rows // 4
+    for at, slot in enumerate(slots):
+        here = pl.ds(at * step, step)
+        values = slot[...].astype(jnp.float32).T
+        x_ref[here, :] = values.astype(jnp.bfloat16)
+        unit, _ = unit_of(values)
         h_ref[here, :] = (unit * vectors_ref[0:1, :] + vectors_ref[1:2, :]).astype(jnp.bfloat16)
-        return carry
-
-    lax.fori_loop(0, rows // step, norm, 0)
     for copy in copies:
         copy.wait()
     leave = pltpu.make_async_copy(weights, all_ref, left)
@@ -731,17 +729,18 @@
     leave.wait()
 
 
-def front(places, rows_in, vectors, pieces):
-    rows, width = rows_in.shape
+def front(places, slots, vectors, pieces):
+    width, step = slots[0].shape
+    rows = 4 * step
     vmem = pl.BlockSpec(memory_space=pltpu.VMEM)
     hbm = pl.BlockSpec(memory_space=pl.ANY)
     shape = jax.ShapeDtypeStruct((rows, width), jnp.bfloat16)
     whole = (16,) + pieces[0].shape
     return pl.pallas_call(
         front_kernel,
-        in_specs=[pl.BlockSpec(memory_space=pltpu.SMEM), vmem, vmem] + [hbm] * 16,
-        out_specs=[vmem] * 4 + [hbm],
-        out_shape=[shape] * 4 + [jax.ShapeDtypeStruct(whole, jnp.bfloat16)],
+        in_specs=[pl.BlockSpec(memory_space=pltpu.SMEM)] + [vmem] * 5 + [hbm] * 16,
+        out_specs=[vmem] * 5 + [hbm],
+        out_shape=[shape] * 5 + [jax.ShapeDtypeStruct(whole, jnp.bfloat16)],
         scratch_shapes=[
             pltpu.VMEM(whole, jnp.bfloat16),
             pltpu.SemaphoreType.DMA((16,)),
@@ -750,7 +749,62 @@
         compiler_params=pltpu.CompilerParams(vmem_limit_bytes=56 * 2**20),
         cost_estimate=block_flops(rows, width, 3),
         name="front",
-    )(places, rows_in, vectors, *pieces)
+    )(places, vectors, *slots, *pieces)
+
+
+def turn_kernel(*refs):
+    slots, out_ref = refs[:-1], refs[-1]
+    step = slots[0].shape[1]
+    for at, slot in enumerate(slots):
+        out_ref[pl.ds(at * step, step), :] = (
+            slot[...].astype(jnp.float32).T.astype(jnp.bfloat16)
+        )
+
+
+def turn(slots):
+    width, step = slots[0].shape
+    return pl.pallas_call(
+        turn_kernel,
+        out_shape=jax.ShapeDtypeStruct((len(slots) * step, width), jnp.bfloat16),
+        compiler_params=pltpu.CompilerParams(vmem_limit_bytes=48 * 2**20),
+        name="turn",
+    )(*slots)
+
+
+def assemble_kernel(place_ref, *refs, plan):
+    pieces, outs = refs[:4], refs[4:]
+    for at, piece in enumerate(pieces):
+        for kind, moves in enumerate(plan):
+
+            @pl.when(place_ref[at] == kind)
+            def _(piece=piece, moves=moves):
+                for out, source, target, size in moves:
+                    outs[out][:, target : target + size] = piece[
+                        :, source : source + size
+                    ].astype(jnp.float32)
+
+
+def assemble(places, pieces, plan, shapes):
+    vmem = pl.BlockSpec(memory_space=pltpu.VMEM)
+    return pl.pallas_call(
+        functools.partial(assemble_kernel, plan=plan),
+        in_specs=[pl.BlockSpec(memory_space=pltpu.SMEM)] + [vmem] * 4,
+        out_specs=[vmem] * len(shapes),
+        out_shape=[jax.ShapeDtypeStruct(shape, jnp.float32) for shape in shapes],
+        compiler_params=pltpu.CompilerParams(vmem_limit_bytes=48 * 2**20),
+        name="assemble",
+    )(places, *pieces)
+
+
+def store_turned(step, refs, values):
+    size = refs[0].shape[1]
+    share = values.shape[0] // size
+    for at, ref in enumerate(refs):
+
+        @pl.when(step == at // share)
+        def _(at=at, ref=ref):
+            first = (at % share) * size
+            ref[...] = values[first : first + size].T.astype(ref.dtype)
 
 
 def fetch(step, copies):
@@ -807,7 +861,8 @@
 
 def down_kernel(middle_ref, vectors_ref, *refs):
     actives, sources = refs[:4], refs[4:8]
-    out_ref, weights, arrived = refs[8:]
+    out_refs = refs[8:12]
+    weights, arrived = refs[12:]
     step = pl.program_id(0)
     copies = [
         pltpu.make_async_copy(source, weights.at[at], arrived.at[at])
@@ -820,7 +875,7 @@
         total = total + jnp.dot(
             actives[at][...], weights[at], preferred_element_type=jnp.float32
         )
-    out_ref[...] = total.astype(jnp.bfloat16)
+    store_turned(step, out_refs, total)
 
 
 def norm_back(values, gain, grad):
@@ -901,7 +956,8 @@
 
 
 def last_kernel(q_ref, k_ref, v_ref, x_ref, grad_ref, vectors_ref, all_ref, *refs):
-    out_ref, sums_ref, weights, arrived = refs
+    out_refs = refs[:4]
+    sums_ref, weights, arrived = refs[4:]
     step = pl.program_id(0)
     width = x_ref.shape[1]
     copies = [
@@ -921,7 +977,7 @@
             preferred_element_type=jnp.float32,
         )
     part, gain_term = norm_back(x_ref[...].astype(jnp.float32), vectors_ref[0:1, :], total)
-    out_ref[...] = (grad_ref[...] + part).astype(jnp.bfloat16)
+    store_turned(step, out_refs, grad_ref[...] + part)
 
     @pl.when(step == 0)
     def _():
@@ -940,8 +996,14 @@
 def by_rows(kernel, name, rows, width, tiled, whole, remote, outs, sums, scratch, sems, blocks):
     step = 512
     tile = pl.BlockSpec((step, width), lambda at: (at, 0))
-    out_specs = [tile] * len(outs)
-    out_shape = [jax.ShapeDtypeStruct((rows, width), dtype) for dtype in outs]
+    out_specs, out_shape = [], []
+    for dtype in outs:
+        if dtype is None:
+            out_specs += [pl.BlockSpec((width, rows // 4), lambda at: (0, 0))] * 4
+            out_shape += [jax.ShapeDtypeStruct((width, rows // 4), jnp.bfloat16)] * 4
+        else:
+            out_specs.append(tile)
+            out_shape.append(jax.ShapeDtypeStruct((rows, width), dtype))
     if sums:
         out_specs.append(pl.BlockSpec((sums, 8, width), lambda at: (0, 0, 0)))
         out_shape.append(jax.ShapeDtypeStruct((sums, 8, width), jnp.float32))
@@ -1002,19 +1064,15 @@
     class_places = jnp.stack(classes)
 
     def spread(values):
-        return jnp.concatenate(
-            [lax.dynamic_index_in_dim(values, c, 0, keepdims=False)]
-            + [
-                ctx_swap(lax.dynamic_index_in_dim(values, c ^ bits, 0, keepdims=False), bits)
-                for bits in range(1, 4)
-            ],
-            axis=0,
-        )
-
-    def collect(values, dtype):
-        pieces = [values[at * block_len : (at + 1) * block_len] for at in range(4)]
+        values = jnp.swapaxes(values, 1, 2)
+        return [lax.dynamic_index_in_dim(values, c, 0, keepdims=False)] + [
+            ctx_swap(lax.dynamic_index_in_dim(values, c ^ bits, 0, keepdims=False), bits)
+            for bits in range(1, 4)
+        ]
+
+    def collect(pieces, dtype):
         moved = [pieces[0]] + [ctx_swap(pieces[bits], bits) for bits in range(1, 4)]
-        return settle(places, moved, dtype)
+        return jnp.swapaxes(settle(places, moved, dtype), 1, 2)
 
     sections = [
         project_in[:, :width],
@@ -1023,10 +1081,28 @@
         project_out,
     ]
     section = chosen(mine, sections)
+    section, inputs = pin((section, inputs))
     shards = [
         lax.ppermute(section, "fsdp", [(device, (device + step) % 4) for device in range(4)])
         for step in range(1, 4)
     ]
+    slots_in = spread(inputs)
+    pieces_in = (
+        first_gain,
+        first_shift,
+        query_bias,
+        value_bias,
+        output_bias,
+        second_gain,
+        second_shift,
+        down_bias,
+        up_bias,
+    )
+    shards[0], cotangent, up_weight, down_weight, *pieces_in = pin(
+        (shards[0], cotangent, up_weight, down_weight, *pieces_in)
+    )
+    vectors = gather_vector(jnp.concatenate(pieces_in), z).astype(wide)
+    slots_back = spread(cotangent)
     up_piece = jnp.concatenate(
         [
             lax.dynamic_slice_in_dim(up_weight, at * width + mine * quarter, quarter, 1)
@@ -1034,27 +1110,9 @@
         ],
         axis=1,
     )
-    vectors = gather_vector(
-        jnp.concatenate(
-            [
-                first_gain,
-                first_shift,
-                query_bias,
-                value_bias,
-                output_bias,
-                second_gain,
-                second_shift,
-                down_bias,
-                up_bias,
-            ]
-        ),
-        z,
-    )
-    rows_in, upstream_low = spread(inputs), spread(cotangent)
-    up_piece, vectors, rows_in, upstream_low, *shards = pin(
-        (up_piece, vectors, rows_in, upstream_low, *shards)
-    )
-    vectors = vectors.astype(wide)
+    up_piece, vectors, shards[1], shards[2], *slots_in = pin(
+        (up_piece, vectors, shards[1], shards[2], *slots_in)
+    )
     near_shards = [plane_swap(shard, "near") for shard in shards]
     around = (
         sections
@@ -1081,13 +1139,14 @@
         axis=0,
     )
 
-    normed_low, queries, key_rows, value_rows, weights = front(
+    rows_in, normed_low, queries, key_rows, value_rows, weights = front(
         around_places,
-        rows_in,
+        slots_in,
         jnp.concatenate([gain_first, shift_first, qbias, vbias], axis=0),
         around,
     )
-    down_piece, queries = pin((down_piece, queries))
+    slots_back[0], down_piece, queries = pin((slots_back[0], down_piece, queries))
+    upstream_low = turn(slots_back)
     down_own = lax.all_gather(down_piece, "fsdp", axis=0, tiled=True)
     attended, logs_one = attend(place, queries, key_rows, value_rows, seq_count, 0, 5, [])
     up_own, late_queries, attended = pin((up_own, queries, attended))
@@ -1209,7 +1268,8 @@
         place, late_queries, key_rows, value_rows, grad_low, attended, logs_one, seq_count, 0, 5, []
     )
     up_first = low_sum(up_terms[0], up_far, up_close)
-    up_first, *in_grads = pin((up_first, *in_grads))
+    up_first, down_shard, *in_grads = pin((up_first, down_shard, *in_grads))
+    up_shard = scatter_rows(up_first)
     in_grads = attend_back(
         place,
         late_queries,
@@ -1223,8 +1283,6 @@
         4,
         in_grads,
     )
-    up_first, down_shard, *in_grads = pin((up_first, down_shard, *in_grads))
-    up_shard = scatter_rows(up_first)
     down_parts = reduce_last(down_shard)
     in_terms = [turned_product(normed_low, grad) for grad in in_grads]
     section_grads = in_terms + [out_term]
@@ -1234,7 +1292,7 @@
     second, far, *in_grads = pin((second, far, *in_grads))
     close = plane_swap(second, "near")
     query_low, key_low, value_low = in_grads
-    input_low, last_sums = by_rows(
+    *input_slots, last_sums = by_rows(
         last_kernel,
         "last",
         rows,
@@ -1242,16 +1300,16 @@
         ([query_low, key_low, value_low, rows_in, middle_grad], []),
         [gain_first],
         [weights],
-        [low],
+        [None],
         4,
         [(12,) + section.shape],
         3,
         3,
     )
     first = low_sum(sections_mine[0], far, close)
-    first, middle, input_low = pin((first, middle, input_low))
-    input_gradient = collect(input_low, wide)
-    (result,) = by_rows(
+    first, middle, up_shard, *input_slots = pin((first, middle, up_shard, *input_slots))
+    input_gradient = collect(input_slots, wide)
+    result_slots = by_rows(
         down_kernel,
         "down",
         rows,
@@ -1259,15 +1317,15 @@
         ([middle], active),
         [dbias],
         down_slots,
-        [low],
+        [None],
         0,
         [(4,) + area],
         4,
         4,
     )
-    outputs = collect(result, low)
+    outputs = collect(result_slots, low)
     up_parts = reduce_last(up_shard)
-    section_parts = reduce_last(scatter_rows(first))
+    shard = scatter_rows(first)
 
     back_sums = jnp.concatenate([hidden_sums, back_sums], axis=0)
     back_sums = jnp.sum(back_sums, axis=1)
@@ -1276,42 +1334,54 @@
     hidden_sums = jnp.stack(
         [chosen(slot_of[kind], hidden_sums) for kind in range(4)], axis=1
     ).reshape(4, 4 * quarter)
-    early = reduce_vector(
+    totals = reduce_vector(
         jnp.concatenate(
-            [back_sums[at].reshape(4, quarter) for at in range(4, 8)] + [hidden_sums], axis=1
+            [back_sums[at].reshape(4, quarter) for at in range(4, 8)]
+            + [last_sums[at].reshape(4, quarter) for at in range(4)]
+            + [hidden_sums],
+            axis=1,
         ),
         z,
     )
-    late = reduce_vector(
-        jnp.concatenate([last_sums[at].reshape(4, quarter) for at in range(4)], axis=1), z
-    )
-    dbias_sum, gain_two_sum, shift_two_sum, obias_sum = (
-        early[at * quarter : (at + 1) * quarter] for at in range(4)
-    )
-    ubias_sum = early[4 * quarter :]
-    gain_one_sum, shift_one_sum, qbias_sum, vbias_sum = (
-        late[at * quarter : (at + 1) * quarter] for at in range(4)
-    )
-    in_parts = [chosen(slot_of[kind], section_parts).astype(wide) for kind in range(4)]
-    up_parts = [chosen(slot_of[kind], up_parts) for kind in range(4)]
-    up_sum = jnp.concatenate(
+    (up_sum,) = assemble(
+        class_places,
+        up_parts,
         [
-            up_parts[kind][:, at * quarter : (at + 1) * quarter]
-            for at in range(4)
+            [(0, at * quarter, at * width + kind * quarter, quarter) for at in range(4)]
             for kind in range(4)
         ],
-        axis=1,
-    ).astype(wide)
+        [up_weight.shape],
+    )
     down_sum = settle(class_places, down_parts, wide).reshape(down_weight.shape)
+    shard, outputs, input_gradient, totals, up_sum, down_sum = pin(
+        (shard, outputs, input_gradient, totals, up_sum, down_sum)
+    )
+    in_sum, out_sum = assemble(
+        class_places,
+        reduce_last(shard),
+        [[(0, 0, kind * width, width)] for kind in range(3)] + [[(1, 0, 0, width)]],
+        [project_in.shape, project_out.shape],
+    )
+    (
+        dbias_sum,
+        gain_two_sum,
+        shift_two_sum,
+        obias_sum,
+        gain_one_sum,
+        shift_one_sum,
+        qbias_sum,
+        vbias_sum,
+    ) = (totals[at * quarter : (at + 1) * quarter] for at in range(8))
+    ubias_sum = totals[8 * quarter :]
     return (
         outputs,
         input_gradient,
         gain_one_sum,
         shift_one_sum,
-        jnp.concatenate(in_parts[:3], axis=1),
+        in_sum,
         qbias_sum,
         vbias_sum,
-        in_parts[3],
+        out_sum,
         obias_sum,
         gain_two_sum,
         shift_two_sum,

time: 663 us -> 698 us (1.053)
  waiting for transfers between devices: 113 us -> 208 us
  local copies, waits for them, and re-layouts: 102 us -> 36 us
  Pallas kernels: 261 us -> 283 us
  other arithmetic: 53 us -> 33.5 us
    ppermute x12, waiting for transfers between devices: 35.7 us -> 94.5 us  [ctx_swap(): lax.ppermute(values, 'ctx', [(device, device ^ bits) for device in range(...]
    ppermute x12 -> x0, local copies, waits for them, and re-layouts: 23.1 us -> none  [ctx_swap(): lax.ppermute(values, 'ctx', [(device, device ^ bits) for device in range(...]
    slice x13 -> x2, local copies, waits for them, and re-layouts: 22.4 us -> 1.27 us  [the longest x1 0.67 us: per_device_exchanged(): totals[at * quarter:(at + 1) * quarter]]
    concatenate x4 -> x1, local copies, waits for them, and re-layouts: 15.3 us -> 0.1 us  [per_device_exchanged(): vectors = gather_vector(jnp.concatenate(pieces_in), z).astype(wide)]
    reduce_scatter x3, waiting for transfers between devices: 0.01 us -> 13.2 us  [scatter_rows(): return lax.psum_scatter(values, 'fsdp', scatter_dimension=0, tiled=True)]
    pallas_call x8, Pallas kernels: 152 us -> 164 us  [by_rows(): pl.pallas_call(kernel, grid=(rows // step,), in_specs=[tile] * len(tiled[...]
    ppermute x36, waiting for transfers between devices: 44.9 us -> 56.4 us  [plane_swap(): lax.ppermute(values, ('dp', 'ctx'), [(device, plane_partner(device, kind)...]
    ppermute x3, waiting for transfers between devices: 25.4 us -> 35.9 us  [per_device_exchanged(): lax.ppermute(section, 'fsdp', [(device, (device + step) % 4) for device i...]
  transfers between devices with their start and end apart: 71 -> 65, of which waited for: 25 -> 28; matrix products, arithmetic and copies ran while one was open for 23% -> 12% of each run, Pallas kernels for 40% -> 38%
where the time goes in v4:
time: 698 us; the launch traced here: 685 us
  Pallas kernels  283 us (41%)
  waiting for transfers between devices  208 us (30%)
  matrix products  59.1 us (8%)
  starting transfers between devices  50.7 us (7%)
  local copies, waits for them, and re-layouts  36 us (5%)
  other arithmetic  33.5 us (5%)
  between operations  15.4 us (2%)
    pallas_call x8, Pallas kernels, by_rows(): pl.pallas_call(kernel, grid=(rows // step,), in_specs=[tile] * len(tiled[...  164 us
    ppermute x12, waiting for transfers between devices, ctx_swap(): lax.ppermute(values, 'ctx', [(device, device ^ bits) for device in range(...  94.5 us
    dot_general x12, matrix products, product(): lax.dot_general(left, right, ((dims[:1], dims[1:]), ((), ())), preferred_...  59.1 us
    ppermute x36, waiting for transfers between devices, plane_swap(): lax.ppermute(values, ('dp', 'ctx'), [(device, plane_partner(device, kind)...  56.4 us
    pallas_call x2, Pallas kernels, attend_back(): pl.pallas_call(functools.partial(attend_back_kernel, count=count, width=w...  48.3 us
    ppermute x3, waiting for transfers between devices, per_device_exchanged(): lax.ppermute(section, 'fsdp', [(device, (device + step) % 4) for device i...  35.9 us
    pallas_call x2, Pallas kernels, attend(): pl.pallas_call(functools.partial(attend_kernel, count=count, width=width,...  33 us
    convert_element_type x8, other arithmetic, low_sum(): sum((term.astype(jnp.float32) for term in terms)).astype(jnp.bfloat16)  26.6 us
  transfers between devices with their start and end apart: 65, of which 28 were waited for; matrix products, arithmetic and copies ran while one was open for 12% of the time, Pallas kernels for 38%

profile of v4, /device:TPU:8, one launch (start us, length us, event | category | flops | bytes accessed | tf_op | source)
XLA Modules:
  0.0 685.4 jit_solution(13791042288732939831)
XLA Ops:
  7.3 3.6 fusion.8
  18.6 35.9 %collective-permute-done.refs_8_ = bf16[272,1088]{1,0:T(8,128)(2,1)S(1)} collective-permute-done((bf16[272,1088]{1,0:T(8,128)(2,1)}, bf16[272,1088]{1,0:T(8,128)(2,1)S(1)}, u32[]{:S(2)}, u32[]{:S(2)}) %collective-permute-start) | collective-permute-done | bytes 591904 | tf_op jit(solution)/shard_map/ppermute | solution.py:1086
  61.4 5.5 collective-permute-done.1
  70.1 12.6 %collective-permute-done.7.refs_2_ = bf16[1088,256]{1,0:T(8,128)(2,1)} collective-permute-done((bf16[1088,256]{1,0:T(8,128)(2,1)}, bf16[1088,256]{1,0:T(8,128)(2,1)}, u32[]{:S(2)}, u32[]{:S(2)}) %collective-permute-start.7) | collective-permute-done | bytes 557088 | tf_op jit(solution)/shard_map/ppermute | solution.py:609
  82.7 11.0 %collective-permute-done.8.refs_3_ = bf16[1088,256]{1,0:T(8,128)(2,1)} collective-permute-done((bf16[1088,256]{1,0:T(8,128)(2,1)}, bf16[1088,256]{1,0:T(8,128)(2,1)}, u32[]{:S(2)}, u32[]{:S(2)}) %collective-permute-start.8) | collective-permute-done | bytes 557088 | tf_op jit(solution)/shard_map/ppermute | solution.py:609
  105.0 6.2 collective-permute-done.10.refs_12_
  111.2 6.7 collective-permute-done.11.refs_13_
  120.5 21.7 %front.1 = (bf16[1024,1088]{1,0:T(8,128)(2,1)}, bf16[1024,1088]{1,0:T(8,128)(2,1)}, bf16[1024,1088]{1,0:T(8,128)(2,1)}, bf16[1024,1088]{1,0:T(8,128)(2,1)}, bf16...) custom-call(s32[16]{0:T(128)} %stack.120.places_ref, f32[4,1088]{1,0:T(4,128)} %pad_maximum_fusion.1.vectors_ref, ...), custom_call_target="tpu_custom_call" | custom-call | flops 7272923136 | bytes 20471808 | tf_op jit(solution)/shard_map/front/pallas_call | solution.py:739
  143.9 18.2 %attend.2 = (bf16[1024,1088]{1,0:T(8,128)(2,1)S(1)}, f32[1024,128]{1,0:T(8,128)S(1)}) custom-call(s32[1]{0:T(128)} %bitcast.24.place_ref, bf16[1024,1088]{1,0:T(8,128)(2,1)S(1)} %copy-done.23, bf16[1024,1088]{1,0:T(8,128)(2,1)} %get-tuple-element.179.k_ref, bf16[1024,1088]{1,0:T(8,128)(2,1)} %get-tuple-element.180.v_ref), custom_call_target="tpu_custom_call" | custom-call | flops 10737418240 | bytes 5242880 | tf_op jit(solution)/shard_map/attend/pallas_call | solution.py:507
  167.9 14.8 %attend.3 = (bf16[1024,1088]{1,0:T(8,128)(2,1)S(1)}, f32[1024,128]{1,0:T(8,128)S(1)}) custom-call(s32[1]{0:T(128)} %bitcast.24.place_ref, bf16[1024,1088]{1,0:T(8,128)(2,1)S(1)} %copy-done.24, bf16[1024,1088]{1,0:T(8,128)(2,1)} %get-tuple-element.179.k_ref, bf16[1024,1088]{1,0:T(8,128)(2,1)} %get-tuple-element.180.v_ref, ...), custom_call_target="tpu_custom_call", output_to_operand_aliasing={{0}: (4, {})} | custom-call | flops 8589934592 | bytes 4194304 | tf_op jit(solution)/shard_map/attend/pallas_call | solution.py:507
  185.0 9.8 %middle.1 = (f32[1024,1088]{1,0:T(8,128)}, bf16[1024,1088]{1,0:T(8,128)(2,1)}) custom-call(bf16[1024,1088]{1,0:T(8,128)(2,1)} %get-tuple-element.185.x_ref, bf16[1024,1088]{1,0:T(8,128)(2,1)} %copy-done.3, f32[3,1088]{1,0:T(4,128)} %pad_maximum_fusion.2.vectors_ref, bf16[16,272,1088]{2,1,0:T(8,128)(2,1)} %get-tuple-element.189.all_ref.refs_8_), custom_call_target="tpu_custom_call" | custom-call | flops 2424307712 | bytes 6823936 | tf_op jit(solution)/shard_map/middle/pallas_call | solution.py:1010
  201.1 10.0 %collective-permute-done.23.refs_2_ = bf16[1088,256]{1,0:T(8,128)(2,1)S(1)} collective-permute-done((bf16[1088,256]{1,0:T(8,128)(2,1)}, bf16[1088,256]{1,0:T(8,128)(2,1)S(1)}, u32[]{:S(2)}, u32[]{:S(2)}) %collective-permute-start.23) | collective-permute-done | bytes 557088 | tf_op jit(solution)/shard_map/ppermute | solution.py:609
  211.9 9.5 %collective-permute-done.24.refs_3_ = bf16[1088,256]{1,0:T(8,128)(2,1)S(1)} collective-permute-done((bf16[1088,256]{1,0:T(8,128)(2,1)S(1)}, bf16[1088,256]{1,0:T(8,128)(2,1)S(1)}, u32[]{:S(2)}, u32[]{:S(2)}) %collective-permute-start.24) | collective-permute-done | bytes 557088 | tf_op jit(solution)/shard_map/ppermute | solution.py:609
  226.0 18.2 %up.2 = (bf16[1024,1088]{1,0:T(8,128)(2,1)}, bf16[1024,1088]{1,0:T(8,128)(2,1)}, bf16[1024,1088]{1,0:T(8,128)(2,1)}, bf16[1024,1088]{1,0:T(8,128)(2,1)}) custom-call(bf16[1024,1088]{1,0:T(8,128)(2,1)} %get-tuple-element.236.h_ref, f32[2,1088]{1,0:T(2,128)} %pad_maximum_fusion.3.biases_ref, bf16[1088,1088]{1,0:T(8,128)(2,1)} %all-gather.3.cloned.1.call-done.refs_0_.refs_4_, ...), custom_call_target="tpu_custom_call" | custom-call | flops 4848615424 | bytes 13647872 | tf_op jit(solution)/shard_map/up/pallas_call | solution.py:1010
  244.3 25.9 %up.3 = (bf16[1024,1088]{1,0:T(8,128)(2,1)}, bf16[1024,1088]{1,0:T(8,128)(2,1)}, bf16[1024,1088]{1,0:T(8,128)(2,1)}, bf16[1024,1088]{1,0:T(8,128)(2,1)}) custom-call(bf16[1024,1088]{1,0:T(8,128)(2,1)} %get-tuple-element.236.h_ref, f32[2,1088]{1,0:T(2,128)} %pad_maximum_fusion.4.biases_ref, bf16[1088,1088]{1,0:T(8,128)(2,1)} %collective-permute-done.18.refs_0_.refs_5_, ...), custom_call_target="tpu_custom_call" | custom-call | flops 4848615424 | bytes 13647872 | tf_op jit(solution)/shard_map/up/pallas_call | solution.py:1010
  272.3 6.2 convolution_convert_fusion.11
  278.5 4.6 convolution_convert_fusion.10
  283.3 4.6 convolution_convert_fusion.9
  287.9 4.6 convolution_convert_fusion.8
  292.4 8.6 %collective-permute-done.21.refs_2_.refs_5_ = bf16[1088,1088]{1,0:T(8,128)(2,1)} collective-permute-done((bf16[1088,1088]{1,0:T(8,128)(2,1)}, bf16[1088,1088]{1,0:T(8,128)(2,1)}, u32[]{:S(2)}, u32[]{:S(2)}) %collective-permute-start.21) | collective-permute-done | bytes 2367520 | tf_op jit(solution)/shard_map/ppermute | solution.py:603
  301.7 14.0 %hidden.2 = (bf16[1024,1088]{1,0:T(8,128)(2,1)}, bf16[1024,1088]{1,0:T(8,128)(2,1)}, f32[3,8,1088]{2,1,0:T(8,128)}) custom-call(bf16[1024,1088]{1,0:T(8,128)(2,1)} %copy-done.2, bf16[1024,1088]{1,0:T(8,128)(2,1)} %get-tuple-element.214.refs_0_, bf16[1024,1088]{1,0:T(8,128)(2,1)} %get-tuple-element.215.refs_1_, ...), custom_call_target="tpu_custom_call" | custom-call | flops 4848615424 | bytes 13647872 | tf_op jit(solution)/shard_map/hidden/pallas_call | solution.py:1010
  315.7 4.5 add_convert_fusion.5
  320.2 14.0 %hidden.3 = (bf16[1024,1088]{1,0:T(8,128)(2,1)}, bf16[1024,1088]{1,0:T(8,128)(2,1)}, f32[3,8,1088]{2,1,0:T(8,128)}) custom-call(bf16[1024,1088]{1,0:T(8,128)(2,1)} %copy-done.2, bf16[1024,1088]{1,0:T(8,128)(2,1)} %get-tuple-element.219.refs_0_, bf16[1024,1088]{1,0:T(8,128)(2,1)} %get-tuple-element.220.refs_1_, ...), custom_call_target="tpu_custom_call" | custom-call | flops 4848615424 | bytes 13647872 | tf_op jit(solution)/shard_map/hidden/pallas_call | solution.py:1010
  336.0 32.1 %back.1 = (f32[1024,1088]{1,0:T(8,128)}, bf16[1024,1088]{1,0:T(8,128)(2,1)}, bf16[1024,1088]{1,0:T(8,128)(2,1)}, f32[3,8,1088]{2,1,0:T(8,128)}) custom-call(bf16[1024,1088]{1,0:T(8,128)(2,1)} %copy-done.2, f32[1024,1088]{1,0:T(8,128)} %get-tuple-element.268.middle_ref, f32[1,1088]{1,0:T(1,128)} %copy-done.42, bf16[1024,1088]{1,0:T(8,128)(2,1)} %get-tuple-element.225.refs_0_, ...), custom_call_target="tpu_custom_call" | custom-call | flops 12121538560 | bytes 34119680 | tf_op jit(solution)/shard_map/back/pallas_call | solution.py:1010
  368.1 4.9 add_convert_fusion.4
  373.0 7.1 %convolution_convert_fusion.7 = bf16[1088,1088]{1,0:T(8,128)(2,1)} fusion(bf16[1024,1088]{1,0:T(8,128)(2,1)} %get-tuple-element.236.h_ref, bf16[1024,1088]{1,0:T(8,128)(2,1)} %get-tuple-element.228.refs_3_), kind=kOutput, calls=%fused_computation.7 | convolution fusion | flops 2425491456 | bytes 6823936 | tf_op jit(solution)/shard_map/dot_general | solution.py:661
  380.1 4.6 convolution_convert_fusion.6
  385.3 4.6 convolution_convert_fusion.4
  391.5 6.4 convolution_convert_fusion.3
  397.9 6.3 add_convert_fusion.3
  406.7 26.7 %attend_back.2 = (bf16[1024,1088]{1,0:T(8,128)(2,1)S(1)}, bf16[1024,1088]{1,0:T(8,128)(2,1)S(1)}, bf16[1024,1088]{1,0:T(8,128)(2,1)}) custom-call(s32[1]{0:T(128)} %bitcast.24.place_ref, bf16[1024,1088]{1,0:T(8,128)(2,1)} %get-tuple-element.182.q_ref, bf16[1024,1088]{1,0:T(8,128)(2,1)} %get-tuple-element.179.k_ref, ...), custom_call_target="tpu_custom_call" | custom-call | flops 20132659200 | bytes 10485760 | tf_op jit(solution)/shard_map/attend_back/pallas_call | solution.py:541
  436.2 5.0 add_convert_fusion.2
  442.9 21.6 %attend_back.3 = (bf16[1024,1088]{1,0:T(8,128)(2,1)S(1)}, bf16[1024,1088]{1,0:T(8,128)(2,1)S(1)}, bf16[1024,1088]{1,0:T(8,128)(2,1)}) custom-call(s32[1]{0:T(128)} %bitcast.24.place_ref, bf16[1024,1088]{1,0:T(8,128)(2,1)} %get-tuple-element.182.q_ref, ...), custom_call_target="tpu_custom_call", output_to_operand_aliasing={{0}: (7, {}), {1}: (8, {}), {2}: (9, {})} | custom-call | flops 16106127360 | bytes 8388608 | tf_op jit(solution)/shard_map/attend_back/pallas_call | solution.py:541
  471.1 3.8 select_select_fusion
  475.5 4.2 collective-permute-done.33
  485.1 24.3 %last.1 = (bf16[1088,256]{1,0:T(8,128)(2,1)}, bf16[1088,256]{1,0:T(8,128)(2,1)}, bf16[1088,256]{1,0:T(8,128)(2,1)}, bf16[1088,256]{1,0:T(8,128)(2,1)}, f32[4,8,1088]{2,1,0:T(8,128)}) custom-call(bf16[1024,1088]{1,0:T(8,128)(2,1)} %copy-done.19, bf16[1024,1088]{1,0:T(8,128)(2,1)} %copy-done.22, bf16[1024,1088]{1,0:T(8,128)(2,1)} %get-tuple-element.261.v_ref, ...), custom_call_target="tpu_custom_call" | custom-call | flops 7272923136 | bytes 20471808 | tf_op jit(solution)/shard_map/last/pallas_call | solution.py:1010
  509.4 4.6 collective-permute-done.35
  514.1 6.5 add_convert_fusion
  520.6 13.2 %reduce-scatter.6.cloned.1.call-done = bf16[272,1088]{1,0:T(8,128)(2,1)} async-done(((bf16[1088,1088]{1,0:T(8,128)(2,1)}), bf16[272,1088]{1,0:T(8,128)(2,1)}) %reduce-scatter.6.cloned.1.call-update) | async-done | bytes 591888 | tf_op jit(solution)/shard_map/reduce_scatter | solution.py:626
  550.6 25.3 %down.1 = (bf16[1088,256]{1,0:T(8,128)(2,1)}, bf16[1088,256]{1,0:T(8,128)(2,1)}, bf16[1088,256]{1,0:T(8,128)(2,1)}, bf16[1088,256]{1,0:T(8,128)(2,1)}) custom-call(f32[1024,1088]{1,0:T(8,128)} %get-tuple-element.268.middle_ref, f32[1,1088]{1,0:T(1,128)} %reshape.451.vectors_ref, bf16[1024,1088]{1,0:T(8,128)(2,1)} %get-tuple-element.206.refs_0_, ...), custom_call_target="tpu_custom_call" | custom-call | flops 9697230848 | bytes 27295744 | tf_op jit(solution)/shard_map/down/pallas_call | solution.py:1010
  582.8 8.9 %collective-permute-done.37.refs_2_ = bf16[1088,256]{1,0:T(8,128)(2,1)S(1)} collective-permute-done((bf16[1088,256]{1,0:T(8,128)(2,1)}, bf16[1088,256]{1,0:T(8,128)(2,1)S(1)}, u32[]{:S(2)}, u32[]{:S(2)}) %collective-permute-start.37) | collective-permute-done | bytes 557088 | tf_op jit(solution)/shard_map/ppermute | solution.py:609
  592.0 10.8 %collective-permute-done.38.refs_3_ = bf16[1088,256]{1,0:T(8,128)(2,1)S(1)} collective-permute-done((bf16[1088,256]{1,0:T(8,128)(2,1)}, bf16[1088,256]{1,0:T(8,128)(2,1)S(1)}, u32[]{:S(2)}, u32[]{:S(2)}) %collective-permute-start.38) | collective-permute-done | bytes 557088 | tf_op jit(solution)/shard_map/ppermute | solution.py:609
  610.2 8.3 %collective-permute-done.40.refs_2_ = bf16[1088,256]{1,0:T(8,128)(2,1)S(1)} collective-permute-done((bf16[1088,256]{1,0:T(8,128)(2,1)}, bf16[1088,256]{1,0:T(8,128)(2,1)S(1)}, u32[]{:S(2)}, u32[]{:S(2)}) %collective-permute-start.40) | collective-permute-done | bytes 557088 | tf_op jit(solution)/shard_map/ppermute | solution.py:609
  618.5 22.0 %collective-permute-done.41.refs_3_ = bf16[1088,256]{1,0:T(8,128)(2,1)S(1)} collective-permute-done((bf16[1088,256]{1,0:T(8,128)(2,1)}, bf16[1088,256]{1,0:T(8,128)(2,1)S(1)}, u32[]{:S(2)}, u32[]{:S(2)}) %collective-permute-start.41) | collective-permute-done | bytes 557088 | tf_op jit(solution)/shard_map/ppermute | solution.py:609
  643.4 3.9 assemble.2
  648.8 9.0 %collective-permute-done.56 = bf16[272,1088]{1,0:T(8,128)(2,1)S(1)} collective-permute-done((bf16[272,1088]{1,0:T(8,128)(2,1)}, bf16[272,1088]{1,0:T(8,128)(2,1)S(1)}, u32[]{:S(2)}, u32[]{:S(2)}) %collective-permute-start.56) | collective-permute-done | bytes 591904 | tf_op jit(solution)/shard_map/ppermute | solution.py:603
  662.5 6.9 %collective-permute-done.57.refs_1_ = bf16[272,1088]{1,0:T(8,128)(2,1)S(1)} collective-permute-done((bf16[272,1088]{1,0:T(8,128)(2,1)S(1)}, bf16[272,1088]{1,0:T(8,128)(2,1)S(1)}, u32[]{:S(2)}, u32[]{:S(2)}) %collective-permute-start.57) | collective-permute-done | bytes 591904 | tf_op jit(solution)/shard_map/ppermute | solution.py:603
  669.4 5.7 collective-permute-done.59.refs_3_
  (329 shorter events, 122.7 us)
Async XLA Ops:
  7.2 155.8 %all-gather.3.cloned.1.call-start = ((), (), s32[]{:S(2)}) async-start(), calls=%async_computation.3 | async-start | bytes 3133440 | tf_op jit(solution)/shard_map/all_gather | solution.py:1128
  10.9 43.5 %collective-permute-start = (bf16[272,1088]{1,0:T(8,128)(2,1)}, bf16[272,1088]{1,0:T(8,128)(2,1)S(1)}, u32[]{:S(2)}, u32[]{:S(2)}) collective-permute-start(bf16[272,1088]{1,0:T(8,128)(2,1)} %get-tuple-element.153), channel_id=1, source_target_pairs={{0,4},{4,8},{8,12},{12,0},{1,5},{5,9},{9,13},{13,1},{2,6},{6,10},{... | collective-permute-start | bytes 1775624 | tf_op jit(solution)/shard_map/ppermute | solution.py:1086
  12.5 81.2 %collective-permute-start.4 = (bf16[272,1088]{1,0:T(8,128)(2,1)}, bf16[272,1088]{1,0:T(8,128)(2,1)}, u32[]{:S(2)}, u32[]{:S(2)}) collective-permute-start(bf16[272,1088]{1,0:T(8,128)(2,1)} %get-tuple-element.153), channel_id=1, source_target_pairs={{0,8},{4,12},{8,0},{12,4},{1,9},{5,13},{9,1},{13,5},{2,10},{6,14},... | collective-permute-start | bytes 1775624 | tf_op jit(solution)/shard_map/ppermute | solution.py:1086
  13.6 80.1 %collective-permute-start.5 = (bf16[272,1088]{1,0:T(8,128)(2,1)}, bf16[272,1088]{1,0:T(8,128)(2,1)}, u32[]{:S(2)}, u32[]{:S(2)}) collective-permute-start(bf16[272,1088]{1,0:T(8,128)(2,1)} %get-tuple-element.153), channel_id=1, source_target_pairs={{0,12},{4,0},{8,4},{12,8},{1,13},{5,1},{9,5},{13,9},{2,14},{6,2},{... | collective-permute-start | bytes 1775624 | tf_op jit(solution)/shard_map/ppermute | solution.py:1086
  54.6 12.3 %collective-permute-start.1 = (bf16[3264]{0:T(1024)(128)(2,1)S(1)}, bf16[3264]{0:T(1024)(128)(2,1)S(1)}, u32[]{:S(2)}, u32[]{:S(2)}) collective-permute-start(bf16[3264]{0:T(1024)(128)(2,1)S(1)} %concatenate.25), channel_id=1, source_target_pairs={{0,4},{4,8},{8,12},{12,0},{1,5},{5,9},{9,13},{13,1},{2,6},{6,10},{... | collective-permute-start | bytes 19592 | tf_op jit(solution)/shard_map/ppermute | solution.py:638
  57.1 11.7 %collective-permute-start.3 = (bf16[3264]{0:T(1024)(128)(2,1)S(1)}, bf16[3264]{0:T(1024)(128)(2,1)S(1)}, u32[]{:S(2)}, u32[]{:S(2)}) collective-permute-start(bf16[3264]{0:T(1024)(128)(2,1)S(1)} %concatenate.25), channel_id=1, source_target_pairs={{0,12},{4,0},{8,4},{12,8},{1,13},{5,1},{9,5},{13,9},{2,14},{6,2},{... | collective-permute-start | bytes 19592 | tf_op jit(solution)/shard_map/ppermute | solution.py:638
  67.0 15.7 %collective-permute-start.7 = (bf16[1088,256]{1,0:T(8,128)(2,1)}, bf16[1088,256]{1,0:T(8,128)(2,1)}, u32[]{:S(2)}, u32[]{:S(2)}) collective-permute-start(bf16[1088,256]{1,0:T(8,128)(2,1)} %get-tuple-element.318), channel_id=1, source_target_pairs={{0,2},{1,3},{2,0},{3,1},{4,6},{5,7},{6,4},{7,5},{8,10},{9,11},{10,... | collective-permute-start | bytes 1671176 | tf_op jit(solution)/shard_map/ppermute | solution.py:609
  68.7 25.0 %collective-permute-start.8 = (bf16[1088,256]{1,0:T(8,128)(2,1)}, bf16[1088,256]{1,0:T(8,128)(2,1)}, u32[]{:S(2)}, u32[]{:S(2)}) collective-permute-start(bf16[1088,256]{1,0:T(8,128)(2,1)} %get-tuple-element.317), channel_id=1, source_target_pairs={{0,3},{1,2},{2,1},{3,0},{4,7},{5,6},{6,5},{7,4},{8,11},{9,10},{10,... | collective-permute-start | bytes 1671176 | tf_op jit(solution)/shard_map/ppermute | solution.py:609
  93.8 176.4 %all-gather.5.cloned.1.call-start = ((), (), s32[]{:S(2)}) async-start(), calls=%async_computation.4 | async-start | bytes 3133440 | tf_op jit(solution)/shard_map/all_gather | solution.py:1150
  93.8 10.7 %collective-permute-start.9 = (bf16[272,1088]{1,0:T(8,128)(2,1)}, bf16[272,1088]{1,0:T(8,128)(2,1)}, u32[]{:S(2)}, u32[]{:S(2)}) collective-permute-start(bf16[272,1088]{1,0:T(8,128)(2,1)} %copy-done.55), channel_id=1, source_target_pairs={{0,16},{1,3},{2,18},{3,1},{16,0},{17,19},{18,2},{19,17},{4,20},{5,... | collective-permute-start | bytes 1775624 | tf_op jit(solution)/shard_map/ppermute | solution.py:603
  95.6 15.6 %collective-permute-start.10 = (bf16[272,1088]{1,0:T(8,128)(2,1)}, bf16[272,1088]{1,0:T(8,128)(2,1)}, u32[]{:S(2)}, u32[]{:S(2)}) collective-permute-start(bf16[272,1088]{1,0:T(8,128)(2,1)} %collective-permute-done.4.refs_9_), channel_id=1, source_target_pairs={{0,16},{1,3},{2,18},{3,1},{16,0},{17,19},{18,2},{19,17},{4,20},{5,... | collective-permute-start | bytes 1775624 | tf_op jit(solution)/shard_map/ppermute | solution.py:603
  97.1 20.8 %collective-permute-start.11 = (bf16[272,1088]{1,0:T(8,128)(2,1)}, bf16[272,1088]{1,0:T(8,128)(2,1)}, u32[]{:S(2)}, u32[]{:S(2)}) collective-permute-start(bf16[272,1088]{1,0:T(8,128)(2,1)} %collective-permute-done.5.refs_10_), channel_id=1, source_target_pairs={{0,16},{1,3},{2,18},{3,1},{16,0},{17,19},{18,2},{19,17},{4,20},{5,... | collective-permute-start | bytes 1775624 | tf_op jit(solution)/shard_map/ppermute | solution.py:603
  101.0 19.4 %collective-permute-start.13 = (bf16[272,1088]{1,0:T(8,128)(2,1)}, bf16[272,1088]{1,0:T(8,128)(2,1)}, u32[]{:S(2)}, u32[]{:S(2)}) collective-permute-start(bf16[272,1088]{1,0:T(8,128)(2,1)} %collective-permute-done.4.refs_9_), channel_id=1, source_target_pairs={{0,1},{1,0},{2,3},{3,2},{16,17},{17,16},{18,19},{19,18},{4,5},{5,4... | collective-permute-start | bytes 1775624 | tf_op jit(solution)/shard_map/ppermute | solution.py:603
  104.5 16.0 %collective-permute-start.14 = (bf16[272,1088]{1,0:T(8,128)(2,1)}, bf16[272,1088]{1,0:T(8,128)(2,1)}, u32[]{:S(2)}, u32[]{:S(2)}) collective-permute-start(bf16[272,1088]{1,0:T(8,128)(2,1)} %collective-permute-done.5.refs_10_), channel_id=1, source_target_pairs={{0,1},{1,0},{2,3},{3,2},{16,17},{17,16},{18,19},{19,18},{4,5},{5,4... | collective-permute-start | bytes 1775624 | tf_op jit(solution)/shard_map/ppermute | solution.py:603
  104.5 16.0 %collective-permute-start.15 = (bf16[272,1088]{1,0:T(8,128)(2,1)}, bf16[272,1088]{1,0:T(8,128)(2,1)}, u32[]{:S(2)}, u32[]{:S(2)}) collective-permute-start(bf16[272,1088]{1,0:T(8,128)(2,1)} %collective-permute-done.9.refs_11_), channel_id=1, source_target_pairs={{0,1},{1,0},{2,3},{3,2},{16,17},{17,16},{18,19},{19,18},{4,5},{5,4... | collective-permute-start | bytes 1775624 | tf_op jit(solution)/shard_map/ppermute | solution.py:603
  163.0 22.0 %collective-permute-start.19 = (bf16[1088,1088]{1,0:T(8,128)(2,1)}, bf16[1088,1088]{1,0:T(8,128)(2,1)}, u32[]{:S(2)}, u32[]{:S(2)}) collective-permute-start(bf16[1088,1088]{1,0:T(8,128)(2,1)} %all-gather.3.cloned.1.call-done.refs_0_.refs_4_), channel_id=1, source_target_pairs={{0,1},{1,0},{2,3},{3,2},{16,17},{17,16},{18,19},{19,18},{4,5},{5,4... | collective-permute-start | bytes 7102472 | tf_op jit(solution)/shard_map/ppermute | solution.py:603
  163.4 31.4 %collective-permute-start.18 = (bf16[1088,1088]{1,0:T(8,128)(2,1)}, bf16[1088,1088]{1,0:T(8,128)(2,1)}, u32[]{:S(2)}, u32[]{:S(2)}) collective-permute-start(bf16[1088,1088]{1,0:T(8,128)(2,1)} %all-gather.3.cloned.1.call-done.refs_0_.refs_4_), channel_id=1, source_target_pairs={{0,16},{1,3},{2,18},{3,1},{16,0},{17,19},{18,2},{19,17},{4,20},{5,... | collective-permute-start | bytes 7102472 | tf_op jit(solution)/shard_map/ppermute | solution.py:603
  165.9 275.3 %reduce-scatter.4.cloned.1.call-start = ((), (), s32[]{:S(2)}) async-start(), calls=%async_computation.5 | async-start | bytes 3133440 | tf_op jit(solution)/shard_map/reduce_scatter | solution.py:626
  194.8 49.4 %collective-permute-start.20 = (bf16[1088,1088]{1,0:T(8,128)(2,1)}, bf16[1088,1088]{1,0:T(8,128)(2,1)}, u32[]{:S(2)}, u32[]{:S(2)}) collective-permute-start(bf16[1088,1088]{1,0:T(8,128)(2,1)} %collective-permute-done.18.refs_0_.refs_5_), channel_id=1, source_target_pairs={{0,1},{1,0},{2,3},{3,2},{16,17},{17,16},{18,19},{19,18},{4,5},{5,4... | collective-permute-start | bytes 7102472 | tf_op jit(solution)/shard_map/ppermute | solution.py:603
  195.4 15.7 %collective-permute-start.23 = (bf16[1088,256]{1,0:T(8,128)(2,1)}, bf16[1088,256]{1,0:T(8,128)(2,1)S(1)}, u32[]{:S(2)}, u32[]{:S(2)}) collective-permute-start(bf16[1088,256]{1,0:T(8,128)(2,1)} %get-tuple-element.314), channel_id=1, source_target_pairs={{0,2},{1,3},{2,0},{3,1},{4,6},{5,7},{6,4},{7,5},{8,10},{9,11},{10,... | collective-permute-start | bytes 1671176 | tf_op jit(solution)/shard_map/ppermute | solution.py:609
  197.0 24.3 %collective-permute-start.24 = (bf16[1088,256]{1,0:T(8,128)(2,1)S(1)}, bf16[1088,256]{1,0:T(8,128)(2,1)S(1)}, u32[]{:S(2)}, u32[]{:S(2)}) collective-permute-start(bf16[1088,256]{1,0:T(8,128)(2,1)S(1)} %copy-done.36), channel_id=1, source_target_pairs={{0,3},{1,2},{2,1},{3,0},{4,7},{5,6},{6,5},{7,4},{8,11},{9,10},{10,... | collective-permute-start | bytes 1671176 | tf_op jit(solution)/shard_map/ppermute | solution.py:609
  270.2 30.8 %collective-permute-start.21 = (bf16[1088,1088]{1,0:T(8,128)(2,1)}, bf16[1088,1088]{1,0:T(8,128)(2,1)}, u32[]{:S(2)}, u32[]{:S(2)}) collective-permute-start(bf16[1088,1088]{1,0:T(8,128)(2,1)} %all-gather.5.cloned.1.call-done.refs_2_.refs_4_), channel_id=1, source_target_pairs={{0,16},{1,3},{2,18},{3,1},{16,0},{17,19},{18,2},{19,17},{4,20},{5,... | collective-permute-start | bytes 7102472 | tf_op jit(solution)/shard_map/ppermute | solution.py:603
  271.9 29.8 %collective-permute-start.27 = (bf16[1088,1088]{1,0:T(8,128)(2,1)}, bf16[1088,1088]{1,0:T(8,128)(2,1)}, u32[]{:S(2)}, u32[]{:S(2)}) collective-permute-start(bf16[1088,1088]{1,0:T(8,128)(2,1)} %all-gather.5.cloned.1.call-done.refs_2_.refs_4_), channel_id=1, source_target_pairs={{0,1},{1,0},{2,3},{3,2},{16,17},{17,16},{18,19},{19,18},{4,5},{5,4... | collective-permute-start | bytes 7102472 | tf_op jit(solution)/shard_map/ppermute | solution.py:603
  283.1 32.6 %collective-permute-start.25 = (bf16[1088,1088]{1,0:T(8,128)(2,1)}, bf16[1088,1088]{1,0:T(8,128)(2,1)}, u32[]{:S(2)}, u32[]{:S(2)}) collective-permute-start(bf16[1088,1088]{1,0:T(8,128)(2,1)} %convolution_convert_fusion.11), channel_id=1, source_target_pairs={{0,1},{1,0},{2,3},{3,2},{16,17},{17,16},{18,19},{19,18},{4,5},{5,4... | collective-permute-start | bytes 7102472 | tf_op jit(solution)/shard_map/ppermute | solution.py:603
  301.0 19.3 %collective-permute-start.28 = (bf16[1088,1088]{1,0:T(8,128)(2,1)}, bf16[1088,1088]{1,0:T(8,128)(2,1)}, u32[]{:S(2)}, u32[]{:S(2)}) collective-permute-start(bf16[1088,1088]{1,0:T(8,128)(2,1)} %collective-permute-done.21.refs_2_.refs_5_), channel_id=1, source_target_pairs={{0,1},{1,0},{2,3},{3,2},{16,17},{17,16},{18,19},{19,18},{4,5},{5,4... | collective-permute-start | bytes 7102472 | tf_op jit(solution)/shard_map/ppermute | solution.py:603
  301.2 33.0 %collective-permute-start.26 = (bf16[1088,1088]{1,0:T(8,128)(2,1)}, bf16[1088,1088]{1,0:T(8,128)(2,1)S(1)}, u32[]{:S(2)}, u32[]{:S(2)}) collective-permute-start(bf16[1088,1088]{1,0:T(8,128)(2,1)} %convolution_convert_fusion.10), channel_id=1, source_target_pairs={{0,1},{1,0},{2,3},{3,2},{16,17},{17,16},{18,19},{19,18},{4,5},{5,4... | collective-permute-start | bytes 7102472 | tf_op jit(solution)/shard_map/ppermute | solution.py:603
  334.3 33.9 %collective-permute-start.29 = (bf16[1088,1088]{1,0:T(8,128)(2,1)}, bf16[1088,1088]{1,0:T(8,128)(2,1)}, u32[]{:S(2)}, u32[]{:S(2)}) collective-permute-start(bf16[1088,1088]{1,0:T(8,128)(2,1)} %add_convert_fusion.5), channel_id=1, source_target_pairs={{0,16},{1,3},{2,18},{3,1},{16,0},{17,19},{18,2},{19,17},{4,20},{5,... | collective-permute-start | bytes 7102472 | tf_op jit(solution)/shard_map/ppermute | solution.py:603
  384.8 13.1 %collective-permute-start.30 = (bf16[1088,1088]{1,0:T(8,128)(2,1)}, bf16[1088,1088]{1,0:T(8,128)(2,1)}, u32[]{:S(2)}, u32[]{:S(2)}) collective-permute-start(bf16[1088,1088]{1,0:T(8,128)(2,1)} %convolution_convert_fusion.7), channel_id=1, source_target_pairs={{0,1},{1,0},{2,3},{3,2},{16,17},{17,16},{18,19},{19,18},{4,5},{5,4... | collective-permute-start | bytes 7102472 | tf_op jit(solution)/shard_map/ppermute | solution.py:603
  384.8 19.5 %collective-permute-start.31 = (bf16[1088,1088]{1,0:T(8,128)(2,1)}, bf16[1088,1088]{1,0:T(8,128)(2,1)}, u32[]{:S(2)}, u32[]{:S(2)}) collective-permute-start(bf16[1088,1088]{1,0:T(8,128)(2,1)} %convolution_convert_fusion.6), channel_id=1, source_target_pairs={{0,1},{1,0},{2,3},{3,2},{16,17},{17,16},{18,19},{19,18},{4,5},{5,4... | collective-permute-start | bytes 7102472 | tf_op jit(solution)/shard_map/ppermute | solution.py:603
  389.9 143.9 %reduce-scatter.6.cloned.1.call-start = ((), (), s32[]{:S(2)}) async-start(), calls=%async_computation.6 | async-start | bytes 3133440 | tf_op jit(solution)/shard_map/reduce_scatter | solution.py:626
  404.3 32.0 %collective-permute-start.32 = (bf16[1088,1088]{1,0:T(8,128)(2,1)}, bf16[1088,1088]{1,0:T(8,128)(2,1)}, u32[]{:S(2)}, u32[]{:S(2)}) collective-permute-start(bf16[1088,1088]{1,0:T(8,128)(2,1)} %add_convert_fusion.3), channel_id=1, source_target_pairs={{0,16},{1,3},{2,18},{3,1},{16,0},{17,19},{18,2},{19,17},{4,20},{5,... | collective-permute-start | bytes 7102472 | tf_op jit(solution)/shard_map/ppermute | solution.py:603
  483.3 30.7 %collective-permute-start.35 = (bf16[1088,1088]{1,0:T(8,128)(2,1)}, bf16[1088,1088]{1,0:T(8,128)(2,1)}, u32[]{:S(2)}, u32[]{:S(2)}) collective-permute-start(bf16[1088,1088]{1,0:T(8,128)(2,1)} %add_convert_fusion.1), channel_id=1, source_target_pairs={{0,16},{1,3},{2,18},{3,1},{16,0},{17,19},{18,2},{19,17},{4,20},{5,... | collective-permute-start | bytes 7102472 | tf_op jit(solution)/shard_map/ppermute | solution.py:603
  484.1 163.2 %reduce-scatter.8.cloned.1.call-start = ((), (), s32[]{:S(2)}) async-start(), calls=%async_computation.7 | async-start | bytes 3133440 | tf_op jit(solution)/shard_map/reduce_scatter | solution.py:626
  546.3 29.6 %collective-permute-start.53 = (bf16[272,1088]{1,0:T(8,128)(2,1)S(1)}, bf16[272,1088]{1,0:T(8,128)(2,1)S(1)}, u32[]{:S(2)}, u32[]{:S(2)}) collective-permute-start(bf16[272,1088]{1,0:T(8,128)(2,1)S(1)} %add_convert_fusion.7.refs_0_), channel_id=1, source_target_pairs={{0,16},{1,3},{2,18},{3,1},{16,0},{17,19},{18,2},{19,17},{4,20},{5,... | collective-permute-start | bytes 1775624 | tf_op jit(solution)/shard_map/ppermute | solution.py:603
  547.8 29.7 %collective-permute-start.54 = (bf16[272,1088]{1,0:T(8,128)(2,1)S(1)}, bf16[272,1088]{1,0:T(8,128)(2,1)S(1)}, u32[]{:S(2)}, u32[]{:S(2)}) collective-permute-start(bf16[272,1088]{1,0:T(8,128)(2,1)S(1)} %add_convert_fusion.7.refs_0_), channel_id=1, source_target_pairs={{0,1},{1,0},{2,3},{3,2},{16,17},{17,16},{18,19},{19,18},{4,5},{5,4... | collective-permute-start | bytes 1775624 | tf_op jit(solution)/shard_map/ppermute | solution.py:603
  547.8 31.2 %collective-permute-start.55 = (bf16[272,1088]{1,0:T(8,128)(2,1)S(1)}, bf16[272,1088]{1,0:T(8,128)(2,1)S(1)}, u32[]{:S(2)}, u32[]{:S(2)}) collective-permute-start(bf16[272,1088]{1,0:T(8,128)(2,1)S(1)} %add_convert_fusion.7.refs_0_), channel_id=1, source_target_pairs={{0,17},{1,2},{2,19},{3,0},{16,1},{17,18},{18,3},{19,16},{4,21},{5,... | collective-permute-start | bytes 1775624 | tf_op jit(solution)/shard_map/ppermute | solution.py:603
  548.5 27.5 %collective-permute-start.46 = (f32[3264]{0:T(1024)S(1)}, f32[3264]{0:T(1024)S(1)}, u32[]{:S(2)}, u32[]{:S(2)}) collective-permute-start(f32[3264]{0:T(1024)S(1)} %add.268), channel_id=1, source_target_pairs={{0,2},{1,3},{2,0},{3,1},{16,18},{17,19},{18,16},{19,17},{4,6},{5,7... | collective-permute-start | bytes 39176 | tf_op jit(solution)/shard_map/ppermute | solution.py:654
  550.0 29.1 %collective-permute-start.48 = (bf16[272,1088]{1,0:T(8,128)(2,1)S(1)}, bf16[272,1088]{1,0:T(8,128)(2,1)}, u32[]{:S(2)}, u32[]{:S(2)}) collective-permute-start(bf16[272,1088]{1,0:T(8,128)(2,1)S(1)} %copy-done.35), channel_id=1, source_target_pairs={{0,2},{1,17},{2,0},{3,19},{16,18},{17,1},{18,16},{19,3},{4,6},{5,2... | collective-permute-start | bytes 1775624 | tf_op jit(solution)/shard_map/ppermute | solution.py:603
  576.0 15.7 %collective-permute-start.37 = (bf16[1088,256]{1,0:T(8,128)(2,1)}, bf16[1088,256]{1,0:T(8,128)(2,1)S(1)}, u32[]{:S(2)}, u32[]{:S(2)}) collective-permute-start(bf16[1088,256]{1,0:T(8,128)(2,1)} %get-tuple-element.271), channel_id=1, source_target_pairs={{0,2},{1,3},{2,0},{3,1},{4,6},{5,7},{6,4},{7,5},{8,10},{9,11},{10,... | collective-permute-start | bytes 1671176 | tf_op jit(solution)/shard_map/ppermute | solution.py:609
  579.0 23.7 %collective-permute-start.38 = (bf16[1088,256]{1,0:T(8,128)(2,1)}, bf16[1088,256]{1,0:T(8,128)(2,1)S(1)}, u32[]{:S(2)}, u32[]{:S(2)}) collective-permute-start(bf16[1088,256]{1,0:T(8,128)(2,1)} %get-tuple-element.272), channel_id=1, source_target_pairs={{0,3},{1,2},{2,1},{3,0},{4,7},{5,6},{6,5},{7,4},{8,11},{9,10},{10,... | collective-permute-start | bytes 1671176 | tf_op jit(solution)/shard_map/ppermute | solution.py:609
  579.1 25.1 %collective-permute-start.39 = (bf16[1088,256]{1,0:T(8,128)(2,1)}, bf16[1088,256]{1,0:T(8,128)(2,1)S(1)}, u32[]{:S(2)}, u32[]{:S(2)}) collective-permute-start(bf16[1088,256]{1,0:T(8,128)(2,1)} %get-tuple-element.274), channel_id=1, source_target_pairs={{0,1},{1,0},{2,3},{3,2},{4,5},{5,4},{6,7},{7,6},{8,9},{9,8},{10,11... | collective-permute-start | bytes 1671176 | tf_op jit(solution)/shard_map/ppermute | solution.py:609
  581.3 62.1 %collective-permute-start.49 = (bf16[272,1088]{1,0:T(8,128)(2,1)S(1)}, bf16[272,1088]{1,0:T(8,128)(2,1)S(1)}, u32[]{:S(2)}, u32[]{:S(2)}) collective-permute-start(bf16[272,1088]{1,0:T(8,128)(2,1)S(1)} %add_convert_fusion.8.refs_0_), channel_id=1, source_target_pairs={{0,16},{1,3},{2,18},{3,1},{16,0},{17,19},{18,2},{19,17},{4,20},{5,... | collective-permute-start | bytes 1775624 | tf_op jit(solution)/shard_map/ppermute | solution.py:603
  582.8 60.6 %collective-permute-start.50 = (bf16[272,1088]{1,0:T(8,128)(2,1)S(1)}, bf16[272,1088]{1,0:T(8,128)(2,1)S(1)}, u32[]{:S(2)}, u32[]{:S(2)}) collective-permute-start(bf16[272,1088]{1,0:T(8,128)(2,1)S(1)} %add_convert_fusion.8.refs_0_), channel_id=1, source_target_pairs={{0,1},{1,0},{2,3},{3,2},{16,17},{17,16},{18,19},{19,18},{4,5},{5,4... | collective-permute-start | bytes 1775624 | tf_op jit(solution)/shard_map/ppermute | solution.py:603
  591.7 51.7 %collective-permute-start.51 = (bf16[272,1088]{1,0:T(8,128)(2,1)S(1)}, bf16[272,1088]{1,0:T(8,128)(2,1)S(1)}, u32[]{:S(2)}, u32[]{:S(2)}) collective-permute-start(bf16[272,1088]{1,0:T(8,128)(2,1)S(1)} %add_convert_fusion.8.refs_0_), channel_id=1, source_target_pairs={{0,17},{1,2},{2,19},{3,0},{16,1},{17,18},{18,3},{19,16},{4,21},{5,... | collective-permute-start | bytes 1775624 | tf_op jit(solution)/shard_map/ppermute | solution.py:603
  602.7 15.8 %collective-permute-start.40 = (bf16[1088,256]{1,0:T(8,128)(2,1)}, bf16[1088,256]{1,0:T(8,128)(2,1)S(1)}, u32[]{:S(2)}, u32[]{:S(2)}) collective-permute-start(bf16[1088,256]{1,0:T(8,128)(2,1)} %get-tuple-element.275), channel_id=1, source_target_pairs={{0,2},{1,3},{2,0},{3,1},{4,6},{5,7},{6,4},{7,5},{8,10},{9,11},{10,... | collective-permute-start | bytes 1671176 | tf_op jit(solution)/shard_map/ppermute | solution.py:609
  604.2 36.3 %collective-permute-start.41 = (bf16[1088,256]{1,0:T(8,128)(2,1)}, bf16[1088,256]{1,0:T(8,128)(2,1)S(1)}, u32[]{:S(2)}, u32[]{:S(2)}) collective-permute-start(bf16[1088,256]{1,0:T(8,128)(2,1)} %get-tuple-element.276), channel_id=1, source_target_pairs={{0,3},{1,2},{2,1},{3,0},{4,7},{5,6},{6,5},{7,4},{8,11},{9,10},{10,... | collective-permute-start | bytes 1671176 | tf_op jit(solution)/shard_map/ppermute | solution.py:609
  647.3 10.5 %collective-permute-start.56 = (bf16[272,1088]{1,0:T(8,128)(2,1)}, bf16[272,1088]{1,0:T(8,128)(2,1)S(1)}, u32[]{:S(2)}, u32[]{:S(2)}) collective-permute-start(bf16[272,1088]{1,0:T(8,128)(2,1)} %reduce-scatter.8.cloned.1.call-done), channel_id=1, source_target_pairs={{0,2},{1,17},{2,0},{3,19},{16,18},{17,1},{18,16},{19,3},{4,6},{5,2... | collective-permute-start | bytes 1775624 | tf_op jit(solution)/shard_map/ppermute | solution.py:603
  660.6 14.5 %collective-permute-start.59 = (bf16[272,1088]{1,0:T(8,128)(2,1)S(1)}, bf16[272,1088]{1,0:T(8,128)(2,1)S(1)}, u32[]{:S(2)}, u32[]{:S(2)}) collective-permute-start(bf16[272,1088]{1,0:T(8,128)(2,1)S(1)} %add_convert_fusion.6.refs_0_), channel_id=1, source_target_pairs={{0,17},{1,2},{2,19},{3,0},{16,1},{17,18},{18,3},{19,16},{4,21},{5,... | collective-permute-start | bytes 1775624 | tf_op jit(solution)/shard_map/ppermute | solution.py:603
  (81 other events, 1141.1 us)
Sparse Core Ops, SparseCore 0:
  93.9 52.4 all-gather.2
  166.0 51.4 all-gather.4
  390.0 49.6 reduce-scatter.3
  484.2 49.5 reduce-scatter.5
  536.5 50.2 reduce-scatter.7

commit v5 on v4

--- a/solution.py
+++ b/solution.py
@@ -617,11 +617,6 @@
     return plane_swap(pieces[2], "core"), plane_swap(pieces[3], "core")
 
 
-def reduce_last(shard):
-    whole = low_sum(shard, plane_swap(shard, "other"))
-    return [whole] + [plane_swap(whole, kind) for kind in ("near", "core", "far")]
-
-
 def scatter_rows(values):
     return lax.psum_scatter(values, "fsdp", scatter_dimension=0, tiled=True)
 
@@ -1063,6 +1058,22 @@
     places = jnp.stack([c ^ at for at in range(4)])
     class_places = jnp.stack(classes)
 
+    late = jnp.where(core == 0, x, y) == 1
+    cut = (width // 2) // 128 * 128
+    share = width - cut
+
+    def halve(*terms):
+        total = sum(term.astype(wide) for term in terms)
+        low_half, high_half = total[:, :share].astype(low), total[:, cut:].astype(low)
+        return jnp.where(late, high_half, low_half), jnp.where(late, low_half, high_half)
+
+    def reduce_last(shard):
+        other = plane_swap(shard, "other")
+        whole = jnp.concatenate(
+            [jnp.where(late, other, shard)[:, :cut], jnp.where(late, shard, other)], axis=1
+        )
+        return [whole] + [plane_swap(whole, kind) for kind in ("near", "core", "far")]
+
     def spread(values):
         values = jnp.swapaxes(values, 1, 2)
         return [lax.dynamic_index_in_dim(values, c, 0, keepdims=False)] + [
@@ -1086,7 +1097,10 @@
         lax.ppermute(section, "fsdp", [(device, (device + step) % 4) for device in range(4)])
         for step in range(1, 4)
     ]
-    slots_in = spread(inputs)
+    turned_in = jnp.swapaxes(inputs, 1, 2)
+    slots_in = [
+        lax.dynamic_index_in_dim(turned_in, c ^ bits, 0, keepdims=False) for bits in range(4)
+    ]
     pieces_in = (
         first_gain,
         first_shift,
@@ -1098,9 +1112,10 @@
         down_bias,
         up_bias,
     )
-    shards[0], cotangent, up_weight, down_weight, *pieces_in = pin(
-        (shards[0], cotangent, up_weight, down_weight, *pieces_in)
-    )
+    slots_in[3], cotangent, up_weight, down_weight, *pieces_in = pin(
+        (slots_in[3], cotangent, up_weight, down_weight, *pieces_in)
+    )
+    slots_in = [slots_in[0]] + [ctx_swap(slots_in[bits], bits) for bits in range(1, 4)]
     vectors = gather_vector(jnp.concatenate(pieces_in), z).astype(wide)
     slots_back = spread(cotangent)
     up_piece = jnp.concatenate(
@@ -1110,9 +1125,7 @@
         ],
         axis=1,
     )
-    up_piece, vectors, shards[1], shards[2], *slots_in = pin(
-        (up_piece, vectors, shards[1], shards[2], *slots_in)
-    )
+    up_piece, shards[1], shards[2] = pin((up_piece, shards[1], shards[2]))
     near_shards = [plane_swap(shard, "near") for shard in shards]
     around = (
         sections
@@ -1250,9 +1263,10 @@
         5,
         5,
     )
-    down_first = low_sum(down_terms[0], down_far, down_close)
-    down_first, normed_two_low = pin((down_first, pin((normed_two_low, middle_low))[0]))
-    down_shard = scatter_rows(down_first)
+    normed_two_low, middle_low = pin((normed_two_low, middle_low))
+    down_keep, down_send = halve(down_terms[0], down_far, down_close)
+    down_keep, down_send, normed_two_low = pin((down_keep, down_send, normed_two_low))
+    down_other = plane_swap(down_send, "other")
     up_terms = [turned_product(normed_two_low, hidden_low[slot]) for slot in (3, 2)]
     normed_two_low, *up_terms = pin((normed_two_low, *up_terms))
     up_terms += [turned_product(normed_two_low, hidden_low[slot]) for slot in (1, 0)]
@@ -1260,16 +1274,18 @@
     up_far, up_far_two = reduce_core(up_terms)
     out_term = turned_product(attended, middle_low)
     up_second = low_sum(up_terms[1], up_far_two)
-    grad_low, up_second, up_far, out_term, *up_terms = pin(
-        (grad_low, up_second, up_far, out_term, *up_terms)
-    )
+    down_half = low_sum(down_keep, down_other)
+    grad_low, up_second, up_far, out_term, down_half, *up_terms = pin(
+        (grad_low, up_second, up_far, out_term, down_half, *up_terms)
+    )
+    down_shard = scatter_rows(down_half)
     up_close = plane_swap(up_second, "near")
     in_grads = attend_back(
         place, late_queries, key_rows, value_rows, grad_low, attended, logs_one, seq_count, 0, 5, []
     )
-    up_first = low_sum(up_terms[0], up_far, up_close)
-    up_first, down_shard, *in_grads = pin((up_first, down_shard, *in_grads))
-    up_shard = scatter_rows(up_first)
+    up_keep, up_send = halve(up_terms[0], up_far, up_close)
+    up_keep, up_send, *in_grads = pin((up_keep, up_send, *in_grads))
+    up_other = plane_swap(up_send, "other")
     in_grads = attend_back(
         place,
         late_queries,
@@ -1283,15 +1299,36 @@
         4,
         in_grads,
     )
+    up_half = low_sum(up_keep, up_other)
+    up_half, down_shard, *in_grads = pin((up_half, down_shard, *in_grads))
+    up_shard = scatter_rows(up_half)
     down_parts = reduce_last(down_shard)
     in_terms = [turned_product(normed_low, grad) for grad in in_grads]
     section_grads = in_terms + [out_term]
     sections_mine = [chosen(kind, section_grads) for kind in classes]
     far, far_two = reduce_core(sections_mine)
     second = low_sum(sections_mine[1], far_two)
-    second, far, *in_grads = pin((second, far, *in_grads))
+    second, far, middle, *in_grads = pin((second, far, middle, *in_grads))
     close = plane_swap(second, "near")
     query_low, key_low, value_low = in_grads
+    result_slots = by_rows(
+        down_kernel,
+        "down",
+        rows,
+        width,
+        ([middle], active),
+        [dbias],
+        down_slots,
+        [None],
+        0,
+        [(4,) + area],
+        4,
+        4,
+    )
+    keep, send = halve(sections_mine[0], far, close)
+    keep, send, query_low, *result_slots = pin((keep, send, query_low, *result_slots))
+    outputs = collect(result_slots, low)
+    other = plane_swap(send, "other")
     *input_slots, last_sums = by_rows(
         last_kernel,
         "last",
@@ -1306,26 +1343,11 @@
         3,
         3,
     )
-    first = low_sum(sections_mine[0], far, close)
-    first, middle, up_shard, *input_slots = pin((first, middle, up_shard, *input_slots))
+    half = low_sum(keep, other)
+    half, up_shard, *input_slots = pin((half, up_shard, *input_slots))
+    shard = scatter_rows(half)
     input_gradient = collect(input_slots, wide)
-    result_slots = by_rows(
-        down_kernel,
-        "down",
-        rows,
-        width,
-        ([middle], active),
-        [dbias],
-        down_slots,
-        [None],
-        0,
-        [(4,) + area],
-        4,
-        4,
-    )
-    outputs = collect(result_slots, low)
     up_parts = reduce_last(up_shard)
-    shard = scatter_rows(first)
 
     back_sums = jnp.concatenate([hidden_sums, back_sums], axis=0)
     back_sums = jnp.sum(back_sums, axis=1)

time: 698 us -> 713 us (1.021)
  local copies, waits for them, and re-layouts: 36 us -> 49.7 us
  waiting for transfers between devices: 208 us -> 200 us
    reduce_scatter x3, waiting for transfers between devices: 13.2 us -> 0.01 us  [scatter_rows(): return lax.psum_scatter(values, 'fsdp', scatter_dimension=0, tiled=True)]
    another operation x0 -> x3, other arithmetic: none -> 11.9 us
    convert_element_type x8 -> x5, other arithmetic: 26.6 us -> 15.3 us  [low_sum(): sum((term.astype(jnp.float32) for term in terms)).astype(jnp.bfloat16)]
    ppermute x36 -> x39, waiting for transfers between devices: 56.4 us -> 46.9 us  [plane_swap(): lax.ppermute(values, ('dp', 'ctx'), [(device, plane_partner(device, kind)...]
    ppermute x3, waiting for transfers between devices: 35.9 us -> 45 us  [per_device_exchanged(): lax.ppermute(section, 'fsdp', [(device, (device + step) % 4) for device i...]
    ppermute x0 -> x3, local copies, waits for them, and re-layouts: none -> 8.55 us  [plane_swap(): lax.ppermute(values, ('dp', 'ctx'), [(device, plane_partner(device, kind)...]
    optimization_barrier x0 -> x3, local copies, waits for them, and re-layouts: none -> 7.79 us  [the longest x1 2.94 us: per_device_exchanged(): pin((down_keep, down_send, normed_two_low))]
    unnamed x133 -> x137, local copies, waits for them, and re-layouts: 19.8 us -> 17.2 us
  transfers between devices with their start and end apart: 65 -> 68, of which waited for: 28 -> 29; matrix products, arithmetic and copies ran while one was open for 12% -> 14% of each run, Pallas kernels for 38% -> 40%
where the time goes in v5:
time: 713 us; the launch traced here: 700 us
  Pallas kernels  282 us (40%)
  waiting for transfers between devices  200 us (28%)
  matrix products  63.4 us (9%)
  starting transfers between devices  50.3 us (7%)
  local copies, waits for them, and re-layouts  49.7 us (7%)
  other arithmetic  39.6 us (6%)
  between operations  15.3 us (2%)
    pallas_call x8, Pallas kernels, by_rows(): pl.pallas_call(kernel, grid=(rows // step,), in_specs=[tile] * len(tiled[...  163 us
    ppermute x12, waiting for transfers between devices, ctx_swap(): lax.ppermute(values, 'ctx', [(device, device ^ bits) for device in range(...  94.1 us
    dot_general x12, matrix products, product(): lax.dot_general(left, right, ((dims[:1], dims[1:]), ((), ())), preferred_...  63.4 us
    pallas_call x2, Pallas kernels, attend_back(): pl.pallas_call(functools.partial(attend_back_kernel, count=count, width=w...  47.7 us
    ppermute x39, waiting for transfers between devices, plane_swap(): lax.ppermute(values, ('dp', 'ctx'), [(device, plane_partner(device, kind)...  46.9 us
    ppermute x3, waiting for transfers between devices, per_device_exchanged(): lax.ppermute(section, 'fsdp', [(device, (device + step) % 4) for device i...  45 us
    pallas_call x2, Pallas kernels, attend(): pl.pallas_call(functools.partial(attend_kernel, count=count, width=width,...  33.2 us
    ppermute x39, starting transfers between devices, plane_swap(): lax.ppermute(values, ('dp', 'ctx'), [(device, plane_partner(device, kind)...  23.5 us
  transfers between devices with their start and end apart: 68, of which 29 were waited for; matrix products, arithmetic and copies ran while one was open for 14% of the time, Pallas kernels for 40%

profile of v5, /device:TPU:8, one launch (start us, length us, event | category | flops | bytes accessed | tf_op | source)
XLA Modules:
  0.0 700.4 jit_solution(15516803159623947003)
XLA Ops:
  7.3 3.6 fusion.8
  23.0 43.2 %collective-permute-done.7.refs_9_ = bf16[272,1088]{1,0:T(8,128)(2,1)} collective-permute-done((bf16[272,1088]{1,0:T(8,128)(2,1)}, bf16[272,1088]{1,0:T(8,128)(2,1)}, u32[]{:S(2)}, u32[]{:S(2)}) %collective-permute-start.7) | collective-permute-done | bytes 591904 | tf_op jit(solution)/shard_map/ppermute | solution.py:1097
  83.8 23.0 %collective-permute-done.5.refs_3_ = bf16[1088,256]{1,0:T(8,128)(2,1)} collective-permute-done((bf16[1088,256]{1,0:T(8,128)(2,1)}, bf16[1088,256]{1,0:T(8,128)(2,1)}, u32[]{:S(2)}, u32[]{:S(2)}) %collective-permute-start.5) | collective-permute-done | bytes 557088 | tf_op jit(solution)/shard_map/ppermute | solution.py:609
  113.5 21.7 %front.1 = (bf16[1024,1088]{1,0:T(8,128)(2,1)}, bf16[1024,1088]{1,0:T(8,128)(2,1)}, bf16[1024,1088]{1,0:T(8,128)(2,1)}, bf16[1024,1088]{1,0:T(8,128)(2,1)}, bf16...) custom-call(s32[16]{0:T(128)} %stack.120.places_ref, f32[4,1088]{1,0:T(4,128)} %pad_maximum_fusion.4.vectors_ref, ...), custom_call_target="tpu_custom_call" | custom-call | flops 7272923136 | bytes 20471808 | tf_op jit(solution)/shard_map/front/pallas_call | solution.py:734
  136.9 18.4 %attend.2 = (bf16[1024,1088]{1,0:T(8,128)(2,1)S(1)}, f32[1024,128]{1,0:T(8,128)S(1)}) custom-call(s32[1]{0:T(128)} %bitcast.26.place_ref, bf16[1024,1088]{1,0:T(8,128)(2,1)S(1)} %copy-done.21, bf16[1024,1088]{1,0:T(8,128)(2,1)} %get-tuple-element.185.k_ref, bf16[1024,1088]{1,0:T(8,128)(2,1)} %get-tuple-element.186.v_ref), custom_call_target="tpu_custom_call" | custom-call | flops 10737418240 | bytes 5242880 | tf_op jit(solution)/shard_map/attend/pallas_call | solution.py:507
  160.6 14.9 %attend.3 = (bf16[1024,1088]{1,0:T(8,128)(2,1)S(1)}, f32[1024,128]{1,0:T(8,128)S(1)}) custom-call(s32[1]{0:T(128)} %bitcast.26.place_ref, bf16[1024,1088]{1,0:T(8,128)(2,1)S(1)} %copy-done.22, bf16[1024,1088]{1,0:T(8,128)(2,1)} %get-tuple-element.185.k_ref, bf16[1024,1088]{1,0:T(8,128)(2,1)} %get-tuple-element.186.v_ref, ...), custom_call_target="tpu_custom_call", output_to_operand_aliasing={{0}: (4, {})} | custom-call | flops 8589934592 | bytes 4194304 | tf_op jit(solution)/shard_map/attend/pallas_call | solution.py:507
  177.7 9.9 %middle.1 = (f32[1024,1088]{1,0:T(8,128)}, bf16[1024,1088]{1,0:T(8,128)(2,1)}) custom-call(bf16[1024,1088]{1,0:T(8,128)(2,1)} %get-tuple-element.189.x_ref, bf16[1024,1088]{1,0:T(8,128)(2,1)} %copy-done.3, f32[3,1088]{1,0:T(4,128)} %pad_maximum_fusion.5.vectors_ref, bf16[16,272,1088]{2,1,0:T(8,128)(2,1)} %get-tuple-element.194.all_ref.refs_8_), custom_call_target="tpu_custom_call" | custom-call | flops 2424307712 | bytes 6823936 | tf_op jit(solution)/shard_map/middle/pallas_call | solution.py:1005
  193.2 10.4 %collective-permute-done.23.refs_2_ = bf16[1088,256]{1,0:T(8,128)(2,1)S(1)} collective-permute-done((bf16[1088,256]{1,0:T(8,128)(2,1)S(1)}, bf16[1088,256]{1,0:T(8,128)(2,1)S(1)}, u32[]{:S(2)}, u32[]{:S(2)}) %collective-permute-start.23) | collective-permute-done | bytes 557088 | tf_op jit(solution)/shard_map/ppermute | solution.py:609
  204.4 9.8 %collective-permute-done.24.refs_3_ = bf16[1088,256]{1,0:T(8,128)(2,1)S(1)} collective-permute-done((bf16[1088,256]{1,0:T(8,128)(2,1)S(1)}, bf16[1088,256]{1,0:T(8,128)(2,1)S(1)}, u32[]{:S(2)}, u32[]{:S(2)}) %collective-permute-start.24) | collective-permute-done | bytes 557088 | tf_op jit(solution)/shard_map/ppermute | solution.py:609
  217.8 18.2 %up.2 = (bf16[1024,1088]{1,0:T(8,128)(2,1)}, bf16[1024,1088]{1,0:T(8,128)(2,1)}, bf16[1024,1088]{1,0:T(8,128)(2,1)}, bf16[1024,1088]{1,0:T(8,128)(2,1)}) custom-call(bf16[1024,1088]{1,0:T(8,128)(2,1)} %get-tuple-element.241.h_ref, f32[2,1088]{1,0:T(2,128)} %pad_maximum_fusion.6.biases_ref, bf16[1088,1088]{1,0:T(8,128)(2,1)} %all-gather.5.cloned.1.call-done.refs_0_.refs_4_, ...), custom_call_target="tpu_custom_call" | custom-call | flops 4848615424 | bytes 13647872 | tf_op jit(solution)/shard_map/up/pallas_call | solution.py:1005
  236.1 25.8 %up.3 = (bf16[1024,1088]{1,0:T(8,128)(2,1)}, bf16[1024,1088]{1,0:T(8,128)(2,1)}, bf16[1024,1088]{1,0:T(8,128)(2,1)}, bf16[1024,1088]{1,0:T(8,128)(2,1)}) custom-call(bf16[1024,1088]{1,0:T(8,128)(2,1)} %get-tuple-element.241.h_ref, f32[2,1088]{1,0:T(2,128)} %pad_maximum_fusion.7.biases_ref, bf16[1088,1088]{1,0:T(8,128)(2,1)} %collective-permute-done.18.refs_0_.refs_5_, ...), custom_call_target="tpu_custom_call" | custom-call | flops 4848615424 | bytes 13647872 | tf_op jit(solution)/shard_map/up/pallas_call | solution.py:1005
  263.7 6.2 convolution_convert_fusion.11
  270.0 4.6 convolution_convert_fusion.10
  275.0 4.6 convolution_convert_fusion.9
  279.6 4.6 convolution_convert_fusion.8
  284.2 8.5 %collective-permute-done.21.refs_2_.refs_5_ = bf16[1088,1088]{1,0:T(8,128)(2,1)} collective-permute-done((bf16[1088,1088]{1,0:T(8,128)(2,1)}, bf16[1088,1088]{1,0:T(8,128)(2,1)}, u32[]{:S(2)}, u32[]{:S(2)}) %collective-permute-start.21) | collective-permute-done | bytes 2367520 | tf_op jit(solution)/shard_map/ppermute | solution.py:603
  294.9 14.1 %hidden.2 = (bf16[1024,1088]{1,0:T(8,128)(2,1)}, bf16[1024,1088]{1,0:T(8,128)(2,1)}, f32[3,8,1088]{2,1,0:T(8,128)}) custom-call(bf16[1024,1088]{1,0:T(8,128)(2,1)} %copy-done.2, bf16[1024,1088]{1,0:T(8,128)(2,1)} %get-tuple-element.219.refs_0_, bf16[1024,1088]{1,0:T(8,128)(2,1)} %get-tuple-element.220.refs_1_, ...), custom_call_target="tpu_custom_call" | custom-call | flops 4848615424 | bytes 13647872 | tf_op jit(solution)/shard_map/hidden/pallas_call | solution.py:1005
  309.1 3.8 add_convert_fusion.5
  312.8 14.0 %hidden.3 = (bf16[1024,1088]{1,0:T(8,128)(2,1)}, bf16[1024,1088]{1,0:T(8,128)(2,1)}, f32[3,8,1088]{2,1,0:T(8,128)}) custom-call(bf16[1024,1088]{1,0:T(8,128)(2,1)} %copy-done.2, bf16[1024,1088]{1,0:T(8,128)(2,1)} %get-tuple-element.224.refs_0_, bf16[1024,1088]{1,0:T(8,128)(2,1)} %get-tuple-element.225.refs_1_, ...), custom_call_target="tpu_custom_call" | custom-call | flops 4848615424 | bytes 13647872 | tf_op jit(solution)/shard_map/hidden/pallas_call | solution.py:1005
  328.7 32.1 %back.1 = (f32[1024,1088]{1,0:T(8,128)}, bf16[1024,1088]{1,0:T(8,128)(2,1)}, bf16[1024,1088]{1,0:T(8,128)(2,1)}, f32[3,8,1088]{2,1,0:T(8,128)}) custom-call(bf16[1024,1088]{1,0:T(8,128)(2,1)} %copy-done.2, f32[1024,1088]{1,0:T(8,128)} %get-tuple-element.272.middle_ref, f32[1,1088]{1,0:T(1,128)} %copy-done.41, bf16[1024,1088]{1,0:T(8,128)(2,1)} %get-tuple-element.230.refs_0_, ...), custom_call_target="tpu_custom_call" | custom-call | flops 12121538560 | bytes 34119680 | tf_op jit(solution)/shard_map/back/pallas_call | solution.py:1005
  360.9 3.4 add_convert_fusion.4
  367.6 4.6 convolution_convert_fusion.7
  372.2 4.6 convolution_convert_fusion.6
  380.6 6.4 convolution_convert_fusion.4
  386.9 4.6 convolution_convert_fusion.3
  391.6 6.9 collective-permute-done.32
  402.4 7.7 %add_convert_fusion.3 = bf16[1088,1088]{1,0:T(8,128)(2,1)} fusion(bf16[1088,1088]{1,0:T(8,128)(2,1)} %collective-permute-done.30, bf16[1024,1088]{1,0:T(8,128)(2,1)} %get-tuple-element.241.h_ref, bf16[1024,1088]{1,0:T(8,128)(2,1)} %get-tuple-element.231.refs_1_), kind=kOutput, calls=%fused_computation.15 | convolution fusion | flops 2430226432 | bytes 9191424 | tf_op jit(solution)/shard_map/dot_general | solution.py:656
  411.8 26.5 %attend_back.2 = (bf16[1024,1088]{1,0:T(8,128)(2,1)S(1)}, bf16[1024,1088]{1,0:T(8,128)(2,1)S(1)}, bf16[1024,1088]{1,0:T(8,128)(2,1)}) custom-call(s32[1]{0:T(128)} %bitcast.26.place_ref, bf16[1024,1088]{1,0:T(8,128)(2,1)} %get-tuple-element.190.q_ref, bf16[1024,1088]{1,0:T(8,128)(2,1)} %get-tuple-element.185.k_ref, ...), custom_call_target="tpu_custom_call" | custom-call | flops 20132659200 | bytes 10485760 | tf_op jit(solution)/shard_map/attend_back/pallas_call | solution.py:541
  440.9 3.4 add_convert_fusion.2
  450.8 21.3 %attend_back.3 = (bf16[1024,1088]{1,0:T(8,128)(2,1)S(1)}, bf16[1024,1088]{1,0:T(8,128)(2,1)S(1)}, bf16[1024,1088]{1,0:T(8,128)(2,1)}) custom-call(s32[1]{0:T(128)} %bitcast.26.place_ref, bf16[1024,1088]{1,0:T(8,128)(2,1)} %get-tuple-element.190.q_ref, ...), custom_call_target="tpu_custom_call", output_to_operand_aliasing={{0}: (7, {}), {1}: (8, {}), {2}: (9, {})} | custom-call | flops 16106127360 | bytes 8388608 | tf_op jit(solution)/shard_map/attend_back/pallas_call | solution.py:541
  473.5 3.6 copy.51
  480.3 5.6 convolution_convert_fusion.1
  489.2 6.8 select_select_fusion
  497.2 3.8 collective-permute-done.35
  501.0 5.5 add_convert_fusion.1
  508.0 25.6 %down.1 = (bf16[1088,256]{1,0:T(8,128)(2,1)}, bf16[1088,256]{1,0:T(8,128)(2,1)}, bf16[1088,256]{1,0:T(8,128)(2,1)}, bf16[1088,256]{1,0:T(8,128)(2,1)}) custom-call(f32[1024,1088]{1,0:T(8,128)} %get-tuple-element.272.middle_ref, f32[1,1088]{1,0:T(1,128)} %reshape.451.vectors_ref, bf16[1024,1088]{1,0:T(8,128)(2,1)} %get-tuple-element.211.refs_0_, ...), custom_call_target="tpu_custom_call" | custom-call | flops 9697230848 | bytes 27295744 | tf_op jit(solution)/shard_map/down/pallas_call | solution.py:1005
  533.6 3.6 collective-permute-done.37
  537.2 5.1 add_convert_fusion
  547.9 23.7 %last.1 = (bf16[1088,256]{1,0:T(8,128)(2,1)}, bf16[1088,256]{1,0:T(8,128)(2,1)}, bf16[1088,256]{1,0:T(8,128)(2,1)}, bf16[1088,256]{1,0:T(8,128)(2,1)}, f32[4,8,1088]{2,1,0:T(8,128)}) custom-call(bf16[1024,1088]{1,0:T(8,128)(2,1)} %copy-done.17, bf16[1024,1088]{1,0:T(8,128)(2,1)} %copy-done.20, bf16[1024,1088]{1,0:T(8,128)(2,1)} %get-tuple-element.282.v_ref, ...), custom_call_target="tpu_custom_call" | custom-call | flops 7272923136 | bytes 20471808 | tf_op jit(solution)/shard_map/last/pallas_call | solution.py:1005
  591.0 3.8 collective-permute-start.39
  601.7 8.9 %collective-permute-done.40.refs_2_ = bf16[1088,256]{1,0:T(8,128)(2,1)S(1)} collective-permute-done((bf16[1088,256]{1,0:T(8,128)(2,1)}, bf16[1088,256]{1,0:T(8,128)(2,1)S(1)}, u32[]{:S(2)}, u32[]{:S(2)}) %collective-permute-start.40) | collective-permute-done | bytes 557088 | tf_op jit(solution)/shard_map/ppermute | solution.py:609
  610.6 10.7 %collective-permute-done.41.refs_3_ = bf16[1088,256]{1,0:T(8,128)(2,1)S(1)} collective-permute-done((bf16[1088,256]{1,0:T(8,128)(2,1)}, bf16[1088,256]{1,0:T(8,128)(2,1)S(1)}, u32[]{:S(2)}, u32[]{:S(2)}) %collective-permute-start.41) | collective-permute-done | bytes 557088 | tf_op jit(solution)/shard_map/ppermute | solution.py:609
  629.1 8.0 %collective-permute-done.43.refs_2_ = bf16[1088,256]{1,0:T(8,128)(2,1)S(1)} collective-permute-done((bf16[1088,256]{1,0:T(8,128)(2,1)}, bf16[1088,256]{1,0:T(8,128)(2,1)S(1)}, u32[]{:S(2)}, u32[]{:S(2)}) %collective-permute-start.43) | collective-permute-done | bytes 557088 | tf_op jit(solution)/shard_map/ppermute | solution.py:609
  637.0 21.9 %collective-permute-done.44.refs_3_ = bf16[1088,256]{1,0:T(8,128)(2,1)S(1)} collective-permute-done((bf16[1088,256]{1,0:T(8,128)(2,1)S(1)}, bf16[1088,256]{1,0:T(8,128)(2,1)S(1)}, u32[]{:S(2)}, u32[]{:S(2)}) %collective-permute-start.44) | collective-permute-done | bytes 557088 | tf_op jit(solution)/shard_map/ppermute | solution.py:609
  661.8 4.1 assemble.2
  667.0 6.4 collective-permute-done.59
  678.2 6.9 collective-permute-done.60.refs_1_
  685.1 5.0 collective-permute-done.62.refs_3_
  (357 shorter events, 145.5 us)
Async XLA Ops:
  7.2 148.9 %all-gather.5.cloned.1.call-start = ((), (), s32[]{:S(2)}) async-start(), calls=%async_computation.4 | async-start | bytes 3133440 | tf_op jit(solution)/shard_map/all_gather | solution.py:1141
  10.8 66.3 %collective-permute-start.6 = (bf16[272,1088]{1,0:T(8,128)(2,1)}, bf16[272,1088]{1,0:T(8,128)(2,1)}, u32[]{:S(2)}, u32[]{:S(2)}) collective-permute-start(bf16[272,1088]{1,0:T(8,128)(2,1)} %get-tuple-element.174), channel_id=1, source_target_pairs={{0,4},{4,8},{8,12},{12,0},{1,5},{5,9},{9,13},{13,1},{2,6},{6,10},{... | collective-permute-start | bytes 1775624 | tf_op jit(solution)/shard_map/ppermute | solution.py:1097
  12.4 53.8 %collective-permute-start.7 = (bf16[272,1088]{1,0:T(8,128)(2,1)}, bf16[272,1088]{1,0:T(8,128)(2,1)}, u32[]{:S(2)}, u32[]{:S(2)}) collective-permute-start(bf16[272,1088]{1,0:T(8,128)(2,1)} %get-tuple-element.174), channel_id=1, source_target_pairs={{0,8},{4,12},{8,0},{12,4},{1,9},{5,13},{9,1},{13,5},{2,10},{6,14},... | collective-permute-start | bytes 1775624 | tf_op jit(solution)/shard_map/ppermute | solution.py:1097
  13.4 54.6 %collective-permute-start.8 = (bf16[272,1088]{1,0:T(8,128)(2,1)}, bf16[272,1088]{1,0:T(8,128)(2,1)}, u32[]{:S(2)}, u32[]{:S(2)}) collective-permute-start(bf16[272,1088]{1,0:T(8,128)(2,1)} %get-tuple-element.174), channel_id=1, source_target_pairs={{0,12},{4,0},{8,4},{12,8},{1,13},{5,1},{9,5},{13,9},{2,14},{6,2},{... | collective-permute-start | bytes 1775624 | tf_op jit(solution)/shard_map/ppermute | solution.py:1097
  18.5 59.2 %collective-permute-start.3 = (bf16[1088,256]{1,0:T(8,128)(2,1)}, bf16[1088,256]{1,0:T(8,128)(2,1)}, u32[]{:S(2)}, u32[]{:S(2)}) collective-permute-start(bf16[1088,256]{1,0:T(8,128)(2,1)} %get-tuple-element.344), channel_id=1, source_target_pairs={{0,1},{1,0},{2,3},{3,2},{4,5},{5,4},{6,7},{7,6},{8,9},{9,8},{10,11... | collective-permute-start | bytes 1671176 | tf_op jit(solution)/shard_map/ppermute | solution.py:609
  18.6 60.0 %collective-permute-start.4 = (bf16[1088,256]{1,0:T(8,128)(2,1)}, bf16[1088,256]{1,0:T(8,128)(2,1)}, u32[]{:S(2)}, u32[]{:S(2)}) collective-permute-start(bf16[1088,256]{1,0:T(8,128)(2,1)} %get-tuple-element.343), channel_id=1, source_target_pairs={{0,2},{1,3},{2,0},{3,1},{4,6},{5,7},{6,4},{7,5},{8,10},{9,11},{10,... | collective-permute-start | bytes 1671176 | tf_op jit(solution)/shard_map/ppermute | solution.py:609
  68.0 193.9 %all-gather.3.cloned.1.call-start = ((), (), s32[]{:S(2)}) async-start(), calls=%async_computation.3 | async-start | bytes 3133440 | tf_op jit(solution)/shard_map/all_gather | solution.py:1163
  73.0 34.3 %collective-permute-start.10 = (bf16[272,1088]{1,0:T(8,128)(2,1)}, bf16[272,1088]{1,0:T(8,128)(2,1)}, u32[]{:S(2)}, u32[]{:S(2)}) collective-permute-start(bf16[272,1088]{1,0:T(8,128)(2,1)} %collective-permute-done.7.refs_9_), channel_id=1, source_target_pairs={{0,16},{1,3},{2,18},{3,1},{16,0},{17,19},{18,2},{19,17},{4,20},{5,... | collective-permute-start | bytes 1775624 | tf_op jit(solution)/shard_map/ppermute | solution.py:603
  75.6 31.8 %collective-permute-start.11 = (bf16[272,1088]{1,0:T(8,128)(2,1)}, bf16[272,1088]{1,0:T(8,128)(2,1)}, u32[]{:S(2)}, u32[]{:S(2)}) collective-permute-start(bf16[272,1088]{1,0:T(8,128)(2,1)} %collective-permute-done.8.refs_10_), channel_id=1, source_target_pairs={{0,16},{1,3},{2,18},{3,1},{16,0},{17,19},{18,2},{19,17},{4,20},{5,... | collective-permute-start | bytes 1775624 | tf_op jit(solution)/shard_map/ppermute | solution.py:603
  77.1 29.7 %collective-permute-start.9 = (bf16[272,1088]{1,0:T(8,128)(2,1)}, bf16[272,1088]{1,0:T(8,128)(2,1)}, u32[]{:S(2)}, u32[]{:S(2)}) collective-permute-start(bf16[272,1088]{1,0:T(8,128)(2,1)} %collective-permute-done.6.refs_8_), channel_id=1, source_target_pairs={{0,16},{1,3},{2,18},{3,1},{16,0},{17,19},{18,2},{19,17},{4,20},{5,... | collective-permute-start | bytes 1775624 | tf_op jit(solution)/shard_map/ppermute | solution.py:603
  77.6 30.2 %collective-permute-start.12 = (bf16[272,1088]{1,0:T(8,128)(2,1)}, bf16[272,1088]{1,0:T(8,128)(2,1)}, u32[]{:S(2)}, u32[]{:S(2)}) collective-permute-start(bf16[272,1088]{1,0:T(8,128)(2,1)} %collective-permute-done.6.refs_8_), channel_id=1, source_target_pairs={{0,1},{1,0},{2,3},{3,2},{16,17},{17,16},{18,19},{19,18},{4,5},{5,4... | collective-permute-start | bytes 1775624 | tf_op jit(solution)/shard_map/ppermute | solution.py:603
  78.5 28.3 %collective-permute-start.5 = (bf16[1088,256]{1,0:T(8,128)(2,1)}, bf16[1088,256]{1,0:T(8,128)(2,1)}, u32[]{:S(2)}, u32[]{:S(2)}) collective-permute-start(bf16[1088,256]{1,0:T(8,128)(2,1)} %get-tuple-element.173), channel_id=1, source_target_pairs={{0,3},{1,2},{2,1},{3,0},{4,7},{5,6},{6,5},{7,4},{8,11},{9,10},{10,... | collective-permute-start | bytes 1671176 | tf_op jit(solution)/shard_map/ppermute | solution.py:609
  156.1 21.6 %collective-permute-start.19 = (bf16[1088,1088]{1,0:T(8,128)(2,1)}, bf16[1088,1088]{1,0:T(8,128)(2,1)}, u32[]{:S(2)}, u32[]{:S(2)}) collective-permute-start(bf16[1088,1088]{1,0:T(8,128)(2,1)} %all-gather.5.cloned.1.call-done.refs_0_.refs_4_), channel_id=1, source_target_pairs={{0,1},{1,0},{2,3},{3,2},{16,17},{17,16},{18,19},{19,18},{4,5},{5,4... | collective-permute-start | bytes 7102472 | tf_op jit(solution)/shard_map/ppermute | solution.py:603
  156.2 31.3 %collective-permute-start.18 = (bf16[1088,1088]{1,0:T(8,128)(2,1)}, bf16[1088,1088]{1,0:T(8,128)(2,1)}, u32[]{:S(2)}, u32[]{:S(2)}) collective-permute-start(bf16[1088,1088]{1,0:T(8,128)(2,1)} %all-gather.5.cloned.1.call-done.refs_0_.refs_4_), channel_id=1, source_target_pairs={{0,16},{1,3},{2,18},{3,1},{16,0},{17,19},{18,2},{19,17},{4,20},{5,... | collective-permute-start | bytes 7102472 | tf_op jit(solution)/shard_map/ppermute | solution.py:603
  158.6 321.7 %reduce-scatter.4.cloned.1.call-start = ((), (), s32[]{:S(2)}) async-start(), calls=%async_computation.5 | async-start | bytes 1740800 | tf_op jit(solution)/shard_map/reduce_scatter | solution.py:621
  187.6 48.5 %collective-permute-start.20 = (bf16[1088,1088]{1,0:T(8,128)(2,1)}, bf16[1088,1088]{1,0:T(8,128)(2,1)}, u32[]{:S(2)}, u32[]{:S(2)}) collective-permute-start(bf16[1088,1088]{1,0:T(8,128)(2,1)} %collective-permute-done.18.refs_0_.refs_5_), channel_id=1, source_target_pairs={{0,1},{1,0},{2,3},{3,2},{16,17},{17,16},{18,19},{19,18},{4,5},{5,4... | collective-permute-start | bytes 7102472 | tf_op jit(solution)/shard_map/ppermute | solution.py:603
  188.2 15.5 %collective-permute-start.23 = (bf16[1088,256]{1,0:T(8,128)(2,1)S(1)}, bf16[1088,256]{1,0:T(8,128)(2,1)S(1)}, u32[]{:S(2)}, u32[]{:S(2)}) collective-permute-start(bf16[1088,256]{1,0:T(8,128)(2,1)S(1)} %copy-done.34), channel_id=1, source_target_pairs={{0,2},{1,3},{2,0},{3,1},{4,6},{5,7},{6,4},{7,5},{8,10},{9,11},{10,... | collective-permute-start | bytes 1671176 | tf_op jit(solution)/shard_map/ppermute | solution.py:609
  189.9 24.3 %collective-permute-start.24 = (bf16[1088,256]{1,0:T(8,128)(2,1)S(1)}, bf16[1088,256]{1,0:T(8,128)(2,1)S(1)}, u32[]{:S(2)}, u32[]{:S(2)}) collective-permute-start(bf16[1088,256]{1,0:T(8,128)(2,1)S(1)} %copy-done.33), channel_id=1, source_target_pairs={{0,3},{1,2},{2,1},{3,0},{4,7},{5,6},{6,5},{7,4},{8,11},{9,10},{10,... | collective-permute-start | bytes 1671176 | tf_op jit(solution)/shard_map/ppermute | solution.py:609
  261.9 30.8 %collective-permute-start.21 = (bf16[1088,1088]{1,0:T(8,128)(2,1)}, bf16[1088,1088]{1,0:T(8,128)(2,1)}, u32[]{:S(2)}, u32[]{:S(2)}) collective-permute-start(bf16[1088,1088]{1,0:T(8,128)(2,1)} %all-gather.3.cloned.1.call-done.refs_2_.refs_4_), channel_id=1, source_target_pairs={{0,16},{1,3},{2,18},{3,1},{16,0},{17,19},{18,2},{19,17},{4,20},{5,... | collective-permute-start | bytes 7102472 | tf_op jit(solution)/shard_map/ppermute | solution.py:603
  263.7 29.7 %collective-permute-start.27 = (bf16[1088,1088]{1,0:T(8,128)(2,1)}, bf16[1088,1088]{1,0:T(8,128)(2,1)S(1)}, u32[]{:S(2)}, u32[]{:S(2)}) collective-permute-start(bf16[1088,1088]{1,0:T(8,128)(2,1)} %all-gather.3.cloned.1.call-done.refs_2_.refs_4_), channel_id=1, source_target_pairs={{0,1},{1,0},{2,3},{3,2},{16,17},{17,16},{18,19},{19,18},{4,5},{5,4... | collective-permute-start | bytes 7102472 | tf_op jit(solution)/shard_map/ppermute | solution.py:603
  274.5 34.5 %collective-permute-start.25 = (bf16[1088,1088]{1,0:T(8,128)(2,1)}, bf16[1088,1088]{1,0:T(8,128)(2,1)}, u32[]{:S(2)}, u32[]{:S(2)}) collective-permute-start(bf16[1088,1088]{1,0:T(8,128)(2,1)} %convolution_convert_fusion.11), channel_id=1, source_target_pairs={{0,1},{1,0},{2,3},{3,2},{16,17},{17,16},{18,19},{19,18},{4,5},{5,4... | collective-permute-start | bytes 7102472 | tf_op jit(solution)/shard_map/ppermute | solution.py:603
  292.7 20.1 %collective-permute-start.28 = (bf16[1088,1088]{1,0:T(8,128)(2,1)}, bf16[1088,1088]{1,0:T(8,128)(2,1)}, u32[]{:S(2)}, u32[]{:S(2)}) collective-permute-start(bf16[1088,1088]{1,0:T(8,128)(2,1)} %collective-permute-done.21.refs_2_.refs_5_), channel_id=1, source_target_pairs={{0,1},{1,0},{2,3},{3,2},{16,17},{17,16},{18,19},{19,18},{4,5},{5,4... | collective-permute-start | bytes 7102472 | tf_op jit(solution)/shard_map/ppermute | solution.py:603
  293.0 33.9 %collective-permute-start.26 = (bf16[1088,1088]{1,0:T(8,128)(2,1)}, bf16[1088,1088]{1,0:T(8,128)(2,1)}, u32[]{:S(2)}, u32[]{:S(2)}) collective-permute-start(bf16[1088,1088]{1,0:T(8,128)(2,1)} %convolution_convert_fusion.10), channel_id=1, source_target_pairs={{0,1},{1,0},{2,3},{3,2},{16,17},{17,16},{18,19},{19,18},{4,5},{5,4... | collective-permute-start | bytes 7102472 | tf_op jit(solution)/shard_map/ppermute | solution.py:603
  326.9 34.0 %collective-permute-start.29 = (bf16[1088,1088]{1,0:T(8,128)(2,1)}, bf16[1088,1088]{1,0:T(8,128)(2,1)}, u32[]{:S(2)}, u32[]{:S(2)}) collective-permute-start(bf16[1088,1088]{1,0:T(8,128)(2,1)} %add_convert_fusion.5), channel_id=1, source_target_pairs={{0,16},{1,3},{2,18},{3,1},{16,0},{17,19},{18,2},{19,17},{4,20},{5,... | collective-permute-start | bytes 7102472 | tf_op jit(solution)/shard_map/ppermute | solution.py:603
  376.8 25.6 %collective-permute-start.30 = (bf16[1088,1088]{1,0:T(8,128)(2,1)}, bf16[1088,1088]{1,0:T(8,128)(2,1)}, u32[]{:S(2)}, u32[]{:S(2)}) collective-permute-start(bf16[1088,1088]{1,0:T(8,128)(2,1)} %convolution_convert_fusion.7), channel_id=1, source_target_pairs={{0,1},{1,0},{2,3},{3,2},{16,17},{17,16},{18,19},{19,18},{4,5},{5,4... | collective-permute-start | bytes 7102472 | tf_op jit(solution)/shard_map/ppermute | solution.py:603
  376.8 33.3 %collective-permute-start.31 = (bf16[1088,1088]{1,0:T(8,128)(2,1)}, bf16[1088,1088]{1,0:T(8,128)(2,1)}, u32[]{:S(2)}, u32[]{:S(2)}) collective-permute-start(bf16[1088,1088]{1,0:T(8,128)(2,1)} %convolution_convert_fusion.6), channel_id=1, source_target_pairs={{0,1},{1,0},{2,3},{3,2},{16,17},{17,16},{18,19},{19,18},{4,5},{5,4... | collective-permute-start | bytes 7102472 | tf_op jit(solution)/shard_map/ppermute | solution.py:603
  380.3 18.2 %collective-permute-start.32 = (bf16[1088,576]{0,1:T(8,128)(2,1)}, bf16[1088,576]{0,1:T(8,128)(2,1)}, u32[]{:S(2)}, u32[]{:S(2)}) collective-permute-start(bf16[1088,576]{0,1:T(8,128)(2,1)} %copy.47), channel_id=1, source_target_pairs={{0,2},{1,17},{2,0},{3,19},{16,18},{17,1},{18,16},{19,3},{4,6},{5,2... | collective-permute-start | bytes 3760136 | tf_op jit(solution)/shard_map/ppermute | solution.py:603
  410.1 30.7 %collective-permute-start.33 = (bf16[1088,1088]{1,0:T(8,128)(2,1)}, bf16[1088,1088]{1,0:T(8,128)(2,1)}, u32[]{:S(2)}, u32[]{:S(2)}) collective-permute-start(bf16[1088,1088]{1,0:T(8,128)(2,1)} %add_convert_fusion.3), channel_id=1, source_target_pairs={{0,16},{1,3},{2,18},{3,1},{16,0},{17,19},{18,2},{19,17},{4,20},{5,... | collective-permute-start | bytes 7102472 | tf_op jit(solution)/shard_map/ppermute | solution.py:603
  411.7 163.8 %reduce-scatter.6.cloned.1.call-start = ((), (), s32[]{:S(2)}) async-start(), calls=%async_computation.6 | async-start | bytes 1740800 | tf_op jit(solution)/shard_map/reduce_scatter | solution.py:621
  448.9 24.6 %collective-permute-start.34 = (bf16[1088,576]{0,1:T(8,128)(2,1)}, bf16[1088,576]{0,1:T(8,128)(2,1)}, u32[]{:S(2)}, u32[]{:S(2)}) collective-permute-start(bf16[1088,576]{0,1:T(8,128)(2,1)} %copy.50), channel_id=1, source_target_pairs={{0,2},{1,17},{2,0},{3,19},{16,18},{17,1},{18,16},{19,3},{4,6},{5,2... | collective-permute-start | bytes 3760136 | tf_op jit(solution)/shard_map/ppermute | solution.py:603
  506.5 30.7 %collective-permute-start.37 = (bf16[1088,1088]{1,0:T(8,128)(2,1)}, bf16[1088,1088]{1,0:T(8,128)(2,1)}, u32[]{:S(2)}, u32[]{:S(2)}) collective-permute-start(bf16[1088,1088]{1,0:T(8,128)(2,1)} %add_convert_fusion.1), channel_id=1, source_target_pairs={{0,16},{1,3},{2,18},{3,1},{16,0},{17,19},{18,2},{19,17},{4,20},{5,... | collective-permute-start | bytes 7102472 | tf_op jit(solution)/shard_map/ppermute | solution.py:603
  508.0 158.0 %reduce-scatter.8.cloned.1.call-start = ((), (), s32[]{:S(2)}) async-start(), calls=%async_computation.7 | async-start | bytes 1740800 | tf_op jit(solution)/shard_map/reduce_scatter | solution.py:621
  544.8 26.9 %collective-permute-start.38 = (bf16[1088,576]{0,1:T(8,128)(2,1)}, bf16[1088,576]{0,1:T(8,128)(2,1)}, u32[]{:S(2)}, u32[]{:S(2)}) collective-permute-start(bf16[1088,576]{0,1:T(8,128)(2,1)} %copy.56), channel_id=1, source_target_pairs={{0,2},{1,17},{2,0},{3,19},{16,18},{17,1},{18,16},{19,3},{4,6},{5,2... | collective-permute-start | bytes 3760136 | tf_op jit(solution)/shard_map/ppermute | solution.py:603
  547.6 28.0 %collective-permute-start.55 = (bf16[272,576]{1,0:T(8,128)(2,1)S(1)}, bf16[272,576]{1,0:T(8,128)(2,1)S(1)}, u32[]{:S(2)}, u32[]{:S(2)}) collective-permute-start(bf16[272,576]{1,0:T(8,128)(2,1)S(1)} %copy-done.31), channel_id=1, source_target_pairs={{0,2},{1,17},{2,0},{3,19},{16,18},{17,1},{18,16},{19,3},{4,6},{5,2... | collective-permute-start | bytes 940040 | tf_op jit(solution)/shard_map/ppermute | solution.py:603
  575.8 19.0 %collective-permute-start.56 = (bf16[272,1088]{1,0:T(8,128)(2,1)S(1)}, bf16[272,1088]{1,0:T(8,128)(2,1)S(1)}, u32[]{:S(2)}, u32[]{:S(2)}) collective-permute-start(bf16[272,1088]{1,0:T(8,128)(2,1)S(1)} %pad_maximum_fusion.1.refs_0_), channel_id=1, source_target_pairs={{0,16},{1,3},{2,18},{3,1},{16,0},{17,19},{18,2},{19,17},{4,20},{5,... | collective-permute-start | bytes 1775624 | tf_op jit(solution)/shard_map/ppermute | solution.py:603
  577.3 18.7 %collective-permute-start.57 = (bf16[272,1088]{1,0:T(8,128)(2,1)S(1)}, bf16[272,1088]{1,0:T(8,128)(2,1)S(1)}, u32[]{:S(2)}, u32[]{:S(2)}) collective-permute-start(bf16[272,1088]{1,0:T(8,128)(2,1)S(1)} %pad_maximum_fusion.1.refs_0_), channel_id=1, source_target_pairs={{0,1},{1,0},{2,3},{3,2},{16,17},{17,16},{18,19},{19,18},{4,5},{5,4... | collective-permute-start | bytes 1775624 | tf_op jit(solution)/shard_map/ppermute | solution.py:603
  580.2 16.0 %collective-permute-start.51 = (bf16[272,576]{1,0:T(8,128)(2,1)S(1)}, bf16[272,576]{1,0:T(8,128)(2,1)S(1)}, u32[]{:S(2)}, u32[]{:S(2)}) collective-permute-start(bf16[272,576]{1,0:T(8,128)(2,1)S(1)} %copy-done.32), channel_id=1, source_target_pairs={{0,2},{1,17},{2,0},{3,19},{16,18},{17,1},{18,16},{19,3},{4,6},{5,2... | collective-permute-start | bytes 940040 | tf_op jit(solution)/shard_map/ppermute | solution.py:603
  584.4 12.7 %collective-permute-start.58 = (bf16[272,1088]{1,0:T(8,128)(2,1)S(1)}, bf16[272,1088]{1,0:T(8,128)(2,1)S(1)}, u32[]{:S(2)}, u32[]{:S(2)}) collective-permute-start(bf16[272,1088]{1,0:T(8,128)(2,1)S(1)} %pad_maximum_fusion.1.refs_0_), channel_id=1, source_target_pairs={{0,17},{1,2},{2,19},{3,0},{16,1},{17,18},{18,3},{19,16},{4,21},{5,... | collective-permute-start | bytes 1775624 | tf_op jit(solution)/shard_map/ppermute | solution.py:603
  591.0 10.7 %collective-permute-start.39 = (bf16[1088,256]{1,0:T(8,128)(2,1)}, bf16[1088,256]{1,0:T(8,128)(2,1)S(1)}, u32[]{:S(2)}, u32[]{:S(2)}) collective-permute-start(bf16[1088,256]{1,0:T(8,128)(2,1)} %get-tuple-element.290), channel_id=1, source_target_pairs={{0,1},{1,0},{2,3},{3,2},{4,5},{5,4},{6,7},{7,6},{8,9},{9,8},{10,11... | collective-permute-start | bytes 1671176 | tf_op jit(solution)/shard_map/ppermute | solution.py:609
  594.8 15.8 %collective-permute-start.40 = (bf16[1088,256]{1,0:T(8,128)(2,1)}, bf16[1088,256]{1,0:T(8,128)(2,1)S(1)}, u32[]{:S(2)}, u32[]{:S(2)}) collective-permute-start(bf16[1088,256]{1,0:T(8,128)(2,1)} %get-tuple-element.291), channel_id=1, source_target_pairs={{0,2},{1,3},{2,0},{3,1},{4,6},{5,7},{6,4},{7,5},{8,10},{9,11},{10,... | collective-permute-start | bytes 1671176 | tf_op jit(solution)/shard_map/ppermute | solution.py:609
  596.0 25.3 %collective-permute-start.41 = (bf16[1088,256]{1,0:T(8,128)(2,1)}, bf16[1088,256]{1,0:T(8,128)(2,1)S(1)}, u32[]{:S(2)}, u32[]{:S(2)}) collective-permute-start(bf16[1088,256]{1,0:T(8,128)(2,1)} %get-tuple-element.292), channel_id=1, source_target_pairs={{0,3},{1,2},{2,1},{3,0},{4,7},{5,6},{6,5},{7,4},{8,11},{9,10},{10,... | collective-permute-start | bytes 1671176 | tf_op jit(solution)/shard_map/ppermute | solution.py:609
  596.2 25.9 %collective-permute-start.42 = (bf16[1088,256]{1,0:T(8,128)(2,1)}, bf16[1088,256]{1,0:T(8,128)(2,1)S(1)}, u32[]{:S(2)}, u32[]{:S(2)}) collective-permute-start(bf16[1088,256]{1,0:T(8,128)(2,1)} %get-tuple-element.294), channel_id=1, source_target_pairs={{0,1},{1,0},{2,3},{3,2},{4,5},{5,4},{6,7},{7,6},{8,9},{9,8},{10,11... | collective-permute-start | bytes 1671176 | tf_op jit(solution)/shard_map/ppermute | solution.py:609
  600.9 60.9 %collective-permute-start.52 = (bf16[272,1088]{1,0:T(8,128)(2,1)S(1)}, bf16[272,1088]{1,0:T(8,128)(2,1)S(1)}, u32[]{:S(2)}, u32[]{:S(2)}) collective-permute-start(bf16[272,1088]{1,0:T(8,128)(2,1)S(1)} %pad_maximum_fusion.refs_0_), channel_id=1, source_target_pairs={{0,16},{1,3},{2,18},{3,1},{16,0},{17,19},{18,2},{19,17},{4,20},{5,... | collective-permute-start | bytes 1775624 | tf_op jit(solution)/shard_map/ppermute | solution.py:603
  601.7 60.1 %collective-permute-start.53 = (bf16[272,1088]{1,0:T(8,128)(2,1)S(1)}, bf16[272,1088]{1,0:T(8,128)(2,1)S(1)}, u32[]{:S(2)}, u32[]{:S(2)}) collective-permute-start(bf16[272,1088]{1,0:T(8,128)(2,1)S(1)} %pad_maximum_fusion.refs_0_), channel_id=1, source_target_pairs={{0,1},{1,0},{2,3},{3,2},{16,17},{17,16},{18,19},{19,18},{4,5},{5,4... | collective-permute-start | bytes 1775624 | tf_op jit(solution)/shard_map/ppermute | solution.py:603
  610.6 51.2 %collective-permute-start.54 = (bf16[272,1088]{1,0:T(8,128)(2,1)S(1)}, bf16[272,1088]{1,0:T(8,128)(2,1)S(1)}, u32[]{:S(2)}, u32[]{:S(2)}) collective-permute-start(bf16[272,1088]{1,0:T(8,128)(2,1)S(1)} %pad_maximum_fusion.refs_0_), channel_id=1, source_target_pairs={{0,17},{1,2},{2,19},{3,0},{16,1},{17,18},{18,3},{19,16},{4,21},{5,... | collective-permute-start | bytes 1775624 | tf_op jit(solution)/shard_map/ppermute | solution.py:603
  621.2 15.8 %collective-permute-start.43 = (bf16[1088,256]{1,0:T(8,128)(2,1)}, bf16[1088,256]{1,0:T(8,128)(2,1)S(1)}, u32[]{:S(2)}, u32[]{:S(2)}) collective-permute-start(bf16[1088,256]{1,0:T(8,128)(2,1)} %get-tuple-element.295), channel_id=1, source_target_pairs={{0,2},{1,3},{2,0},{3,1},{4,6},{5,7},{6,4},{7,5},{8,10},{9,11},{10,... | collective-permute-start | bytes 1671176 | tf_op jit(solution)/shard_map/ppermute | solution.py:609
  622.2 36.7 %collective-permute-start.44 = (bf16[1088,256]{1,0:T(8,128)(2,1)S(1)}, bf16[1088,256]{1,0:T(8,128)(2,1)S(1)}, u32[]{:S(2)}, u32[]{:S(2)}) collective-permute-start(bf16[1088,256]{1,0:T(8,128)(2,1)S(1)} %copy-done.57), channel_id=1, source_target_pairs={{0,3},{1,2},{2,1},{3,0},{4,7},{5,6},{6,5},{7,4},{8,11},{9,10},{10,... | collective-permute-start | bytes 1671176 | tf_op jit(solution)/shard_map/ppermute | solution.py:609
  675.6 14.5 %collective-permute-start.62 = (bf16[272,1088]{1,0:T(8,128)(2,1)S(1)}, bf16[272,1088]{1,0:T(8,128)(2,1)S(1)}, u32[]{:S(2)}, u32[]{:S(2)}) collective-permute-start(bf16[272,1088]{1,0:T(8,128)(2,1)S(1)} %pad_maximum_fusion.2.refs_0_), channel_id=1, source_target_pairs={{0,17},{1,2},{2,19},{3,0},{16,1},{17,18},{18,3},{19,16},{4,21},{5,... | collective-permute-start | bytes 1775624 | tf_op jit(solution)/shard_map/ppermute | solution.py:603
  (86 other events, 1134.2 us)
Sparse Core Ops, SparseCore 0:
  68.1 51.5 all-gather.4
  158.8 49.8 all-gather.2
  411.8 29.2 reduce-scatter.3
  508.1 29.5 reduce-scatter.5
  575.7 31.1 reduce-scatter.7

commit v6 on v5

--- a/solution.py
+++ b/solution.py
@@ -617,6 +617,10 @@
     return plane_swap(pieces[2], "core"), plane_swap(pieces[3], "core")
 
 
+def share_out(whole):
+    return [whole] + [plane_swap(whole, kind) for kind in ("near", "core", "far")]
+
+
 def scatter_rows(values):
     return lax.psum_scatter(values, "fsdp", scatter_dimension=0, tiled=True)
 
@@ -1058,22 +1062,6 @@
     places = jnp.stack([c ^ at for at in range(4)])
     class_places = jnp.stack(classes)
 
-    late = jnp.where(core == 0, x, y) == 1
-    cut = (width // 2) // 128 * 128
-    share = width - cut
-
-    def halve(*terms):
-        total = sum(term.astype(wide) for term in terms)
-        low_half, high_half = total[:, :share].astype(low), total[:, cut:].astype(low)
-        return jnp.where(late, high_half, low_half), jnp.where(late, low_half, high_half)
-
-    def reduce_last(shard):
-        other = plane_swap(shard, "other")
-        whole = jnp.concatenate(
-            [jnp.where(late, other, shard)[:, :cut], jnp.where(late, shard, other)], axis=1
-        )
-        return [whole] + [plane_swap(whole, kind) for kind in ("near", "core", "far")]
-
     def spread(values):
         values = jnp.swapaxes(values, 1, 2)
         return [lax.dynamic_index_in_dim(values, c, 0, keepdims=False)] + [
@@ -1081,8 +1069,10 @@
             for bits in range(1, 4)
         ]
 
-    def collect(pieces, dtype):
-        moved = [pieces[0]] + [ctx_swap(pieces[bits], bits) for bits in range(1, 4)]
+    def exchange(pieces):
+        return [pieces[0]] + [ctx_swap(pieces[bits], bits) for bits in range(1, 4)]
+
+    def collect(moved, dtype):
         return jnp.swapaxes(settle(places, moved, dtype), 1, 2)
 
     sections = [
@@ -1125,7 +1115,8 @@
         ],
         axis=1,
     )
-    up_piece, shards[1], shards[2] = pin((up_piece, shards[1], shards[2]))
+    up_piece, vectors, *moved = pin((up_piece, vectors, *shards, *slots_in, *slots_back))
+    shards, slots_in, slots_back = moved[:3], moved[3:7], moved[7:]
     near_shards = [plane_swap(shard, "near") for shard in shards]
     around = (
         sections
@@ -1158,17 +1149,14 @@
         jnp.concatenate([gain_first, shift_first, qbias, vbias], axis=0),
         around,
     )
-    slots_back[0], down_piece, queries = pin((slots_back[0], down_piece, queries))
+    slots_back[0], up_own, queries = pin((slots_back[0], up_own, queries))
     upstream_low = turn(slots_back)
+    up_near, up_core = plane_swap(up_own, "near"), plane_swap(up_own, "core")
+    attended, logs = attend(place, queries, key_rows, value_rows, seq_count, 0, 9, [])
+    down_piece, up_core, up_near, attended = pin((down_piece, up_core, up_near, attended))
     down_own = lax.all_gather(down_piece, "fsdp", axis=0, tiled=True)
-    attended, logs_one = attend(place, queries, key_rows, value_rows, seq_count, 0, 5, [])
-    up_own, late_queries, attended = pin((up_own, queries, attended))
-    up_near, up_core = plane_swap(up_own, "near"), plane_swap(up_own, "core")
-    attended, logs_two = attend(
-        place, late_queries, key_rows, value_rows, seq_count, 5, 4, [attended]
-    )
-    up_core, attended = pin((up_core, attended))
-    logs_one, logs_two = (logs.T.reshape(64, 2, rows) for logs in (logs_one, logs_two))
+    logs = logs.T.reshape(64, 2, rows)
+    logs_one, logs_two = logs[:5], logs[5:9]
     middle, normed_two_low = by_rows(
         middle_kernel,
         "middle",
@@ -1183,7 +1171,6 @@
         1,
         1,
     )
-    up_near, normed_two_low = pin((up_near, normed_two_low))
     up_slots = [up_own, up_near, up_core, plane_swap(up_near, "core")]
     active, slopes = [None] * 4, [None] * 4
 
@@ -1263,10 +1250,9 @@
         5,
         5,
     )
-    normed_two_low, middle_low = pin((normed_two_low, middle_low))
-    down_keep, down_send = halve(down_terms[0], down_far, down_close)
-    down_keep, down_send, normed_two_low = pin((down_keep, down_send, normed_two_low))
-    down_other = plane_swap(down_send, "other")
+    down_first = low_sum(down_terms[0], down_far, down_close)
+    down_first, normed_two_low = pin((down_first, pin((normed_two_low, middle_low))[0]))
+    down_shard = scatter_rows(down_first)
     up_terms = [turned_product(normed_two_low, hidden_low[slot]) for slot in (3, 2)]
     normed_two_low, *up_terms = pin((normed_two_low, *up_terms))
     up_terms += [turned_product(normed_two_low, hidden_low[slot]) for slot in (1, 0)]
@@ -1274,21 +1260,20 @@
     up_far, up_far_two = reduce_core(up_terms)
     out_term = turned_product(attended, middle_low)
     up_second = low_sum(up_terms[1], up_far_two)
-    down_half = low_sum(down_keep, down_other)
-    grad_low, up_second, up_far, out_term, down_half, *up_terms = pin(
-        (grad_low, up_second, up_far, out_term, down_half, *up_terms)
-    )
-    down_shard = scatter_rows(down_half)
+    grad_low, up_second, up_far, out_term, *up_terms = pin(
+        (grad_low, up_second, up_far, out_term, *up_terms)
+    )
     up_close = plane_swap(up_second, "near")
     in_grads = attend_back(
-        place, late_queries, key_rows, value_rows, grad_low, attended, logs_one, seq_count, 0, 5, []
-    )
-    up_keep, up_send = halve(up_terms[0], up_far, up_close)
-    up_keep, up_send, *in_grads = pin((up_keep, up_send, *in_grads))
-    up_other = plane_swap(up_send, "other")
+        place, queries, key_rows, value_rows, grad_low, attended, logs_one, seq_count, 0, 5, []
+    )
+    up_first = low_sum(up_terms[0], up_far, up_close)
+    up_first, down_shard, *in_grads = pin((up_first, down_shard, *in_grads))
+    up_shard = scatter_rows(up_first)
+    down_whole = low_sum(down_shard, plane_swap(down_shard, "other"))
     in_grads = attend_back(
         place,
-        late_queries,
+        queries,
         key_rows,
         value_rows,
         grad_low,
@@ -1299,18 +1284,17 @@
         4,
         in_grads,
     )
-    up_half = low_sum(up_keep, up_other)
-    up_half, down_shard, *in_grads = pin((up_half, down_shard, *in_grads))
-    up_shard = scatter_rows(up_half)
-    down_parts = reduce_last(down_shard)
+    down_whole, *in_grads = pin((down_whole, *in_grads))
+    down_parts = share_out(down_whole)
     in_terms = [turned_product(normed_low, grad) for grad in in_grads]
     section_grads = in_terms + [out_term]
     sections_mine = [chosen(kind, section_grads) for kind in classes]
     far, far_two = reduce_core(sections_mine)
     second = low_sum(sections_mine[1], far_two)
-    second, far, middle, *in_grads = pin((second, far, middle, *in_grads))
+    second, far, middle, *moved = pin((second, far, middle, *in_grads, *down_parts))
+    query_low, key_low, value_low = moved[:3]
+    down_parts = moved[3:]
     close = plane_swap(second, "near")
-    query_low, key_low, value_low = in_grads
     result_slots = by_rows(
         down_kernel,
         "down",
@@ -1325,10 +1309,13 @@
         4,
         4,
     )
-    keep, send = halve(sections_mine[0], far, close)
-    keep, send, query_low, *result_slots = pin((keep, send, query_low, *result_slots))
-    outputs = collect(result_slots, low)
-    other = plane_swap(send, "other")
+    first = low_sum(sections_mine[0], far, close)
+    first, up_shard, query_low, *result_slots = pin(
+        (first, up_shard, query_low, *result_slots)
+    )
+    shard = scatter_rows(first)
+    outputs = exchange(result_slots)
+    up_whole = low_sum(up_shard, plane_swap(up_shard, "other"))
     *input_slots, last_sums = by_rows(
         last_kernel,
         "last",
@@ -1343,11 +1330,9 @@
         3,
         3,
     )
-    half = low_sum(keep, other)
-    half, up_shard, *input_slots = pin((half, up_shard, *input_slots))
-    shard = scatter_rows(half)
-    input_gradient = collect(input_slots, wide)
-    up_parts = reduce_last(up_shard)
+    up_whole, last_sums, *moved = pin((up_whole, last_sums, *input_slots, *outputs))
+    input_slots, outputs = exchange(moved[:4]), moved[4:]
+    up_parts = share_out(up_whole)
 
     back_sums = jnp.concatenate([hidden_sums, back_sums], axis=0)
     back_sums = jnp.sum(back_sums, axis=1)
@@ -1365,6 +1350,10 @@
         ),
         z,
     )
+    moved = pin((*input_slots, *up_parts))
+    outputs = collect(outputs, low)
+    input_gradient = collect(moved[:4], wide)
+    up_parts = moved[4:]
     (up_sum,) = assemble(
         class_places,
         up_parts,
@@ -1380,7 +1369,7 @@
     )
     in_sum, out_sum = assemble(
         class_places,
-        reduce_last(shard),
+        share_out(low_sum(shard, plane_swap(shard, "other"))),
         [[(0, 0, kind * width, width)] for kind in range(3)] + [[(1, 0, 0, width)]],
         [project_in.shape, project_out.shape],
     )

time: 713 us -> 653 us (0.916)
  waiting for transfers between devices: 200 us -> 173 us
  local copies, waits for them, and re-layouts: 49.7 us -> 33.7 us
    ppermute x12, waiting for transfers between devices: 94.1 us -> 41.9 us  [ctx_swap(): lax.ppermute(values, 'ctx', [(device, device ^ bits) for device in range(...]
    ppermute x39 -> x36, waiting for transfers between devices: 46.9 us -> 72.5 us  [plane_swap(): lax.ppermute(values, ('dp', 'ctx'), [(device, plane_partner(device, kind)...]
    ppermute x3, waiting for transfers between devices: 45 us -> 22.1 us  [per_device_exchanged(): lax.ppermute(section, 'fsdp', [(device, (device + step) % 4) for device i...]
    convert_element_type x5 -> x8, other arithmetic: 15.3 us -> 27.8 us  [low_sum(): sum((term.astype(jnp.float32) for term in terms)).astype(jnp.bfloat16)]
    another operation x3 -> x0, other arithmetic: 11.9 us -> none
    reduce_scatter x3, waiting for transfers between devices: 0.01 us -> 11.8 us  [scatter_rows(): return lax.psum_scatter(values, 'fsdp', scatter_dimension=0, tiled=True)]
    ppermute x3 -> x0, local copies, waits for them, and re-layouts: 8.55 us -> none  [plane_swap(): lax.ppermute(values, ('dp', 'ctx'), [(device, plane_partner(device, kind)...]
    optimization_barrier x3 -> x0, local copies, waits for them, and re-layouts: 7.79 us -> none  [the longest x1 2.94 us: per_device_exchanged(): pin((down_keep, down_send, normed_two_low))]
  transfers between devices with their start and end apart: 68 -> 65, of which waited for: 29 -> 29; matrix products, arithmetic and copies ran while one was open for 14% -> 12% of each run, Pallas kernels for 40% -> 42%
where the time goes in v6:
time: 653 us; the launch traced here: 646 us
  Pallas kernels  277 us (42%)
  waiting for transfers between devices  173 us (26%)
  matrix products  59.1 us (9%)
  starting transfers between devices  51.8 us (8%)
  other arithmetic  35.5 us (5%)
  local copies, waits for them, and re-layouts  33.7 us (5%)
  between operations  15.3 us (2%)
    pallas_call x8, Pallas kernels, by_rows(): pl.pallas_call(kernel, grid=(rows // step,), in_specs=[tile] * len(tiled[...  156 us
    ppermute x36, waiting for transfers between devices, plane_swap(): lax.ppermute(values, ('dp', 'ctx'), [(device, plane_partner(device, kind)...  72.5 us
    dot_general x12, matrix products, product(): lax.dot_general(left, right, ((dims[:1], dims[1:]), ((), ())), preferred_...  59.1 us
    pallas_call x2, Pallas kernels, attend_back(): pl.pallas_call(functools.partial(attend_back_kernel, count=count, width=w...  48.3 us
    ppermute x12, waiting for transfers between devices, ctx_swap(): lax.ppermute(values, 'ctx', [(device, device ^ bits) for device in range(...  41.9 us
    pallas_call x1, Pallas kernels, attend(): pl.pallas_call(functools.partial(attend_kernel, count=count, width=width,...  32.3 us
    convert_element_type x8, other arithmetic, low_sum(): sum((term.astype(jnp.float32) for term in terms)).astype(jnp.bfloat16)  27.8 us
    ppermute x36, starting transfers between devices, plane_swap(): lax.ppermute(values, ('dp', 'ctx'), [(device, plane_partner(device, kind)...  24.4 us
  transfers between devices with their start and end apart: 65, of which 29 were waited for; matrix products, arithmetic and copies ran while one was open for 12% of the time, Pallas kernels for 42%

profile of v6, /device:TPU:8, one launch (start us, length us, event | category | flops | bytes accessed | tf_op | source)
XLA Modules:
  0.0 645.6 jit_solution(2066485188382221653)
XLA Ops:
  7.3 3.6 fusion.8
  22.3 4.4 collective-permute-start.1
  37.7 3.7 collective-permute-done.7.refs_2_
  44.4 8.8 %collective-permute-done.11.refs_3_ = bf16[1088,256]{1,0:T(8,128)(2,1)} collective-permute-done((bf16[1088,256]{1,0:T(8,128)(2,1)}, bf16[1088,256]{1,0:T(8,128)(2,1)}, u32[]{:S(2)}, u32[]{:S(2)}) %collective-permute-start.11) | collective-permute-done | bytes 557088 | tf_op jit(solution)/shard_map/ppermute | solution.py:609
  53.5 11.5 %collective-permute-done.10.refs_2_ = bf16[1088,256]{1,0:T(8,128)(2,1)S(1)} collective-permute-done((bf16[1088,256]{1,0:T(8,128)(2,1)}, bf16[1088,256]{1,0:T(8,128)(2,1)S(1)}, u32[]{:S(2)}, u32[]{:S(2)}) %collective-permute-start.10) | collective-permute-done | bytes 557088 | tf_op jit(solution)/shard_map/ppermute | solution.py:609
  66.7 11.7 %collective-permute-done.5.refs_10_ = bf16[272,1088]{1,0:T(8,128)(2,1)} collective-permute-done((bf16[272,1088]{1,0:T(8,128)(2,1)}, bf16[272,1088]{1,0:T(8,128)(2,1)}, u32[]{:S(2)}, u32[]{:S(2)}) %collective-permute-start.5) | collective-permute-done | bytes 591904 | tf_op jit(solution)/shard_map/ppermute | solution.py:1087
  78.4 10.4 %collective-permute-done.3.refs_8_ = bf16[272,1088]{1,0:T(8,128)(2,1)} collective-permute-done((bf16[272,1088]{1,0:T(8,128)(2,1)}, bf16[272,1088]{1,0:T(8,128)(2,1)}, u32[]{:S(2)}, u32[]{:S(2)}) %collective-permute-start.3) | collective-permute-done | bytes 591904 | tf_op jit(solution)/shard_map/ppermute | solution.py:1087
  93.3 6.5 %collective-permute-done.12.refs_11_ = bf16[272,1088]{1,0:T(8,128)(2,1)} collective-permute-done((bf16[272,1088]{1,0:T(8,128)(2,1)}, bf16[272,1088]{1,0:T(8,128)(2,1)}, u32[]{:S(2)}, u32[]{:S(2)}) %collective-permute-start.12) | collective-permute-done | bytes 591904 | tf_op jit(solution)/shard_map/ppermute | solution.py:603
  99.9 6.7 %collective-permute-done.13.refs_12_ = bf16[272,1088]{1,0:T(8,128)(2,1)} collective-permute-done((bf16[272,1088]{1,0:T(8,128)(2,1)}, bf16[272,1088]{1,0:T(8,128)(2,1)}, u32[]{:S(2)}, u32[]{:S(2)}) %collective-permute-start.13) | collective-permute-done | bytes 591904 | tf_op jit(solution)/shard_map/ppermute | solution.py:603
  106.6 6.7 %collective-permute-done.14.refs_13_ = bf16[272,1088]{1,0:T(8,128)(2,1)} collective-permute-done((bf16[272,1088]{1,0:T(8,128)(2,1)}, bf16[272,1088]{1,0:T(8,128)(2,1)}, u32[]{:S(2)}, u32[]{:S(2)}) %collective-permute-start.14) | collective-permute-done | bytes 591904 | tf_op jit(solution)/shard_map/ppermute | solution.py:603
  115.7 21.7 %front.1 = (bf16[1024,1088]{1,0:T(8,128)(2,1)}, bf16[1024,1088]{1,0:T(8,128)(2,1)}, bf16[1024,1088]{1,0:T(8,128)(2,1)}, bf16[1024,1088]{1,0:T(8,128)(2,1)}, bf16...) custom-call(s32[16]{0:T(128)} %stack.120.places_ref, f32[4,1088]{1,0:T(4,128)} %pad_maximum_fusion.1.vectors_ref, ...), custom_call_target="tpu_custom_call" | custom-call | flops 7272923136 | bytes 20471808 | tf_op jit(solution)/shard_map/front/pallas_call | solution.py:738
  144.4 32.3 %attend.1 = (bf16[1024,1088]{1,0:T(8,128)(2,1)S(1)}, f32[1024,128]{1,0:T(8,128)S(1)}) custom-call(s32[1]{0:T(128)} %bitcast.32.place_ref, bf16[1024,1088]{1,0:T(8,128)(2,1)S(1)} %copy-done.19, bf16[1024,1088]{1,0:T(8,128)(2,1)} %get-tuple-element.209.k_ref, bf16[1024,1088]{1,0:T(8,128)(2,1)} %get-tuple-element.210.v_ref), custom_call_target="tpu_custom_call" | custom-call | flops 19327352832 | bytes 9437184 | tf_op jit(solution)/shard_map/attend/pallas_call | solution.py:507
  186.0 10.8 %middle.1 = (f32[1024,1088]{1,0:T(8,128)}, bf16[1024,1088]{1,0:T(8,128)(2,1)}) custom-call(bf16[1024,1088]{1,0:T(8,128)(2,1)} %get-tuple-element.214.x_ref, bf16[1024,1088]{1,0:T(8,128)(2,1)} %copy-done.3, f32[3,1088]{1,0:T(4,128)} %pad_maximum_fusion.2.vectors_ref, bf16[16,272,1088]{2,1,0:T(8,128)(2,1)} %get-tuple-element.216.all_ref.refs_8_), custom_call_target="tpu_custom_call" | custom-call | flops 2424307712 | bytes 6823936 | tf_op jit(solution)/shard_map/middle/pallas_call | solution.py:1009
  196.8 17.5 %up.2 = (bf16[1024,1088]{1,0:T(8,128)(2,1)}, bf16[1024,1088]{1,0:T(8,128)(2,1)}, bf16[1024,1088]{1,0:T(8,128)(2,1)}, bf16[1024,1088]{1,0:T(8,128)(2,1)}) custom-call(bf16[1024,1088]{1,0:T(8,128)(2,1)} %get-tuple-element.264.h_ref, f32[2,1088]{1,0:T(2,128)} %pad_maximum_fusion.3.biases_ref, bf16[1088,1088]{1,0:T(8,128)(2,1)} %all-gather.3.cloned.1.call-done.refs_0_.refs_4_, ...), custom_call_target="tpu_custom_call" | custom-call | flops 4848615424 | bytes 13647872 | tf_op jit(solution)/shard_map/up/pallas_call | solution.py:1009
  214.3 17.6 %up.3 = (bf16[1024,1088]{1,0:T(8,128)(2,1)}, bf16[1024,1088]{1,0:T(8,128)(2,1)}, bf16[1024,1088]{1,0:T(8,128)(2,1)}, bf16[1024,1088]{1,0:T(8,128)(2,1)}) custom-call(bf16[1024,1088]{1,0:T(8,128)(2,1)} %get-tuple-element.264.h_ref, f32[2,1088]{1,0:T(2,128)} %pad_maximum_fusion.4.biases_ref, bf16[1088,1088]{1,0:T(8,128)(2,1)} %collective-permute-done.22.refs_0_.refs_5_, ...), custom_call_target="tpu_custom_call" | custom-call | flops 4848615424 | bytes 13647872 | tf_op jit(solution)/shard_map/up/pallas_call | solution.py:1009
  232.9 6.2 convolution_convert_fusion.11
  239.1 4.6 convolution_convert_fusion.10
  244.6 4.6 convolution_convert_fusion.8
  249.1 4.6 convolution_convert_fusion.9
  253.7 9.2 %collective-permute-done.24.refs_2_.refs_5_ = bf16[1088,1088]{1,0:T(8,128)(2,1)} collective-permute-done((bf16[1088,1088]{1,0:T(8,128)(2,1)}, bf16[1088,1088]{1,0:T(8,128)(2,1)}, u32[]{:S(2)}, u32[]{:S(2)}) %collective-permute-start.24) | collective-permute-done | bytes 2367520 | tf_op jit(solution)/shard_map/ppermute | solution.py:603
  263.6 14.0 %hidden.2 = (bf16[1024,1088]{1,0:T(8,128)(2,1)}, bf16[1024,1088]{1,0:T(8,128)(2,1)}, f32[3,8,1088]{2,1,0:T(8,128)}) custom-call(bf16[1024,1088]{1,0:T(8,128)(2,1)} %copy-done.2, bf16[1024,1088]{1,0:T(8,128)(2,1)} %get-tuple-element.242.refs_0_, bf16[1024,1088]{1,0:T(8,128)(2,1)} %get-tuple-element.243.refs_1_, ...), custom_call_target="tpu_custom_call" | custom-call | flops 4848615424 | bytes 13647872 | tf_op jit(solution)/shard_map/hidden/pallas_call | solution.py:1009
  277.6 4.5 add_convert_fusion.5
  282.2 14.1 %hidden.3 = (bf16[1024,1088]{1,0:T(8,128)(2,1)}, bf16[1024,1088]{1,0:T(8,128)(2,1)}, f32[3,8,1088]{2,1,0:T(8,128)}) custom-call(bf16[1024,1088]{1,0:T(8,128)(2,1)} %copy-done.2, bf16[1024,1088]{1,0:T(8,128)(2,1)} %get-tuple-element.247.refs_0_, bf16[1024,1088]{1,0:T(8,128)(2,1)} %get-tuple-element.248.refs_1_, ...), custom_call_target="tpu_custom_call" | custom-call | flops 4848615424 | bytes 13647872 | tf_op jit(solution)/shard_map/hidden/pallas_call | solution.py:1009
  297.7 32.1 %back.1 = (f32[1024,1088]{1,0:T(8,128)}, bf16[1024,1088]{1,0:T(8,128)(2,1)}, bf16[1024,1088]{1,0:T(8,128)(2,1)}, f32[3,8,1088]{2,1,0:T(8,128)}) custom-call(bf16[1024,1088]{1,0:T(8,128)(2,1)} %copy-done.2, f32[1024,1088]{1,0:T(8,128)} %get-tuple-element.292.middle_ref, f32[1,1088]{1,0:T(1,128)} %copy-done.33, bf16[1024,1088]{1,0:T(8,128)(2,1)} %get-tuple-element.253.refs_0_, ...), custom_call_target="tpu_custom_call" | custom-call | flops 12121538560 | bytes 34119680 | tf_op jit(solution)/shard_map/back/pallas_call | solution.py:1009
  329.9 4.9 add_convert_fusion.4
  334.8 7.2 %convolution_convert_fusion.6 = bf16[1088,1088]{1,0:T(8,128)(2,1)} fusion(bf16[1024,1088]{1,0:T(8,128)(2,1)} %get-tuple-element.264.h_ref, bf16[1024,1088]{1,0:T(8,128)(2,1)} %get-tuple-element.255.refs_2_), kind=kOutput, calls=%fused_computation.6 | convolution fusion | flops 2425491456 | bytes 6823936 | tf_op jit(solution)/shard_map/dot_general | solution.py:660
  342.0 4.6 convolution_convert_fusion.7
  347.1 4.6 convolution_convert_fusion.4
  353.3 6.4 convolution_convert_fusion.3
  359.7 6.3 add_convert_fusion.3
  367.4 26.7 %attend_back.2 = (bf16[1024,1088]{1,0:T(8,128)(2,1)S(1)}, bf16[1024,1088]{1,0:T(8,128)(2,1)S(1)}, bf16[1024,1088]{1,0:T(8,128)(2,1)}) custom-call(s32[1]{0:T(128)} %bitcast.32.place_ref, bf16[1024,1088]{1,0:T(8,128)(2,1)} %get-tuple-element.208.q_ref, bf16[1024,1088]{1,0:T(8,128)(2,1)} %get-tuple-element.209.k_ref, ...), custom_call_target="tpu_custom_call" | custom-call | flops 20132659200 | bytes 10485760 | tf_op jit(solution)/shard_map/attend_back/pallas_call | solution.py:541
  396.8 5.0 add_convert_fusion.2
  404.9 21.6 %attend_back.3 = (bf16[1024,1088]{1,0:T(8,128)(2,1)S(1)}, bf16[1024,1088]{1,0:T(8,128)(2,1)S(1)}, bf16[1024,1088]{1,0:T(8,128)(2,1)}) custom-call(s32[1]{0:T(128)} %bitcast.32.place_ref, bf16[1024,1088]{1,0:T(8,128)(2,1)} %get-tuple-element.208.q_ref, ...), custom_call_target="tpu_custom_call", output_to_operand_aliasing={{0}: (7, {}), {1}: (8, {}), {2}: (9, {})} | custom-call | flops 16106127360 | bytes 8388608 | tf_op jit(solution)/shard_map/attend_back/pallas_call | solution.py:541
  433.2 3.9 select_select_fusion
  439.4 5.3 collective-permute-done.34
  448.0 6.4 collective-permute-done.36.refs_1_
  456.9 25.6 %down.1 = (bf16[1088,256]{1,0:T(8,128)(2,1)}, bf16[1088,256]{1,0:T(8,128)(2,1)}, bf16[1088,256]{1,0:T(8,128)(2,1)}, bf16[1088,256]{1,0:T(8,128)(2,1)}) custom-call(f32[1024,1088]{1,0:T(8,128)} %get-tuple-element.292.middle_ref, f32[1,1088]{1,0:T(1,128)} %reshape.446.vectors_ref, bf16[1024,1088]{1,0:T(8,128)(2,1)} %get-tuple-element.234.refs_0_, ...), custom_call_target="tpu_custom_call" | custom-call | flops 9697230848 | bytes 27295744 | tf_op jit(solution)/shard_map/down/pallas_call | solution.py:1009
  485.1 7.3 %add_convert_fusion = bf16[1088,1088]{1,0:T(8,128)(2,1)} fusion(bf16[1088,1088]{1,0:T(8,128)(2,1)} %collective-permute-done.39, bf16[1088,1088]{1,0:T(8,128)(2,1)} %collective-permute-done.35, bf16[1088,1088]{1,0:T(8,128)(2,1)} %copy-done.23, bf16[1088,1088]{1,0:T(8,128)(2,1)} %copy-done.21, bf16[1088,1088]{1,0:T(8,128)(2,1)} %copy-done.22, ...), kind=kLoop, calls=%fused_computation.12 | loop fusion | flops 10653696 | bytes 16572419 | tf_op jit(solution)/shard_map/convert_element_type | solution.py:613
  492.4 11.8 %reduce-scatter.6.cloned.1.call-done = bf16[272,1088]{1,0:T(8,128)(2,1)} async-done(((bf16[1088,1088]{1,0:T(8,128)(2,1)}), bf16[272,1088]{1,0:T(8,128)(2,1)}) %reduce-scatter.6.cloned.1.call-update) | async-done | bytes 591888 | tf_op jit(solution)/shard_map/reduce_scatter | solution.py:625
  511.8 24.2 %last.1 = (bf16[1088,256]{1,0:T(8,128)(2,1)}, bf16[1088,256]{1,0:T(8,128)(2,1)}, bf16[1088,256]{1,0:T(8,128)(2,1)}, bf16[1088,256]{1,0:T(8,128)(2,1)}, f32[4,8,1088]{2,1,0:T(8,128)}) custom-call(bf16[1024,1088]{1,0:T(8,128)(2,1)} %copy-done.15, bf16[1024,1088]{1,0:T(8,128)(2,1)} %copy-done.18, bf16[1024,1088]{1,0:T(8,128)(2,1)} %get-tuple-element.301.v_ref, ...), custom_call_target="tpu_custom_call" | custom-call | flops 7272923136 | bytes 20471808 | tf_op jit(solution)/shard_map/last/pallas_call | solution.py:1009
  536.0 6.5 %collective-permute-done.40 = bf16[272,1088]{1,0:T(8,128)(2,1)} collective-permute-done((bf16[272,1088]{1,0:T(8,128)(2,1)S(1)}, bf16[272,1088]{1,0:T(8,128)(2,1)}, u32[]{:S(2)}, u32[]{:S(2)}) %collective-permute-start.40) | collective-permute-done | bytes 591904 | tf_op jit(solution)/shard_map/ppermute | solution.py:603
  562.1 9.6 %collective-permute-done.55 = f32[3264]{0:T(1024)S(1)} collective-permute-done((f32[3264]{0:T(1024)S(1)}, f32[3264]{0:T(1024)S(1)}, u32[]{:S(2)}, u32[]{:S(2)}) %collective-permute-start.55) | collective-permute-done | bytes 13088 | tf_op jit(solution)/shard_map/ppermute | solution.py:653
  581.4 4.6 collective-permute-done.45.refs_2_
  586.1 13.3 %collective-permute-done.46.refs_3_ = bf16[1088,256]{1,0:T(8,128)(2,1)S(1)} collective-permute-done((bf16[1088,256]{1,0:T(8,128)(2,1)}, bf16[1088,256]{1,0:T(8,128)(2,1)S(1)}, u32[]{:S(2)}, u32[]{:S(2)}) %collective-permute-start.46) | collective-permute-done | bytes 557088 | tf_op jit(solution)/shard_map/ppermute | solution.py:609
  602.8 4.2 assemble.2
  608.4 9.0 %collective-permute-done.56 = bf16[272,1088]{1,0:T(8,128)(2,1)S(1)} collective-permute-done((bf16[272,1088]{1,0:T(8,128)(2,1)}, bf16[272,1088]{1,0:T(8,128)(2,1)S(1)}, u32[]{:S(2)}, u32[]{:S(2)}) %collective-permute-start.56) | collective-permute-done | bytes 591904 | tf_op jit(solution)/shard_map/ppermute | solution.py:603
  623.1 5.4 collective-permute-done.59.refs_3_
  628.4 6.7 %collective-permute-done.57.refs_1_ = bf16[272,1088]{1,0:T(8,128)(2,1)S(1)} collective-permute-done((bf16[272,1088]{1,0:T(8,128)(2,1)S(1)}, bf16[272,1088]{1,0:T(8,128)(2,1)S(1)}, u32[]{:S(2)}, u32[]{:S(2)}) %collective-permute-start.57) | collective-permute-done | bytes 591904 | tf_op jit(solution)/shard_map/ppermute | solution.py:603
  (309 shorter events, 131.4 us)
Async XLA Ops:
  7.2 133.2 %all-gather.3.cloned.1.call-start = ((), (), s32[]{:S(2)}) async-start(), calls=%async_computation.3 | async-start | bytes 3133440 | tf_op jit(solution)/shard_map/all_gather | solution.py:1132
  14.0 20.7 %collective-permute-start.8 = (bf16[1088,256]{1,0:T(8,128)(2,1)}, bf16[1088,256]{1,0:T(8,128)(2,1)}, u32[]{:S(2)}, u32[]{:S(2)}) collective-permute-start(bf16[1088,256]{1,0:T(8,128)(2,1)} %get-tuple-element.192), channel_id=1, source_target_pairs={{0,3},{1,2},{2,1},{3,0},{4,7},{5,6},{6,5},{7,4},{8,11},{9,10},{10,... | collective-permute-start | bytes 1671176 | tf_op jit(solution)/shard_map/ppermute | solution.py:609
  15.0 26.3 %collective-permute-start.7 = (bf16[1088,256]{1,0:T(8,128)(2,1)}, bf16[1088,256]{1,0:T(8,128)(2,1)}, u32[]{:S(2)}, u32[]{:S(2)}) collective-permute-start(bf16[1088,256]{1,0:T(8,128)(2,1)} %get-tuple-element.371), channel_id=1, source_target_pairs={{0,2},{1,3},{2,0},{3,1},{4,6},{5,7},{6,4},{7,5},{8,10},{9,11},{10,... | collective-permute-start | bytes 1671176 | tf_op jit(solution)/shard_map/ppermute | solution.py:609
  15.7 27.2 %collective-permute-start.6 = (bf16[1088,256]{1,0:T(8,128)(2,1)}, bf16[1088,256]{1,0:T(8,128)(2,1)}, u32[]{:S(2)}, u32[]{:S(2)}) collective-permute-start(bf16[1088,256]{1,0:T(8,128)(2,1)} %get-tuple-element.372), channel_id=1, source_target_pairs={{0,1},{1,0},{2,3},{3,2},{4,5},{5,4},{6,7},{7,6},{8,9},{9,8},{10,11... | collective-permute-start | bytes 1671176 | tf_op jit(solution)/shard_map/ppermute | solution.py:609
  17.2 36.0 %collective-permute-start.11 = (bf16[1088,256]{1,0:T(8,128)(2,1)}, bf16[1088,256]{1,0:T(8,128)(2,1)}, u32[]{:S(2)}, u32[]{:S(2)}) collective-permute-start(bf16[1088,256]{1,0:T(8,128)(2,1)} %get-tuple-element.367), channel_id=1, source_target_pairs={{0,3},{1,2},{2,1},{3,0},{4,7},{5,6},{6,5},{7,4},{8,11},{9,10},{10,... | collective-permute-start | bytes 1671176 | tf_op jit(solution)/shard_map/ppermute | solution.py:609
  32.8 45.6 %collective-permute-start.5 = (bf16[272,1088]{1,0:T(8,128)(2,1)}, bf16[272,1088]{1,0:T(8,128)(2,1)}, u32[]{:S(2)}, u32[]{:S(2)}) collective-permute-start(bf16[272,1088]{1,0:T(8,128)(2,1)} %get-tuple-element.191), channel_id=1, source_target_pairs={{0,12},{4,0},{8,4},{12,8},{1,13},{5,1},{9,5},{13,9},{2,14},{6,2},{... | collective-permute-start | bytes 1775624 | tf_op jit(solution)/shard_map/ppermute | solution.py:1087
  34.7 43.7 %collective-permute-start.4 = (bf16[272,1088]{1,0:T(8,128)(2,1)}, bf16[272,1088]{1,0:T(8,128)(2,1)}, u32[]{:S(2)}, u32[]{:S(2)}) collective-permute-start(bf16[272,1088]{1,0:T(8,128)(2,1)} %get-tuple-element.191), channel_id=1, source_target_pairs={{0,8},{4,12},{8,0},{12,4},{1,9},{5,13},{9,1},{13,5},{2,10},{6,14},... | collective-permute-start | bytes 1775624 | tf_op jit(solution)/shard_map/ppermute | solution.py:1087
  41.3 47.5 %collective-permute-start.3 = (bf16[272,1088]{1,0:T(8,128)(2,1)}, bf16[272,1088]{1,0:T(8,128)(2,1)}, u32[]{:S(2)}, u32[]{:S(2)}) collective-permute-start(bf16[272,1088]{1,0:T(8,128)(2,1)} %get-tuple-element.191), channel_id=1, source_target_pairs={{0,4},{4,8},{8,12},{12,0},{1,5},{5,9},{9,13},{13,1},{2,6},{6,10},{... | collective-permute-start | bytes 1775624 | tf_op jit(solution)/shard_map/ppermute | solution.py:1087
  42.9 22.1 %collective-permute-start.10 = (bf16[1088,256]{1,0:T(8,128)(2,1)}, bf16[1088,256]{1,0:T(8,128)(2,1)S(1)}, u32[]{:S(2)}, u32[]{:S(2)}) collective-permute-start(bf16[1088,256]{1,0:T(8,128)(2,1)} %get-tuple-element.368), channel_id=1, source_target_pairs={{0,2},{1,3},{2,0},{3,1},{4,6},{5,7},{6,4},{7,5},{8,10},{9,11},{10,... | collective-permute-start | bytes 1671176 | tf_op jit(solution)/shard_map/ppermute | solution.py:609
  53.2 12.7 %collective-permute-start.9 = (bf16[1088,256]{1,0:T(8,128)(2,1)}, bf16[1088,256]{1,0:T(8,128)(2,1)S(1)}, u32[]{:S(2)}, u32[]{:S(2)}) collective-permute-start(bf16[1088,256]{1,0:T(8,128)(2,1)} %get-tuple-element.369), channel_id=1, source_target_pairs={{0,1},{1,0},{2,3},{3,2},{4,5},{5,4},{6,7},{7,6},{8,9},{9,8},{10,11... | collective-permute-start | bytes 1671176 | tf_op jit(solution)/shard_map/ppermute | solution.py:609
  88.9 143.1 %all-gather.5.cloned.1.call-start = ((), (), s32[]{:S(2)}) async-start(), calls=%async_computation.4 | async-start | bytes 3133440 | tf_op jit(solution)/shard_map/all_gather | solution.py:1157
  89.2 10.7 %collective-permute-start.12 = (bf16[272,1088]{1,0:T(8,128)(2,1)}, bf16[272,1088]{1,0:T(8,128)(2,1)}, u32[]{:S(2)}, u32[]{:S(2)}) collective-permute-start(bf16[272,1088]{1,0:T(8,128)(2,1)} %collective-permute-done.3.refs_8_), channel_id=1, source_target_pairs={{0,16},{1,3},{2,18},{3,1},{16,0},{17,19},{18,2},{19,17},{4,20},{5,... | collective-permute-start | bytes 1775624 | tf_op jit(solution)/shard_map/ppermute | solution.py:603
  90.8 15.8 %collective-permute-start.13 = (bf16[272,1088]{1,0:T(8,128)(2,1)}, bf16[272,1088]{1,0:T(8,128)(2,1)}, u32[]{:S(2)}, u32[]{:S(2)}) collective-permute-start(bf16[272,1088]{1,0:T(8,128)(2,1)} %collective-permute-done.4.refs_9_), channel_id=1, source_target_pairs={{0,16},{1,3},{2,18},{3,1},{16,0},{17,19},{18,2},{19,17},{4,20},{5,... | collective-permute-start | bytes 1775624 | tf_op jit(solution)/shard_map/ppermute | solution.py:603
  91.3 22.0 %collective-permute-start.14 = (bf16[272,1088]{1,0:T(8,128)(2,1)}, bf16[272,1088]{1,0:T(8,128)(2,1)}, u32[]{:S(2)}, u32[]{:S(2)}) collective-permute-start(bf16[272,1088]{1,0:T(8,128)(2,1)} %collective-permute-done.5.refs_10_), channel_id=1, source_target_pairs={{0,16},{1,3},{2,18},{3,1},{16,0},{17,19},{18,2},{19,17},{4,20},{5,... | collective-permute-start | bytes 1775624 | tf_op jit(solution)/shard_map/ppermute | solution.py:603
  92.8 22.8 %collective-permute-start.16 = (bf16[272,1088]{1,0:T(8,128)(2,1)}, bf16[272,1088]{1,0:T(8,128)(2,1)}, u32[]{:S(2)}, u32[]{:S(2)}) collective-permute-start(bf16[272,1088]{1,0:T(8,128)(2,1)} %collective-permute-done.4.refs_9_), channel_id=1, source_target_pairs={{0,1},{1,0},{2,3},{3,2},{16,17},{17,16},{18,19},{19,18},{4,5},{5,4... | collective-permute-start | bytes 1775624 | tf_op jit(solution)/shard_map/ppermute | solution.py:603
  92.8 22.8 %collective-permute-start.17 = (bf16[272,1088]{1,0:T(8,128)(2,1)}, bf16[272,1088]{1,0:T(8,128)(2,1)}, u32[]{:S(2)}, u32[]{:S(2)}) collective-permute-start(bf16[272,1088]{1,0:T(8,128)(2,1)} %collective-permute-done.5.refs_10_), channel_id=1, source_target_pairs={{0,1},{1,0},{2,3},{3,2},{16,17},{17,16},{18,19},{19,18},{4,5},{5,4... | collective-permute-start | bytes 1775624 | tf_op jit(solution)/shard_map/ppermute | solution.py:603
  99.9 15.7 %collective-permute-start.18 = (bf16[272,1088]{1,0:T(8,128)(2,1)}, bf16[272,1088]{1,0:T(8,128)(2,1)}, u32[]{:S(2)}, u32[]{:S(2)}) collective-permute-start(bf16[272,1088]{1,0:T(8,128)(2,1)} %collective-permute-done.12.refs_11_), channel_id=1, source_target_pairs={{0,1},{1,0},{2,3},{3,2},{16,17},{17,16},{18,19},{19,18},{4,5},{5,4... | collective-permute-start | bytes 1775624 | tf_op jit(solution)/shard_map/ppermute | solution.py:603
  140.4 38.5 %collective-permute-start.22 = (bf16[1088,1088]{1,0:T(8,128)(2,1)}, bf16[1088,1088]{1,0:T(8,128)(2,1)}, u32[]{:S(2)}, u32[]{:S(2)}) collective-permute-start(bf16[1088,1088]{1,0:T(8,128)(2,1)} %all-gather.3.cloned.1.call-done.refs_0_.refs_4_), channel_id=1, source_target_pairs={{0,16},{1,3},{2,18},{3,1},{16,0},{17,19},{18,2},{19,17},{4,20},{5,... | collective-permute-start | bytes 7102472 | tf_op jit(solution)/shard_map/ppermute | solution.py:603
  141.8 37.1 %collective-permute-start.21 = (bf16[1088,1088]{1,0:T(8,128)(2,1)}, bf16[1088,1088]{1,0:T(8,128)(2,1)}, u32[]{:S(2)}, u32[]{:S(2)}) collective-permute-start(bf16[1088,1088]{1,0:T(8,128)(2,1)} %all-gather.3.cloned.1.call-done.refs_0_.refs_4_), channel_id=1, source_target_pairs={{0,1},{1,0},{2,3},{3,2},{16,17},{17,16},{18,19},{19,18},{4,5},{5,4... | collective-permute-start | bytes 7102472 | tf_op jit(solution)/shard_map/ppermute | solution.py:603
  178.9 222.9 %reduce-scatter.4.cloned.1.call-start = ((), (), s32[]{:S(2)}) async-start(), calls=%async_computation.5 | async-start | bytes 3133440 | tf_op jit(solution)/shard_map/reduce_scatter | solution.py:625
  179.0 35.4 %collective-permute-start.23 = (bf16[1088,1088]{1,0:T(8,128)(2,1)}, bf16[1088,1088]{1,0:T(8,128)(2,1)}, u32[]{:S(2)}, u32[]{:S(2)}) collective-permute-start(bf16[1088,1088]{1,0:T(8,128)(2,1)} %collective-permute-done.22.refs_0_.refs_5_), channel_id=1, source_target_pairs={{0,1},{1,0},{2,3},{3,2},{16,17},{17,16},{18,19},{19,18},{4,5},{5,4... | collective-permute-start | bytes 7102472 | tf_op jit(solution)/shard_map/ppermute | solution.py:603
  232.0 31.6 %collective-permute-start.27 = (bf16[1088,1088]{1,0:T(8,128)(2,1)}, bf16[1088,1088]{1,0:T(8,128)(2,1)}, u32[]{:S(2)}, u32[]{:S(2)}) collective-permute-start(bf16[1088,1088]{1,0:T(8,128)(2,1)} %all-gather.5.cloned.1.call-done.refs_2_.refs_4_), channel_id=1, source_target_pairs={{0,1},{1,0},{2,3},{3,2},{16,17},{17,16},{18,19},{19,18},{4,5},{5,4... | collective-permute-start | bytes 7102472 | tf_op jit(solution)/shard_map/ppermute | solution.py:603
  232.1 30.8 %collective-permute-start.24 = (bf16[1088,1088]{1,0:T(8,128)(2,1)}, bf16[1088,1088]{1,0:T(8,128)(2,1)}, u32[]{:S(2)}, u32[]{:S(2)}) collective-permute-start(bf16[1088,1088]{1,0:T(8,128)(2,1)} %all-gather.5.cloned.1.call-done.refs_2_.refs_4_), channel_id=1, source_target_pairs={{0,16},{1,3},{2,18},{3,1},{16,0},{17,19},{18,2},{19,17},{4,20},{5,... | collective-permute-start | bytes 7102472 | tf_op jit(solution)/shard_map/ppermute | solution.py:603
  243.7 33.9 %collective-permute-start.25 = (bf16[1088,1088]{1,0:T(8,128)(2,1)}, bf16[1088,1088]{1,0:T(8,128)(2,1)}, u32[]{:S(2)}, u32[]{:S(2)}) collective-permute-start(bf16[1088,1088]{1,0:T(8,128)(2,1)} %convolution_convert_fusion.11), channel_id=1, source_target_pairs={{0,1},{1,0},{2,3},{3,2},{16,17},{17,16},{18,19},{19,18},{4,5},{5,4... | collective-permute-start | bytes 7102472 | tf_op jit(solution)/shard_map/ppermute | solution.py:603
  262.9 19.3 %collective-permute-start.28 = (bf16[1088,1088]{1,0:T(8,128)(2,1)}, bf16[1088,1088]{1,0:T(8,128)(2,1)}, u32[]{:S(2)}, u32[]{:S(2)}) collective-permute-start(bf16[1088,1088]{1,0:T(8,128)(2,1)} %collective-permute-done.24.refs_2_.refs_5_), channel_id=1, source_target_pairs={{0,1},{1,0},{2,3},{3,2},{16,17},{17,16},{18,19},{19,18},{4,5},{5,4... | collective-permute-start | bytes 7102472 | tf_op jit(solution)/shard_map/ppermute | solution.py:603
  263.1 33.1 %collective-permute-start.26 = (bf16[1088,1088]{1,0:T(8,128)(2,1)}, bf16[1088,1088]{1,0:T(8,128)(2,1)S(1)}, u32[]{:S(2)}, u32[]{:S(2)}) collective-permute-start(bf16[1088,1088]{1,0:T(8,128)(2,1)} %convolution_convert_fusion.10), channel_id=1, source_target_pairs={{0,1},{1,0},{2,3},{3,2},{16,17},{17,16},{18,19},{19,18},{4,5},{5,4... | collective-permute-start | bytes 7102472 | tf_op jit(solution)/shard_map/ppermute | solution.py:603
  296.3 33.6 %collective-permute-start.29 = (bf16[1088,1088]{1,0:T(8,128)(2,1)}, bf16[1088,1088]{1,0:T(8,128)(2,1)}, u32[]{:S(2)}, u32[]{:S(2)}) collective-permute-start(bf16[1088,1088]{1,0:T(8,128)(2,1)} %add_convert_fusion.5), channel_id=1, source_target_pairs={{0,16},{1,3},{2,18},{3,1},{16,0},{17,19},{18,2},{19,17},{4,20},{5,... | collective-permute-start | bytes 7102472 | tf_op jit(solution)/shard_map/ppermute | solution.py:603
  346.6 13.1 %collective-permute-start.30 = (bf16[1088,1088]{1,0:T(8,128)(2,1)}, bf16[1088,1088]{1,0:T(8,128)(2,1)}, u32[]{:S(2)}, u32[]{:S(2)}) collective-permute-start(bf16[1088,1088]{1,0:T(8,128)(2,1)} %convolution_convert_fusion.7), channel_id=1, source_target_pairs={{0,1},{1,0},{2,3},{3,2},{16,17},{17,16},{18,19},{19,18},{4,5},{5,4... | collective-permute-start | bytes 7102472 | tf_op jit(solution)/shard_map/ppermute | solution.py:603
  346.6 19.4 %collective-permute-start.31 = (bf16[1088,1088]{1,0:T(8,128)(2,1)}, bf16[1088,1088]{1,0:T(8,128)(2,1)}, u32[]{:S(2)}, u32[]{:S(2)}) collective-permute-start(bf16[1088,1088]{1,0:T(8,128)(2,1)} %convolution_convert_fusion.6), channel_id=1, source_target_pairs={{0,1},{1,0},{2,3},{3,2},{16,17},{17,16},{18,19},{19,18},{4,5},{5,4... | collective-permute-start | bytes 7102472 | tf_op jit(solution)/shard_map/ppermute | solution.py:603
  351.7 152.6 %reduce-scatter.6.cloned.1.call-start = ((), (), s32[]{:S(2)}) async-start(), calls=%async_computation.6 | async-start | bytes 3133440 | tf_op jit(solution)/shard_map/reduce_scatter | solution.py:625
  366.0 30.7 %collective-permute-start.32 = (bf16[1088,1088]{1,0:T(8,128)(2,1)}, bf16[1088,1088]{1,0:T(8,128)(2,1)}, u32[]{:S(2)}, u32[]{:S(2)}) collective-permute-start(bf16[1088,1088]{1,0:T(8,128)(2,1)} %add_convert_fusion.3), channel_id=1, source_target_pairs={{0,16},{1,3},{2,18},{3,1},{16,0},{17,19},{18,2},{19,17},{4,20},{5,... | collective-permute-start | bytes 7102472 | tf_op jit(solution)/shard_map/ppermute | solution.py:603
  401.8 24.8 %collective-permute-start.33 = (bf16[272,1088]{1,0:T(8,128)(2,1)}, bf16[272,1088]{1,0:T(8,128)(2,1)S(1)}, u32[]{:S(2)}, u32[]{:S(2)}) collective-permute-start(bf16[272,1088]{1,0:T(8,128)(2,1)} %reduce-scatter.4.cloned.1.call-done), channel_id=1, source_target_pairs={{0,2},{1,17},{2,0},{3,19},{16,18},{17,1},{18,16},{19,3},{4,6},{5,2... | collective-permute-start | bytes 1775624 | tf_op jit(solution)/shard_map/ppermute | solution.py:603
  437.2 17.2 %collective-permute-start.35 = (bf16[1088,1088]{1,0:T(8,128)(2,1)S(1)}, bf16[1088,1088]{1,0:T(8,128)(2,1)}, u32[]{:S(2)}, u32[]{:S(2)}) collective-permute-start(bf16[1088,1088]{1,0:T(8,128)(2,1)S(1)} %get-tuple-element.361), channel_id=1, source_target_pairs={{0,1},{1,0},{2,3},{3,2},{16,17},{17,16},{18,19},{19,18},{4,5},{5,4... | collective-permute-start | bytes 7102472 | tf_op jit(solution)/shard_map/ppermute | solution.py:603
  438.4 16.0 %collective-permute-start.36 = (bf16[272,1088]{1,0:T(8,128)(2,1)S(1)}, bf16[272,1088]{1,0:T(8,128)(2,1)S(1)}, u32[]{:S(2)}, u32[]{:S(2)}) collective-permute-start(bf16[272,1088]{1,0:T(8,128)(2,1)S(1)} %add_convert_fusion.8.refs_0_), channel_id=1, source_target_pairs={{0,16},{1,3},{2,18},{3,1},{16,0},{17,19},{18,2},{19,17},{4,20},{5,... | collective-permute-start | bytes 1775624 | tf_op jit(solution)/shard_map/ppermute | solution.py:603
  454.4 30.7 %collective-permute-start.39 = (bf16[1088,1088]{1,0:T(8,128)(2,1)}, bf16[1088,1088]{1,0:T(8,128)(2,1)}, u32[]{:S(2)}, u32[]{:S(2)}) collective-permute-start(bf16[1088,1088]{1,0:T(8,128)(2,1)} %add_convert_fusion.1), channel_id=1, source_target_pairs={{0,16},{1,3},{2,18},{3,1},{16,0},{17,19},{18,2},{19,17},{4,20},{5,... | collective-permute-start | bytes 7102472 | tf_op jit(solution)/shard_map/ppermute | solution.py:603
  455.3 151.7 %reduce-scatter.8.cloned.1.call-start = ((), (), s32[]{:S(2)}) async-start(), calls=%async_computation.7 | async-start | bytes 3133440 | tf_op jit(solution)/shard_map/reduce_scatter | solution.py:625
  508.5 35.5 %collective-permute-start.41 = (bf16[1088,256]{1,0:T(8,128)(2,1)}, bf16[1088,256]{1,0:T(8,128)(2,1)S(1)}, u32[]{:S(2)}, u32[]{:S(2)}) collective-permute-start(bf16[1088,256]{1,0:T(8,128)(2,1)} %get-tuple-element.309), channel_id=1, source_target_pairs={{0,1},{1,0},{2,3},{3,2},{4,5},{5,4},{6,7},{7,6},{8,9},{9,8},{10,11... | collective-permute-start | bytes 1671176 | tf_op jit(solution)/shard_map/ppermute | solution.py:609
  508.5 36.2 %collective-permute-start.42 = (bf16[1088,256]{1,0:T(8,128)(2,1)}, bf16[1088,256]{1,0:T(8,128)(2,1)}, u32[]{:S(2)}, u32[]{:S(2)}) collective-permute-start(bf16[1088,256]{1,0:T(8,128)(2,1)} %get-tuple-element.310), channel_id=1, source_target_pairs={{0,2},{1,3},{2,0},{3,1},{4,6},{5,7},{6,4},{7,5},{8,10},{9,11},{10,... | collective-permute-start | bytes 1671176 | tf_op jit(solution)/shard_map/ppermute | solution.py:609
  510.0 34.7 %collective-permute-start.43 = (bf16[1088,256]{1,0:T(8,128)(2,1)}, bf16[1088,256]{1,0:T(8,128)(2,1)}, u32[]{:S(2)}, u32[]{:S(2)}) collective-permute-start(bf16[1088,256]{1,0:T(8,128)(2,1)} %get-tuple-element.311), channel_id=1, source_target_pairs={{0,3},{1,2},{2,1},{3,0},{4,7},{5,6},{6,5},{7,4},{8,11},{9,10},{10,... | collective-permute-start | bytes 1671176 | tf_op jit(solution)/shard_map/ppermute | solution.py:609
  510.4 32.1 %collective-permute-start.40 = (bf16[272,1088]{1,0:T(8,128)(2,1)S(1)}, bf16[272,1088]{1,0:T(8,128)(2,1)}, u32[]{:S(2)}, u32[]{:S(2)}) collective-permute-start(bf16[272,1088]{1,0:T(8,128)(2,1)S(1)} %copy-done.28), channel_id=1, source_target_pairs={{0,2},{1,17},{2,0},{3,19},{16,18},{17,1},{18,16},{19,3},{4,6},{5,2... | collective-permute-start | bytes 1775624 | tf_op jit(solution)/shard_map/ppermute | solution.py:603
  545.7 27.4 %collective-permute-start.44 = (bf16[1088,256]{1,0:T(8,128)(2,1)}, bf16[1088,256]{1,0:T(8,128)(2,1)}, u32[]{:S(2)}, u32[]{:S(2)}) collective-permute-start(bf16[1088,256]{1,0:T(8,128)(2,1)} %get-tuple-element.317), channel_id=1, source_target_pairs={{0,1},{1,0},{2,3},{3,2},{4,5},{5,4},{6,7},{7,6},{8,9},{9,8},{10,11... | collective-permute-start | bytes 1671176 | tf_op jit(solution)/shard_map/ppermute | solution.py:609
  554.4 44.9 %collective-permute-start.49 = (bf16[272,1088]{1,0:T(8,128)(2,1)S(1)}, bf16[272,1088]{1,0:T(8,128)(2,1)S(1)}, u32[]{:S(2)}, u32[]{:S(2)}) collective-permute-start(bf16[272,1088]{1,0:T(8,128)(2,1)S(1)} %add_convert_fusion.7.refs_0_), channel_id=1, source_target_pairs={{0,17},{1,2},{2,19},{3,0},{16,1},{17,18},{18,3},{19,16},{4,21},{5,... | collective-permute-start | bytes 1775624 | tf_op jit(solution)/shard_map/ppermute | solution.py:603
  556.0 43.4 %collective-permute-start.48 = (bf16[272,1088]{1,0:T(8,128)(2,1)S(1)}, bf16[272,1088]{1,0:T(8,128)(2,1)S(1)}, u32[]{:S(2)}, u32[]{:S(2)}) collective-permute-start(bf16[272,1088]{1,0:T(8,128)(2,1)S(1)} %add_convert_fusion.7.refs_0_), channel_id=1, source_target_pairs={{0,1},{1,0},{2,3},{3,2},{16,17},{17,16},{18,19},{19,18},{4,5},{5,4... | collective-permute-start | bytes 1775624 | tf_op jit(solution)/shard_map/ppermute | solution.py:603
  556.0 43.3 %collective-permute-start.47 = (bf16[272,1088]{1,0:T(8,128)(2,1)S(1)}, bf16[272,1088]{1,0:T(8,128)(2,1)S(1)}, u32[]{:S(2)}, u32[]{:S(2)}) collective-permute-start(bf16[272,1088]{1,0:T(8,128)(2,1)S(1)} %add_convert_fusion.7.refs_0_), channel_id=1, source_target_pairs={{0,16},{1,3},{2,18},{3,1},{16,0},{17,19},{18,2},{19,17},{4,20},{5,... | collective-permute-start | bytes 1775624 | tf_op jit(solution)/shard_map/ppermute | solution.py:603
  571.7 14.4 %collective-permute-start.45 = (bf16[1088,256]{1,0:T(8,128)(2,1)}, bf16[1088,256]{1,0:T(8,128)(2,1)S(1)}, u32[]{:S(2)}, u32[]{:S(2)}) collective-permute-start(bf16[1088,256]{1,0:T(8,128)(2,1)} %get-tuple-element.318), channel_id=1, source_target_pairs={{0,2},{1,3},{2,0},{3,1},{4,6},{5,7},{6,4},{7,5},{8,10},{9,11},{10,... | collective-permute-start | bytes 1671176 | tf_op jit(solution)/shard_map/ppermute | solution.py:609
  573.1 26.2 %collective-permute-start.46 = (bf16[1088,256]{1,0:T(8,128)(2,1)}, bf16[1088,256]{1,0:T(8,128)(2,1)S(1)}, u32[]{:S(2)}, u32[]{:S(2)}) collective-permute-start(bf16[1088,256]{1,0:T(8,128)(2,1)} %get-tuple-element.319), channel_id=1, source_target_pairs={{0,3},{1,2},{2,1},{3,0},{4,7},{5,6},{6,5},{7,4},{8,11},{9,10},{10,... | collective-permute-start | bytes 1671176 | tf_op jit(solution)/shard_map/ppermute | solution.py:609
  607.0 10.5 %collective-permute-start.56 = (bf16[272,1088]{1,0:T(8,128)(2,1)}, bf16[272,1088]{1,0:T(8,128)(2,1)S(1)}, u32[]{:S(2)}, u32[]{:S(2)}) collective-permute-start(bf16[272,1088]{1,0:T(8,128)(2,1)} %reduce-scatter.8.cloned.1.call-done), channel_id=1, source_target_pairs={{0,2},{1,17},{2,0},{3,19},{16,18},{17,1},{18,16},{19,3},{4,6},{5,2... | collective-permute-start | bytes 1775624 | tf_op jit(solution)/shard_map/ppermute | solution.py:603
  620.3 14.9 %collective-permute-start.57 = (bf16[272,1088]{1,0:T(8,128)(2,1)S(1)}, bf16[272,1088]{1,0:T(8,128)(2,1)S(1)}, u32[]{:S(2)}, u32[]{:S(2)}) collective-permute-start(bf16[272,1088]{1,0:T(8,128)(2,1)S(1)} %add_convert_fusion.6.refs_0_), channel_id=1, source_target_pairs={{0,16},{1,3},{2,18},{3,1},{16,0},{17,19},{18,2},{19,17},{4,20},{5,... | collective-permute-start | bytes 1775624 | tf_op jit(solution)/shard_map/ppermute | solution.py:603
  (71 other events, 716.1 us)
Sparse Core Ops, SparseCore 0:
  89.0 51.3 all-gather.2
  179.0 50.9 all-gather.4
  351.8 49.2 reduce-scatter.3
  455.4 48.8 reduce-scatter.5
  507.0 51.5 reduce-scatter.7

commit v7 on v6

--- a/solution.py
+++ b/solution.py
@@ -621,6 +621,11 @@
     return [whole] + [plane_swap(whole, kind) for kind in ("near", "core", "far")]
 
 
+def share_by_core(whole):
+    near = plane_swap(whole, "near")
+    return [whole, near, plane_swap(whole, "core"), plane_swap(near, "core")]
+
+
 def scatter_rows(values):
     return lax.psum_scatter(values, "fsdp", scatter_dimension=0, tiled=True)
 
@@ -640,7 +645,7 @@
     return jnp.stack([chosen((z - at) % 4, around) for at in range(4)])
 
 
-def reduce_vector(values, z):
+def scatter_vector(values, z):
     rows = [values[at] for at in range(4)]
     total = chosen(z, rows)
     for step in range(1, 4):
@@ -649,11 +654,13 @@
             "fsdp",
             [(device, (device + step) % 4) for device in range(4)],
         )
-    for bits in (1, 2, 4):
-        total = total + lax.ppermute(
-            total, ("dp", "ctx"), [(device, device ^ bits) for device in range(8)]
-        )
     return total
+
+
+def swap_sum(total, bits):
+    return total + lax.ppermute(
+        total, ("dp", "ctx"), [(device, device ^ bits) for device in range(8)]
+    )
 
 
 def product(left, right, dims):
@@ -1102,12 +1109,11 @@
         down_bias,
         up_bias,
     )
-    slots_in[3], cotangent, up_weight, down_weight, *pieces_in = pin(
-        (slots_in[3], cotangent, up_weight, down_weight, *pieces_in)
+    slots_in[3], up_weight, down_weight, *pieces_in = pin(
+        (slots_in[3], up_weight, down_weight, *pieces_in)
     )
     slots_in = [slots_in[0]] + [ctx_swap(slots_in[bits], bits) for bits in range(1, 4)]
     vectors = gather_vector(jnp.concatenate(pieces_in), z).astype(wide)
-    slots_back = spread(cotangent)
     up_piece = jnp.concatenate(
         [
             lax.dynamic_slice_in_dim(up_weight, at * width + mine * quarter, quarter, 1)
@@ -1115,9 +1121,11 @@
         ],
         axis=1,
     )
-    up_piece, vectors, *moved = pin((up_piece, vectors, *shards, *slots_in, *slots_back))
-    shards, slots_in, slots_back = moved[:3], moved[3:7], moved[7:]
+    up_piece, vectors, *moved = pin((up_piece, vectors, *shards, *slots_in))
+    shards, slots_in = moved[:3], moved[3:]
     near_shards = [plane_swap(shard, "near") for shard in shards]
+    cotangent, *near_shards = pin((cotangent, *near_shards))
+    slots_back = spread(cotangent)
     around = (
         sections
         + shards
@@ -1236,6 +1244,17 @@
     down_second = low_sum(down_terms[1], down_far_two)
     down_second, down_far, *hidden_low = pin((down_second, down_far, *hidden_low))
     down_close = plane_swap(down_second, "near")
+    up_terms = [turned_product(normed_two_low, hidden_low[slot]) for slot in (3, 2)]
+    down_first = low_sum(down_terms[0], down_far, down_close)
+    normed_two_low, down_first, *up_terms = pin((normed_two_low, down_first, *up_terms))
+    down_shard = scatter_rows(down_first)
+    up_terms += [turned_product(normed_two_low, hidden_low[slot]) for slot in (1, 0)]
+    up_terms = up_terms[::-1]
+    up_far, up_far_two = reduce_core(up_terms)
+    up_second = low_sum(up_terms[1], up_far_two)
+    up_second, up_far, moved, *hidden_low = pin((up_second, up_far, up_terms[0], *hidden_low))
+    up_terms[0] = moved
+    up_close = plane_swap(up_second, "near")
     middle_grad, middle_low, grad_low, back_sums = by_rows(
         back_kernel,
         "back",
@@ -1250,24 +1269,12 @@
         5,
         5,
     )
-    down_first = low_sum(down_terms[0], down_far, down_close)
-    down_first, normed_two_low = pin((down_first, pin((normed_two_low, middle_low))[0]))
-    down_shard = scatter_rows(down_first)
-    up_terms = [turned_product(normed_two_low, hidden_low[slot]) for slot in (3, 2)]
-    normed_two_low, *up_terms = pin((normed_two_low, *up_terms))
-    up_terms += [turned_product(normed_two_low, hidden_low[slot]) for slot in (1, 0)]
-    up_terms = up_terms[::-1]
-    up_far, up_far_two = reduce_core(up_terms)
     out_term = turned_product(attended, middle_low)
-    up_second = low_sum(up_terms[1], up_far_two)
-    grad_low, up_second, up_far, out_term, *up_terms = pin(
-        (grad_low, up_second, up_far, out_term, *up_terms)
-    )
-    up_close = plane_swap(up_second, "near")
+    up_first = low_sum(up_terms[0], up_far, up_close)
+    grad_low, out_term, up_first = pin((grad_low, out_term, up_first))
     in_grads = attend_back(
         place, queries, key_rows, value_rows, grad_low, attended, logs_one, seq_count, 0, 5, []
     )
-    up_first = low_sum(up_terms[0], up_far, up_close)
     up_first, down_shard, *in_grads = pin((up_first, down_shard, *in_grads))
     up_shard = scatter_rows(up_first)
     down_whole = low_sum(down_shard, plane_swap(down_shard, "other"))
@@ -1285,15 +1292,14 @@
         in_grads,
     )
     down_whole, *in_grads = pin((down_whole, *in_grads))
-    down_parts = share_out(down_whole)
+    down_parts = share_by_core(down_whole)
     in_terms = [turned_product(normed_low, grad) for grad in in_grads]
     section_grads = in_terms + [out_term]
     sections_mine = [chosen(kind, section_grads) for kind in classes]
     far, far_two = reduce_core(sections_mine)
     second = low_sum(sections_mine[1], far_two)
-    second, far, middle, *moved = pin((second, far, middle, *in_grads, *down_parts))
-    query_low, key_low, value_low = moved[:3]
-    down_parts = moved[3:]
+    second, far, middle, *in_grads = pin((second, far, middle, *in_grads))
+    query_low, key_low, value_low = in_grads
     close = plane_swap(second, "near")
     result_slots = by_rows(
         down_kernel,
@@ -1330,9 +1336,8 @@
         3,
         3,
     )
-    up_whole, last_sums, *moved = pin((up_whole, last_sums, *input_slots, *outputs))
-    input_slots, outputs = exchange(moved[:4]), moved[4:]
-    up_parts = share_out(up_whole)
+    moved = pin((*input_slots, *outputs, *down_parts))
+    input_slots, outputs, down_parts = exchange(moved[:4]), moved[4:8], moved[8:]
 
     back_sums = jnp.concatenate([hidden_sums, back_sums], axis=0)
     back_sums = jnp.sum(back_sums, axis=1)
@@ -1341,19 +1346,27 @@
     hidden_sums = jnp.stack(
         [chosen(slot_of[kind], hidden_sums) for kind in range(4)], axis=1
     ).reshape(4, 4 * quarter)
-    totals = reduce_vector(
-        jnp.concatenate(
-            [back_sums[at].reshape(4, quarter) for at in range(4, 8)]
-            + [last_sums[at].reshape(4, quarter) for at in range(4)]
-            + [hidden_sums],
-            axis=1,
+    totals = swap_sum(
+        scatter_vector(
+            jnp.concatenate(
+                [back_sums[at].reshape(4, quarter) for at in range(4, 8)]
+                + [last_sums[at].reshape(4, quarter) for at in range(4)]
+                + [hidden_sums],
+                axis=1,
+            ),
+            z,
         ),
-        z,
-    )
-    moved = pin((*input_slots, *up_parts))
+        1,
+    )
+    shard, up_whole, totals, *input_slots = pin((shard, up_whole, totals, *input_slots))
+    section_whole = low_sum(shard, plane_swap(shard, "other"))
+    up_parts = share_by_core(up_whole)
+    totals = swap_sum(totals, 2)
+    section_whole, totals, *up_parts = pin((section_whole, totals, *up_parts))
+    section_parts = share_out(section_whole)
+    totals = swap_sum(totals, 4)
     outputs = collect(outputs, low)
-    input_gradient = collect(moved[:4], wide)
-    up_parts = moved[4:]
+    input_gradient = collect(input_slots, wide)
     (up_sum,) = assemble(
         class_places,
         up_parts,
@@ -1364,12 +1377,12 @@
         [up_weight.shape],
     )
     down_sum = settle(class_places, down_parts, wide).reshape(down_weight.shape)
-    shard, outputs, input_gradient, totals, up_sum, down_sum = pin(
-        (shard, outputs, input_gradient, totals, up_sum, down_sum)
-    )
+    moved = pin((*section_parts, outputs, input_gradient, totals, up_sum, down_sum))
+    section_parts = moved[:4]
+    outputs, input_gradient, totals, up_sum, down_sum = moved[4:]
     in_sum, out_sum = assemble(
         class_places,
-        share_out(low_sum(shard, plane_swap(shard, "other"))),
+        section_parts,
         [[(0, 0, kind * width, width)] for kind in range(3)] + [[(1, 0, 0, width)]],
         [project_in.shape, project_out.shape],
     )

time: 653 us -> 664 us (1.017)
  waiting for transfers between devices: 173 us -> 186 us
    ppermute x3, waiting for transfers between devices: 22.1 us -> 35.2 us  [per_device_exchanged(): lax.ppermute(section, 'fsdp', [(device, (device + step) % 4) for device i...]
    ppermute x6, waiting for transfers between devices: 17 us -> 4.41 us  [the longest x3 2.76 us: swap_sum(): lax.ppermute(total, ('dp', 'ctx'), [(device, device ^ bits) for device in...]
    ppermute x12, waiting for transfers between devices: 41.9 us -> 54.2 us  [ctx_swap(): lax.ppermute(values, 'ctx', [(device, device ^ bits) for device in range(...]
    unnamed x113 -> x127, local copies, waits for them, and re-layouts: 17.8 us -> 20 us
  transfers between devices with their start and end apart: 65 -> 65, of which waited for: 29 -> 25; matrix products, arithmetic and copies ran while one was open for 12% -> 13% of each run, Pallas kernels for 42% -> 42%
where the time goes in v7:
time: 664 us; the launch traced here: 651 us
  Pallas kernels  274 us (41%)
  waiting for transfers between devices  186 us (28%)
  matrix products  60.4 us (9%)
  starting transfers between devices  48.2 us (7%)
  local copies, waits for them, and re-layouts  35.7 us (5%)
  other arithmetic  32.2 us (5%)
  between operations  15.2 us (2%)
    pallas_call x8, Pallas kernels, by_rows(): pl.pallas_call(kernel, grid=(rows // step,), in_specs=[tile] * len(tiled[...  155 us
    ppermute x36, waiting for transfers between devices, plane_swap(): lax.ppermute(values, ('dp', 'ctx'), [(device, plane_partner(device, kind)...  78.2 us
    dot_general x12, matrix products, product(): lax.dot_general(left, right, ((dims[:1], dims[1:]), ((), ())), preferred_...  60.4 us
    ppermute x12, waiting for transfers between devices, ctx_swap(): lax.ppermute(values, 'ctx', [(device, device ^ bits) for device in range(...  54.2 us
    pallas_call x2, Pallas kernels, attend_back(): pl.pallas_call(functools.partial(attend_back_kernel, count=count, width=w...  48 us
    ppermute x3, waiting for transfers between devices, per_device_exchanged(): lax.ppermute(section, 'fsdp', [(device, (device + step) % 4) for device i...  35.2 us
    pallas_call x1, Pallas kernels, attend(): pl.pallas_call(functools.partial(attend_kernel, count=count, width=width,...  32.3 us
    convert_element_type x8, other arithmetic, low_sum(): sum((term.astype(jnp.float32) for term in terms)).astype(jnp.bfloat16)  24.5 us
  transfers between devices with their start and end apart: 65, of which 25 were waited for; matrix products, arithmetic and copies ran while one was open for 13% of the time, Pallas kernels for 42%

profile of v7, /device:TPU:8, one launch (start us, length us, event | category | flops | bytes accessed | tf_op | source)
XLA Modules:
  0.0 651.4 jit_solution(10603419026713034234)
XLA Ops:
  7.3 3.6 fusion.11
  29.4 12.0 %collective-permute-done.7.refs_2_ = bf16[1088,256]{1,0:T(8,128)(2,1)} collective-permute-done((bf16[1088,256]{1,0:T(8,128)(2,1)}, bf16[1088,256]{1,0:T(8,128)(2,1)}, u32[]{:S(2)}, u32[]{:S(2)}) %collective-permute-start.7) | collective-permute-done | bytes 557088 | tf_op jit(solution)/shard_map/ppermute | solution.py:609
  41.5 23.3 %collective-permute-done.5.refs_10_ = bf16[272,1088]{1,0:T(8,128)(2,1)} collective-permute-done((bf16[272,1088]{1,0:T(8,128)(2,1)}, bf16[272,1088]{1,0:T(8,128)(2,1)}, u32[]{:S(2)}, u32[]{:S(2)}) %collective-permute-start.5) | collective-permute-done | bytes 591904 | tf_op jit(solution)/shard_map/ppermute | solution.py:1094
  64.8 12.0 %collective-permute-done.3.refs_8_ = bf16[272,1088]{1,0:T(8,128)(2,1)} collective-permute-done((bf16[272,1088]{1,0:T(8,128)(2,1)}, bf16[272,1088]{1,0:T(8,128)(2,1)}, u32[]{:S(2)}, u32[]{:S(2)}) %collective-permute-start.3) | collective-permute-done | bytes 591904 | tf_op jit(solution)/shard_map/ppermute | solution.py:1094
  81.5 6.0 collective-permute-done.9.refs_11_
  87.5 6.7 %collective-permute-done.10.refs_12_ = bf16[272,1088]{1,0:T(8,128)(2,1)} collective-permute-done((bf16[272,1088]{1,0:T(8,128)(2,1)}, bf16[272,1088]{1,0:T(8,128)(2,1)}, u32[]{:S(2)}, u32[]{:S(2)}) %collective-permute-start.10) | collective-permute-done | bytes 591904 | tf_op jit(solution)/shard_map/ppermute | solution.py:603
  94.2 6.7 %collective-permute-done.11.refs_13_ = bf16[272,1088]{1,0:T(8,128)(2,1)} collective-permute-done((bf16[272,1088]{1,0:T(8,128)(2,1)}, bf16[272,1088]{1,0:T(8,128)(2,1)}, u32[]{:S(2)}, u32[]{:S(2)}) %collective-permute-start.11) | collective-permute-done | bytes 591904 | tf_op jit(solution)/shard_map/ppermute | solution.py:603
  106.2 21.7 %front.1 = (bf16[1024,1088]{1,0:T(8,128)(2,1)}, bf16[1024,1088]{1,0:T(8,128)(2,1)}, bf16[1024,1088]{1,0:T(8,128)(2,1)}, bf16[1024,1088]{1,0:T(8,128)(2,1)}, bf16...) custom-call(s32[16]{0:T(128)} %stack.120.places_ref, f32[4,1088]{1,0:T(4,128)} %pad_maximum_fusion.1.vectors_ref, ...), custom_call_target="tpu_custom_call" | custom-call | flops 7272923136 | bytes 20471808 | tf_op jit(solution)/shard_map/front/pallas_call | solution.py:745
  132.3 32.3 %attend.1 = (bf16[1024,1088]{1,0:T(8,128)(2,1)S(1)}, f32[1024,128]{1,0:T(8,128)S(1)}) custom-call(s32[1]{0:T(128)} %bitcast.26.place_ref, bf16[1024,1088]{1,0:T(8,128)(2,1)S(1)} %copy-done.28, bf16[1024,1088]{1,0:T(8,128)(2,1)} %get-tuple-element.219.k_ref, bf16[1024,1088]{1,0:T(8,128)(2,1)} %get-tuple-element.220.v_ref), custom_call_target="tpu_custom_call" | custom-call | flops 19327352832 | bytes 9437184 | tf_op jit(solution)/shard_map/attend/pallas_call | solution.py:507
  172.2 10.8 %collective-permute-done.24.refs_3_ = bf16[1088,256]{1,0:T(8,128)(2,1)S(1)} collective-permute-done((bf16[1088,256]{1,0:T(8,128)(2,1)}, bf16[1088,256]{1,0:T(8,128)(2,1)S(1)}, u32[]{:S(2)}, u32[]{:S(2)}) %collective-permute-start.24) | collective-permute-done | bytes 557088 | tf_op jit(solution)/shard_map/ppermute | solution.py:609
  183.7 11.4 %collective-permute-done.23.refs_2_ = bf16[1088,256]{1,0:T(8,128)(2,1)S(1)} collective-permute-done((bf16[1088,256]{1,0:T(8,128)(2,1)}, bf16[1088,256]{1,0:T(8,128)(2,1)S(1)}, u32[]{:S(2)}, u32[]{:S(2)}) %collective-permute-start.23) | collective-permute-done | bytes 557088 | tf_op jit(solution)/shard_map/ppermute | solution.py:609
  200.6 10.6 %middle.1 = (f32[1024,1088]{1,0:T(8,128)}, bf16[1024,1088]{1,0:T(8,128)(2,1)}) custom-call(bf16[1024,1088]{1,0:T(8,128)(2,1)} %get-tuple-element.224.x_ref, bf16[1024,1088]{1,0:T(8,128)(2,1)} %copy-done.3, f32[3,1088]{1,0:T(4,128)} %pad_maximum_fusion.2.vectors_ref, bf16[16,272,1088]{2,1,0:T(8,128)(2,1)} %get-tuple-element.226.all_ref.refs_8_), custom_call_target="tpu_custom_call" | custom-call | flops 2424307712 | bytes 6823936 | tf_op jit(solution)/shard_map/middle/pallas_call | solution.py:1016
  211.2 17.4 %up.2 = (bf16[1024,1088]{1,0:T(8,128)(2,1)}, bf16[1024,1088]{1,0:T(8,128)(2,1)}, bf16[1024,1088]{1,0:T(8,128)(2,1)}, bf16[1024,1088]{1,0:T(8,128)(2,1)}) custom-call(bf16[1024,1088]{1,0:T(8,128)(2,1)} %get-tuple-element.265.h_ref, f32[2,1088]{1,0:T(2,128)} %pad_maximum_fusion.3.biases_ref, bf16[1088,1088]{1,0:T(8,128)(2,1)} %all-gather.3.cloned.1.call-done.refs_0_.refs_4_, ...), custom_call_target="tpu_custom_call" | custom-call | flops 4848615424 | bytes 13647872 | tf_op jit(solution)/shard_map/up/pallas_call | solution.py:1016
  228.6 17.8 %up.3 = (bf16[1024,1088]{1,0:T(8,128)(2,1)}, bf16[1024,1088]{1,0:T(8,128)(2,1)}, bf16[1024,1088]{1,0:T(8,128)(2,1)}, bf16[1024,1088]{1,0:T(8,128)(2,1)}) custom-call(bf16[1024,1088]{1,0:T(8,128)(2,1)} %get-tuple-element.265.h_ref, f32[2,1088]{1,0:T(2,128)} %pad_maximum_fusion.4.biases_ref, bf16[1088,1088]{1,0:T(8,128)(2,1)} %collective-permute-done.19.refs_0_.refs_5_, ...), custom_call_target="tpu_custom_call" | custom-call | flops 4848615424 | bytes 13647872 | tf_op jit(solution)/shard_map/up/pallas_call | solution.py:1016
  247.1 6.2 convolution_convert_fusion.11
  253.3 4.6 convolution_convert_fusion.10
  259.0 4.6 convolution_convert_fusion.8
  263.6 4.6 convolution_convert_fusion.9
  268.2 9.1 %collective-permute-done.21.refs_2_.refs_5_ = bf16[1088,1088]{1,0:T(8,128)(2,1)} collective-permute-done((bf16[1088,1088]{1,0:T(8,128)(2,1)}, bf16[1088,1088]{1,0:T(8,128)(2,1)}, u32[]{:S(2)}, u32[]{:S(2)}) %collective-permute-start.21) | collective-permute-done | bytes 2367520 | tf_op jit(solution)/shard_map/ppermute | solution.py:603
  278.0 14.0 %hidden.2 = (bf16[1024,1088]{1,0:T(8,128)(2,1)}, bf16[1024,1088]{1,0:T(8,128)(2,1)}, f32[3,8,1088]{2,1,0:T(8,128)}) custom-call(bf16[1024,1088]{1,0:T(8,128)(2,1)} %copy-done.2, bf16[1024,1088]{1,0:T(8,128)(2,1)} %get-tuple-element.250.refs_0_, bf16[1024,1088]{1,0:T(8,128)(2,1)} %get-tuple-element.251.refs_1_, ...), custom_call_target="tpu_custom_call" | custom-call | flops 4848615424 | bytes 13647872 | tf_op jit(solution)/shard_map/hidden/pallas_call | solution.py:1016
  292.0 4.5 add_convert_fusion.4
  296.5 14.0 %hidden.3 = (bf16[1024,1088]{1,0:T(8,128)(2,1)}, bf16[1024,1088]{1,0:T(8,128)(2,1)}, f32[3,8,1088]{2,1,0:T(8,128)}) custom-call(bf16[1024,1088]{1,0:T(8,128)(2,1)} %copy-done.2, bf16[1024,1088]{1,0:T(8,128)(2,1)} %get-tuple-element.255.refs_0_, bf16[1024,1088]{1,0:T(8,128)(2,1)} %get-tuple-element.256.refs_1_, ...), custom_call_target="tpu_custom_call" | custom-call | flops 4848615424 | bytes 13647872 | tf_op jit(solution)/shard_map/hidden/pallas_call | solution.py:1016
  311.2 7.2 %convolution_convert_fusion.7 = bf16[1088,1088]{1,0:T(8,128)(2,1)} fusion(bf16[1024,1088]{1,0:T(8,128)(2,1)} %get-tuple-element.265.h_ref, bf16[1024,1088]{1,0:T(8,128)(2,1)} %get-tuple-element.273.refs_3_), kind=kOutput, calls=%fused_computation.9 | convolution fusion | flops 2425491456 | bytes 6823936 | tf_op jit(solution)/shard_map/dot_general | solution.py:667
  318.5 4.6 convolution_convert_fusion.6
  323.1 18.2 %collective-permute-done.29 = bf16[1088,1088]{1,0:T(8,128)(2,1)S(1)} collective-permute-done((bf16[1088,1088]{1,0:T(8,128)(2,1)}, bf16[1088,1088]{1,0:T(8,128)(2,1)S(1)}, u32[]{:S(2)}, u32[]{:S(2)}) %collective-permute-start.29) | collective-permute-done | bytes 2367520 | tf_op jit(solution)/shard_map/ppermute | solution.py:603
  344.2 7.1 %convolution_convert_fusion.4 = bf16[1088,1088]{1,0:T(8,128)(2,1)} fusion(bf16[1024,1088]{1,0:T(8,128)(2,1)} %get-tuple-element.265.h_ref, bf16[1024,1088]{1,0:T(8,128)(2,1)} %get-tuple-element.270.refs_0_), kind=kOutput, calls=%fused_computation.4 | convolution fusion | flops 2425491456 | bytes 6823936 | tf_op jit(solution)/shard_map/dot_general | solution.py:667
  351.9 5.0 fusion.2
  358.2 31.8 %back.1 = (f32[1024,1088]{1,0:T(8,128)}, bf16[1024,1088]{1,0:T(8,128)(2,1)}, bf16[1024,1088]{1,0:T(8,128)(2,1)}, f32[3,8,1088]{2,1,0:T(8,128)}) custom-call(bf16[1024,1088]{1,0:T(8,128)(2,1)} %copy-done.2, f32[1024,1088]{1,0:T(8,128)} %get-tuple-element.301.middle_ref, f32[1,1088]{1,0:T(1,128)} %copy-done.42, bf16[1024,1088]{1,0:T(8,128)(2,1)} %get-tuple-element.270.refs_0_, ...), custom_call_target="tpu_custom_call" | custom-call | flops 12121538560 | bytes 34119680 | tf_op jit(solution)/shard_map/back/pallas_call | solution.py:1016
  390.0 6.4 convolution_convert_fusion.3
  396.4 5.0 add_convert_fusion.2
  401.3 26.3 %attend_back.2 = (bf16[1024,1088]{1,0:T(8,128)(2,1)S(1)}, bf16[1024,1088]{1,0:T(8,128)(2,1)S(1)}, bf16[1024,1088]{1,0:T(8,128)(2,1)}) custom-call(s32[1]{0:T(128)} %bitcast.26.place_ref, bf16[1024,1088]{1,0:T(8,128)(2,1)} %get-tuple-element.218.q_ref, bf16[1024,1088]{1,0:T(8,128)(2,1)} %get-tuple-element.219.k_ref, ...), custom_call_target="tpu_custom_call" | custom-call | flops 20132659200 | bytes 10485760 | tf_op jit(solution)/shard_map/attend_back/pallas_call | solution.py:541
  432.2 21.7 %attend_back.3 = (bf16[1024,1088]{1,0:T(8,128)(2,1)S(1)}, bf16[1024,1088]{1,0:T(8,128)(2,1)S(1)}, bf16[1024,1088]{1,0:T(8,128)(2,1)}) custom-call(s32[1]{0:T(128)} %bitcast.26.place_ref, bf16[1024,1088]{1,0:T(8,128)(2,1)} %get-tuple-element.218.q_ref, ...), custom_call_target="tpu_custom_call", output_to_operand_aliasing={{0}: (7, {}), {1}: (8, {}), {2}: (9, {})} | custom-call | flops 16106127360 | bytes 8388608 | tf_op jit(solution)/shard_map/attend_back/pallas_call | solution.py:541
  455.5 3.1 convolution_convert_fusion.1
  458.7 3.1 convolution_convert_fusion
  462.0 3.9 select_select_fusion
  466.5 7.0 %collective-permute-done.34 = bf16[1088,1088]{1,0:T(8,128)(2,1)S(1)} collective-permute-done((bf16[1088,1088]{1,0:T(8,128)(2,1)S(1)}, bf16[1088,1088]{1,0:T(8,128)(2,1)S(1)}, u32[]{:S(2)}, u32[]{:S(2)}) %collective-permute-start.34) | collective-permute-done | bytes 2367520 | tf_op jit(solution)/shard_map/ppermute | solution.py:603
  473.5 3.2 add_convert_fusion.1
  479.0 25.9 %down.1 = (bf16[1088,256]{1,0:T(8,128)(2,1)}, bf16[1088,256]{1,0:T(8,128)(2,1)}, bf16[1088,256]{1,0:T(8,128)(2,1)}, bf16[1088,256]{1,0:T(8,128)(2,1)}) custom-call(f32[1024,1088]{1,0:T(8,128)} %get-tuple-element.301.middle_ref, f32[1,1088]{1,0:T(1,128)} %reshape.446.vectors_ref, bf16[1024,1088]{1,0:T(8,128)(2,1)} %get-tuple-element.241.refs_0_, ...), custom_call_target="tpu_custom_call" | custom-call | flops 9697230848 | bytes 27295744 | tf_op jit(solution)/shard_map/down/pallas_call | solution.py:1016
  507.5 6.6 %add_convert_fusion = bf16[1088,1088]{1,0:T(8,128)(2,1)} fusion(bf16[1088,1088]{1,0:T(8,128)(2,1)} %collective-permute-done.36, bf16[1088,1088]{1,0:T(8,128)(2,1)} %collective-permute-done.35, bf16[1088,1088]{1,0:T(8,128)(2,1)} %copy-done.32, bf16[1088,1088]{1,0:T(8,128)(2,1)} %copy-done.30, bf16[1088,1088]{1,0:T(8,128)(2,1)} %copy-done.31, ...), kind=kLoop, calls=%fused_computation.15 | loop fusion | flops 10653696 | bytes 16572419 | tf_op jit(solution)/shard_map/convert_element_type | solution.py:613
  514.0 13.2 %reduce-scatter.6.cloned.1.call-done = bf16[272,1088]{1,0:T(8,128)(2,1)} async-done(((bf16[1088,1088]{1,0:T(8,128)(2,1)}), bf16[272,1088]{1,0:T(8,128)(2,1)}) %reduce-scatter.6.cloned.1.call-update) | async-done | bytes 591888 | tf_op jit(solution)/shard_map/reduce_scatter | solution.py:630
  530.1 7.7 %collective-permute-done.45.refs_1_ = bf16[272,1088]{1,0:T(8,128)(2,1)S(1)} collective-permute-done((bf16[272,1088]{1,0:T(8,128)(2,1)S(1)}, bf16[272,1088]{1,0:T(8,128)(2,1)S(1)}, u32[]{:S(2)}, u32[]{:S(2)}) %collective-permute-start.45) | collective-permute-done | bytes 591904 | tf_op jit(solution)/shard_map/ppermute | solution.py:603
  539.8 23.7 %last.1 = (bf16[1088,256]{1,0:T(8,128)(2,1)}, bf16[1088,256]{1,0:T(8,128)(2,1)}, bf16[1088,256]{1,0:T(8,128)(2,1)}, bf16[1088,256]{1,0:T(8,128)(2,1)}, f32[4,8,1088]{2,1,0:T(8,128)}) custom-call(bf16[1024,1088]{1,0:T(8,128)(2,1)} %copy-done.23, bf16[1024,1088]{1,0:T(8,128)(2,1)} %copy-done.27, bf16[1024,1088]{1,0:T(8,128)(2,1)} %get-tuple-element.313.v_ref, ...), custom_call_target="tpu_custom_call" | custom-call | flops 7272923136 | bytes 20471808 | tf_op jit(solution)/shard_map/last/pallas_call | solution.py:1016
  578.7 8.9 %collective-permute-done.49.refs_2_ = bf16[1088,256]{1,0:T(8,128)(2,1)S(1)} collective-permute-done((bf16[1088,256]{1,0:T(8,128)(2,1)}, bf16[1088,256]{1,0:T(8,128)(2,1)S(1)}, u32[]{:S(2)}, u32[]{:S(2)}) %collective-permute-start.49) | collective-permute-done | bytes 557088 | tf_op jit(solution)/shard_map/ppermute | solution.py:609
  588.5 9.9 %collective-permute-done.50.refs_3_ = bf16[1088,256]{1,0:T(8,128)(2,1)S(1)} collective-permute-done((bf16[1088,256]{1,0:T(8,128)(2,1)}, bf16[1088,256]{1,0:T(8,128)(2,1)S(1)}, u32[]{:S(2)}, u32[]{:S(2)}) %collective-permute-start.50) | collective-permute-done | bytes 557088 | tf_op jit(solution)/shard_map/ppermute | solution.py:609
  601.9 13.6 %collective-permute-done.53.refs_1_ = bf16[272,1088]{1,0:T(8,128)(2,1)S(1)} collective-permute-done((bf16[272,1088]{1,0:T(8,128)(2,1)S(1)}, bf16[272,1088]{1,0:T(8,128)(2,1)S(1)}, u32[]{:S(2)}, u32[]{:S(2)}) %collective-permute-start.53) | collective-permute-done | bytes 591904 | tf_op jit(solution)/shard_map/ppermute | solution.py:603
  629.8 3.2 settle.5
  635.9 4.1 assemble.2
  641.3 3.4 assemble.3
  (323 shorter events, 108.9 us)
Async XLA Ops:
  7.2 121.0 %all-gather.3.cloned.1.call-start = ((), (), s32[]{:S(2)}) async-start(), calls=%async_computation.3 | async-start | bytes 3133440 | tf_op jit(solution)/shard_map/all_gather | solution.py:1140
  13.9 15.2 %collective-permute-start.8 = (bf16[1088,256]{1,0:T(8,128)(2,1)}, bf16[1088,256]{1,0:T(8,128)(2,1)}, u32[]{:S(2)}, u32[]{:S(2)}) collective-permute-start(bf16[1088,256]{1,0:T(8,128)(2,1)} %get-tuple-element.200), channel_id=1, source_target_pairs={{0,3},{1,2},{2,1},{3,0},{4,7},{5,6},{6,5},{7,4},{8,11},{9,10},{10,... | collective-permute-start | bytes 1671176 | tf_op jit(solution)/shard_map/ppermute | solution.py:609
  20.6 44.2 %collective-permute-start.5 = (bf16[272,1088]{1,0:T(8,128)(2,1)}, bf16[272,1088]{1,0:T(8,128)(2,1)}, u32[]{:S(2)}, u32[]{:S(2)}) collective-permute-start(bf16[272,1088]{1,0:T(8,128)(2,1)} %get-tuple-element.199), channel_id=1, source_target_pairs={{0,12},{4,0},{8,4},{12,8},{1,13},{5,1},{9,5},{13,9},{2,14},{6,2},{... | collective-permute-start | bytes 1775624 | tf_op jit(solution)/shard_map/ppermute | solution.py:1094
  23.5 41.3 %collective-permute-start.4 = (bf16[272,1088]{1,0:T(8,128)(2,1)}, bf16[272,1088]{1,0:T(8,128)(2,1)}, u32[]{:S(2)}, u32[]{:S(2)}) collective-permute-start(bf16[272,1088]{1,0:T(8,128)(2,1)} %get-tuple-element.199), channel_id=1, source_target_pairs={{0,8},{4,12},{8,0},{12,4},{1,9},{5,13},{9,1},{13,5},{2,10},{6,14},... | collective-permute-start | bytes 1775624 | tf_op jit(solution)/shard_map/ppermute | solution.py:1094
  25.0 51.8 %collective-permute-start.3 = (bf16[272,1088]{1,0:T(8,128)(2,1)}, bf16[272,1088]{1,0:T(8,128)(2,1)}, u32[]{:S(2)}, u32[]{:S(2)}) collective-permute-start(bf16[272,1088]{1,0:T(8,128)(2,1)} %get-tuple-element.199), channel_id=1, source_target_pairs={{0,4},{4,8},{8,12},{12,0},{1,5},{5,9},{9,13},{13,1},{2,6},{6,10},{... | collective-permute-start | bytes 1775624 | tf_op jit(solution)/shard_map/ppermute | solution.py:1094
  27.3 14.2 %collective-permute-start.7 = (bf16[1088,256]{1,0:T(8,128)(2,1)}, bf16[1088,256]{1,0:T(8,128)(2,1)}, u32[]{:S(2)}, u32[]{:S(2)}) collective-permute-start(bf16[1088,256]{1,0:T(8,128)(2,1)} %get-tuple-element.387), channel_id=1, source_target_pairs={{0,2},{1,3},{2,0},{3,1},{4,6},{5,7},{6,4},{7,5},{8,10},{9,11},{10,... | collective-permute-start | bytes 1671176 | tf_op jit(solution)/shard_map/ppermute | solution.py:609
  29.1 12.4 %collective-permute-start.6 = (bf16[1088,256]{1,0:T(8,128)(2,1)}, bf16[1088,256]{1,0:T(8,128)(2,1)}, u32[]{:S(2)}, u32[]{:S(2)}) collective-permute-start(bf16[1088,256]{1,0:T(8,128)(2,1)} %get-tuple-element.388), channel_id=1, source_target_pairs={{0,1},{1,0},{2,3},{3,2},{4,5},{5,4},{6,7},{7,6},{8,9},{9,8},{10,11... | collective-permute-start | bytes 1671176 | tf_op jit(solution)/shard_map/ppermute | solution.py:609
  76.7 169.6 %all-gather.5.cloned.1.call-start = ((), (), s32[]{:S(2)}) async-start(), calls=%async_computation.4 | async-start | bytes 3133440 | tf_op jit(solution)/shard_map/all_gather | solution.py:1165
  78.4 15.8 %collective-permute-start.10 = (bf16[272,1088]{1,0:T(8,128)(2,1)}, bf16[272,1088]{1,0:T(8,128)(2,1)}, u32[]{:S(2)}, u32[]{:S(2)}) collective-permute-start(bf16[272,1088]{1,0:T(8,128)(2,1)} %collective-permute-done.4.refs_9_), channel_id=1, source_target_pairs={{0,16},{1,3},{2,18},{3,1},{16,0},{17,19},{18,2},{19,17},{4,20},{5,... | collective-permute-start | bytes 1775624 | tf_op jit(solution)/shard_map/ppermute | solution.py:603
  78.9 22.0 %collective-permute-start.11 = (bf16[272,1088]{1,0:T(8,128)(2,1)}, bf16[272,1088]{1,0:T(8,128)(2,1)}, u32[]{:S(2)}, u32[]{:S(2)}) collective-permute-start(bf16[272,1088]{1,0:T(8,128)(2,1)} %collective-permute-done.5.refs_10_), channel_id=1, source_target_pairs={{0,16},{1,3},{2,18},{3,1},{16,0},{17,19},{18,2},{19,17},{4,20},{5,... | collective-permute-start | bytes 1775624 | tf_op jit(solution)/shard_map/ppermute | solution.py:603
  80.4 21.0 %collective-permute-start.12 = (bf16[272,1088]{1,0:T(8,128)(2,1)}, bf16[272,1088]{1,0:T(8,128)(2,1)}, u32[]{:S(2)}, u32[]{:S(2)}) collective-permute-start(bf16[272,1088]{1,0:T(8,128)(2,1)} %collective-permute-done.3.refs_8_), channel_id=1, source_target_pairs={{0,1},{1,0},{2,3},{3,2},{16,17},{17,16},{18,19},{19,18},{4,5},{5,4... | collective-permute-start | bytes 1775624 | tf_op jit(solution)/shard_map/ppermute | solution.py:603
  81.0 25.2 %collective-permute-start.13 = (bf16[272,1088]{1,0:T(8,128)(2,1)}, bf16[272,1088]{1,0:T(8,128)(2,1)}, u32[]{:S(2)}, u32[]{:S(2)}) collective-permute-start(bf16[272,1088]{1,0:T(8,128)(2,1)} %collective-permute-done.4.refs_9_), channel_id=1, source_target_pairs={{0,1},{1,0},{2,3},{3,2},{16,17},{17,16},{18,19},{19,18},{4,5},{5,4... | collective-permute-start | bytes 1775624 | tf_op jit(solution)/shard_map/ppermute | solution.py:603
  87.5 18.7 %collective-permute-start.14 = (bf16[272,1088]{1,0:T(8,128)(2,1)}, bf16[272,1088]{1,0:T(8,128)(2,1)}, u32[]{:S(2)}, u32[]{:S(2)}) collective-permute-start(bf16[272,1088]{1,0:T(8,128)(2,1)} %collective-permute-done.5.refs_10_), channel_id=1, source_target_pairs={{0,1},{1,0},{2,3},{3,2},{16,17},{17,16},{18,19},{19,18},{4,5},{5,4... | collective-permute-start | bytes 1775624 | tf_op jit(solution)/shard_map/ppermute | solution.py:603
  128.2 38.5 %collective-permute-start.19 = (bf16[1088,1088]{1,0:T(8,128)(2,1)}, bf16[1088,1088]{1,0:T(8,128)(2,1)}, u32[]{:S(2)}, u32[]{:S(2)}) collective-permute-start(bf16[1088,1088]{1,0:T(8,128)(2,1)} %all-gather.3.cloned.1.call-done.refs_0_.refs_4_), channel_id=1, source_target_pairs={{0,16},{1,3},{2,18},{3,1},{16,0},{17,19},{18,2},{19,17},{4,20},{5,... | collective-permute-start | bytes 7102472 | tf_op jit(solution)/shard_map/ppermute | solution.py:603
  129.7 37.1 %collective-permute-start.18 = (bf16[1088,1088]{1,0:T(8,128)(2,1)}, bf16[1088,1088]{1,0:T(8,128)(2,1)}, u32[]{:S(2)}, u32[]{:S(2)}) collective-permute-start(bf16[1088,1088]{1,0:T(8,128)(2,1)} %all-gather.3.cloned.1.call-done.refs_0_.refs_4_), channel_id=1, source_target_pairs={{0,1},{1,0},{2,3},{3,2},{16,17},{17,16},{18,19},{19,18},{4,5},{5,4... | collective-permute-start | bytes 7102472 | tf_op jit(solution)/shard_map/ppermute | solution.py:603
  166.8 262.2 %reduce-scatter.4.cloned.1.call-start = ((), (), s32[]{:S(2)}) async-start(), calls=%async_computation.5 | async-start | bytes 3133440 | tf_op jit(solution)/shard_map/reduce_scatter | solution.py:630
  167.0 61.5 %collective-permute-start.20 = (bf16[1088,1088]{1,0:T(8,128)(2,1)}, bf16[1088,1088]{1,0:T(8,128)(2,1)}, u32[]{:S(2)}, u32[]{:S(2)}) collective-permute-start(bf16[1088,1088]{1,0:T(8,128)(2,1)} %collective-permute-done.19.refs_0_.refs_5_), channel_id=1, source_target_pairs={{0,1},{1,0},{2,3},{3,2},{16,17},{17,16},{18,19},{19,18},{4,5},{5,4... | collective-permute-start | bytes 7102472 | tf_op jit(solution)/shard_map/ppermute | solution.py:603
  167.9 15.0 %collective-permute-start.24 = (bf16[1088,256]{1,0:T(8,128)(2,1)}, bf16[1088,256]{1,0:T(8,128)(2,1)S(1)}, u32[]{:S(2)}, u32[]{:S(2)}) collective-permute-start(bf16[1088,256]{1,0:T(8,128)(2,1)} %get-tuple-element.383), channel_id=1, source_target_pairs={{0,3},{1,2},{2,1},{3,0},{4,7},{5,6},{6,5},{7,4},{8,11},{9,10},{10,... | collective-permute-start | bytes 1671176 | tf_op jit(solution)/shard_map/ppermute | solution.py:609
  169.2 25.9 %collective-permute-start.23 = (bf16[1088,256]{1,0:T(8,128)(2,1)}, bf16[1088,256]{1,0:T(8,128)(2,1)S(1)}, u32[]{:S(2)}, u32[]{:S(2)}) collective-permute-start(bf16[1088,256]{1,0:T(8,128)(2,1)} %get-tuple-element.384), channel_id=1, source_target_pairs={{0,2},{1,3},{2,0},{3,1},{4,6},{5,7},{6,4},{7,5},{8,10},{9,11},{10,... | collective-permute-start | bytes 1671176 | tf_op jit(solution)/shard_map/ppermute | solution.py:609
  169.7 26.2 %collective-permute-start.22 = (bf16[1088,256]{1,0:T(8,128)(2,1)S(1)}, bf16[1088,256]{1,0:T(8,128)(2,1)S(1)}, u32[]{:S(2)}, u32[]{:S(2)}) collective-permute-start(bf16[1088,256]{1,0:T(8,128)(2,1)S(1)} %copy-done.36), channel_id=1, source_target_pairs={{0,1},{1,0},{2,3},{3,2},{4,5},{5,4},{6,7},{7,6},{8,9},{9,8},{10,11... | collective-permute-start | bytes 1671176 | tf_op jit(solution)/shard_map/ppermute | solution.py:609
  246.4 31.6 %collective-permute-start.27 = (bf16[1088,1088]{1,0:T(8,128)(2,1)}, bf16[1088,1088]{1,0:T(8,128)(2,1)}, u32[]{:S(2)}, u32[]{:S(2)}) collective-permute-start(bf16[1088,1088]{1,0:T(8,128)(2,1)} %all-gather.5.cloned.1.call-done.refs_2_.refs_4_), channel_id=1, source_target_pairs={{0,1},{1,0},{2,3},{3,2},{16,17},{17,16},{18,19},{19,18},{4,5},{5,4... | collective-permute-start | bytes 7102472 | tf_op jit(solution)/shard_map/ppermute | solution.py:603
  246.5 30.8 %collective-permute-start.21 = (bf16[1088,1088]{1,0:T(8,128)(2,1)}, bf16[1088,1088]{1,0:T(8,128)(2,1)}, u32[]{:S(2)}, u32[]{:S(2)}) collective-permute-start(bf16[1088,1088]{1,0:T(8,128)(2,1)} %all-gather.5.cloned.1.call-done.refs_2_.refs_4_), channel_id=1, source_target_pairs={{0,16},{1,3},{2,18},{3,1},{16,0},{17,19},{18,2},{19,17},{4,20},{5,... | collective-permute-start | bytes 7102472 | tf_op jit(solution)/shard_map/ppermute | solution.py:603
  257.9 34.0 %collective-permute-start.25 = (bf16[1088,1088]{1,0:T(8,128)(2,1)}, bf16[1088,1088]{1,0:T(8,128)(2,1)}, u32[]{:S(2)}, u32[]{:S(2)}) collective-permute-start(bf16[1088,1088]{1,0:T(8,128)(2,1)} %convolution_convert_fusion.11), channel_id=1, source_target_pairs={{0,1},{1,0},{2,3},{3,2},{16,17},{17,16},{18,19},{19,18},{4,5},{5,4... | collective-permute-start | bytes 7102472 | tf_op jit(solution)/shard_map/ppermute | solution.py:603
  277.3 19.2 %collective-permute-start.28 = (bf16[1088,1088]{1,0:T(8,128)(2,1)}, bf16[1088,1088]{1,0:T(8,128)(2,1)}, u32[]{:S(2)}, u32[]{:S(2)}) collective-permute-start(bf16[1088,1088]{1,0:T(8,128)(2,1)} %collective-permute-done.21.refs_2_.refs_5_), channel_id=1, source_target_pairs={{0,1},{1,0},{2,3},{3,2},{16,17},{17,16},{18,19},{19,18},{4,5},{5,4... | collective-permute-start | bytes 7102472 | tf_op jit(solution)/shard_map/ppermute | solution.py:603
  277.5 33.1 %collective-permute-start.26 = (bf16[1088,1088]{1,0:T(8,128)(2,1)}, bf16[1088,1088]{1,0:T(8,128)(2,1)S(1)}, u32[]{:S(2)}, u32[]{:S(2)}) collective-permute-start(bf16[1088,1088]{1,0:T(8,128)(2,1)} %convolution_convert_fusion.10), channel_id=1, source_target_pairs={{0,1},{1,0},{2,3},{3,2},{16,17},{17,16},{18,19},{19,18},{4,5},{5,4... | collective-permute-start | bytes 7102472 | tf_op jit(solution)/shard_map/ppermute | solution.py:603
  310.5 30.7 %collective-permute-start.29 = (bf16[1088,1088]{1,0:T(8,128)(2,1)}, bf16[1088,1088]{1,0:T(8,128)(2,1)S(1)}, u32[]{:S(2)}, u32[]{:S(2)}) collective-permute-start(bf16[1088,1088]{1,0:T(8,128)(2,1)} %add_convert_fusion.4), channel_id=1, source_target_pairs={{0,16},{1,3},{2,18},{3,1},{16,0},{17,19},{18,2},{19,17},{4,20},{5,... | collective-permute-start | bytes 7102472 | tf_op jit(solution)/shard_map/ppermute | solution.py:603
  343.7 13.2 %collective-permute-start.31 = (bf16[1088,1088]{1,0:T(8,128)(2,1)}, bf16[1088,1088]{1,0:T(8,128)(2,1)}, u32[]{:S(2)}, u32[]{:S(2)}) collective-permute-start(bf16[1088,1088]{1,0:T(8,128)(2,1)} %convolution_convert_fusion.6), channel_id=1, source_target_pairs={{0,1},{1,0},{2,3},{3,2},{16,17},{17,16},{18,19},{19,18},{4,5},{5,4... | collective-permute-start | bytes 7102472 | tf_op jit(solution)/shard_map/ppermute | solution.py:603
  356.8 39.5 %collective-permute-start.32 = (bf16[1088,1088]{1,0:T(8,128)(2,1)}, bf16[1088,1088]{1,0:T(8,128)(2,1)}, u32[]{:S(2)}, u32[]{:S(2)}) collective-permute-start(bf16[1088,1088]{1,0:T(8,128)(2,1)} %fusion.2), channel_id=1, source_target_pairs={{0,16},{1,3},{2,18},{3,1},{16,0},{17,19},{18,2},{19,17},{4,20},{5,... | collective-permute-start | bytes 7102472 | tf_op jit(solution)/shard_map/ppermute | solution.py:603
  358.1 169.1 %reduce-scatter.6.cloned.1.call-start = ((), (), s32[]{:S(2)}) async-start(), calls=%async_computation.6 | async-start | bytes 3133440 | tf_op jit(solution)/shard_map/reduce_scatter | solution.py:630
  429.0 26.3 %collective-permute-start.33 = (bf16[272,1088]{1,0:T(8,128)(2,1)}, bf16[272,1088]{1,0:T(8,128)(2,1)S(1)}, u32[]{:S(2)}, u32[]{:S(2)}) collective-permute-start(bf16[272,1088]{1,0:T(8,128)(2,1)} %reduce-scatter.4.cloned.1.call-done), channel_id=1, source_target_pairs={{0,2},{1,17},{2,0},{3,19},{16,18},{17,1},{18,16},{19,3},{4,6},{5,2... | collective-permute-start | bytes 1775624 | tf_op jit(solution)/shard_map/ppermute | solution.py:603
  466.0 10.7 %collective-permute-start.35 = (bf16[1088,1088]{1,0:T(8,128)(2,1)S(1)}, bf16[1088,1088]{1,0:T(8,128)(2,1)}, u32[]{:S(2)}, u32[]{:S(2)}) collective-permute-start(bf16[1088,1088]{1,0:T(8,128)(2,1)S(1)} %get-tuple-element.377), channel_id=1, source_target_pairs={{0,1},{1,0},{2,3},{3,2},{16,17},{17,16},{18,19},{19,18},{4,5},{5,4... | collective-permute-start | bytes 7102472 | tf_op jit(solution)/shard_map/ppermute | solution.py:603
  476.7 30.8 %collective-permute-start.36 = (bf16[1088,1088]{1,0:T(8,128)(2,1)}, bf16[1088,1088]{1,0:T(8,128)(2,1)}, u32[]{:S(2)}, u32[]{:S(2)}) collective-permute-start(bf16[1088,1088]{1,0:T(8,128)(2,1)} %add_convert_fusion.1), channel_id=1, source_target_pairs={{0,16},{1,3},{2,18},{3,1},{16,0},{17,19},{18,2},{19,17},{4,20},{5,... | collective-permute-start | bytes 7102472 | tf_op jit(solution)/shard_map/ppermute | solution.py:603
  478.2 120.9 %reduce-scatter.8.cloned.1.call-start = ((), (), s32[]{:S(2)}) async-start(), calls=%async_computation.7 | async-start | bytes 3133440 | tf_op jit(solution)/shard_map/reduce_scatter | solution.py:630
  530.1 34.5 %collective-permute-start.46 = (bf16[272,1088]{1,0:T(8,128)(2,1)S(1)}, bf16[272,1088]{1,0:T(8,128)(2,1)S(1)}, u32[]{:S(2)}, u32[]{:S(2)}) collective-permute-start(bf16[272,1088]{1,0:T(8,128)(2,1)S(1)} %add_convert_fusion.7.refs_0_), channel_id=1, source_target_pairs={{0,1},{1,0},{2,3},{3,2},{16,17},{17,16},{18,19},{19,18},{4,5},{5,4... | collective-permute-start | bytes 1775624 | tf_op jit(solution)/shard_map/ppermute | solution.py:603
  537.8 28.9 %collective-permute-start.47 = (bf16[272,1088]{1,0:T(8,128)(2,1)S(1)}, bf16[272,1088]{1,0:T(8,128)(2,1)S(1)}, u32[]{:S(2)}, u32[]{:S(2)}) collective-permute-start(bf16[272,1088]{1,0:T(8,128)(2,1)S(1)} %collective-permute-done.45.refs_1_), channel_id=1, source_target_pairs={{0,1},{1,0},{2,3},{3,2},{16,17},{17,16},{18,19},{19,18},{4,5},{5,4... | collective-permute-start | bytes 1775624 | tf_op jit(solution)/shard_map/ppermute | solution.py:603
  537.8 30.8 %collective-permute-start.42 = (bf16[1088,256]{1,0:T(8,128)(2,1)}, bf16[1088,256]{1,0:T(8,128)(2,1)S(1)}, u32[]{:S(2)}, u32[]{:S(2)}) collective-permute-start(bf16[1088,256]{1,0:T(8,128)(2,1)} %get-tuple-element.321), channel_id=1, source_target_pairs={{0,1},{1,0},{2,3},{3,2},{4,5},{5,4},{6,7},{7,6},{8,9},{9,8},{10,11... | collective-permute-start | bytes 1671176 | tf_op jit(solution)/shard_map/ppermute | solution.py:609
  538.3 32.7 %collective-permute-start.43 = (bf16[1088,256]{1,0:T(8,128)(2,1)}, bf16[1088,256]{1,0:T(8,128)(2,1)}, u32[]{:S(2)}, u32[]{:S(2)}) collective-permute-start(bf16[1088,256]{1,0:T(8,128)(2,1)} %get-tuple-element.322), channel_id=1, source_target_pairs={{0,2},{1,3},{2,0},{3,1},{4,6},{5,7},{6,4},{7,5},{8,10},{9,11},{10,... | collective-permute-start | bytes 1671176 | tf_op jit(solution)/shard_map/ppermute | solution.py:609
  539.8 31.7 %collective-permute-start.44 = (bf16[1088,256]{1,0:T(8,128)(2,1)}, bf16[1088,256]{1,0:T(8,128)(2,1)}, u32[]{:S(2)}, u32[]{:S(2)}) collective-permute-start(bf16[1088,256]{1,0:T(8,128)(2,1)} %get-tuple-element.323), channel_id=1, source_target_pairs={{0,3},{1,2},{2,1},{3,0},{4,7},{5,6},{6,5},{7,4},{8,11},{9,10},{10,... | collective-permute-start | bytes 1671176 | tf_op jit(solution)/shard_map/ppermute | solution.py:609
  564.5 12.0 %collective-permute-start.37 = (bf16[272,1088]{1,0:T(8,128)(2,1)}, bf16[272,1088]{1,0:T(8,128)(2,1)}, u32[]{:S(2)}, u32[]{:S(2)}) collective-permute-start(bf16[272,1088]{1,0:T(8,128)(2,1)} %reduce-scatter.6.cloned.1.call-done), channel_id=1, source_target_pairs={{0,2},{1,17},{2,0},{3,19},{16,18},{17,1},{18,16},{19,3},{4,6},{5,2... | collective-permute-start | bytes 1775624 | tf_op jit(solution)/shard_map/ppermute | solution.py:603
  571.9 15.7 %collective-permute-start.49 = (bf16[1088,256]{1,0:T(8,128)(2,1)}, bf16[1088,256]{1,0:T(8,128)(2,1)S(1)}, u32[]{:S(2)}, u32[]{:S(2)}) collective-permute-start(bf16[1088,256]{1,0:T(8,128)(2,1)} %get-tuple-element.327), channel_id=1, source_target_pairs={{0,2},{1,3},{2,0},{3,1},{4,6},{5,7},{6,4},{7,5},{8,10},{9,11},{10,... | collective-permute-start | bytes 1671176 | tf_op jit(solution)/shard_map/ppermute | solution.py:609
  573.8 24.5 %collective-permute-start.50 = (bf16[1088,256]{1,0:T(8,128)(2,1)}, bf16[1088,256]{1,0:T(8,128)(2,1)S(1)}, u32[]{:S(2)}, u32[]{:S(2)}) collective-permute-start(bf16[1088,256]{1,0:T(8,128)(2,1)} %get-tuple-element.328), channel_id=1, source_target_pairs={{0,3},{1,2},{2,1},{3,0},{4,7},{5,6},{6,5},{7,4},{8,11},{9,10},{10,... | collective-permute-start | bytes 1671176 | tf_op jit(solution)/shard_map/ppermute | solution.py:609
  599.2 16.3 %collective-permute-start.53 = (bf16[272,1088]{1,0:T(8,128)(2,1)S(1)}, bf16[272,1088]{1,0:T(8,128)(2,1)S(1)}, u32[]{:S(2)}, u32[]{:S(2)}) collective-permute-start(bf16[272,1088]{1,0:T(8,128)(2,1)S(1)} %add_convert_fusion.6.refs_0_), channel_id=1, source_target_pairs={{0,16},{1,3},{2,18},{3,1},{16,0},{17,19},{18,2},{19,17},{4,20},{5,... | collective-permute-start | bytes 1775624 | tf_op jit(solution)/shard_map/ppermute | solution.py:603
  600.6 18.7 %collective-permute-start.51 = (bf16[272,1088]{1,0:T(8,128)(2,1)}, bf16[272,1088]{1,0:T(8,128)(2,1)S(1)}, u32[]{:S(2)}, u32[]{:S(2)}) collective-permute-start(bf16[272,1088]{1,0:T(8,128)(2,1)} %reduce-scatter.8.cloned.1.call-done), channel_id=1, source_target_pairs={{0,2},{1,17},{2,0},{3,19},{16,18},{17,1},{18,16},{19,3},{4,6},{5,2... | collective-permute-start | bytes 1775624 | tf_op jit(solution)/shard_map/ppermute | solution.py:603
  601.7 18.9 %collective-permute-start.54 = (bf16[272,1088]{1,0:T(8,128)(2,1)S(1)}, bf16[272,1088]{1,0:T(8,128)(2,1)S(1)}, u32[]{:S(2)}, u32[]{:S(2)}) collective-permute-start(bf16[272,1088]{1,0:T(8,128)(2,1)S(1)} %add_convert_fusion.6.refs_0_), channel_id=1, source_target_pairs={{0,1},{1,0},{2,3},{3,2},{16,17},{17,16},{18,19},{19,18},{4,5},{5,4... | collective-permute-start | bytes 1775624 | tf_op jit(solution)/shard_map/ppermute | solution.py:603
  620.6 19.4 %collective-permute-start.58 = (bf16[272,1088]{1,0:T(8,128)(2,1)S(1)}, bf16[272,1088]{1,0:T(8,128)(2,1)S(1)}, u32[]{:S(2)}, u32[]{:S(2)}) collective-permute-start(bf16[272,1088]{1,0:T(8,128)(2,1)S(1)} %add_convert_fusion.5.refs_0_), channel_id=1, source_target_pairs={{0,17},{1,2},{2,19},{3,0},{16,1},{17,18},{18,3},{19,16},{4,21},{5,... | collective-permute-start | bytes 1775624 | tf_op jit(solution)/shard_map/ppermute | solution.py:603
  621.0 19.1 %collective-permute-start.57 = (bf16[272,1088]{1,0:T(8,128)(2,1)S(1)}, bf16[272,1088]{1,0:T(8,128)(2,1)S(1)}, u32[]{:S(2)}, u32[]{:S(2)}) collective-permute-start(bf16[272,1088]{1,0:T(8,128)(2,1)S(1)} %add_convert_fusion.5.refs_0_), channel_id=1, source_target_pairs={{0,1},{1,0},{2,3},{3,2},{16,17},{17,16},{18,19},{19,18},{4,5},{5,4... | collective-permute-start | bytes 1775624 | tf_op jit(solution)/shard_map/ppermute | solution.py:603
  622.8 17.3 %collective-permute-start.56 = (bf16[272,1088]{1,0:T(8,128)(2,1)S(1)}, bf16[272,1088]{1,0:T(8,128)(2,1)S(1)}, u32[]{:S(2)}, u32[]{:S(2)}) collective-permute-start(bf16[272,1088]{1,0:T(8,128)(2,1)S(1)} %add_convert_fusion.5.refs_0_), channel_id=1, source_target_pairs={{0,16},{1,3},{2,18},{3,1},{16,0},{17,19},{18,2},{19,17},{4,20},{5,... | collective-permute-start | bytes 1775624 | tf_op jit(solution)/shard_map/ppermute | solution.py:603
  623.6 16.4 %collective-permute-start.59 = (f32[3264]{0:T(1024)S(1)}, f32[3264]{0:T(1024)S(1)}, u32[]{:S(2)}, u32[]{:S(2)}) collective-permute-start(f32[3264]{0:T(1024)S(1)} %add.272), channel_id=1, source_target_pairs={{0,16},{1,17},{2,18},{3,19},{16,0},{17,1},{18,2},{19,3},{4,20},{5,... | collective-permute-start | bytes 39176 | tf_op jit(solution)/shard_map/ppermute | solution.py:661
  (78 other events, 708.4 us)
Sparse Core Ops, SparseCore 0:
  76.9 51.3 all-gather.2
  166.9 51.4 all-gather.4
  358.2 50.1 reduce-scatter.3
  478.4 48.8 reduce-scatter.5
  530.0 51.5 reduce-scatter.7

commit v8 on v7

--- a/solution.py
+++ b/solution.py
@@ -522,11 +522,7 @@
         ],
         input_output_aliases={4 + at: at for at in range(len(before))},
         compiler_params=pltpu.CompilerParams(vmem_limit_bytes=48 * 2**20),
-        cost_estimate=pl.CostEstimate(
-            flops=4 * length * length * PAIR * pairs * 4,
-            bytes_accessed=8 * length * PAIR * pairs,
-            transcendentals=length * length * pairs,
-        ),
+        cost_estimate=SMALL,
         name="attend",
     )(place, queries, key_rows, value_rows, *before)
 
@@ -561,11 +557,7 @@
         out_shape=[jax.ShapeDtypeStruct((length, width), jnp.bfloat16)] * 3,
         input_output_aliases={7 + at: at for at in range(len(before))},
         compiler_params=pltpu.CompilerParams(vmem_limit_bytes=48 * 2**20),
-        cost_estimate=pl.CostEstimate(
-            flops=10 * length * length * PAIR * pairs * 3,
-            bytes_accessed=16 * length * PAIR * pairs,
-            transcendentals=length * length * pairs,
-        ),
+        cost_estimate=SMALL,
         name="attend_back",
     )(place, queries, key_rows, value_rows, grads, attended, logs, *before)
 
@@ -584,6 +576,7 @@
         out_specs=pl.BlockSpec(memory_space=pltpu.VMEM),
         out_shape=jax.ShapeDtypeStruct((len(pieces),) + pieces[0].shape, dtype),
         compiler_params=pltpu.CompilerParams(vmem_limit_bytes=48 * 2**20),
+        cost_estimate=SMALL,
         name="settle",
     )(places, *pieces)
 
@@ -679,12 +672,7 @@
     return active, slope
 
 
-def block_flops(rows, width, count):
-    return pl.CostEstimate(
-        flops=2 * rows * width * width * count,
-        bytes_accessed=2 * width * width * count + 4 * rows * width * count,
-        transcendentals=0,
-    )
+SMALL = pl.CostEstimate(flops=1024, bytes_accessed=1024, transcendentals=0)
 
 
 def unit_of(values):
@@ -753,7 +741,7 @@
             pltpu.SemaphoreType.DMA,
         ],
         compiler_params=pltpu.CompilerParams(vmem_limit_bytes=56 * 2**20),
-        cost_estimate=block_flops(rows, width, 3),
+        cost_estimate=SMALL,
         name="front",
     )(places, vectors, *slots, *pieces)
 
@@ -773,6 +761,7 @@
         turn_kernel,
         out_shape=jax.ShapeDtypeStruct((len(slots) * step, width), jnp.bfloat16),
         compiler_params=pltpu.CompilerParams(vmem_limit_bytes=48 * 2**20),
+        cost_estimate=SMALL,
         name="turn",
     )(*slots)
 
@@ -798,6 +787,7 @@
         out_specs=[vmem] * len(shapes),
         out_shape=[jax.ShapeDtypeStruct(shape, jnp.float32) for shape in shapes],
         compiler_params=pltpu.CompilerParams(vmem_limit_bytes=48 * 2**20),
+        cost_estimate=SMALL,
         name="assemble",
     )(places, *pieces)
 
@@ -999,7 +989,7 @@
         sums_ref[at] += fold(term)
 
 
-def by_rows(kernel, name, rows, width, tiled, whole, remote, outs, sums, scratch, sems, blocks):
+def by_rows(kernel, name, rows, width, tiled, whole, remote, outs, sums, scratch, sems):
     step = 512
     tile = pl.BlockSpec((step, width), lambda at: (at, 0))
     out_specs, out_shape = [], []
@@ -1025,7 +1015,7 @@
         scratch_shapes=[pltpu.VMEM(shape, jnp.bfloat16) for shape in scratch]
         + [pltpu.SemaphoreType.DMA((sems,)) if sems > 1 else pltpu.SemaphoreType.DMA],
         compiler_params=pltpu.CompilerParams(vmem_limit_bytes=60 * 2**20),
-        cost_estimate=block_flops(rows, width, blocks),
+        cost_estimate=SMALL,
         name=name,
     )(*tiled[0], *whole, *tiled[1], *remote)
 
@@ -1157,8 +1147,7 @@
         jnp.concatenate([gain_first, shift_first, qbias, vbias], axis=0),
         around,
     )
-    slots_back[0], up_own, queries = pin((slots_back[0], up_own, queries))
-    upstream_low = turn(slots_back)
+    up_own, queries = pin((up_own, queries))
     up_near, up_core = plane_swap(up_own, "near"), plane_swap(up_own, "core")
     attended, logs = attend(place, queries, key_rows, value_rows, seq_count, 0, 9, [])
     down_piece, up_core, up_near, attended = pin((down_piece, up_core, up_near, attended))
@@ -1177,7 +1166,6 @@
         0,
         [(4,) + section.shape],
         1,
-        1,
     )
     up_slots = [up_own, up_near, up_core, plane_swap(up_near, "core")]
     active, slopes = [None] * 4, [None] * 4
@@ -1195,12 +1183,14 @@
             0,
             [(2,) + area],
             2,
-            2,
         )
         active[first], active[first + 2], slopes[first], slopes[first + 2] = outs
 
     up(0)
-    up_slots[3], active[0], active[2] = pin((up_slots[3], active[0], active[2]))
+    up_slots[3], slots_back[3], active[0], active[2] = pin(
+        (up_slots[3], slots_back[3], active[0], active[2])
+    )
+    upstream_low = turn(slots_back)
     up(1)
     down_own, *active = pin((down_own, *active))
     down_near, down_core = plane_swap(down_own, "near"), plane_swap(down_own, "core")
@@ -1229,31 +1219,32 @@
             3,
             [(2,) + area],
             2,
-            2,
         )
         return sums
 
     down_near, upstream_low = pin((down_near, upstream_low))
     down_slots = [down_own, down_near, down_core, plane_swap(down_near, "core")]
     sums_even = hidden(0, upstream_low)
-    upstream_late, sums_even = pin((upstream_low, sums_even))
+    down_second = low_sum(down_terms[1], down_far_two)
+    upstream_late, sums_even, down_second = pin((upstream_low, sums_even, down_second))
+    down_close = plane_swap(down_second, "near")
     sums_odd = hidden(1, upstream_late)
     hidden_sums = jnp.stack(
         [sums_even[0], sums_odd[0], sums_even[1], sums_odd[1], sums_even[2]]
     )
-    down_second = low_sum(down_terms[1], down_far_two)
-    down_second, down_far, *hidden_low = pin((down_second, down_far, *hidden_low))
-    down_close = plane_swap(down_second, "near")
+    down_far, *hidden_low = pin((down_far, *hidden_low))
     up_terms = [turned_product(normed_two_low, hidden_low[slot]) for slot in (3, 2)]
-    down_first = low_sum(down_terms[0], down_far, down_close)
-    normed_two_low, down_first, *up_terms = pin((normed_two_low, down_first, *up_terms))
-    down_shard = scatter_rows(down_first)
+    normed_two_low, *up_terms = pin((normed_two_low, *up_terms))
     up_terms += [turned_product(normed_two_low, hidden_low[slot]) for slot in (1, 0)]
     up_terms = up_terms[::-1]
     up_far, up_far_two = reduce_core(up_terms)
     up_second = low_sum(up_terms[1], up_far_two)
-    up_second, up_far, moved, *hidden_low = pin((up_second, up_far, up_terms[0], *hidden_low))
+    down_first = low_sum(down_terms[0], down_far, down_close)
+    up_second, up_far, down_first, moved, *hidden_low = pin(
+        (up_second, up_far, down_first, up_terms[0], *hidden_low)
+    )
     up_terms[0] = moved
+    down_shard = scatter_rows(down_first)
     up_close = plane_swap(up_second, "near")
     middle_grad, middle_low, grad_low, back_sums = by_rows(
         back_kernel,
@@ -1266,7 +1257,6 @@
         [wide, low, low],
         3,
         [(4,) + area, (4,) + section.shape],
-        5,
         5,
     )
     out_term = turned_product(attended, middle_low)
@@ -1313,7 +1303,6 @@
         0,
         [(4,) + area],
         4,
-        4,
     )
     first = low_sum(sections_mine[0], far, close)
     first, up_shard, query_low, *result_slots = pin(
@@ -1333,7 +1322,6 @@
         [None],
         4,
         [(12,) + section.shape],
-        3,
         3,
     )
     moved = pin((*input_slots, *outputs, *down_parts))

time: 664 us -> 629 us (0.947)
  waiting for transfers between devices: 186 us -> 152 us
    ppermute x12, waiting for transfers between devices: 54.2 us -> 32 us  [ctx_swap(): lax.ppermute(values, 'ctx', [(device, device ^ bits) for device in range(...]
    ppermute x36, waiting for transfers between devices: 78.2 us -> 64.2 us  [plane_swap(): lax.ppermute(values, ('dp', 'ctx'), [(device, plane_partner(device, kind)...]
    unnamed x127 -> x133, local copies, waits for them, and re-layouts: 20 us -> 18.3 us
  transfers between devices with their start and end apart: 65 -> 65, of which waited for: 25 -> 24; matrix products, arithmetic and copies ran while one was open for 13% -> 15% of each run, Pallas kernels for 42% -> 44%
where the time goes in v8:
time: 629 us; the launch traced here: 617 us
  Pallas kernels  274 us (44%)
  waiting for transfers between devices  152 us (24%)
  matrix products  62.6 us (10%)
  starting transfers between devices  44.7 us (7%)
  other arithmetic  36.3 us (6%)
  local copies, waits for them, and re-layouts  32 us (5%)
  between operations  15.3 us (2%)
    pallas_call x8, Pallas kernels, by_rows(): pl.pallas_call(kernel, grid=(rows // step,), in_specs=[tile] * len(tiled[...  155 us
    ppermute x36, waiting for transfers between devices, plane_swap(): lax.ppermute(values, ('dp', 'ctx'), [(device, plane_partner(device, kind)...  64.2 us
    dot_general x12, matrix products, product(): lax.dot_general(left, right, ((dims[:1], dims[1:]), ((), ())), preferred_...  62.6 us
    pallas_call x2, Pallas kernels, attend_back(): pl.pallas_call(functools.partial(attend_back_kernel, count=count, width=w...  47.9 us
    ppermute x3, waiting for transfers between devices, per_device_exchanged(): lax.ppermute(section, 'fsdp', [(device, (device + step) % 4) for device i...  35.3 us
    pallas_call x1, Pallas kernels, attend(): pl.pallas_call(functools.partial(attend_kernel, count=count, width=width,...  32.2 us
    ppermute x12, waiting for transfers between devices, ctx_swap(): lax.ppermute(values, 'ctx', [(device, device ^ bits) for device in range(...  32 us
    convert_element_type x8, other arithmetic, low_sum(): sum((term.astype(jnp.float32) for term in terms)).astype(jnp.bfloat16)  28.6 us
  transfers between devices with their start and end apart: 65, of which 24 were waited for; matrix products, arithmetic and copies ran while one was open for 15% of the time, Pallas kernels for 44%

profile of v8, /device:TPU:8, one launch (start us, length us, event | category | flops | bytes accessed | tf_op | source)
XLA Modules:
  0.0 617.1 jit_solution(13621703507519358506)
XLA Ops:
  7.3 3.6 fusion.11
  10.9 3.0 dynamic-slice_bitcast_fusion.4
  29.5 11.9 %collective-permute-done.7.refs_2_ = bf16[1088,256]{1,0:T(8,128)(2,1)S(1)} collective-permute-done((bf16[1088,256]{1,0:T(8,128)(2,1)}, bf16[1088,256]{1,0:T(8,128)(2,1)S(1)}, u32[]{:S(2)}, u32[]{:S(2)}) %collective-permute-start.7) | collective-permute-done | bytes 557088 | tf_op jit(solution)/shard_map/ppermute | solution.py:602
  41.4 23.4 %collective-permute-done.5.refs_10_ = bf16[272,1088]{1,0:T(8,128)(2,1)} collective-permute-done((bf16[272,1088]{1,0:T(8,128)(2,1)}, bf16[272,1088]{1,0:T(8,128)(2,1)}, u32[]{:S(2)}, u32[]{:S(2)}) %collective-permute-start.5) | collective-permute-done | bytes 591904 | tf_op jit(solution)/shard_map/ppermute | solution.py:1084
  64.8 12.0 %collective-permute-done.3.refs_8_ = bf16[272,1088]{1,0:T(8,128)(2,1)} collective-permute-done((bf16[272,1088]{1,0:T(8,128)(2,1)}, bf16[272,1088]{1,0:T(8,128)(2,1)}, u32[]{:S(2)}, u32[]{:S(2)}) %collective-permute-start.3) | collective-permute-done | bytes 591904 | tf_op jit(solution)/shard_map/ppermute | solution.py:1084
  80.9 6.5 %collective-permute-done.9.refs_11_ = bf16[272,1088]{1,0:T(8,128)(2,1)} collective-permute-done((bf16[272,1088]{1,0:T(8,128)(2,1)}, bf16[272,1088]{1,0:T(8,128)(2,1)}, u32[]{:S(2)}, u32[]{:S(2)}) %collective-permute-start.9) | collective-permute-done | bytes 591904 | tf_op jit(solution)/shard_map/ppermute | solution.py:596
  87.5 6.7 %collective-permute-done.10.refs_12_ = bf16[272,1088]{1,0:T(8,128)(2,1)} collective-permute-done((bf16[272,1088]{1,0:T(8,128)(2,1)S(1)}, bf16[272,1088]{1,0:T(8,128)(2,1)}, u32[]{:S(2)}, u32[]{:S(2)}) %collective-permute-start.10) | collective-permute-done | bytes 591904 | tf_op jit(solution)/shard_map/ppermute | solution.py:596
  94.2 6.7 %collective-permute-done.11.refs_13_ = bf16[272,1088]{1,0:T(8,128)(2,1)} collective-permute-done((bf16[272,1088]{1,0:T(8,128)(2,1)}, bf16[272,1088]{1,0:T(8,128)(2,1)}, u32[]{:S(2)}, u32[]{:S(2)}) %collective-permute-start.11) | collective-permute-done | bytes 591904 | tf_op jit(solution)/shard_map/ppermute | solution.py:596
  105.1 21.8 %front.1 = (bf16[1024,1088]{1,0:T(8,128)(2,1)}, bf16[1024,1088]{1,0:T(8,128)(2,1)}, bf16[1024,1088]{1,0:T(8,128)(2,1)}, bf16[1024,1088]{1,0:T(8,128)(2,1)}, bf16...) custom-call(s32[16]{0:T(128)} %stack.120.places_ref, f32[4,1088]{1,0:T(4,128)} %pad_maximum_fusion.1.vectors_ref, ...), custom_call_target="tpu_custom_call" | custom-call | flops 1024 | bytes 1024 | tf_op jit(solution)/shard_map/front/pallas_call | solution.py:733
  132.3 32.2 %attend.1 = (bf16[1024,1088]{1,0:T(8,128)(2,1)S(1)}, f32[1024,128]{1,0:T(8,128)S(1)}) custom-call(s32[1]{0:T(128)} %bitcast.24.place_ref, bf16[1024,1088]{1,0:T(8,128)(2,1)S(1)} %copy-done.3, bf16[1024,1088]{1,0:T(8,128)(2,1)} %get-tuple-element.218.k_ref, bf16[1024,1088]{1,0:T(8,128)(2,1)} %get-tuple-element.219.v_ref), custom_call_target="tpu_custom_call" | custom-call | flops 1024 | bytes 1024 | tf_op jit(solution)/shard_map/attend/pallas_call | solution.py:507
  172.8 10.0 %middle.1 = (f32[1024,1088]{1,0:T(8,128)}, bf16[1024,1088]{1,0:T(8,128)(2,1)}) custom-call(bf16[1024,1088]{1,0:T(8,128)(2,1)} %get-tuple-element.224.x_ref, bf16[1024,1088]{1,0:T(8,128)(2,1)} %copy-done.4, f32[3,1088]{1,0:T(4,128)} %pad_maximum_fusion.2.vectors_ref, bf16[16,272,1088]{2,1,0:T(8,128)(2,1)} %get-tuple-element.226.all_ref.refs_8_), custom_call_target="tpu_custom_call" | custom-call | flops 1024 | bytes 1024 | tf_op jit(solution)/shard_map/middle/pallas_call | solution.py:1006
  182.8 17.4 %up.2 = (bf16[1024,1088]{1,0:T(8,128)(2,1)}, bf16[1024,1088]{1,0:T(8,128)(2,1)}, bf16[1024,1088]{1,0:T(8,128)(2,1)}, bf16[1024,1088]{1,0:T(8,128)(2,1)}) custom-call(bf16[1024,1088]{1,0:T(8,128)(2,1)} %get-tuple-element.262.h_ref, f32[2,1088]{1,0:T(2,128)} %pad_maximum_fusion.3.biases_ref, bf16[1088,1088]{1,0:T(8,128)(2,1)} %all-gather.3.cloned.1.call-done.refs_0_.refs_4_, ...), custom_call_target="tpu_custom_call" | custom-call | flops 1024 | bytes 1024 | tf_op jit(solution)/shard_map/up/pallas_call | solution.py:1006
  200.2 17.9 %up.3 = (bf16[1024,1088]{1,0:T(8,128)(2,1)}, bf16[1024,1088]{1,0:T(8,128)(2,1)}, bf16[1024,1088]{1,0:T(8,128)(2,1)}, bf16[1024,1088]{1,0:T(8,128)(2,1)}) custom-call(bf16[1024,1088]{1,0:T(8,128)(2,1)} %get-tuple-element.262.h_ref, f32[2,1088]{1,0:T(2,128)} %pad_maximum_fusion.4.biases_ref, bf16[1088,1088]{1,0:T(8,128)(2,1)} %collective-permute-done.19.refs_0_.refs_5_, ...), custom_call_target="tpu_custom_call" | custom-call | flops 1024 | bytes 1024 | tf_op jit(solution)/shard_map/up/pallas_call | solution.py:1006
  224.4 7.1 %convolution_convert_fusion.11 = bf16[1088,1088]{1,0:T(8,128)(2,1)} fusion(bf16[1024,1088]{1,0:T(8,128)(2,1)} %get-tuple-element.238.refs_3_, bf16[1024,1088]{1,0:T(8,128)(2,1)S(1)} %turn.1.g_ref), kind=kOutput, calls=%fused_computation.13 | convolution fusion | flops 2425491456 | bytes 6823936 | tf_op jit(solution)/shard_map/dot_general | solution.py:660
  231.4 4.6 convolution_convert_fusion.10
  236.2 4.6 convolution_convert_fusion.8
  240.8 4.8 convolution_convert_fusion.9
  245.6 9.0 %collective-permute-done.22.refs_2_.refs_5_ = bf16[1088,1088]{1,0:T(8,128)(2,1)} collective-permute-done((bf16[1088,1088]{1,0:T(8,128)(2,1)}, bf16[1088,1088]{1,0:T(8,128)(2,1)}, u32[]{:S(2)}, u32[]{:S(2)}) %collective-permute-start.22) | collective-permute-done | bytes 2367520 | tf_op jit(solution)/shard_map/ppermute | solution.py:596
  255.1 14.0 %hidden.2 = (bf16[1024,1088]{1,0:T(8,128)(2,1)}, bf16[1024,1088]{1,0:T(8,128)(2,1)}, f32[3,8,1088]{2,1,0:T(8,128)}) custom-call(bf16[1024,1088]{1,0:T(8,128)(2,1)} %copy-done.2, bf16[1024,1088]{1,0:T(8,128)(2,1)} %get-tuple-element.248.refs_0_, bf16[1024,1088]{1,0:T(8,128)(2,1)} %get-tuple-element.249.refs_1_, ...), custom_call_target="tpu_custom_call" | custom-call | flops 1024 | bytes 1024 | tf_op jit(solution)/shard_map/hidden/pallas_call | solution.py:1006
  269.1 4.6 add_convert_fusion.4
  275.7 14.2 %hidden.3 = (bf16[1024,1088]{1,0:T(8,128)(2,1)}, bf16[1024,1088]{1,0:T(8,128)(2,1)}, f32[3,8,1088]{2,1,0:T(8,128)}) custom-call(bf16[1024,1088]{1,0:T(8,128)(2,1)} %copy-done.2, bf16[1024,1088]{1,0:T(8,128)(2,1)} %get-tuple-element.254.refs_0_, bf16[1024,1088]{1,0:T(8,128)(2,1)} %get-tuple-element.255.refs_1_, ...), custom_call_target="tpu_custom_call" | custom-call | flops 1024 | bytes 1024 | tf_op jit(solution)/shard_map/hidden/pallas_call | solution.py:1006
  289.9 7.1 %convolution_convert_fusion.7 = bf16[1088,1088]{1,0:T(8,128)(2,1)} fusion(bf16[1024,1088]{1,0:T(8,128)(2,1)} %get-tuple-element.262.h_ref, bf16[1024,1088]{1,0:T(8,128)(2,1)} %get-tuple-element.273.refs_3_), kind=kOutput, calls=%fused_computation.9 | convolution fusion | flops 2425491456 | bytes 6823936 | tf_op jit(solution)/shard_map/dot_general | solution.py:660
  297.0 4.6 convolution_convert_fusion.6
  302.3 4.6 convolution_convert_fusion.4
  306.8 4.9 add_convert_fusion.3
  311.7 7.4 %fusion.2 = bf16[1088,1088]{1,0:T(8,128)(2,1)} fusion(bf16[1024,1088]{1,0:T(8,128)(2,1)S(1)} %copy-done.34, bf16[1024,1088]{1,0:T(8,128)(2,1)} %get-tuple-element.271.refs_1_, bf16[1088,1088]{1,0:T(8,128)(2,1)} %collective-permute-done.29), kind=kOutput, calls=%fused_computation.14 | convolution fusion | flops 2430226432 | bytes 9191424 | tf_op jit(solution)/shard_map/dot_general | solution.py:660
  320.8 31.9 %back.1 = (f32[1024,1088]{1,0:T(8,128)}, bf16[1024,1088]{1,0:T(8,128)(2,1)}, bf16[1024,1088]{1,0:T(8,128)(2,1)}, f32[3,8,1088]{2,1,0:T(8,128)}) custom-call(bf16[1024,1088]{1,0:T(8,128)(2,1)} %copy-done.2, f32[1024,1088]{1,0:T(8,128)} %get-tuple-element.301.middle_ref, f32[1,1088]{1,0:T(1,128)} %copy-done.53, bf16[1024,1088]{1,0:T(8,128)(2,1)} %get-tuple-element.270.refs_0_, ...), custom_call_target="tpu_custom_call" | custom-call | flops 1024 | bytes 1024 | tf_op jit(solution)/shard_map/back/pallas_call | solution.py:1006
  352.8 6.4 %convolution_convert_fusion.3 = bf16[1088,1088]{1,0:T(8,128)(2,1)} fusion(bf16[1024,1088]{1,0:T(8,128)(2,1)S(1)} %copy-done.5, bf16[1024,1088]{1,0:T(8,128)(2,1)} %get-tuple-element.275), kind=kOutput, calls=%fused_computation.3 | convolution fusion | flops 2425491456 | bytes 6823936 | tf_op jit(solution)/shard_map/dot_general | solution.py:660
  359.1 5.0 add_convert_fusion.2
  364.1 26.2 %attend_back.2 = (bf16[1024,1088]{1,0:T(8,128)(2,1)S(1)}, bf16[1024,1088]{1,0:T(8,128)(2,1)S(1)}, bf16[1024,1088]{1,0:T(8,128)(2,1)}) custom-call(s32[1]{0:T(128)} %bitcast.24.place_ref, bf16[1024,1088]{1,0:T(8,128)(2,1)} %get-tuple-element.217.q_ref, bf16[1024,1088]{1,0:T(8,128)(2,1)} %get-tuple-element.218.k_ref, ...), custom_call_target="tpu_custom_call" | custom-call | flops 1024 | bytes 1024 | tf_op jit(solution)/shard_map/attend_back/pallas_call | solution.py:537
  395.3 21.7 %attend_back.3 = (bf16[1024,1088]{1,0:T(8,128)(2,1)S(1)}, bf16[1024,1088]{1,0:T(8,128)(2,1)S(1)}, bf16[1024,1088]{1,0:T(8,128)(2,1)}) custom-call(s32[1]{0:T(128)} %bitcast.24.place_ref, bf16[1024,1088]{1,0:T(8,128)(2,1)} %get-tuple-element.217.q_ref, ...), custom_call_target="tpu_custom_call", output_to_operand_aliasing={{0}: (7, {}), {1}: (8, {}), {2}: (9, {})} | custom-call | flops 1024 | bytes 1024 | tf_op jit(solution)/shard_map/attend_back/pallas_call | solution.py:537
  418.7 3.1 convolution_convert_fusion.1
  421.9 3.1 convolution_convert_fusion
  425.0 5.3 select_select_fusion
  430.9 7.8 %collective-permute-done.34 = bf16[1088,1088]{1,0:T(8,128)(2,1)S(1)} collective-permute-done((bf16[1088,1088]{1,0:T(8,128)(2,1)S(1)}, bf16[1088,1088]{1,0:T(8,128)(2,1)S(1)}, u32[]{:S(2)}, u32[]{:S(2)}) %collective-permute-start.34) | collective-permute-done | bytes 2367520 | tf_op jit(solution)/shard_map/ppermute | solution.py:596
  438.7 3.2 add_convert_fusion.1
  444.9 26.1 %down.1 = (bf16[1088,256]{1,0:T(8,128)(2,1)}, bf16[1088,256]{1,0:T(8,128)(2,1)}, bf16[1088,256]{1,0:T(8,128)(2,1)}, bf16[1088,256]{1,0:T(8,128)(2,1)}) custom-call(f32[1024,1088]{1,0:T(8,128)} %get-tuple-element.301.middle_ref, f32[1,1088]{1,0:T(1,128)} %reshape.446.vectors_ref, bf16[1024,1088]{1,0:T(8,128)(2,1)} %get-tuple-element.241.refs_0_, ...), custom_call_target="tpu_custom_call" | custom-call | flops 1024 | bytes 1024 | tf_op jit(solution)/shard_map/down/pallas_call | solution.py:1006
  471.0 3.1 collective-permute-done.36
  474.1 6.6 %add_convert_fusion = bf16[1088,1088]{1,0:T(8,128)(2,1)} fusion(bf16[1088,1088]{1,0:T(8,128)(2,1)} %collective-permute-done.36, bf16[1088,1088]{1,0:T(8,128)(2,1)} %copy-done.38, bf16[1088,1088]{1,0:T(8,128)(2,1)} %copy-done.33, bf16[1088,1088]{1,0:T(8,128)(2,1)} %copy-done.31, bf16[1088,1088]{1,0:T(8,128)(2,1)} %copy-done.32, ...), kind=kLoop, calls=%fused_computation.15 | loop fusion | flops 10653696 | bytes 16572419 | tf_op jit(solution)/shard_map/convert_element_type | solution.py:606
  480.7 12.7 %reduce-scatter.6.cloned.1.call-done = bf16[272,1088]{1,0:T(8,128)(2,1)} async-done(((bf16[1088,1088]{1,0:T(8,128)(2,1)}), bf16[272,1088]{1,0:T(8,128)(2,1)}) %reduce-scatter.6.cloned.1.call-update) | async-done | bytes 591888 | tf_op jit(solution)/shard_map/reduce_scatter | solution.py:623
  495.5 8.6 %collective-permute-done.45.refs_1_ = bf16[272,1088]{1,0:T(8,128)(2,1)S(1)} collective-permute-done((bf16[272,1088]{1,0:T(8,128)(2,1)S(1)}, bf16[272,1088]{1,0:T(8,128)(2,1)S(1)}, u32[]{:S(2)}, u32[]{:S(2)}) %collective-permute-start.45) | collective-permute-done | bytes 591904 | tf_op jit(solution)/shard_map/ppermute | solution.py:596
  506.9 23.8 %last.1 = (bf16[1088,256]{1,0:T(8,128)(2,1)}, bf16[1088,256]{1,0:T(8,128)(2,1)}, bf16[1088,256]{1,0:T(8,128)(2,1)}, bf16[1088,256]{1,0:T(8,128)(2,1)}, f32[4,8,1088]{2,1,0:T(8,128)}) custom-call(bf16[1024,1088]{1,0:T(8,128)(2,1)} %copy-done.6, bf16[1024,1088]{1,0:T(8,128)(2,1)} %copy-done.9, bf16[1024,1088]{1,0:T(8,128)(2,1)} %get-tuple-element.313.v_ref, ...), custom_call_target="tpu_custom_call" | custom-call | flops 1024 | bytes 1024 | tf_op jit(solution)/shard_map/last/pallas_call | solution.py:1006
  545.9 8.7 %collective-permute-done.49.refs_2_ = bf16[1088,256]{1,0:T(8,128)(2,1)S(1)} collective-permute-done((bf16[1088,256]{1,0:T(8,128)(2,1)}, bf16[1088,256]{1,0:T(8,128)(2,1)S(1)}, u32[]{:S(2)}, u32[]{:S(2)}) %collective-permute-start.49) | collective-permute-done | bytes 557088 | tf_op jit(solution)/shard_map/ppermute | solution.py:602
  555.4 10.1 %collective-permute-done.50.refs_3_ = bf16[1088,256]{1,0:T(8,128)(2,1)S(1)} collective-permute-done((bf16[1088,256]{1,0:T(8,128)(2,1)}, bf16[1088,256]{1,0:T(8,128)(2,1)S(1)}, u32[]{:S(2)}, u32[]{:S(2)}) %collective-permute-start.50) | collective-permute-done | bytes 557088 | tf_op jit(solution)/shard_map/ppermute | solution.py:602
  568.9 13.9 %collective-permute-done.53.refs_1_ = bf16[272,1088]{1,0:T(8,128)(2,1)S(1)} collective-permute-done((bf16[272,1088]{1,0:T(8,128)(2,1)S(1)}, bf16[272,1088]{1,0:T(8,128)(2,1)S(1)}, u32[]{:S(2)}, u32[]{:S(2)}) %collective-permute-start.53) | collective-permute-done | bytes 591904 | tf_op jit(solution)/shard_map/ppermute | solution.py:596
  595.5 3.2 settle.5
  601.6 4.1 assemble.2
  607.0 3.4 assemble.3
  (329 shorter events, 99.6 us)
Async XLA Ops:
  7.2 121.0 %all-gather.3.cloned.1.call-start = ((), (), s32[]{:S(2)}) async-start(), calls=%async_computation.3 | async-start | bytes 3133440 | tf_op jit(solution)/shard_map/all_gather | solution.py:1130
  13.9 15.2 %collective-permute-start.8 = (bf16[1088,256]{1,0:T(8,128)(2,1)}, bf16[1088,256]{1,0:T(8,128)(2,1)}, u32[]{:S(2)}, u32[]{:S(2)}) collective-permute-start(bf16[1088,256]{1,0:T(8,128)(2,1)} %get-tuple-element.200), channel_id=1, source_target_pairs={{0,3},{1,2},{2,1},{3,0},{4,7},{5,6},{6,5},{7,4},{8,11},{9,10},{10,... | collective-permute-start | bytes 1671176 | tf_op jit(solution)/shard_map/ppermute | solution.py:602
  20.6 44.2 %collective-permute-start.5 = (bf16[272,1088]{1,0:T(8,128)(2,1)}, bf16[272,1088]{1,0:T(8,128)(2,1)}, u32[]{:S(2)}, u32[]{:S(2)}) collective-permute-start(bf16[272,1088]{1,0:T(8,128)(2,1)} %get-tuple-element.199), channel_id=1, source_target_pairs={{0,12},{4,0},{8,4},{12,8},{1,13},{5,1},{9,5},{13,9},{2,14},{6,2},{... | collective-permute-start | bytes 1775624 | tf_op jit(solution)/shard_map/ppermute | solution.py:1084
  23.5 41.3 %collective-permute-start.4 = (bf16[272,1088]{1,0:T(8,128)(2,1)}, bf16[272,1088]{1,0:T(8,128)(2,1)S(1)}, u32[]{:S(2)}, u32[]{:S(2)}) collective-permute-start(bf16[272,1088]{1,0:T(8,128)(2,1)} %get-tuple-element.199), channel_id=1, source_target_pairs={{0,8},{4,12},{8,0},{12,4},{1,9},{5,13},{9,1},{13,5},{2,10},{6,14},... | collective-permute-start | bytes 1775624 | tf_op jit(solution)/shard_map/ppermute | solution.py:1084
  25.0 51.8 %collective-permute-start.3 = (bf16[272,1088]{1,0:T(8,128)(2,1)}, bf16[272,1088]{1,0:T(8,128)(2,1)}, u32[]{:S(2)}, u32[]{:S(2)}) collective-permute-start(bf16[272,1088]{1,0:T(8,128)(2,1)} %get-tuple-element.199), channel_id=1, source_target_pairs={{0,4},{4,8},{8,12},{12,0},{1,5},{5,9},{9,13},{13,1},{2,6},{6,10},{... | collective-permute-start | bytes 1775624 | tf_op jit(solution)/shard_map/ppermute | solution.py:1084
  27.3 14.1 %collective-permute-start.7 = (bf16[1088,256]{1,0:T(8,128)(2,1)}, bf16[1088,256]{1,0:T(8,128)(2,1)S(1)}, u32[]{:S(2)}, u32[]{:S(2)}) collective-permute-start(bf16[1088,256]{1,0:T(8,128)(2,1)} %get-tuple-element.387), channel_id=1, source_target_pairs={{0,2},{1,3},{2,0},{3,1},{4,6},{5,7},{6,4},{7,5},{8,10},{9,11},{10,... | collective-permute-start | bytes 1671176 | tf_op jit(solution)/shard_map/ppermute | solution.py:602
  29.1 12.3 %collective-permute-start.6 = (bf16[1088,256]{1,0:T(8,128)(2,1)}, bf16[1088,256]{1,0:T(8,128)(2,1)S(1)}, u32[]{:S(2)}, u32[]{:S(2)}) collective-permute-start(bf16[1088,256]{1,0:T(8,128)(2,1)} %get-tuple-element.388), channel_id=1, source_target_pairs={{0,1},{1,0},{2,3},{3,2},{4,5},{5,4},{6,7},{7,6},{8,9},{9,8},{10,11... | collective-permute-start | bytes 1671176 | tf_op jit(solution)/shard_map/ppermute | solution.py:602
  76.8 146.9 %all-gather.5.cloned.1.call-start = ((), (), s32[]{:S(2)}) async-start(), calls=%async_computation.4 | async-start | bytes 3133440 | tf_op jit(solution)/shard_map/all_gather | solution.py:1154
  78.4 15.8 %collective-permute-start.10 = (bf16[272,1088]{1,0:T(8,128)(2,1)S(1)}, bf16[272,1088]{1,0:T(8,128)(2,1)}, u32[]{:S(2)}, u32[]{:S(2)}) collective-permute-start(bf16[272,1088]{1,0:T(8,128)(2,1)S(1)} %collective-permute-done.4.refs_9_), channel_id=1, source_target_pairs={{0,16},{1,3},{2,18},{3,1},{16,0},{17,19},{18,2},{19,17},{4,20},{5,... | collective-permute-start | bytes 1775624 | tf_op jit(solution)/shard_map/ppermute | solution.py:596
  78.9 22.0 %collective-permute-start.11 = (bf16[272,1088]{1,0:T(8,128)(2,1)}, bf16[272,1088]{1,0:T(8,128)(2,1)}, u32[]{:S(2)}, u32[]{:S(2)}) collective-permute-start(bf16[272,1088]{1,0:T(8,128)(2,1)} %collective-permute-done.5.refs_10_), channel_id=1, source_target_pairs={{0,16},{1,3},{2,18},{3,1},{16,0},{17,19},{18,2},{19,17},{4,20},{5,... | collective-permute-start | bytes 1775624 | tf_op jit(solution)/shard_map/ppermute | solution.py:596
  80.4 21.0 %collective-permute-start.12 = (bf16[272,1088]{1,0:T(8,128)(2,1)}, bf16[272,1088]{1,0:T(8,128)(2,1)}, u32[]{:S(2)}, u32[]{:S(2)}) collective-permute-start(bf16[272,1088]{1,0:T(8,128)(2,1)} %collective-permute-done.3.refs_8_), channel_id=1, source_target_pairs={{0,1},{1,0},{2,3},{3,2},{16,17},{17,16},{18,19},{19,18},{4,5},{5,4... | collective-permute-start | bytes 1775624 | tf_op jit(solution)/shard_map/ppermute | solution.py:596
  80.4 22.8 %collective-permute-start.13 = (bf16[272,1088]{1,0:T(8,128)(2,1)S(1)}, bf16[272,1088]{1,0:T(8,128)(2,1)}, u32[]{:S(2)}, u32[]{:S(2)}) collective-permute-start(bf16[272,1088]{1,0:T(8,128)(2,1)S(1)} %collective-permute-done.4.refs_9_), channel_id=1, source_target_pairs={{0,1},{1,0},{2,3},{3,2},{16,17},{17,16},{18,19},{19,18},{4,5},{5,4... | collective-permute-start | bytes 1775624 | tf_op jit(solution)/shard_map/ppermute | solution.py:596
  87.5 15.7 %collective-permute-start.14 = (bf16[272,1088]{1,0:T(8,128)(2,1)}, bf16[272,1088]{1,0:T(8,128)(2,1)}, u32[]{:S(2)}, u32[]{:S(2)}) collective-permute-start(bf16[272,1088]{1,0:T(8,128)(2,1)} %collective-permute-done.5.refs_10_), channel_id=1, source_target_pairs={{0,1},{1,0},{2,3},{3,2},{16,17},{17,16},{18,19},{19,18},{4,5},{5,4... | collective-permute-start | bytes 1775624 | tf_op jit(solution)/shard_map/ppermute | solution.py:596
  128.2 37.6 %collective-permute-start.19 = (bf16[1088,1088]{1,0:T(8,128)(2,1)}, bf16[1088,1088]{1,0:T(8,128)(2,1)}, u32[]{:S(2)}, u32[]{:S(2)}) collective-permute-start(bf16[1088,1088]{1,0:T(8,128)(2,1)} %all-gather.3.cloned.1.call-done.refs_0_.refs_4_), channel_id=1, source_target_pairs={{0,16},{1,3},{2,18},{3,1},{16,0},{17,19},{18,2},{19,17},{4,20},{5,... | collective-permute-start | bytes 7102472 | tf_op jit(solution)/shard_map/ppermute | solution.py:596
  129.7 36.2 %collective-permute-start.18 = (bf16[1088,1088]{1,0:T(8,128)(2,1)}, bf16[1088,1088]{1,0:T(8,128)(2,1)}, u32[]{:S(2)}, u32[]{:S(2)}) collective-permute-start(bf16[1088,1088]{1,0:T(8,128)(2,1)} %all-gather.3.cloned.1.call-done.refs_0_.refs_4_), channel_id=1, source_target_pairs={{0,1},{1,0},{2,3},{3,2},{16,17},{17,16},{18,19},{19,18},{4,5},{5,4... | collective-permute-start | bytes 7102472 | tf_op jit(solution)/shard_map/ppermute | solution.py:596
  165.9 225.8 %reduce-scatter.4.cloned.1.call-start = ((), (), s32[]{:S(2)}) async-start(), calls=%async_computation.5 | async-start | bytes 3133440 | tf_op jit(solution)/shard_map/reduce_scatter | solution.py:623
  166.2 34.0 %collective-permute-start.20 = (bf16[1088,1088]{1,0:T(8,128)(2,1)}, bf16[1088,1088]{1,0:T(8,128)(2,1)}, u32[]{:S(2)}, u32[]{:S(2)}) collective-permute-start(bf16[1088,1088]{1,0:T(8,128)(2,1)} %collective-permute-done.19.refs_0_.refs_5_), channel_id=1, source_target_pairs={{0,1},{1,0},{2,3},{3,2},{16,17},{17,16},{18,19},{19,18},{4,5},{5,4... | collective-permute-start | bytes 7102472 | tf_op jit(solution)/shard_map/ppermute | solution.py:596
  168.3 49.8 %collective-permute-start.24 = (bf16[1088,256]{1,0:T(8,128)(2,1)}, bf16[1088,256]{1,0:T(8,128)(2,1)S(1)}, u32[]{:S(2)}, u32[]{:S(2)}) collective-permute-start(bf16[1088,256]{1,0:T(8,128)(2,1)} %get-tuple-element.383), channel_id=1, source_target_pairs={{0,2},{1,3},{2,0},{3,1},{4,6},{5,7},{6,4},{7,5},{8,10},{9,11},{10,... | collective-permute-start | bytes 1671176 | tf_op jit(solution)/shard_map/ppermute | solution.py:602
  169.8 49.2 %collective-permute-start.23 = (bf16[1088,256]{1,0:T(8,128)(2,1)}, bf16[1088,256]{1,0:T(8,128)(2,1)S(1)}, u32[]{:S(2)}, u32[]{:S(2)}) collective-permute-start(bf16[1088,256]{1,0:T(8,128)(2,1)} %get-tuple-element.384), channel_id=1, source_target_pairs={{0,1},{1,0},{2,3},{3,2},{4,5},{5,4},{6,7},{7,6},{8,9},{9,8},{10,11... | collective-permute-start | bytes 1671176 | tf_op jit(solution)/shard_map/ppermute | solution.py:602
  169.8 30.4 %collective-permute-start.21 = (bf16[1088,256]{1,0:T(8,128)(2,1)}, bf16[1088,256]{1,0:T(8,128)(2,1)S(1)}, u32[]{:S(2)}, u32[]{:S(2)}) collective-permute-start(bf16[1088,256]{1,0:T(8,128)(2,1)} %get-tuple-element.386), channel_id=1, source_target_pairs={{0,3},{1,2},{2,1},{3,0},{4,7},{5,6},{6,5},{7,4},{8,11},{9,10},{10,... | collective-permute-start | bytes 1671176 | tf_op jit(solution)/shard_map/ppermute | solution.py:602
  223.7 31.4 %collective-permute-start.26 = (bf16[1088,1088]{1,0:T(8,128)(2,1)}, bf16[1088,1088]{1,0:T(8,128)(2,1)}, u32[]{:S(2)}, u32[]{:S(2)}) collective-permute-start(bf16[1088,1088]{1,0:T(8,128)(2,1)} %all-gather.5.cloned.1.call-done.refs_2_.refs_4_), channel_id=1, source_target_pairs={{0,1},{1,0},{2,3},{3,2},{16,17},{17,16},{18,19},{19,18},{4,5},{5,4... | collective-permute-start | bytes 7102472 | tf_op jit(solution)/shard_map/ppermute | solution.py:596
  223.8 30.8 %collective-permute-start.22 = (bf16[1088,1088]{1,0:T(8,128)(2,1)}, bf16[1088,1088]{1,0:T(8,128)(2,1)}, u32[]{:S(2)}, u32[]{:S(2)}) collective-permute-start(bf16[1088,1088]{1,0:T(8,128)(2,1)} %all-gather.5.cloned.1.call-done.refs_2_.refs_4_), channel_id=1, source_target_pairs={{0,16},{1,3},{2,18},{3,1},{16,0},{17,19},{18,2},{19,17},{4,20},{5,... | collective-permute-start | bytes 7102472 | tf_op jit(solution)/shard_map/ppermute | solution.py:596
  236.0 33.1 %collective-permute-start.27 = (bf16[1088,1088]{1,0:T(8,128)(2,1)}, bf16[1088,1088]{1,0:T(8,128)(2,1)}, u32[]{:S(2)}, u32[]{:S(2)}) collective-permute-start(bf16[1088,1088]{1,0:T(8,128)(2,1)} %convolution_convert_fusion.11), channel_id=1, source_target_pairs={{0,1},{1,0},{2,3},{3,2},{16,17},{17,16},{18,19},{19,18},{4,5},{5,4... | collective-permute-start | bytes 7102472 | tf_op jit(solution)/shard_map/ppermute | solution.py:596
  254.6 19.7 %collective-permute-start.28 = (bf16[1088,1088]{1,0:T(8,128)(2,1)}, bf16[1088,1088]{1,0:T(8,128)(2,1)S(1)}, u32[]{:S(2)}, u32[]{:S(2)}) collective-permute-start(bf16[1088,1088]{1,0:T(8,128)(2,1)} %collective-permute-done.22.refs_2_.refs_5_), channel_id=1, source_target_pairs={{0,1},{1,0},{2,3},{3,2},{16,17},{17,16},{18,19},{19,18},{4,5},{5,4... | collective-permute-start | bytes 7102472 | tf_op jit(solution)/shard_map/ppermute | solution.py:596
  254.6 35.3 %collective-permute-start.25 = (bf16[1088,1088]{1,0:T(8,128)(2,1)}, bf16[1088,1088]{1,0:T(8,128)(2,1)}, u32[]{:S(2)}, u32[]{:S(2)}) collective-permute-start(bf16[1088,1088]{1,0:T(8,128)(2,1)} %convolution_convert_fusion.10), channel_id=1, source_target_pairs={{0,1},{1,0},{2,3},{3,2},{16,17},{17,16},{18,19},{19,18},{4,5},{5,4... | collective-permute-start | bytes 7102472 | tf_op jit(solution)/shard_map/ppermute | solution.py:596
  273.7 33.1 %collective-permute-start.31 = (bf16[1088,1088]{1,0:T(8,128)(2,1)}, bf16[1088,1088]{1,0:T(8,128)(2,1)}, u32[]{:S(2)}, u32[]{:S(2)}) collective-permute-start(bf16[1088,1088]{1,0:T(8,128)(2,1)} %add_convert_fusion.4), channel_id=1, source_target_pairs={{0,16},{1,3},{2,18},{3,1},{16,0},{17,19},{18,2},{19,17},{4,20},{5,... | collective-permute-start | bytes 7102472 | tf_op jit(solution)/shard_map/ppermute | solution.py:596
  302.3 16.8 %collective-permute-start.30 = (bf16[1088,1088]{1,0:T(8,128)(2,1)}, bf16[1088,1088]{1,0:T(8,128)(2,1)}, u32[]{:S(2)}, u32[]{:S(2)}) collective-permute-start(bf16[1088,1088]{1,0:T(8,128)(2,1)} %convolution_convert_fusion.6), channel_id=1, source_target_pairs={{0,1},{1,0},{2,3},{3,2},{16,17},{17,16},{18,19},{19,18},{4,5},{5,4... | collective-permute-start | bytes 7102472 | tf_op jit(solution)/shard_map/ppermute | solution.py:596
  319.1 174.3 %reduce-scatter.6.cloned.1.call-start = ((), (), s32[]{:S(2)}) async-start(), calls=%async_computation.6 | async-start | bytes 3133440 | tf_op jit(solution)/shard_map/reduce_scatter | solution.py:623
  319.1 40.0 %collective-permute-start.32 = (bf16[1088,1088]{1,0:T(8,128)(2,1)}, bf16[1088,1088]{1,0:T(8,128)(2,1)}, u32[]{:S(2)}, u32[]{:S(2)}) collective-permute-start(bf16[1088,1088]{1,0:T(8,128)(2,1)} %fusion.2), channel_id=1, source_target_pairs={{0,16},{1,3},{2,18},{3,1},{16,0},{17,19},{18,2},{19,17},{4,20},{5,... | collective-permute-start | bytes 7102472 | tf_op jit(solution)/shard_map/ppermute | solution.py:596
  391.7 25.2 %collective-permute-start.33 = (bf16[272,1088]{1,0:T(8,128)(2,1)}, bf16[272,1088]{1,0:T(8,128)(2,1)}, u32[]{:S(2)}, u32[]{:S(2)}) collective-permute-start(bf16[272,1088]{1,0:T(8,128)(2,1)} %reduce-scatter.4.cloned.1.call-done), channel_id=1, source_target_pairs={{0,2},{1,17},{2,0},{3,19},{16,18},{17,1},{18,16},{19,3},{4,6},{5,2... | collective-permute-start | bytes 1775624 | tf_op jit(solution)/shard_map/ppermute | solution.py:596
  430.4 11.5 %collective-permute-start.35 = (bf16[1088,1088]{1,0:T(8,128)(2,1)}, bf16[1088,1088]{1,0:T(8,128)(2,1)S(1)}, u32[]{:S(2)}, u32[]{:S(2)}) collective-permute-start(bf16[1088,1088]{1,0:T(8,128)(2,1)} %get-tuple-element.377), channel_id=1, source_target_pairs={{0,1},{1,0},{2,3},{3,2},{16,17},{17,16},{18,19},{19,18},{4,5},{5,4... | collective-permute-start | bytes 7102472 | tf_op jit(solution)/shard_map/ppermute | solution.py:596
  443.4 30.7 %collective-permute-start.36 = (bf16[1088,1088]{1,0:T(8,128)(2,1)}, bf16[1088,1088]{1,0:T(8,128)(2,1)}, u32[]{:S(2)}, u32[]{:S(2)}) collective-permute-start(bf16[1088,1088]{1,0:T(8,128)(2,1)} %add_convert_fusion.1), channel_id=1, source_target_pairs={{0,16},{1,3},{2,18},{3,1},{16,0},{17,19},{18,2},{19,17},{4,20},{5,... | collective-permute-start | bytes 7102472 | tf_op jit(solution)/shard_map/ppermute | solution.py:596
  444.2 122.2 %reduce-scatter.8.cloned.1.call-start = ((), (), s32[]{:S(2)}) async-start(), calls=%async_computation.7 | async-start | bytes 3133440 | tf_op jit(solution)/shard_map/reduce_scatter | solution.py:623
  493.6 38.0 %collective-permute-start.46 = (bf16[272,1088]{1,0:T(8,128)(2,1)S(1)}, bf16[272,1088]{1,0:T(8,128)(2,1)S(1)}, u32[]{:S(2)}, u32[]{:S(2)}) collective-permute-start(bf16[272,1088]{1,0:T(8,128)(2,1)S(1)} %add_convert_fusion.7.refs_0_), channel_id=1, source_target_pairs={{0,1},{1,0},{2,3},{3,2},{16,17},{17,16},{18,19},{19,18},{4,5},{5,4... | collective-permute-start | bytes 1775624 | tf_op jit(solution)/shard_map/ppermute | solution.py:596
  504.0 29.7 %collective-permute-start.47 = (bf16[272,1088]{1,0:T(8,128)(2,1)S(1)}, bf16[272,1088]{1,0:T(8,128)(2,1)S(1)}, u32[]{:S(2)}, u32[]{:S(2)}) collective-permute-start(bf16[272,1088]{1,0:T(8,128)(2,1)S(1)} %collective-permute-done.45.refs_1_), channel_id=1, source_target_pairs={{0,1},{1,0},{2,3},{3,2},{16,17},{17,16},{18,19},{19,18},{4,5},{5,4... | collective-permute-start | bytes 1775624 | tf_op jit(solution)/shard_map/ppermute | solution.py:596
  504.0 31.7 %collective-permute-start.42 = (bf16[1088,256]{1,0:T(8,128)(2,1)}, bf16[1088,256]{1,0:T(8,128)(2,1)S(1)}, u32[]{:S(2)}, u32[]{:S(2)}) collective-permute-start(bf16[1088,256]{1,0:T(8,128)(2,1)} %get-tuple-element.321), channel_id=1, source_target_pairs={{0,1},{1,0},{2,3},{3,2},{4,5},{5,4},{6,7},{7,6},{8,9},{9,8},{10,11... | collective-permute-start | bytes 1671176 | tf_op jit(solution)/shard_map/ppermute | solution.py:602
  504.6 33.6 %collective-permute-start.43 = (bf16[1088,256]{1,0:T(8,128)(2,1)}, bf16[1088,256]{1,0:T(8,128)(2,1)}, u32[]{:S(2)}, u32[]{:S(2)}) collective-permute-start(bf16[1088,256]{1,0:T(8,128)(2,1)} %get-tuple-element.322), channel_id=1, source_target_pairs={{0,2},{1,3},{2,0},{3,1},{4,6},{5,7},{6,4},{7,5},{8,10},{9,11},{10,... | collective-permute-start | bytes 1671176 | tf_op jit(solution)/shard_map/ppermute | solution.py:602
  506.0 32.6 %collective-permute-start.44 = (bf16[1088,256]{1,0:T(8,128)(2,1)}, bf16[1088,256]{1,0:T(8,128)(2,1)}, u32[]{:S(2)}, u32[]{:S(2)}) collective-permute-start(bf16[1088,256]{1,0:T(8,128)(2,1)} %get-tuple-element.323), channel_id=1, source_target_pairs={{0,3},{1,2},{2,1},{3,0},{4,7},{5,6},{6,5},{7,4},{8,11},{9,10},{10,... | collective-permute-start | bytes 1671176 | tf_op jit(solution)/shard_map/ppermute | solution.py:602
  531.6 12.0 %collective-permute-start.37 = (bf16[272,1088]{1,0:T(8,128)(2,1)}, bf16[272,1088]{1,0:T(8,128)(2,1)}, u32[]{:S(2)}, u32[]{:S(2)}) collective-permute-start(bf16[272,1088]{1,0:T(8,128)(2,1)} %reduce-scatter.6.cloned.1.call-done), channel_id=1, source_target_pairs={{0,2},{1,17},{2,0},{3,19},{16,18},{17,1},{18,16},{19,3},{4,6},{5,2... | collective-permute-start | bytes 1775624 | tf_op jit(solution)/shard_map/ppermute | solution.py:596
  538.9 15.7 %collective-permute-start.49 = (bf16[1088,256]{1,0:T(8,128)(2,1)}, bf16[1088,256]{1,0:T(8,128)(2,1)S(1)}, u32[]{:S(2)}, u32[]{:S(2)}) collective-permute-start(bf16[1088,256]{1,0:T(8,128)(2,1)} %get-tuple-element.327), channel_id=1, source_target_pairs={{0,2},{1,3},{2,0},{3,1},{4,6},{5,7},{6,4},{7,5},{8,10},{9,11},{10,... | collective-permute-start | bytes 1671176 | tf_op jit(solution)/shard_map/ppermute | solution.py:602
  542.2 23.4 %collective-permute-start.50 = (bf16[1088,256]{1,0:T(8,128)(2,1)}, bf16[1088,256]{1,0:T(8,128)(2,1)S(1)}, u32[]{:S(2)}, u32[]{:S(2)}) collective-permute-start(bf16[1088,256]{1,0:T(8,128)(2,1)} %get-tuple-element.328), channel_id=1, source_target_pairs={{0,3},{1,2},{2,1},{3,0},{4,7},{5,6},{6,5},{7,4},{8,11},{9,10},{10,... | collective-permute-start | bytes 1671176 | tf_op jit(solution)/shard_map/ppermute | solution.py:602
  566.4 16.4 %collective-permute-start.53 = (bf16[272,1088]{1,0:T(8,128)(2,1)S(1)}, bf16[272,1088]{1,0:T(8,128)(2,1)S(1)}, u32[]{:S(2)}, u32[]{:S(2)}) collective-permute-start(bf16[272,1088]{1,0:T(8,128)(2,1)S(1)} %add_convert_fusion.6.refs_0_), channel_id=1, source_target_pairs={{0,16},{1,3},{2,18},{3,1},{16,0},{17,19},{18,2},{19,17},{4,20},{5,... | collective-permute-start | bytes 1775624 | tf_op jit(solution)/shard_map/ppermute | solution.py:596
  567.7 18.8 %collective-permute-start.51 = (bf16[272,1088]{1,0:T(8,128)(2,1)}, bf16[272,1088]{1,0:T(8,128)(2,1)S(1)}, u32[]{:S(2)}, u32[]{:S(2)}) collective-permute-start(bf16[272,1088]{1,0:T(8,128)(2,1)} %reduce-scatter.8.cloned.1.call-done), channel_id=1, source_target_pairs={{0,2},{1,17},{2,0},{3,19},{16,18},{17,1},{18,16},{19,3},{4,6},{5,2... | collective-permute-start | bytes 1775624 | tf_op jit(solution)/shard_map/ppermute | solution.py:596
  568.9 19.0 %collective-permute-start.54 = (bf16[272,1088]{1,0:T(8,128)(2,1)S(1)}, bf16[272,1088]{1,0:T(8,128)(2,1)S(1)}, u32[]{:S(2)}, u32[]{:S(2)}) collective-permute-start(bf16[272,1088]{1,0:T(8,128)(2,1)S(1)} %add_convert_fusion.6.refs_0_), channel_id=1, source_target_pairs={{0,1},{1,0},{2,3},{3,2},{16,17},{17,16},{18,19},{19,18},{4,5},{5,4... | collective-permute-start | bytes 1775624 | tf_op jit(solution)/shard_map/ppermute | solution.py:596
  587.9 17.8 %collective-permute-start.58 = (bf16[272,1088]{1,0:T(8,128)(2,1)S(1)}, bf16[272,1088]{1,0:T(8,128)(2,1)S(1)}, u32[]{:S(2)}, u32[]{:S(2)}) collective-permute-start(bf16[272,1088]{1,0:T(8,128)(2,1)S(1)} %add_convert_fusion.5.refs_0_), channel_id=1, source_target_pairs={{0,17},{1,2},{2,19},{3,0},{16,1},{17,18},{18,3},{19,16},{4,21},{5,... | collective-permute-start | bytes 1775624 | tf_op jit(solution)/shard_map/ppermute | solution.py:596
  588.1 17.6 %collective-permute-start.57 = (bf16[272,1088]{1,0:T(8,128)(2,1)S(1)}, bf16[272,1088]{1,0:T(8,128)(2,1)S(1)}, u32[]{:S(2)}, u32[]{:S(2)}) collective-permute-start(bf16[272,1088]{1,0:T(8,128)(2,1)S(1)} %add_convert_fusion.5.refs_0_), channel_id=1, source_target_pairs={{0,1},{1,0},{2,3},{3,2},{16,17},{17,16},{18,19},{19,18},{4,5},{5,4... | collective-permute-start | bytes 1775624 | tf_op jit(solution)/shard_map/ppermute | solution.py:596
  589.5 16.2 %collective-permute-start.56 = (bf16[272,1088]{1,0:T(8,128)(2,1)S(1)}, bf16[272,1088]{1,0:T(8,128)(2,1)S(1)}, u32[]{:S(2)}, u32[]{:S(2)}) collective-permute-start(bf16[272,1088]{1,0:T(8,128)(2,1)S(1)} %add_convert_fusion.5.refs_0_), channel_id=1, source_target_pairs={{0,16},{1,3},{2,18},{3,1},{16,0},{17,19},{18,2},{19,17},{4,20},{5,... | collective-permute-start | bytes 1775624 | tf_op jit(solution)/shard_map/ppermute | solution.py:596
  590.9 14.8 %collective-permute-start.59 = (f32[3264]{0:T(1024)S(1)}, f32[3264]{0:T(1024)S(1)}, u32[]{:S(2)}, u32[]{:S(2)}) collective-permute-start(f32[3264]{0:T(1024)S(1)} %add.272), channel_id=1, source_target_pairs={{0,16},{1,17},{2,18},{3,19},{16,0},{17,1},{18,2},{19,3},{4,20},{5,... | collective-permute-start | bytes 39176 | tf_op jit(solution)/shard_map/ppermute | solution.py:654
  (81 other events, 905.0 us)
Sparse Core Ops, SparseCore 0:
  76.9 51.3 all-gather.2
  166.0 50.9 all-gather.4
  319.2 49.9 reduce-scatter.3
  444.3 49.0 reduce-scatter.5
  496.1 51.5 reduce-scatter.7

commit v9 on v8

--- a/solution.py
+++ b/solution.py
@@ -614,8 +614,7 @@
     return [whole] + [plane_swap(whole, kind) for kind in ("near", "core", "far")]
 
 
-def share_by_core(whole):
-    near = plane_swap(whole, "near")
+def share_by_core(whole, near):
     return [whole, near, plane_swap(whole, "core"), plane_swap(near, "core")]
 
 
@@ -1099,10 +1098,11 @@
         down_bias,
         up_bias,
     )
-    slots_in[3], up_weight, down_weight, *pieces_in = pin(
-        (slots_in[3], up_weight, down_weight, *pieces_in)
-    )
     slots_in = [slots_in[0]] + [ctx_swap(slots_in[bits], bits) for bits in range(1, 4)]
+    up_weight, down_weight, *moved = pin(
+        (up_weight, down_weight, *shards, *slots_in, *pieces_in)
+    )
+    shards, slots_in, pieces_in = moved[:3], moved[3:7], moved[7:]
     vectors = gather_vector(jnp.concatenate(pieces_in), z).astype(wide)
     up_piece = jnp.concatenate(
         [
@@ -1111,8 +1111,6 @@
         ],
         axis=1,
     )
-    up_piece, vectors, *moved = pin((up_piece, vectors, *shards, *slots_in))
-    shards, slots_in = moved[:3], moved[3:]
     near_shards = [plane_swap(shard, "near") for shard in shards]
     cotangent, *near_shards = pin((cotangent, *near_shards))
     slots_back = spread(cotangent)
@@ -1147,11 +1145,11 @@
         jnp.concatenate([gain_first, shift_first, qbias, vbias], axis=0),
         around,
     )
-    up_own, queries = pin((up_own, queries))
+    up_own, down_piece, queries = pin((up_own, down_piece, queries))
+    down_own = lax.all_gather(down_piece, "fsdp", axis=0, tiled=True)
     up_near, up_core = plane_swap(up_own, "near"), plane_swap(up_own, "core")
     attended, logs = attend(place, queries, key_rows, value_rows, seq_count, 0, 9, [])
-    down_piece, up_core, up_near, attended = pin((down_piece, up_core, up_near, attended))
-    down_own = lax.all_gather(down_piece, "fsdp", axis=0, tiled=True)
+    up_core, up_near, attended = pin((up_core, up_near, attended))
     logs = logs.T.reshape(64, 2, rows)
     logs_one, logs_two = logs[:5], logs[5:9]
     middle, normed_two_low = by_rows(
@@ -1187,19 +1185,18 @@
         active[first], active[first + 2], slopes[first], slopes[first + 2] = outs
 
     up(0)
-    up_slots[3], slots_back[3], active[0], active[2] = pin(
-        (up_slots[3], slots_back[3], active[0], active[2])
-    )
+    up_slots[3], slots_back[3], down_own, active[0], active[2] = pin(
+        (up_slots[3], slots_back[3], down_own, active[0], active[2])
+    )
+    down_near, down_core = plane_swap(down_own, "near"), plane_swap(down_own, "core")
     upstream_low = turn(slots_back)
     up(1)
-    down_own, *active = pin((down_own, *active))
-    down_near, down_core = plane_swap(down_own, "near"), plane_swap(down_own, "core")
 
     def turned_product(left, right):
         return product(left, right, (0, 0)).astype(low)
 
     down_terms = [turned_product(active[slot], upstream_low) for slot in (3, 2)]
-    upstream_low, *down_terms = pin((upstream_low, *down_terms))
+    upstream_low, down_near, *down_terms = pin((upstream_low, down_near, *down_terms))
     down_terms += [turned_product(active[slot], upstream_low) for slot in (1, 0)]
     down_terms = down_terms[::-1]
     down_far, down_far_two = reduce_core(down_terms)
@@ -1222,7 +1219,6 @@
         )
         return sums
 
-    down_near, upstream_low = pin((down_near, upstream_low))
     down_slots = [down_own, down_near, down_core, plane_swap(down_near, "core")]
     sums_even = hidden(0, upstream_low)
     down_second = low_sum(down_terms[1], down_far_two)
@@ -1282,7 +1278,7 @@
         in_grads,
     )
     down_whole, *in_grads = pin((down_whole, *in_grads))
-    down_parts = share_by_core(down_whole)
+    down_beside = plane_swap(down_whole, "near")
     in_terms = [turned_product(normed_low, grad) for grad in in_grads]
     section_grads = in_terms + [out_term]
     sections_mine = [chosen(kind, section_grads) for kind in classes]
@@ -1305,9 +1301,10 @@
         4,
     )
     first = low_sum(sections_mine[0], far, close)
-    first, up_shard, query_low, *result_slots = pin(
-        (first, up_shard, query_low, *result_slots)
-    )
+    first, up_shard, query_low, down_beside, *result_slots = pin(
+        (first, up_shard, query_low, down_beside, *result_slots)
+    )
+    down_parts = share_by_core(down_whole, down_beside)
     shard = scatter_rows(first)
     outputs = exchange(result_slots)
     up_whole = low_sum(up_shard, plane_swap(up_shard, "other"))
@@ -1346,9 +1343,10 @@
         ),
         1,
     )
-    shard, up_whole, totals, *input_slots = pin((shard, up_whole, totals, *input_slots))
+    up_beside = plane_swap(up_whole, "near")
+    shard, up_whole, up_beside, totals = pin((shard, up_whole, up_beside, totals))
     section_whole = low_sum(shard, plane_swap(shard, "other"))
-    up_parts = share_by_core(up_whole)
+    up_parts = share_by_core(up_whole, up_beside)
     totals = swap_sum(totals, 2)
     section_whole, totals, *up_parts = pin((section_whole, totals, *up_parts))
     section_parts = share_out(section_whole)

time: 629 us -> 663 us (1.054)
  waiting for transfers between devices: 152 us -> 176 us
  starting transfers between devices: 44.7 us -> 57.9 us
  Pallas kernels: 274 us -> 283 us
  matrix products: 62.6 us -> 55.1 us
    ppermute x12, waiting for transfers between devices: 32 us -> 63.1 us  [ctx_swap(): lax.ppermute(values, 'ctx', [(device, device ^ bits) for device in range(...]
    ppermute x36, waiting for transfers between devices: 64.2 us -> 39.9 us  [plane_swap(): lax.ppermute(values, ('dp', 'ctx'), [(device, plane_partner(device, kind)...]
    reduce_scatter x3, waiting for transfers between devices: 12.7 us -> 26.4 us  [scatter_rows(): return lax.psum_scatter(values, 'fsdp', scatter_dimension=0, tiled=True)]
    ppermute x36, starting transfers between devices: 21.9 us -> 34.3 us  [plane_swap(): lax.ppermute(values, ('dp', 'ctx'), [(device, plane_partner(device, kind)...]
    pallas_call x8, Pallas kernels: 155 us -> 163 us  [by_rows(): pl.pallas_call(kernel, grid=(rows // step,), in_specs=[tile] * len(tiled[...]
    dot_general x12, matrix products: 62.6 us -> 55.1 us  [product(): lax.dot_general(left, right, ((dims[:1], dims[1:]), ((), ())), preferred_...]
    ppermute x3, waiting for transfers between devices: 0.01 us -> 6.67 us  [gather_vector(): lax.ppermute(values, 'fsdp', [(device, (device + step) % 4) for device in...]
    unnamed x133 -> x129, local copies, waits for them, and re-layouts: 18.3 us -> 17.3 us
  transfers between devices with their start and end apart: 65 -> 65, of which waited for: 24 -> 25; matrix products, arithmetic and copies ran while one was open for 15% -> 11% of each run, Pallas kernels for 44% -> 43%
where the time goes in v9:
time: 663 us; the launch traced here: 654 us
  Pallas kernels  283 us (43%)
  waiting for transfers between devices  176 us (27%)
  starting transfers between devices  57.9 us (9%)
  matrix products  55.1 us (8%)
  other arithmetic  35 us (5%)
  local copies, waits for them, and re-layouts  32.1 us (5%)
  between operations  15.2 us (2%)
    pallas_call x8, Pallas kernels, by_rows(): pl.pallas_call(kernel, grid=(rows // step,), in_specs=[tile] * len(tiled[...  163 us
    ppermute x12, waiting for transfers between devices, ctx_swap(): lax.ppermute(values, 'ctx', [(device, device ^ bits) for device in range(...  63.1 us
    dot_general x12, matrix products, product(): lax.dot_general(left, right, ((dims[:1], dims[1:]), ((), ())), preferred_...  55.1 us
    pallas_call x2, Pallas kernels, attend_back(): pl.pallas_call(functools.partial(attend_back_kernel, count=count, width=w...  48.1 us
    ppermute x36, waiting for transfers between devices, plane_swap(): lax.ppermute(values, ('dp', 'ctx'), [(device, plane_partner(device, kind)...  39.9 us
    ppermute x36, starting transfers between devices, plane_swap(): lax.ppermute(values, ('dp', 'ctx'), [(device, plane_partner(device, kind)...  34.3 us
    pallas_call x1, Pallas kernels, attend(): pl.pallas_call(functools.partial(attend_kernel, count=count, width=width,...  32 us
    ppermute x3, waiting for transfers between devices, per_device_exchanged(): lax.ppermute(section, 'fsdp', [(device, (device + step) % 4) for device i...  31.3 us
  transfers between devices with their start and end apart: 65, of which 25 were waited for; matrix products, arithmetic and copies ran while one was open for 11% of the time, Pallas kernels for 43%

profile of v9, /device:TPU:8, one launch (start us, length us, event | category | flops | bytes accessed | tf_op | source)
XLA Modules:
  0.0 654.0 jit_solution(10200053666832776896)
XLA Ops:
  7.3 3.4 fusion.11
  20.6 7.8 %collective-permute-done.5.refs_3_ = bf16[1088,256]{1,0:T(8,128)(2,1)S(1)} collective-permute-done((bf16[1088,256]{1,0:T(8,128)(2,1)S(1)}, bf16[1088,256]{1,0:T(8,128)(2,1)S(1)}, u32[]{:S(2)}, u32[]{:S(2)}) %collective-permute-start.5) | collective-permute-done | bytes 557088 | tf_op jit(solution)/shard_map/ppermute | solution.py:602
  29.6 11.0 %collective-permute-done.4.refs_2_ = bf16[1088,256]{1,0:T(8,128)(2,1)} collective-permute-done((bf16[1088,256]{1,0:T(8,128)(2,1)}, bf16[1088,256]{1,0:T(8,128)(2,1)}, u32[]{:S(2)}, u32[]{:S(2)}) %collective-permute-start.4) | collective-permute-done | bytes 557088 | tf_op jit(solution)/shard_map/ppermute | solution.py:602
  40.5 18.3 %collective-permute-done.1.refs_9_ = bf16[272,1088]{1,0:T(8,128)(2,1)} collective-permute-done((bf16[272,1088]{1,0:T(8,128)(2,1)S(1)}, bf16[272,1088]{1,0:T(8,128)(2,1)}, u32[]{:S(2)}, u32[]{:S(2)}) %collective-permute-start.1) | collective-permute-done | bytes 591904 | tf_op jit(solution)/shard_map/ppermute | solution.py:1083
  58.9 13.0 %collective-permute-done.refs_8_ = bf16[272,1088]{1,0:T(8,128)(2,1)} collective-permute-done((bf16[272,1088]{1,0:T(8,128)(2,1)S(1)}, bf16[272,1088]{1,0:T(8,128)(2,1)}, u32[]{:S(2)}, u32[]{:S(2)}) %collective-permute-start) | collective-permute-done | bytes 591904 | tf_op jit(solution)/shard_map/ppermute | solution.py:1083
  79.7 3.0 collective-permute-done.8
  92.1 6.7 %collective-permute-done.11.refs_13_ = bf16[272,1088]{1,0:T(8,128)(2,1)} collective-permute-done((bf16[272,1088]{1,0:T(8,128)(2,1)}, bf16[272,1088]{1,0:T(8,128)(2,1)}, u32[]{:S(2)}, u32[]{:S(2)}) %collective-permute-start.11) | collective-permute-done | bytes 591904 | tf_op jit(solution)/shard_map/ppermute | solution.py:596
  103.3 21.7 %front.1 = (bf16[1024,1088]{1,0:T(8,128)(2,1)}, bf16[1024,1088]{1,0:T(8,128)(2,1)}, bf16[1024,1088]{1,0:T(8,128)(2,1)}, bf16[1024,1088]{1,0:T(8,128)(2,1)}, bf16...) custom-call(s32[16]{0:T(128)} %stack.120.places_ref, f32[4,1088]{1,0:T(4,128)} %pad_maximum_fusion.1.vectors_ref, ...), custom_call_target="tpu_custom_call" | custom-call | flops 1024 | bytes 1024 | tf_op jit(solution)/shard_map/front/pallas_call | solution.py:732
  129.8 32.0 %attend.1 = (bf16[1024,1088]{1,0:T(8,128)(2,1)S(1)}, f32[1024,128]{1,0:T(8,128)S(1)}) custom-call(s32[1]{0:T(128)} %bitcast.30.place_ref, bf16[1024,1088]{1,0:T(8,128)(2,1)S(1)} %copy-done.3, bf16[1024,1088]{1,0:T(8,128)(2,1)} %get-tuple-element.206.k_ref, bf16[1024,1088]{1,0:T(8,128)(2,1)} %get-tuple-element.207.v_ref), custom_call_target="tpu_custom_call" | custom-call | flops 1024 | bytes 1024 | tf_op jit(solution)/shard_map/attend/pallas_call | solution.py:507
  170.6 9.7 %middle.1 = (f32[1024,1088]{1,0:T(8,128)}, bf16[1024,1088]{1,0:T(8,128)(2,1)}) custom-call(bf16[1024,1088]{1,0:T(8,128)(2,1)} %get-tuple-element.211.x_ref, bf16[1024,1088]{1,0:T(8,128)(2,1)} %copy-done.4, f32[3,1088]{1,0:T(4,128)} %pad_maximum_fusion.2.vectors_ref, bf16[16,272,1088]{2,1,0:T(8,128)(2,1)} %get-tuple-element.213.all_ref.refs_8_), custom_call_target="tpu_custom_call" | custom-call | flops 1024 | bytes 1024 | tf_op jit(solution)/shard_map/middle/pallas_call | solution.py:1005
  180.3 17.5 %up.2 = (bf16[1024,1088]{1,0:T(8,128)(2,1)}, bf16[1024,1088]{1,0:T(8,128)(2,1)}, bf16[1024,1088]{1,0:T(8,128)(2,1)}, bf16[1024,1088]{1,0:T(8,128)(2,1)}) custom-call(bf16[1024,1088]{1,0:T(8,128)(2,1)} %get-tuple-element.244.h_ref, f32[2,1088]{1,0:T(2,128)} %pad_maximum_fusion.3.biases_ref, bf16[1088,1088]{1,0:T(8,128)(2,1)} %all-gather.3.cloned.1.call-done.refs_0_.refs_4_, ...), custom_call_target="tpu_custom_call" | custom-call | flops 1024 | bytes 1024 | tf_op jit(solution)/shard_map/up/pallas_call | solution.py:1005
  200.3 25.8 %up.3 = (bf16[1024,1088]{1,0:T(8,128)(2,1)}, bf16[1024,1088]{1,0:T(8,128)(2,1)}, bf16[1024,1088]{1,0:T(8,128)(2,1)}, bf16[1024,1088]{1,0:T(8,128)(2,1)}) custom-call(bf16[1024,1088]{1,0:T(8,128)(2,1)} %get-tuple-element.244.h_ref, f32[2,1088]{1,0:T(2,128)} %pad_maximum_fusion.4.biases_ref, bf16[1088,1088]{1,0:T(8,128)(2,1)} %collective-permute-done.21.refs_0_.refs_5_, ...), custom_call_target="tpu_custom_call" | custom-call | flops 1024 | bytes 1024 | tf_op jit(solution)/shard_map/up/pallas_call | solution.py:1005
  232.6 4.6 convolution_convert_fusion.10
  237.2 4.6 convolution_convert_fusion.11
  241.8 13.1 %collective-permute-start.27 = (bf16[1088,1088]{1,0:T(8,128)(2,1)}, bf16[1088,1088]{1,0:T(8,128)(2,1)}, u32[]{:S(2)}, u32[]{:S(2)}) collective-permute-start(bf16[1088,1088]{1,0:T(8,128)(2,1)} %convolution_convert_fusion.11), channel_id=1, source_target_pairs={{0,1},{1,0},{2,3},{3,2},{16,17},{17,16},{18,19},{19,18},{4,5},{5,4... | collective-permute-start | bytes 7102472 | tf_op jit(solution)/shard_map/ppermute | solution.py:596
  255.4 4.6 convolution_convert_fusion.8
  260.0 4.8 convolution_convert_fusion.9
  264.8 14.1 %hidden.2 = (bf16[1024,1088]{1,0:T(8,128)(2,1)}, bf16[1024,1088]{1,0:T(8,128)(2,1)}, f32[3,8,1088]{2,1,0:T(8,128)}) custom-call(bf16[1024,1088]{1,0:T(8,128)(2,1)} %copy-done.2, bf16[1024,1088]{1,0:T(8,128)(2,1)} %get-tuple-element.230.refs_0_, bf16[1024,1088]{1,0:T(8,128)(2,1)} %get-tuple-element.231.refs_1_, ...), custom_call_target="tpu_custom_call" | custom-call | flops 1024 | bytes 1024 | tf_op jit(solution)/shard_map/hidden/pallas_call | solution.py:1005
  279.0 3.8 add_convert_fusion.4
  282.8 14.6 %hidden.3 = (bf16[1024,1088]{1,0:T(8,128)(2,1)}, bf16[1024,1088]{1,0:T(8,128)(2,1)}, f32[3,8,1088]{2,1,0:T(8,128)}) custom-call(bf16[1024,1088]{1,0:T(8,128)(2,1)} %copy-done.2, bf16[1024,1088]{1,0:T(8,128)(2,1)} %get-tuple-element.236.refs_0_, bf16[1024,1088]{1,0:T(8,128)(2,1)} %get-tuple-element.237.refs_1_, ...), custom_call_target="tpu_custom_call" | custom-call | flops 1024 | bytes 1024 | tf_op jit(solution)/shard_map/hidden/pallas_call | solution.py:1005
  297.4 4.9 convolution_convert_fusion.7
  302.4 4.5 convolution_convert_fusion.6
  307.7 4.6 convolution_convert_fusion.4
  312.3 4.5 fusion.2
  316.8 20.6 %collective-permute-done.31 = bf16[1088,1088]{1,0:T(8,128)(2,1)S(1)} collective-permute-done((bf16[1088,1088]{1,0:T(8,128)(2,1)S(1)}, bf16[1088,1088]{1,0:T(8,128)(2,1)S(1)}, u32[]{:S(2)}, u32[]{:S(2)}) %collective-permute-start.31) | collective-permute-done | bytes 2367520 | tf_op jit(solution)/shard_map/ppermute | solution.py:596
  337.4 4.3 add_convert_fusion.3
  342.6 31.9 %back.1 = (f32[1024,1088]{1,0:T(8,128)}, bf16[1024,1088]{1,0:T(8,128)(2,1)}, bf16[1024,1088]{1,0:T(8,128)(2,1)}, f32[3,8,1088]{2,1,0:T(8,128)}) custom-call(bf16[1024,1088]{1,0:T(8,128)(2,1)} %copy-done.2, f32[1024,1088]{1,0:T(8,128)} %get-tuple-element.284.middle_ref, f32[1,1088]{1,0:T(1,128)} %copy-done.51, bf16[1024,1088]{1,0:T(8,128)(2,1)} %get-tuple-element.252.refs_0_, ...), custom_call_target="tpu_custom_call" | custom-call | flops 1024 | bytes 1024 | tf_op jit(solution)/shard_map/back/pallas_call | solution.py:1005
  374.5 6.4 convolution_convert_fusion.3
  380.9 5.0 add_convert_fusion.2
  385.9 26.3 %attend_back.2 = (bf16[1024,1088]{1,0:T(8,128)(2,1)S(1)}, bf16[1024,1088]{1,0:T(8,128)(2,1)S(1)}, bf16[1024,1088]{1,0:T(8,128)(2,1)}) custom-call(s32[1]{0:T(128)} %bitcast.30.place_ref, bf16[1024,1088]{1,0:T(8,128)(2,1)} %get-tuple-element.205.q_ref, bf16[1024,1088]{1,0:T(8,128)(2,1)} %get-tuple-element.206.k_ref, ...), custom_call_target="tpu_custom_call" | custom-call | flops 1024 | bytes 1024 | tf_op jit(solution)/shard_map/attend_back/pallas_call | solution.py:537
  416.6 21.8 %attend_back.3 = (bf16[1024,1088]{1,0:T(8,128)(2,1)S(1)}, bf16[1024,1088]{1,0:T(8,128)(2,1)S(1)}, bf16[1024,1088]{1,0:T(8,128)(2,1)}) custom-call(s32[1]{0:T(128)} %bitcast.30.place_ref, bf16[1024,1088]{1,0:T(8,128)(2,1)} %get-tuple-element.205.q_ref, ...), custom_call_target="tpu_custom_call", output_to_operand_aliasing={{0}: (7, {}), {1}: (8, {}), {2}: (9, {})} | custom-call | flops 1024 | bytes 1024 | tf_op jit(solution)/shard_map/attend_back/pallas_call | solution.py:537
  441.0 3.1 convolution_convert_fusion.1
  444.1 3.1 convolution_convert_fusion
  447.3 5.3 select_select_fusion
  453.1 7.8 %collective-permute-done.34 = bf16[1088,1088]{1,0:T(8,128)(2,1)S(1)} collective-permute-done((bf16[1088,1088]{1,0:T(8,128)(2,1)S(1)}, bf16[1088,1088]{1,0:T(8,128)(2,1)S(1)}, u32[]{:S(2)}, u32[]{:S(2)}) %collective-permute-start.34) | collective-permute-done | bytes 2367520 | tf_op jit(solution)/shard_map/ppermute | solution.py:596
  460.9 3.2 add_convert_fusion.1
  468.4 25.6 %down.1 = (bf16[1088,256]{1,0:T(8,128)(2,1)}, bf16[1088,256]{1,0:T(8,128)(2,1)}, bf16[1088,256]{1,0:T(8,128)(2,1)}, bf16[1088,256]{1,0:T(8,128)(2,1)}) custom-call(f32[1024,1088]{1,0:T(8,128)} %get-tuple-element.284.middle_ref, f32[1,1088]{1,0:T(1,128)} %reshape.446.vectors_ref, bf16[1024,1088]{1,0:T(8,128)(2,1)} %get-tuple-element.224.refs_0_, ...), custom_call_target="tpu_custom_call" | custom-call | flops 1024 | bytes 1024 | tf_op jit(solution)/shard_map/down/pallas_call | solution.py:1005
  496.3 7.3 %add_convert_fusion = bf16[1088,1088]{1,0:T(8,128)(2,1)} fusion(bf16[1088,1088]{1,0:T(8,128)(2,1)} %collective-permute-done.36, bf16[1088,1088]{1,0:T(8,128)(2,1)} %copy-done.29, bf16[1088,1088]{1,0:T(8,128)(2,1)} %copy-done.24, bf16[1088,1088]{1,0:T(8,128)(2,1)} %copy-done.22, bf16[1088,1088]{1,0:T(8,128)(2,1)} %copy-done.23, ...), kind=kLoop, calls=%fused_computation.15 | loop fusion | flops 10653696 | bytes 16572419 | tf_op jit(solution)/shard_map/convert_element_type | solution.py:606
  503.6 12.6 %reduce-scatter.6.cloned.1.call-done = bf16[272,1088]{1,0:T(8,128)(2,1)} async-done(((bf16[1088,1088]{1,0:T(8,128)(2,1)}), bf16[272,1088]{1,0:T(8,128)(2,1)}) %reduce-scatter.6.cloned.1.call-update) | async-done | bytes 591888 | tf_op jit(solution)/shard_map/reduce_scatter | solution.py:622
  519.9 24.2 %last.1 = (bf16[1088,256]{1,0:T(8,128)(2,1)}, bf16[1088,256]{1,0:T(8,128)(2,1)}, bf16[1088,256]{1,0:T(8,128)(2,1)}, bf16[1088,256]{1,0:T(8,128)(2,1)}, f32[4,8,1088]{2,1,0:T(8,128)}) custom-call(bf16[1024,1088]{1,0:T(8,128)(2,1)} %copy-done.6, bf16[1024,1088]{1,0:T(8,128)(2,1)} %copy-done.9, bf16[1024,1088]{1,0:T(8,128)(2,1)} %get-tuple-element.296.v_ref, ...), custom_call_target="tpu_custom_call" | custom-call | flops 1024 | bytes 1024 | tf_op jit(solution)/shard_map/last/pallas_call | solution.py:1005
  556.7 13.8 %reduce-scatter.8.cloned.1.call-done = bf16[272,1088]{1,0:T(8,128)(2,1)} async-done(((bf16[1088,1088]{1,0:T(8,128)(2,1)}), bf16[272,1088]{1,0:T(8,128)(2,1)}) %reduce-scatter.8.cloned.1.call-update) | async-done | bytes 591888 | tf_op jit(solution)/shard_map/reduce_scatter | solution.py:622
  573.2 18.8 %collective-permute-done.53.refs_3_ = bf16[1088,256]{1,0:T(8,128)(2,1)S(1)} collective-permute-done((bf16[1088,256]{1,0:T(8,128)(2,1)}, bf16[1088,256]{1,0:T(8,128)(2,1)S(1)}, u32[]{:S(2)}, u32[]{:S(2)}) %collective-permute-start.53) | collective-permute-done | bytes 557088 | tf_op jit(solution)/shard_map/ppermute | solution.py:602
  600.9 10.6 %collective-permute-done.57.refs_2_ = bf16[1088,256]{1,0:T(8,128)(2,1)S(1)} collective-permute-done((bf16[1088,256]{1,0:T(8,128)(2,1)}, bf16[1088,256]{1,0:T(8,128)(2,1)S(1)}, u32[]{:S(2)}, u32[]{:S(2)}) %collective-permute-start.57) | collective-permute-done | bytes 557088 | tf_op jit(solution)/shard_map/ppermute | solution.py:602
  616.9 3.8 settle.5
  620.6 14.8 %collective-permute-done.58.refs_3_ = bf16[1088,256]{1,0:T(8,128)(2,1)S(1)} collective-permute-done((bf16[1088,256]{1,0:T(8,128)(2,1)}, bf16[1088,256]{1,0:T(8,128)(2,1)S(1)}, u32[]{:S(2)}, u32[]{:S(2)}) %collective-permute-start.58) | collective-permute-done | bytes 557088 | tf_op jit(solution)/shard_map/ppermute | solution.py:602
  635.5 2.9 settle.4
  638.4 4.1 assemble.2
  643.8 3.4 assemble.3
  (325 shorter events, 105.4 us)
Async XLA Ops:
  7.2 119.2 %all-gather.3.cloned.1.call-start = ((), (), s32[]{:S(2)}) async-start(), calls=%async_computation.3 | async-start | bytes 3133440 | tf_op jit(solution)/shard_map/all_gather | solution.py:1128
  13.5 14.9 %collective-permute-start.5 = (bf16[1088,256]{1,0:T(8,128)(2,1)S(1)}, bf16[1088,256]{1,0:T(8,128)(2,1)S(1)}, u32[]{:S(2)}, u32[]{:S(2)}) collective-permute-start(bf16[1088,256]{1,0:T(8,128)(2,1)S(1)} %get-tuple-element.367), channel_id=1, source_target_pairs={{0,3},{1,2},{2,1},{3,0},{4,7},{5,6},{6,5},{7,4},{8,11},{9,10},{10,... | collective-permute-start | bytes 1671176 | tf_op jit(solution)/shard_map/ppermute | solution.py:602
  14.5 26.0 %collective-permute-start.2 = (bf16[272,1088]{1,0:T(8,128)(2,1)S(1)}, bf16[272,1088]{1,0:T(8,128)(2,1)}, u32[]{:S(2)}, u32[]{:S(2)}) collective-permute-start(bf16[272,1088]{1,0:T(8,128)(2,1)S(1)} %get-tuple-element.178), channel_id=1, source_target_pairs={{0,12},{4,0},{8,4},{12,8},{1,13},{5,1},{9,5},{13,9},{2,14},{6,2},{... | collective-permute-start | bytes 1775624 | tf_op jit(solution)/shard_map/ppermute | solution.py:1083
  14.9 43.9 %collective-permute-start.1 = (bf16[272,1088]{1,0:T(8,128)(2,1)S(1)}, bf16[272,1088]{1,0:T(8,128)(2,1)}, u32[]{:S(2)}, u32[]{:S(2)}) collective-permute-start(bf16[272,1088]{1,0:T(8,128)(2,1)S(1)} %get-tuple-element.178), channel_id=1, source_target_pairs={{0,8},{4,12},{8,0},{12,4},{1,9},{5,13},{9,1},{13,5},{2,10},{6,14},... | collective-permute-start | bytes 1775624 | tf_op jit(solution)/shard_map/ppermute | solution.py:1083
  17.5 54.3 %collective-permute-start = (bf16[272,1088]{1,0:T(8,128)(2,1)S(1)}, bf16[272,1088]{1,0:T(8,128)(2,1)}, u32[]{:S(2)}, u32[]{:S(2)}) collective-permute-start(bf16[272,1088]{1,0:T(8,128)(2,1)S(1)} %get-tuple-element.178), channel_id=1, source_target_pairs={{0,4},{4,8},{8,12},{12,0},{1,5},{5,9},{9,13},{13,1},{2,6},{6,10},{... | collective-permute-start | bytes 1775624 | tf_op jit(solution)/shard_map/ppermute | solution.py:1083
  20.0 20.5 %collective-permute-start.4 = (bf16[1088,256]{1,0:T(8,128)(2,1)}, bf16[1088,256]{1,0:T(8,128)(2,1)}, u32[]{:S(2)}, u32[]{:S(2)}) collective-permute-start(bf16[1088,256]{1,0:T(8,128)(2,1)} %get-tuple-element.368), channel_id=1, source_target_pairs={{0,2},{1,3},{2,0},{3,1},{4,6},{5,7},{6,4},{7,5},{8,10},{9,11},{10,... | collective-permute-start | bytes 1671176 | tf_op jit(solution)/shard_map/ppermute | solution.py:602
  74.6 123.2 %all-gather.5.cloned.1.call-start = ((), (), s32[]{:S(2)}) async-start(), calls=%async_computation.4 | async-start | bytes 3133440 | tf_op jit(solution)/shard_map/all_gather | solution.py:1149
  74.7 16.8 %collective-permute-start.9 = (bf16[272,1088]{1,0:T(8,128)(2,1)}, bf16[272,1088]{1,0:T(8,128)(2,1)S(1)}, u32[]{:S(2)}, u32[]{:S(2)}) collective-permute-start(bf16[272,1088]{1,0:T(8,128)(2,1)} %collective-permute-done.refs_8_), channel_id=1, source_target_pairs={{0,16},{1,3},{2,18},{3,1},{16,0},{17,19},{18,2},{19,17},{4,20},{5,... | collective-permute-start | bytes 1775624 | tf_op jit(solution)/shard_map/ppermute | solution.py:596
  76.3 15.8 %collective-permute-start.10 = (bf16[272,1088]{1,0:T(8,128)(2,1)}, bf16[272,1088]{1,0:T(8,128)(2,1)}, u32[]{:S(2)}, u32[]{:S(2)}) collective-permute-start(bf16[272,1088]{1,0:T(8,128)(2,1)} %collective-permute-done.1.refs_9_), channel_id=1, source_target_pairs={{0,16},{1,3},{2,18},{3,1},{16,0},{17,19},{18,2},{19,17},{4,20},{5,... | collective-permute-start | bytes 1775624 | tf_op jit(solution)/shard_map/ppermute | solution.py:596
  76.8 22.0 %collective-permute-start.11 = (bf16[272,1088]{1,0:T(8,128)(2,1)}, bf16[272,1088]{1,0:T(8,128)(2,1)}, u32[]{:S(2)}, u32[]{:S(2)}) collective-permute-start(bf16[272,1088]{1,0:T(8,128)(2,1)} %collective-permute-done.2.refs_10_), channel_id=1, source_target_pairs={{0,16},{1,3},{2,18},{3,1},{16,0},{17,19},{18,2},{19,17},{4,20},{5,... | collective-permute-start | bytes 1775624 | tf_op jit(solution)/shard_map/ppermute | solution.py:596
  78.3 21.0 %collective-permute-start.12 = (bf16[272,1088]{1,0:T(8,128)(2,1)}, bf16[272,1088]{1,0:T(8,128)(2,1)}, u32[]{:S(2)}, u32[]{:S(2)}) collective-permute-start(bf16[272,1088]{1,0:T(8,128)(2,1)} %collective-permute-done.refs_8_), channel_id=1, source_target_pairs={{0,1},{1,0},{2,3},{3,2},{16,17},{17,16},{18,19},{19,18},{4,5},{5,4... | collective-permute-start | bytes 1775624 | tf_op jit(solution)/shard_map/ppermute | solution.py:596
  126.4 36.9 %collective-permute-start.21 = (bf16[1088,1088]{1,0:T(8,128)(2,1)}, bf16[1088,1088]{1,0:T(8,128)(2,1)}, u32[]{:S(2)}, u32[]{:S(2)}) collective-permute-start(bf16[1088,1088]{1,0:T(8,128)(2,1)} %all-gather.3.cloned.1.call-done.refs_0_.refs_4_), channel_id=1, source_target_pairs={{0,16},{1,3},{2,18},{3,1},{16,0},{17,19},{18,2},{19,17},{4,20},{5,... | collective-permute-start | bytes 7102472 | tf_op jit(solution)/shard_map/ppermute | solution.py:596
  127.8 35.4 %collective-permute-start.20 = (bf16[1088,1088]{1,0:T(8,128)(2,1)}, bf16[1088,1088]{1,0:T(8,128)(2,1)S(1)}, u32[]{:S(2)}, u32[]{:S(2)}) collective-permute-start(bf16[1088,1088]{1,0:T(8,128)(2,1)} %all-gather.3.cloned.1.call-done.refs_0_.refs_4_), channel_id=1, source_target_pairs={{0,1},{1,0},{2,3},{3,2},{16,17},{17,16},{18,19},{19,18},{4,5},{5,4... | collective-permute-start | bytes 7102472 | tf_op jit(solution)/shard_map/ppermute | solution.py:596
  127.9 285.7 %reduce-scatter.4.cloned.1.call-start = ((), (), s32[]{:S(2)}) async-start(), calls=%async_computation.5 | async-start | bytes 3133440 | tf_op jit(solution)/shard_map/reduce_scatter | solution.py:622
  163.3 34.5 %collective-permute-start.22 = (bf16[1088,1088]{1,0:T(8,128)(2,1)}, bf16[1088,1088]{1,0:T(8,128)(2,1)}, u32[]{:S(2)}, u32[]{:S(2)}) collective-permute-start(bf16[1088,1088]{1,0:T(8,128)(2,1)} %collective-permute-done.21.refs_0_.refs_5_), channel_id=1, source_target_pairs={{0,1},{1,0},{2,3},{3,2},{16,17},{17,16},{18,19},{19,18},{4,5},{5,4... | collective-permute-start | bytes 7102472 | tf_op jit(solution)/shard_map/ppermute | solution.py:596
  167.3 30.5 %collective-permute-start.23 = (bf16[1088,256]{1,0:T(8,128)(2,1)S(1)}, bf16[1088,256]{1,0:T(8,128)(2,1)S(1)}, u32[]{:S(2)}, u32[]{:S(2)}) collective-permute-start(bf16[1088,256]{1,0:T(8,128)(2,1)S(1)} %get-tuple-element.363), channel_id=1, source_target_pairs={{0,3},{1,2},{2,1},{3,0},{4,7},{5,6},{6,5},{7,4},{8,11},{9,10},{10,... | collective-permute-start | bytes 1671176 | tf_op jit(solution)/shard_map/ppermute | solution.py:602
  197.8 44.0 %collective-permute-start.24 = (bf16[1088,1088]{1,0:T(8,128)(2,1)}, bf16[1088,1088]{1,0:T(8,128)(2,1)}, u32[]{:S(2)}, u32[]{:S(2)}) collective-permute-start(bf16[1088,1088]{1,0:T(8,128)(2,1)} %all-gather.5.cloned.1.call-done.refs_2_.refs_4_), channel_id=1, source_target_pairs={{0,16},{1,3},{2,18},{3,1},{16,0},{17,19},{18,2},{19,17},{4,20},{5,... | collective-permute-start | bytes 7102472 | tf_op jit(solution)/shard_map/ppermute | solution.py:596
  198.4 27.7 %collective-permute-start.19 = (bf16[1088,256]{1,0:T(8,128)(2,1)}, bf16[1088,256]{1,0:T(8,128)(2,1)S(1)}, u32[]{:S(2)}, u32[]{:S(2)}) collective-permute-start(bf16[1088,256]{1,0:T(8,128)(2,1)} %get-tuple-element.364), channel_id=1, source_target_pairs={{0,2},{1,3},{2,0},{3,1},{4,6},{5,7},{6,4},{7,5},{8,10},{9,11},{10,... | collective-permute-start | bytes 1671176 | tf_op jit(solution)/shard_map/ppermute | solution.py:602
  199.0 28.0 %collective-permute-start.18 = (bf16[1088,256]{1,0:T(8,128)(2,1)S(1)}, bf16[1088,256]{1,0:T(8,128)(2,1)S(1)}, u32[]{:S(2)}, u32[]{:S(2)}) collective-permute-start(bf16[1088,256]{1,0:T(8,128)(2,1)S(1)} %get-tuple-element.365), channel_id=1, source_target_pairs={{0,1},{1,0},{2,3},{3,2},{4,5},{5,4},{6,7},{7,6},{8,9},{9,8},{10,11... | collective-permute-start | bytes 1671176 | tf_op jit(solution)/shard_map/ppermute | solution.py:602
  200.1 64.7 %collective-permute-start.26 = (bf16[1088,1088]{1,0:T(8,128)(2,1)}, bf16[1088,1088]{1,0:T(8,128)(2,1)}, u32[]{:S(2)}, u32[]{:S(2)}) collective-permute-start(bf16[1088,1088]{1,0:T(8,128)(2,1)} %all-gather.5.cloned.1.call-done.refs_2_.refs_4_), channel_id=1, source_target_pairs={{0,1},{1,0},{2,3},{3,2},{16,17},{17,16},{18,19},{19,18},{4,5},{5,4... | collective-permute-start | bytes 7102472 | tf_op jit(solution)/shard_map/ppermute | solution.py:596
  241.8 37.2 %collective-permute-start.27 = (bf16[1088,1088]{1,0:T(8,128)(2,1)}, bf16[1088,1088]{1,0:T(8,128)(2,1)}, u32[]{:S(2)}, u32[]{:S(2)}) collective-permute-start(bf16[1088,1088]{1,0:T(8,128)(2,1)} %convolution_convert_fusion.11), channel_id=1, source_target_pairs={{0,1},{1,0},{2,3},{3,2},{16,17},{17,16},{18,19},{19,18},{4,5},{5,4... | collective-permute-start | bytes 7102472 | tf_op jit(solution)/shard_map/ppermute | solution.py:596
  254.9 42.5 %collective-permute-start.25 = (bf16[1088,1088]{1,0:T(8,128)(2,1)}, bf16[1088,1088]{1,0:T(8,128)(2,1)}, u32[]{:S(2)}, u32[]{:S(2)}) collective-permute-start(bf16[1088,1088]{1,0:T(8,128)(2,1)} %convolution_convert_fusion.10), channel_id=1, source_target_pairs={{0,1},{1,0},{2,3},{3,2},{16,17},{17,16},{18,19},{19,18},{4,5},{5,4... | collective-permute-start | bytes 7102472 | tf_op jit(solution)/shard_map/ppermute | solution.py:596
  254.9 27.9 %collective-permute-start.28 = (bf16[1088,1088]{1,0:T(8,128)(2,1)}, bf16[1088,1088]{1,0:T(8,128)(2,1)}, u32[]{:S(2)}, u32[]{:S(2)}) collective-permute-start(bf16[1088,1088]{1,0:T(8,128)(2,1)} %collective-permute-done.24.refs_2_.refs_5_), channel_id=1, source_target_pairs={{0,1},{1,0},{2,3},{3,2},{16,17},{17,16},{18,19},{19,18},{4,5},{5,4... | collective-permute-start | bytes 7102472 | tf_op jit(solution)/shard_map/ppermute | solution.py:596
  306.9 30.5 %collective-permute-start.31 = (bf16[1088,1088]{1,0:T(8,128)(2,1)S(1)}, bf16[1088,1088]{1,0:T(8,128)(2,1)S(1)}, u32[]{:S(2)}, u32[]{:S(2)}) collective-permute-start(bf16[1088,1088]{1,0:T(8,128)(2,1)S(1)} %copy-done.30), channel_id=1, source_target_pairs={{0,16},{1,3},{2,18},{3,1},{16,0},{17,19},{18,2},{19,17},{4,20},{5,... | collective-permute-start | bytes 7102472 | tf_op jit(solution)/shard_map/ppermute | solution.py:596
  307.5 34.2 %collective-permute-start.30 = (bf16[1088,1088]{1,0:T(8,128)(2,1)}, bf16[1088,1088]{1,0:T(8,128)(2,1)}, u32[]{:S(2)}, u32[]{:S(2)}) collective-permute-start(bf16[1088,1088]{1,0:T(8,128)(2,1)} %convolution_convert_fusion.6), channel_id=1, source_target_pairs={{0,1},{1,0},{2,3},{3,2},{16,17},{17,16},{18,19},{19,18},{4,5},{5,4... | collective-permute-start | bytes 7102472 | tf_op jit(solution)/shard_map/ppermute | solution.py:596
  341.7 174.5 %reduce-scatter.6.cloned.1.call-start = ((), (), s32[]{:S(2)}) async-start(), calls=%async_computation.6 | async-start | bytes 3133440 | tf_op jit(solution)/shard_map/reduce_scatter | solution.py:622
  341.8 39.1 %collective-permute-start.32 = (bf16[1088,1088]{1,0:T(8,128)(2,1)}, bf16[1088,1088]{1,0:T(8,128)(2,1)}, u32[]{:S(2)}, u32[]{:S(2)}) collective-permute-start(bf16[1088,1088]{1,0:T(8,128)(2,1)} %fusion.2), channel_id=1, source_target_pairs={{0,16},{1,3},{2,18},{3,1},{16,0},{17,19},{18,2},{19,17},{4,20},{5,... | collective-permute-start | bytes 7102472 | tf_op jit(solution)/shard_map/ppermute | solution.py:596
  413.5 24.9 %collective-permute-start.33 = (bf16[272,1088]{1,0:T(8,128)(2,1)}, bf16[272,1088]{1,0:T(8,128)(2,1)}, u32[]{:S(2)}, u32[]{:S(2)}) collective-permute-start(bf16[272,1088]{1,0:T(8,128)(2,1)} %reduce-scatter.4.cloned.1.call-done), channel_id=1, source_target_pairs={{0,2},{1,17},{2,0},{3,19},{16,18},{17,1},{18,16},{19,3},{4,6},{5,2... | collective-permute-start | bytes 1775624 | tf_op jit(solution)/shard_map/ppermute | solution.py:596
  452.6 11.5 %collective-permute-start.35 = (bf16[1088,1088]{1,0:T(8,128)(2,1)}, bf16[1088,1088]{1,0:T(8,128)(2,1)S(1)}, u32[]{:S(2)}, u32[]{:S(2)}) collective-permute-start(bf16[1088,1088]{1,0:T(8,128)(2,1)} %get-tuple-element.357), channel_id=1, source_target_pairs={{0,1},{1,0},{2,3},{3,2},{16,17},{17,16},{18,19},{19,18},{4,5},{5,4... | collective-permute-start | bytes 7102472 | tf_op jit(solution)/shard_map/ppermute | solution.py:596
  465.6 30.7 %collective-permute-start.36 = (bf16[1088,1088]{1,0:T(8,128)(2,1)}, bf16[1088,1088]{1,0:T(8,128)(2,1)}, u32[]{:S(2)}, u32[]{:S(2)}) collective-permute-start(bf16[1088,1088]{1,0:T(8,128)(2,1)} %add_convert_fusion.1), channel_id=1, source_target_pairs={{0,16},{1,3},{2,18},{3,1},{16,0},{17,19},{18,2},{19,17},{4,20},{5,... | collective-permute-start | bytes 7102472 | tf_op jit(solution)/shard_map/ppermute | solution.py:596
  466.9 103.6 %reduce-scatter.8.cloned.1.call-start = ((), (), s32[]{:S(2)}) async-start(), calls=%async_computation.7 | async-start | bytes 3133440 | tf_op jit(solution)/shard_map/reduce_scatter | solution.py:622
  467.6 36.0 %collective-permute-start.37 = (bf16[272,1088]{1,0:T(8,128)(2,1)}, bf16[272,1088]{1,0:T(8,128)(2,1)S(1)}, u32[]{:S(2)}, u32[]{:S(2)}) collective-permute-start(bf16[272,1088]{1,0:T(8,128)(2,1)} %add_convert_fusion.7.refs_0_), channel_id=1, source_target_pairs={{0,16},{1,3},{2,18},{3,1},{16,0},{17,19},{18,2},{19,17},{4,20},{5,... | collective-permute-start | bytes 1775624 | tf_op jit(solution)/shard_map/ppermute | solution.py:596
  517.3 27.7 %collective-permute-start.38 = (bf16[272,1088]{1,0:T(8,128)(2,1)S(1)}, bf16[272,1088]{1,0:T(8,128)(2,1)S(1)}, u32[]{:S(2)}, u32[]{:S(2)}) collective-permute-start(bf16[272,1088]{1,0:T(8,128)(2,1)S(1)} %copy-done.39), channel_id=1, source_target_pairs={{0,2},{1,17},{2,0},{3,19},{16,18},{17,1},{18,16},{19,3},{4,6},{5,2... | collective-permute-start | bytes 1775624 | tf_op jit(solution)/shard_map/ppermute | solution.py:596
  519.8 52.2 %collective-permute-start.54 = (bf16[272,1088]{1,0:T(8,128)(2,1)}, bf16[272,1088]{1,0:T(8,128)(2,1)S(1)}, u32[]{:S(2)}, u32[]{:S(2)}) collective-permute-start(bf16[272,1088]{1,0:T(8,128)(2,1)} %add_convert_fusion.7.refs_0_), channel_id=1, source_target_pairs={{0,1},{1,0},{2,3},{3,2},{16,17},{17,16},{18,19},{19,18},{4,5},{5,4... | collective-permute-start | bytes 1775624 | tf_op jit(solution)/shard_map/ppermute | solution.py:596
  545.2 11.5 %collective-permute-start.39 = (bf16[272,1088]{1,0:T(8,128)(2,1)S(1)}, bf16[272,1088]{1,0:T(8,128)(2,1)S(1)}, u32[]{:S(2)}, u32[]{:S(2)}) collective-permute-start(bf16[272,1088]{1,0:T(8,128)(2,1)S(1)} %add_convert_fusion.6.refs_0_), channel_id=1, source_target_pairs={{0,16},{1,3},{2,18},{3,1},{16,0},{17,19},{18,2},{19,17},{4,20},{5,... | collective-permute-start | bytes 1775624 | tf_op jit(solution)/shard_map/ppermute | solution.py:596
  552.5 20.2 %collective-permute-start.51 = (bf16[1088,256]{1,0:T(8,128)(2,1)}, bf16[1088,256]{1,0:T(8,128)(2,1)}, u32[]{:S(2)}, u32[]{:S(2)}) collective-permute-start(bf16[1088,256]{1,0:T(8,128)(2,1)} %get-tuple-element.309), channel_id=1, source_target_pairs={{0,1},{1,0},{2,3},{3,2},{4,5},{5,4},{6,7},{7,6},{8,9},{9,8},{10,11... | collective-permute-start | bytes 1671176 | tf_op jit(solution)/shard_map/ppermute | solution.py:602
  555.0 17.7 %collective-permute-start.52 = (bf16[1088,256]{1,0:T(8,128)(2,1)}, bf16[1088,256]{1,0:T(8,128)(2,1)}, u32[]{:S(2)}, u32[]{:S(2)}) collective-permute-start(bf16[1088,256]{1,0:T(8,128)(2,1)} %get-tuple-element.310), channel_id=1, source_target_pairs={{0,2},{1,3},{2,0},{3,1},{4,6},{5,7},{6,4},{7,5},{8,10},{9,11},{10,... | collective-permute-start | bytes 1671176 | tf_op jit(solution)/shard_map/ppermute | solution.py:602
  556.5 36.1 %collective-permute-start.55 = (bf16[272,1088]{1,0:T(8,128)(2,1)S(1)}, bf16[272,1088]{1,0:T(8,128)(2,1)S(1)}, u32[]{:S(2)}, u32[]{:S(2)}) collective-permute-start(bf16[272,1088]{1,0:T(8,128)(2,1)S(1)} %collective-permute-done.37.refs_1_), channel_id=1, source_target_pairs={{0,1},{1,0},{2,3},{3,2},{16,17},{17,16},{18,19},{19,18},{4,5},{5,4... | collective-permute-start | bytes 1775624 | tf_op jit(solution)/shard_map/ppermute | solution.py:596
  570.5 25.8 %collective-permute-start.44 = (bf16[272,1088]{1,0:T(8,128)(2,1)}, bf16[272,1088]{1,0:T(8,128)(2,1)S(1)}, u32[]{:S(2)}, u32[]{:S(2)}) collective-permute-start(bf16[272,1088]{1,0:T(8,128)(2,1)} %reduce-scatter.8.cloned.1.call-done), channel_id=1, source_target_pairs={{0,2},{1,17},{2,0},{3,19},{16,18},{17,1},{18,16},{19,3},{4,6},{5,2... | collective-permute-start | bytes 1775624 | tf_op jit(solution)/shard_map/ppermute | solution.py:596
  572.0 20.0 %collective-permute-start.53 = (bf16[1088,256]{1,0:T(8,128)(2,1)}, bf16[1088,256]{1,0:T(8,128)(2,1)S(1)}, u32[]{:S(2)}, u32[]{:S(2)}) collective-permute-start(bf16[1088,256]{1,0:T(8,128)(2,1)} %get-tuple-element.311), channel_id=1, source_target_pairs={{0,3},{1,2},{2,1},{3,0},{4,7},{5,6},{6,5},{7,4},{8,11},{9,10},{10,... | collective-permute-start | bytes 1671176 | tf_op jit(solution)/shard_map/ppermute | solution.py:602
  572.7 24.9 %collective-permute-start.46 = (bf16[272,1088]{1,0:T(8,128)(2,1)S(1)}, bf16[272,1088]{1,0:T(8,128)(2,1)S(1)}, u32[]{:S(2)}, u32[]{:S(2)}) collective-permute-start(bf16[272,1088]{1,0:T(8,128)(2,1)S(1)} %add_convert_fusion.6.refs_0_), channel_id=1, source_target_pairs={{0,1},{1,0},{2,3},{3,2},{16,17},{17,16},{18,19},{19,18},{4,5},{5,4... | collective-permute-start | bytes 1775624 | tf_op jit(solution)/shard_map/ppermute | solution.py:596
  572.7 24.9 %collective-permute-start.47 = (bf16[272,1088]{1,0:T(8,128)(2,1)S(1)}, bf16[272,1088]{1,0:T(8,128)(2,1)S(1)}, u32[]{:S(2)}, u32[]{:S(2)}) collective-permute-start(bf16[272,1088]{1,0:T(8,128)(2,1)S(1)} %collective-permute-done.39.refs_1_), channel_id=1, source_target_pairs={{0,1},{1,0},{2,3},{3,2},{16,17},{17,16},{18,19},{19,18},{4,5},{5,4... | collective-permute-start | bytes 1775624 | tf_op jit(solution)/shard_map/ppermute | solution.py:596
  595.8 15.8 %collective-permute-start.57 = (bf16[1088,256]{1,0:T(8,128)(2,1)}, bf16[1088,256]{1,0:T(8,128)(2,1)S(1)}, u32[]{:S(2)}, u32[]{:S(2)}) collective-permute-start(bf16[1088,256]{1,0:T(8,128)(2,1)} %get-tuple-element.319), channel_id=1, source_target_pairs={{0,2},{1,3},{2,0},{3,1},{4,6},{5,7},{6,4},{7,5},{8,10},{9,11},{10,... | collective-permute-start | bytes 1671176 | tf_op jit(solution)/shard_map/ppermute | solution.py:602
  597.6 44.9 %collective-permute-start.50 = (bf16[272,1088]{1,0:T(8,128)(2,1)S(1)}, bf16[272,1088]{1,0:T(8,128)(2,1)S(1)}, u32[]{:S(2)}, u32[]{:S(2)}) collective-permute-start(bf16[272,1088]{1,0:T(8,128)(2,1)S(1)} %add_convert_fusion.5.refs_0_), channel_id=1, source_target_pairs={{0,17},{1,2},{2,19},{3,0},{16,1},{17,18},{18,3},{19,16},{4,21},{5,... | collective-permute-start | bytes 1775624 | tf_op jit(solution)/shard_map/ppermute | solution.py:596
  598.9 43.6 %collective-permute-start.49 = (bf16[272,1088]{1,0:T(8,128)(2,1)S(1)}, bf16[272,1088]{1,0:T(8,128)(2,1)S(1)}, u32[]{:S(2)}, u32[]{:S(2)}) collective-permute-start(bf16[272,1088]{1,0:T(8,128)(2,1)S(1)} %add_convert_fusion.5.refs_0_), channel_id=1, source_target_pairs={{0,1},{1,0},{2,3},{3,2},{16,17},{17,16},{18,19},{19,18},{4,5},{5,4... | collective-permute-start | bytes 1775624 | tf_op jit(solution)/shard_map/ppermute | solution.py:596
  599.2 43.3 %collective-permute-start.48 = (bf16[272,1088]{1,0:T(8,128)(2,1)S(1)}, bf16[272,1088]{1,0:T(8,128)(2,1)S(1)}, u32[]{:S(2)}, u32[]{:S(2)}) collective-permute-start(bf16[272,1088]{1,0:T(8,128)(2,1)S(1)} %add_convert_fusion.5.refs_0_), channel_id=1, source_target_pairs={{0,16},{1,3},{2,18},{3,1},{16,0},{17,19},{18,2},{19,17},{4,20},{5,... | collective-permute-start | bytes 1775624 | tf_op jit(solution)/shard_map/ppermute | solution.py:596
  600.7 34.8 %collective-permute-start.58 = (bf16[1088,256]{1,0:T(8,128)(2,1)}, bf16[1088,256]{1,0:T(8,128)(2,1)S(1)}, u32[]{:S(2)}, u32[]{:S(2)}) collective-permute-start(bf16[1088,256]{1,0:T(8,128)(2,1)} %get-tuple-element.320), channel_id=1, source_target_pairs={{0,3},{1,2},{2,1},{3,0},{4,7},{5,6},{6,5},{7,4},{8,11},{9,10},{10,... | collective-permute-start | bytes 1671176 | tf_op jit(solution)/shard_map/ppermute | solution.py:602
  611.5 31.0 %collective-permute-start.59 = (f32[3264]{0:T(1024)S(1)}, f32[3264]{0:T(1024)S(1)}, u32[]{:S(2)}, u32[]{:S(2)}) collective-permute-start(f32[3264]{0:T(1024)S(1)} %add.272), channel_id=1, source_target_pairs={{0,16},{1,17},{2,18},{3,19},{16,0},{17,1},{18,2},{19,3},{4,20},{5,... | collective-permute-start | bytes 39176 | tf_op jit(solution)/shard_map/ppermute | solution.py:653
  (79 other events, 1285.9 us)
Sparse Core Ops, SparseCore 0:
  74.8 51.5 all-gather.2
  128.0 51.6 all-gather.4
  341.8 48.9 reduce-scatter.3
  467.0 49.1 reduce-scatter.5
  519.0 51.5 reduce-scatter.7

commit v10 on v8

--- a/solution.py
+++ b/solution.py
@@ -614,13 +614,26 @@
     return [whole] + [plane_swap(whole, kind) for kind in ("near", "core", "far")]
 
 
-def share_by_core(whole):
-    near = plane_swap(whole, "near")
+def share_by_core(whole, near):
     return [whole, near, plane_swap(whole, "core"), plane_swap(near, "core")]
 
 
 def scatter_rows(values):
     return lax.psum_scatter(values, "fsdp", scatter_dimension=0, tiled=True)
+
+
+def scatter_pieces(values, z):
+    rows = values.reshape(4, values.shape[0] // 4, values.shape[1])
+
+    def share(step):
+        return lax.dynamic_index_in_dim(rows, (z + step) % 4, 0, keepdims=False)
+
+    return [share(0)] + [
+        lax.ppermute(
+            share(step), "fsdp", [(device, (device + step) % 4) for device in range(4)]
+        )
+        for step in range(1, 4)
+    ]
 
 
 def chosen(index, options):
@@ -1262,11 +1275,11 @@
     out_term = turned_product(attended, middle_low)
     up_first = low_sum(up_terms[0], up_far, up_close)
     grad_low, out_term, up_first = pin((grad_low, out_term, up_first))
+    up_pieces = scatter_pieces(up_first, z)
     in_grads = attend_back(
         place, queries, key_rows, value_rows, grad_low, attended, logs_one, seq_count, 0, 5, []
     )
-    up_first, down_shard, *in_grads = pin((up_first, down_shard, *in_grads))
-    up_shard = scatter_rows(up_first)
+    down_shard, *in_grads = pin((down_shard, *in_grads))
     down_whole = low_sum(down_shard, plane_swap(down_shard, "other"))
     in_grads = attend_back(
         place,
@@ -1281,14 +1294,20 @@
         4,
         in_grads,
     )
-    down_whole, *in_grads = pin((down_whole, *in_grads))
-    down_parts = share_by_core(down_whole)
+    down_whole, *moved = pin((down_whole, *up_pieces, *in_grads))
+    up_pieces, in_grads = moved[:4], moved[4:]
+    down_beside = plane_swap(down_whole, "near")
+    up_shard = low_sum(*up_pieces)
+    up_whole = low_sum(up_shard, plane_swap(up_shard, "other"))
     in_terms = [turned_product(normed_low, grad) for grad in in_grads]
     section_grads = in_terms + [out_term]
     sections_mine = [chosen(kind, section_grads) for kind in classes]
     far, far_two = reduce_core(sections_mine)
     second = low_sum(sections_mine[1], far_two)
-    second, far, middle, *in_grads = pin((second, far, middle, *in_grads))
+    second, far, middle, up_whole, down_beside, *in_grads = pin(
+        (second, far, middle, up_whole, down_beside, *in_grads)
+    )
+    up_beside = plane_swap(up_whole, "near")
     query_low, key_low, value_low = in_grads
     close = plane_swap(second, "near")
     result_slots = by_rows(
@@ -1305,12 +1324,13 @@
         4,
     )
     first = low_sum(sections_mine[0], far, close)
-    first, up_shard, query_low, *result_slots = pin(
-        (first, up_shard, query_low, *result_slots)
-    )
+    first, up_beside, query_low, *result_slots = pin(
+        (first, up_beside, query_low, *result_slots)
+    )
+    down_parts = share_by_core(down_whole, down_beside)
+    up_parts = share_by_core(up_whole, up_beside)
     shard = scatter_rows(first)
     outputs = exchange(result_slots)
-    up_whole = low_sum(up_shard, plane_swap(up_shard, "other"))
     *input_slots, last_sums = by_rows(
         last_kernel,
         "last",
@@ -1324,8 +1344,9 @@
         [(12,) + section.shape],
         3,
     )
-    moved = pin((*input_slots, *outputs, *down_parts))
-    input_slots, outputs, down_parts = exchange(moved[:4]), moved[4:8], moved[8:]
+    moved = pin((*input_slots, *outputs, *down_parts, *up_parts))
+    input_slots, outputs = exchange(moved[:4]), moved[4:8]
+    down_parts, up_parts = moved[8:12], moved[12:]
 
     back_sums = jnp.concatenate([hidden_sums, back_sums], axis=0)
     back_sums = jnp.sum(back_sums, axis=1)
@@ -1346,11 +1367,10 @@
         ),
         1,
     )
-    shard, up_whole, totals, *input_slots = pin((shard, up_whole, totals, *input_slots))
+    shard, totals, *input_slots = pin((shard, totals, *input_slots))
     section_whole = low_sum(shard, plane_swap(shard, "other"))
-    up_parts = share_by_core(up_whole)
     totals = swap_sum(totals, 2)
-    section_whole, totals, *up_parts = pin((section_whole, totals, *up_parts))
+    section_whole, totals = pin((section_whole, totals))
     section_parts = share_out(section_whole)
     totals = swap_sum(totals, 4)
     outputs = collect(outputs, low)

time: 629 us -> 635 us (level)
  waiting for transfers between devices: 152 us -> 160 us
    ppermute x0 -> x3, waiting for transfers between devices: none -> 27.7 us  [scatter_pieces(): lax.ppermute(share(step), 'fsdp', [(device, (device + step) % 4) for devi...]
    ppermute x36, waiting for transfers between devices: 64.2 us -> 50.8 us  [plane_swap(): lax.ppermute(values, ('dp', 'ctx'), [(device, plane_partner(device, kind)...]
    reduce_scatter x3 -> x2, waiting for transfers between devices: 12.7 us -> 0.01 us  [scatter_rows(): return lax.psum_scatter(values, 'fsdp', scatter_dimension=0, tiled=True)]
    ppermute x3, waiting for transfers between devices: 35.3 us -> 26.4 us  [per_device_exchanged(): lax.ppermute(section, 'fsdp', [(device, (device + step) % 4) for device i...]
    ppermute x3, waiting for transfers between devices: 3.45 us -> 9.99 us  [swap_sum(): lax.ppermute(total, ('dp', 'ctx'), [(device, device ^ bits) for device in...]
    unnamed x133 -> x121, local copies, waits for them, and re-layouts: 18.3 us -> 15.1 us
    convert_element_type x8 -> x9, other arithmetic: 28.6 us -> 31 us  [low_sum(): sum((term.astype(jnp.float32) for term in terms)).astype(jnp.bfloat16)]
  transfers between devices with their start and end apart: 65 -> 67, of which waited for: 24 -> 25; matrix products, arithmetic and copies ran while one was open for 15% -> 15% of each run, Pallas kernels for 44% -> 43%
where the time goes in v10:
time: 635 us; the launch traced here: 626 us
  Pallas kernels  275 us (43%)
  waiting for transfers between devices  160 us (25%)
  matrix products  60.2 us (9%)
  starting transfers between devices  44.6 us (7%)
  other arithmetic  38.7 us (6%)
  local copies, waits for them, and re-layouts  32 us (5%)
  between operations  15.3 us (2%)
    pallas_call x8, Pallas kernels, by_rows(): pl.pallas_call(kernel, grid=(rows // step,), in_specs=[tile] * len(tiled[...  154 us
    dot_general x12, matrix products, product(): lax.dot_general(left, right, ((dims[:1], dims[1:]), ((), ())), preferred_...  60.2 us
    ppermute x36, waiting for transfers between devices, plane_swap(): lax.ppermute(values, ('dp', 'ctx'), [(device, plane_partner(device, kind)...  50.8 us
    pallas_call x2, Pallas kernels, attend_back(): pl.pallas_call(functools.partial(attend_back_kernel, count=count, width=w...  47.9 us
    ppermute x12, waiting for transfers between devices, ctx_swap(): lax.ppermute(values, 'ctx', [(device, device ^ bits) for device in range(...  35.3 us
    pallas_call x1, Pallas kernels, attend(): pl.pallas_call(functools.partial(attend_kernel, count=count, width=width,...  32.2 us
    convert_element_type x9, other arithmetic, low_sum(): sum((term.astype(jnp.float32) for term in terms)).astype(jnp.bfloat16)  31 us
    ppermute x3, waiting for transfers between devices, scatter_pieces(): lax.ppermute(share(step), 'fsdp', [(device, (device + step) % 4) for devi...  27.7 us
  transfers between devices with their start and end apart: 67, of which 25 were waited for; matrix products, arithmetic and copies ran while one was open for 15% of the time, Pallas kernels for 43%

profile of v10, /device:TPU:8, one launch (start us, length us, event | category | flops | bytes accessed | tf_op | source)
XLA Modules:
  0.0 626.1 jit_solution(11302345318321219269)
XLA Ops:
  7.3 3.6 fusion.11
  21.8 3.6 collective-permute-start.4
  27.2 14.1 %collective-permute-done.7.refs_2_ = bf16[1088,256]{1,0:T(8,128)(2,1)S(1)} collective-permute-done((bf16[1088,256]{1,0:T(8,128)(2,1)}, bf16[1088,256]{1,0:T(8,128)(2,1)S(1)}, u32[]{:S(2)}, u32[]{:S(2)}) %collective-permute-start.7) | collective-permute-done | bytes 557088 | tf_op jit(solution)/shard_map/ppermute | solution.py:602
  41.3 9.1 %collective-permute-done.8.refs_3_ = bf16[1088,256]{1,0:T(8,128)(2,1)S(1)} collective-permute-done((bf16[1088,256]{1,0:T(8,128)(2,1)}, bf16[1088,256]{1,0:T(8,128)(2,1)S(1)}, u32[]{:S(2)}, u32[]{:S(2)}) %collective-permute-start.8) | collective-permute-done | bytes 557088 | tf_op jit(solution)/shard_map/ppermute | solution.py:602
  50.4 22.8 %collective-permute-done.4.refs_9_ = bf16[272,1088]{1,0:T(8,128)(2,1)S(1)} collective-permute-done((bf16[272,1088]{1,0:T(8,128)(2,1)}, bf16[272,1088]{1,0:T(8,128)(2,1)S(1)}, u32[]{:S(2)}, u32[]{:S(2)}) %collective-permute-start.4) | collective-permute-done | bytes 591904 | tf_op jit(solution)/shard_map/ppermute | solution.py:1097
  73.2 3.6 collective-permute-done.5.refs_10_
  81.0 6.5 %collective-permute-done.9.refs_11_ = bf16[272,1088]{1,0:T(8,128)(2,1)} collective-permute-done((bf16[272,1088]{1,0:T(8,128)(2,1)}, bf16[272,1088]{1,0:T(8,128)(2,1)}, u32[]{:S(2)}, u32[]{:S(2)}) %collective-permute-start.9) | collective-permute-done | bytes 591904 | tf_op jit(solution)/shard_map/ppermute | solution.py:596
  87.6 6.7 %collective-permute-done.10.refs_12_ = bf16[272,1088]{1,0:T(8,128)(2,1)} collective-permute-done((bf16[272,1088]{1,0:T(8,128)(2,1)S(1)}, bf16[272,1088]{1,0:T(8,128)(2,1)}, u32[]{:S(2)}, u32[]{:S(2)}) %collective-permute-start.10) | collective-permute-done | bytes 591904 | tf_op jit(solution)/shard_map/ppermute | solution.py:596
  94.3 6.7 %collective-permute-done.11.refs_13_ = bf16[272,1088]{1,0:T(8,128)(2,1)} collective-permute-done((bf16[272,1088]{1,0:T(8,128)(2,1)}, bf16[272,1088]{1,0:T(8,128)(2,1)}, u32[]{:S(2)}, u32[]{:S(2)}) %collective-permute-start.11) | collective-permute-done | bytes 591904 | tf_op jit(solution)/shard_map/ppermute | solution.py:596
  105.2 21.7 %front.1 = (bf16[1024,1088]{1,0:T(8,128)(2,1)}, bf16[1024,1088]{1,0:T(8,128)(2,1)}, bf16[1024,1088]{1,0:T(8,128)(2,1)}, bf16[1024,1088]{1,0:T(8,128)(2,1)}, bf16...) custom-call(s32[16]{0:T(128)} %stack.120.places_ref, f32[4,1088]{1,0:T(4,128)} %pad_maximum_fusion.1.vectors_ref, ...), custom_call_target="tpu_custom_call" | custom-call | flops 1024 | bytes 1024 | tf_op jit(solution)/shard_map/front/pallas_call | solution.py:746
  131.4 32.2 %attend.1 = (bf16[1024,1088]{1,0:T(8,128)(2,1)S(1)}, f32[1024,128]{1,0:T(8,128)S(1)}) custom-call(s32[1]{0:T(128)} %bitcast.24.place_ref, bf16[1024,1088]{1,0:T(8,128)(2,1)S(1)} %copy-done.3, bf16[1024,1088]{1,0:T(8,128)(2,1)} %get-tuple-element.223.k_ref, bf16[1024,1088]{1,0:T(8,128)(2,1)} %get-tuple-element.224.v_ref), custom_call_target="tpu_custom_call" | custom-call | flops 1024 | bytes 1024 | tf_op jit(solution)/shard_map/attend/pallas_call | solution.py:507
  171.3 10.1 %middle.1 = (f32[1024,1088]{1,0:T(8,128)}, bf16[1024,1088]{1,0:T(8,128)(2,1)}) custom-call(bf16[1024,1088]{1,0:T(8,128)(2,1)} %get-tuple-element.217.x_ref, bf16[1024,1088]{1,0:T(8,128)(2,1)} %copy-done.4, f32[3,1088]{1,0:T(4,128)} %pad_maximum_fusion.2.vectors_ref, bf16[16,272,1088]{2,1,0:T(8,128)(2,1)} %get-tuple-element.227.all_ref.refs_8_), custom_call_target="tpu_custom_call" | custom-call | flops 1024 | bytes 1024 | tf_op jit(solution)/shard_map/middle/pallas_call | solution.py:1019
  181.4 17.4 %up.2 = (bf16[1024,1088]{1,0:T(8,128)(2,1)}, bf16[1024,1088]{1,0:T(8,128)(2,1)}, bf16[1024,1088]{1,0:T(8,128)(2,1)}, bf16[1024,1088]{1,0:T(8,128)(2,1)}) custom-call(bf16[1024,1088]{1,0:T(8,128)(2,1)} %get-tuple-element.265.h_ref, f32[2,1088]{1,0:T(2,128)} %pad_maximum_fusion.3.biases_ref, bf16[1088,1088]{1,0:T(8,128)(2,1)} %all-gather.3.cloned.1.call-done.refs_0_.refs_4_, ...), custom_call_target="tpu_custom_call" | custom-call | flops 1024 | bytes 1024 | tf_op jit(solution)/shard_map/up/pallas_call | solution.py:1019
  198.8 18.0 %up.3 = (bf16[1024,1088]{1,0:T(8,128)(2,1)}, bf16[1024,1088]{1,0:T(8,128)(2,1)}, bf16[1024,1088]{1,0:T(8,128)(2,1)}, bf16[1024,1088]{1,0:T(8,128)(2,1)}) custom-call(bf16[1024,1088]{1,0:T(8,128)(2,1)} %get-tuple-element.265.h_ref, f32[2,1088]{1,0:T(2,128)} %pad_maximum_fusion.4.biases_ref, bf16[1088,1088]{1,0:T(8,128)(2,1)} %collective-permute-done.19.refs_0_.refs_5_, ...), custom_call_target="tpu_custom_call" | custom-call | flops 1024 | bytes 1024 | tf_op jit(solution)/shard_map/up/pallas_call | solution.py:1019
  224.1 6.2 convolution_convert_fusion.11
  230.3 4.6 convolution_convert_fusion.10
  235.2 4.6 convolution_convert_fusion.9
  239.8 4.8 convolution_convert_fusion.8
  244.5 8.6 %collective-permute-done.25.refs_2_.refs_5_ = bf16[1088,1088]{1,0:T(8,128)(2,1)} collective-permute-done((bf16[1088,1088]{1,0:T(8,128)(2,1)}, bf16[1088,1088]{1,0:T(8,128)(2,1)}, u32[]{:S(2)}, u32[]{:S(2)}) %collective-permute-start.25) | collective-permute-done | bytes 2367520 | tf_op jit(solution)/shard_map/ppermute | solution.py:596
  253.6 14.0 %hidden.2 = (bf16[1024,1088]{1,0:T(8,128)(2,1)}, bf16[1024,1088]{1,0:T(8,128)(2,1)}, f32[3,8,1088]{2,1,0:T(8,128)}) custom-call(bf16[1024,1088]{1,0:T(8,128)(2,1)} %copy-done.2, bf16[1024,1088]{1,0:T(8,128)(2,1)} %get-tuple-element.251.refs_0_, bf16[1024,1088]{1,0:T(8,128)(2,1)} %get-tuple-element.252.refs_1_, ...), custom_call_target="tpu_custom_call" | custom-call | flops 1024 | bytes 1024 | tf_op jit(solution)/shard_map/hidden/pallas_call | solution.py:1019
  267.7 4.6 add_convert_fusion.4
  275.2 14.2 %hidden.3 = (bf16[1024,1088]{1,0:T(8,128)(2,1)}, bf16[1024,1088]{1,0:T(8,128)(2,1)}, f32[3,8,1088]{2,1,0:T(8,128)}) custom-call(bf16[1024,1088]{1,0:T(8,128)(2,1)} %copy-done.2, bf16[1024,1088]{1,0:T(8,128)(2,1)} %get-tuple-element.257.refs_0_, bf16[1024,1088]{1,0:T(8,128)(2,1)} %get-tuple-element.258.refs_1_, ...), custom_call_target="tpu_custom_call" | custom-call | flops 1024 | bytes 1024 | tf_op jit(solution)/shard_map/hidden/pallas_call | solution.py:1019
  289.4 7.1 %convolution_convert_fusion.7 = bf16[1088,1088]{1,0:T(8,128)(2,1)} fusion(bf16[1024,1088]{1,0:T(8,128)(2,1)} %get-tuple-element.265.h_ref, bf16[1024,1088]{1,0:T(8,128)(2,1)} %get-tuple-element.278.refs_3_), kind=kOutput, calls=%fused_computation.9 | convolution fusion | flops 2425491456 | bytes 6823936 | tf_op jit(solution)/shard_map/dot_general | solution.py:673
  296.5 4.6 convolution_convert_fusion.6
  301.6 4.6 convolution_convert_fusion.4
  306.2 4.9 add_convert_fusion.3
  311.0 7.4 %fusion.2 = bf16[1088,1088]{1,0:T(8,128)(2,1)} fusion(bf16[1024,1088]{1,0:T(8,128)(2,1)S(1)} %copy-done.28, bf16[1024,1088]{1,0:T(8,128)(2,1)} %get-tuple-element.276.refs_1_, bf16[1088,1088]{1,0:T(8,128)(2,1)} %collective-permute-done.29), kind=kOutput, calls=%fused_computation.14 | convolution fusion | flops 2430226432 | bytes 9191424 | tf_op jit(solution)/shard_map/dot_general | solution.py:673
  319.3 31.9 %back.1 = (f32[1024,1088]{1,0:T(8,128)}, bf16[1024,1088]{1,0:T(8,128)(2,1)}, bf16[1024,1088]{1,0:T(8,128)(2,1)}, f32[3,8,1088]{2,1,0:T(8,128)}) custom-call(bf16[1024,1088]{1,0:T(8,128)(2,1)} %copy-done.2, f32[1024,1088]{1,0:T(8,128)} %get-tuple-element.310.middle_ref, f32[1,1088]{1,0:T(1,128)} %copy-done.46, bf16[1024,1088]{1,0:T(8,128)(2,1)} %get-tuple-element.275.refs_0_, ...), custom_call_target="tpu_custom_call" | custom-call | flops 1024 | bytes 1024 | tf_op jit(solution)/shard_map/back/pallas_call | solution.py:1019
  351.3 6.4 %convolution_convert_fusion.3 = bf16[1088,1088]{1,0:T(8,128)(2,1)} fusion(bf16[1024,1088]{1,0:T(8,128)(2,1)S(1)} %copy-done.5, bf16[1024,1088]{1,0:T(8,128)(2,1)} %get-tuple-element.280), kind=kOutput, calls=%fused_computation.3 | convolution fusion | flops 2425491456 | bytes 6823936 | tf_op jit(solution)/shard_map/dot_general | solution.py:673
  357.6 5.0 add_convert_fusion.2
  362.6 26.2 %attend_back.2 = (bf16[1024,1088]{1,0:T(8,128)(2,1)S(1)}, bf16[1024,1088]{1,0:T(8,128)(2,1)S(1)}, bf16[1024,1088]{1,0:T(8,128)(2,1)}) custom-call(s32[1]{0:T(128)} %bitcast.24.place_ref, bf16[1024,1088]{1,0:T(8,128)(2,1)} %get-tuple-element.222.q_ref, bf16[1024,1088]{1,0:T(8,128)(2,1)} %get-tuple-element.223.k_ref, ...), custom_call_target="tpu_custom_call" | custom-call | flops 1024 | bytes 1024 | tf_op jit(solution)/shard_map/attend_back/pallas_call | solution.py:537
  401.3 21.6 %attend_back.3 = (bf16[1024,1088]{1,0:T(8,128)(2,1)S(1)}, bf16[1024,1088]{1,0:T(8,128)(2,1)S(1)}, bf16[1024,1088]{1,0:T(8,128)(2,1)}) custom-call(s32[1]{0:T(128)} %bitcast.24.place_ref, bf16[1024,1088]{1,0:T(8,128)(2,1)} %get-tuple-element.222.q_ref, ...), custom_call_target="tpu_custom_call", output_to_operand_aliasing={{0}: (7, {}), {1}: (8, {}), {2}: (9, {})} | custom-call | flops 1024 | bytes 1024 | tf_op jit(solution)/shard_map/attend_back/pallas_call | solution.py:537
  424.7 13.8 %collective-permute-done.34 = bf16[272,1088]{1,0:T(8,128)(2,1)} collective-permute-done((bf16[272,1088]{1,0:T(8,128)(2,1)}, bf16[272,1088]{1,0:T(8,128)(2,1)}, u32[]{:S(2)}, u32[]{:S(2)}) %collective-permute-start.34) | collective-permute-done | bytes 591904 | tf_op jit(solution)/shard_map/ppermute | solution.py:632
  438.5 11.8 %collective-permute-done.35 = bf16[272,1088]{1,0:T(8,128)(2,1)} collective-permute-done((bf16[272,1088]{1,0:T(8,128)(2,1)}, bf16[272,1088]{1,0:T(8,128)(2,1)}, u32[]{:S(2)}, u32[]{:S(2)}) %collective-permute-start.35) | collective-permute-done | bytes 591904 | tf_op jit(solution)/shard_map/ppermute | solution.py:632
  458.9 3.9 select_select_fusion
  467.8 14.6 %collective-permute-done.39 = bf16[272,1088]{1,0:T(8,128)(2,1)S(1)} collective-permute-done((bf16[272,1088]{1,0:T(8,128)(2,1)S(1)}, bf16[272,1088]{1,0:T(8,128)(2,1)S(1)}, u32[]{:S(2)}, u32[]{:S(2)}) %collective-permute-start.39) | collective-permute-done | bytes 591904 | tf_op jit(solution)/shard_map/ppermute | solution.py:596
  482.6 3.6 add_convert_fusion.1
  489.0 25.0 %down.1 = (bf16[1088,256]{1,0:T(8,128)(2,1)}, bf16[1088,256]{1,0:T(8,128)(2,1)}, bf16[1088,256]{1,0:T(8,128)(2,1)}, bf16[1088,256]{1,0:T(8,128)(2,1)}) custom-call(f32[1024,1088]{1,0:T(8,128)} %get-tuple-element.310.middle_ref, f32[1,1088]{1,0:T(1,128)} %reshape.450.vectors_ref, bf16[1024,1088]{1,0:T(8,128)(2,1)} %get-tuple-element.246.refs_0_, ...), custom_call_target="tpu_custom_call" | custom-call | flops 1024 | bytes 1024 | tf_op jit(solution)/shard_map/down/pallas_call | solution.py:1019
  517.0 7.3 %add_convert_fusion = bf16[1088,1088]{1,0:T(8,128)(2,1)} fusion(bf16[1088,1088]{1,0:T(8,128)(2,1)} %collective-permute-done.41, bf16[1088,1088]{1,0:T(8,128)(2,1)} %collective-permute-done.38, bf16[1088,1088]{1,0:T(8,128)(2,1)} %copy-done.26, bf16[1088,1088]{1,0:T(8,128)(2,1)} %copy-done.24, bf16[1088,1088]{1,0:T(8,128)(2,1)} %copy-done.25, ...), kind=kLoop, calls=%fused_computation.15 | loop fusion | flops 10653696 | bytes 16572419 | tf_op jit(solution)/shard_map/convert_element_type | solution.py:606
  531.9 23.7 %last.1 = (bf16[1088,256]{1,0:T(8,128)(2,1)}, bf16[1088,256]{1,0:T(8,128)(2,1)}, bf16[1088,256]{1,0:T(8,128)(2,1)}, bf16[1088,256]{1,0:T(8,128)(2,1)}, f32[4,8,1088]{2,1,0:T(8,128)}) custom-call(bf16[1024,1088]{1,0:T(8,128)(2,1)} %copy-done.6, bf16[1024,1088]{1,0:T(8,128)(2,1)} %copy-done.9, bf16[1024,1088]{1,0:T(8,128)(2,1)} %get-tuple-element.321.v_ref, ...), custom_call_target="tpu_custom_call" | custom-call | flops 1024 | bytes 1024 | tf_op jit(solution)/shard_map/last/pallas_call | solution.py:1019
  560.8 5.0 collective-permute-done.45
  565.8 4.2 collective-permute-done.43
  572.9 10.4 %collective-permute-done.56.refs_3_ = bf16[1088,256]{1,0:T(8,128)(2,1)} collective-permute-done((bf16[1088,256]{1,0:T(8,128)(2,1)}, bf16[1088,256]{1,0:T(8,128)(2,1)}, u32[]{:S(2)}, u32[]{:S(2)}) %collective-permute-start.56) | collective-permute-done | bytes 557088 | tf_op jit(solution)/shard_map/ppermute | solution.py:602
  585.3 8.8 %collective-permute-done.58 = f32[3264]{0:T(1024)S(1)} collective-permute-done((f32[3264]{0:T(1024)S(1)}, f32[3264]{0:T(1024)S(1)}, u32[]{:S(2)}, u32[]{:S(2)}) %collective-permute-start.58) | collective-permute-done | bytes 13088 | tf_op jit(solution)/shard_map/ppermute | solution.py:667
  599.4 4.7 assemble.2
  604.2 3.8 settle.5
  610.7 3.9 settle.4
  616.0 3.4 assemble.3
  (322 shorter events, 105.8 us)
Async XLA Ops:
  7.2 120.1 %all-gather.3.cloned.1.call-start = ((), (), s32[]{:S(2)}) async-start(), calls=%async_computation.2 | async-start | bytes 3133440 | tf_op jit(solution)/shard_map/all_gather | solution.py:1143
  18.8 31.6 %collective-permute-start.3 = (bf16[272,1088]{1,0:T(8,128)(2,1)}, bf16[272,1088]{1,0:T(8,128)(2,1)}, u32[]{:S(2)}, u32[]{:S(2)}) collective-permute-start(bf16[272,1088]{1,0:T(8,128)(2,1)} %get-tuple-element.203), channel_id=1, source_target_pairs={{0,4},{4,8},{8,12},{12,0},{1,5},{5,9},{9,13},{13,1},{2,6},{6,10},{... | collective-permute-start | bytes 1775624 | tf_op jit(solution)/shard_map/ppermute | solution.py:1097
  21.8 51.4 %collective-permute-start.4 = (bf16[272,1088]{1,0:T(8,128)(2,1)}, bf16[272,1088]{1,0:T(8,128)(2,1)S(1)}, u32[]{:S(2)}, u32[]{:S(2)}) collective-permute-start(bf16[272,1088]{1,0:T(8,128)(2,1)} %get-tuple-element.203), channel_id=1, source_target_pairs={{0,8},{4,12},{8,0},{12,4},{1,9},{5,13},{9,1},{13,5},{2,10},{6,14},... | collective-permute-start | bytes 1775624 | tf_op jit(solution)/shard_map/ppermute | solution.py:1097
  25.4 51.4 %collective-permute-start.5 = (bf16[272,1088]{1,0:T(8,128)(2,1)}, bf16[272,1088]{1,0:T(8,128)(2,1)}, u32[]{:S(2)}, u32[]{:S(2)}) collective-permute-start(bf16[272,1088]{1,0:T(8,128)(2,1)} %get-tuple-element.203), channel_id=1, source_target_pairs={{0,12},{4,0},{8,4},{12,8},{1,13},{5,1},{9,5},{13,9},{2,14},{6,2},{... | collective-permute-start | bytes 1775624 | tf_op jit(solution)/shard_map/ppermute | solution.py:1097
  25.4 15.8 %collective-permute-start.7 = (bf16[1088,256]{1,0:T(8,128)(2,1)}, bf16[1088,256]{1,0:T(8,128)(2,1)S(1)}, u32[]{:S(2)}, u32[]{:S(2)}) collective-permute-start(bf16[1088,256]{1,0:T(8,128)(2,1)} %get-tuple-element.399), channel_id=1, source_target_pairs={{0,2},{1,3},{2,0},{3,1},{4,6},{5,7},{6,4},{7,5},{8,10},{9,11},{10,... | collective-permute-start | bytes 1671176 | tf_op jit(solution)/shard_map/ppermute | solution.py:602
  27.0 23.4 %collective-permute-start.8 = (bf16[1088,256]{1,0:T(8,128)(2,1)}, bf16[1088,256]{1,0:T(8,128)(2,1)S(1)}, u32[]{:S(2)}, u32[]{:S(2)}) collective-permute-start(bf16[1088,256]{1,0:T(8,128)(2,1)} %get-tuple-element.204), channel_id=1, source_target_pairs={{0,3},{1,2},{2,1},{3,0},{4,7},{5,6},{6,5},{7,4},{8,11},{9,10},{10,... | collective-permute-start | bytes 1671176 | tf_op jit(solution)/shard_map/ppermute | solution.py:602
  76.8 145.5 %all-gather.5.cloned.1.call-start = ((), (), s32[]{:S(2)}) async-start(), calls=%async_computation.3 | async-start | bytes 3133440 | tf_op jit(solution)/shard_map/all_gather | solution.py:1167
  78.5 15.8 %collective-permute-start.10 = (bf16[272,1088]{1,0:T(8,128)(2,1)S(1)}, bf16[272,1088]{1,0:T(8,128)(2,1)}, u32[]{:S(2)}, u32[]{:S(2)}) collective-permute-start(bf16[272,1088]{1,0:T(8,128)(2,1)S(1)} %collective-permute-done.4.refs_9_), channel_id=1, source_target_pairs={{0,16},{1,3},{2,18},{3,1},{16,0},{17,19},{18,2},{19,17},{4,20},{5,... | collective-permute-start | bytes 1775624 | tf_op jit(solution)/shard_map/ppermute | solution.py:596
  79.0 22.0 %collective-permute-start.11 = (bf16[272,1088]{1,0:T(8,128)(2,1)}, bf16[272,1088]{1,0:T(8,128)(2,1)}, u32[]{:S(2)}, u32[]{:S(2)}) collective-permute-start(bf16[272,1088]{1,0:T(8,128)(2,1)} %collective-permute-done.5.refs_10_), channel_id=1, source_target_pairs={{0,16},{1,3},{2,18},{3,1},{16,0},{17,19},{18,2},{19,17},{4,20},{5,... | collective-permute-start | bytes 1775624 | tf_op jit(solution)/shard_map/ppermute | solution.py:596
  80.5 21.0 %collective-permute-start.12 = (bf16[272,1088]{1,0:T(8,128)(2,1)}, bf16[272,1088]{1,0:T(8,128)(2,1)}, u32[]{:S(2)}, u32[]{:S(2)}) collective-permute-start(bf16[272,1088]{1,0:T(8,128)(2,1)} %collective-permute-done.3.refs_8_), channel_id=1, source_target_pairs={{0,1},{1,0},{2,3},{3,2},{16,17},{17,16},{18,19},{19,18},{4,5},{5,4... | collective-permute-start | bytes 1775624 | tf_op jit(solution)/shard_map/ppermute | solution.py:596
  80.5 22.8 %collective-permute-start.13 = (bf16[272,1088]{1,0:T(8,128)(2,1)S(1)}, bf16[272,1088]{1,0:T(8,128)(2,1)}, u32[]{:S(2)}, u32[]{:S(2)}) collective-permute-start(bf16[272,1088]{1,0:T(8,128)(2,1)S(1)} %collective-permute-done.4.refs_9_), channel_id=1, source_target_pairs={{0,1},{1,0},{2,3},{3,2},{16,17},{17,16},{18,19},{19,18},{4,5},{5,4... | collective-permute-start | bytes 1775624 | tf_op jit(solution)/shard_map/ppermute | solution.py:596
  127.3 37.6 %collective-permute-start.18 = (bf16[1088,1088]{1,0:T(8,128)(2,1)}, bf16[1088,1088]{1,0:T(8,128)(2,1)}, u32[]{:S(2)}, u32[]{:S(2)}) collective-permute-start(bf16[1088,1088]{1,0:T(8,128)(2,1)} %all-gather.3.cloned.1.call-done.refs_0_.refs_4_), channel_id=1, source_target_pairs={{0,1},{1,0},{2,3},{3,2},{16,17},{17,16},{18,19},{19,18},{4,5},{5,4... | collective-permute-start | bytes 7102472 | tf_op jit(solution)/shard_map/ppermute | solution.py:596
  127.3 37.6 %collective-permute-start.19 = (bf16[1088,1088]{1,0:T(8,128)(2,1)}, bf16[1088,1088]{1,0:T(8,128)(2,1)}, u32[]{:S(2)}, u32[]{:S(2)}) collective-permute-start(bf16[1088,1088]{1,0:T(8,128)(2,1)} %all-gather.3.cloned.1.call-done.refs_0_.refs_4_), channel_id=1, source_target_pairs={{0,16},{1,3},{2,18},{3,1},{16,0},{17,19},{18,2},{19,17},{4,20},{5,... | collective-permute-start | bytes 7102472 | tf_op jit(solution)/shard_map/ppermute | solution.py:596
  165.0 225.2 %reduce-scatter.3.cloned.1.call-start = ((), (), s32[]{:S(2)}) async-start(), calls=%async_computation.4 | async-start | bytes 3133440 | tf_op jit(solution)/shard_map/reduce_scatter | solution.py:622
  165.3 33.6 %collective-permute-start.22 = (bf16[1088,1088]{1,0:T(8,128)(2,1)}, bf16[1088,1088]{1,0:T(8,128)(2,1)}, u32[]{:S(2)}, u32[]{:S(2)}) collective-permute-start(bf16[1088,1088]{1,0:T(8,128)(2,1)} %collective-permute-done.19.refs_0_.refs_5_), channel_id=1, source_target_pairs={{0,1},{1,0},{2,3},{3,2},{16,17},{17,16},{18,19},{19,18},{4,5},{5,4... | collective-permute-start | bytes 7102472 | tf_op jit(solution)/shard_map/ppermute | solution.py:596
  167.1 49.7 %collective-permute-start.20 = (bf16[1088,256]{1,0:T(8,128)(2,1)}, bf16[1088,256]{1,0:T(8,128)(2,1)S(1)}, u32[]{:S(2)}, u32[]{:S(2)}) collective-permute-start(bf16[1088,256]{1,0:T(8,128)(2,1)} %get-tuple-element.397), channel_id=1, source_target_pairs={{0,1},{1,0},{2,3},{3,2},{4,5},{5,4},{6,7},{7,6},{8,9},{9,8},{10,11... | collective-permute-start | bytes 1671176 | tf_op jit(solution)/shard_map/ppermute | solution.py:602
  167.4 50.2 %collective-permute-start.21 = (bf16[1088,256]{1,0:T(8,128)(2,1)}, bf16[1088,256]{1,0:T(8,128)(2,1)S(1)}, u32[]{:S(2)}, u32[]{:S(2)}) collective-permute-start(bf16[1088,256]{1,0:T(8,128)(2,1)} %get-tuple-element.396), channel_id=1, source_target_pairs={{0,2},{1,3},{2,0},{3,1},{4,6},{5,7},{6,4},{7,5},{8,10},{9,11},{10,... | collective-permute-start | bytes 1671176 | tf_op jit(solution)/shard_map/ppermute | solution.py:602
  168.9 29.9 %collective-permute-start.23 = (bf16[1088,256]{1,0:T(8,128)(2,1)}, bf16[1088,256]{1,0:T(8,128)(2,1)S(1)}, u32[]{:S(2)}, u32[]{:S(2)}) collective-permute-start(bf16[1088,256]{1,0:T(8,128)(2,1)} %get-tuple-element.395), channel_id=1, source_target_pairs={{0,3},{1,2},{2,1},{3,0},{4,7},{5,6},{6,5},{7,4},{8,11},{9,10},{10,... | collective-permute-start | bytes 1671176 | tf_op jit(solution)/shard_map/ppermute | solution.py:602
  222.3 30.8 %collective-permute-start.25 = (bf16[1088,1088]{1,0:T(8,128)(2,1)}, bf16[1088,1088]{1,0:T(8,128)(2,1)}, u32[]{:S(2)}, u32[]{:S(2)}) collective-permute-start(bf16[1088,1088]{1,0:T(8,128)(2,1)} %all-gather.5.cloned.1.call-done.refs_2_.refs_4_), channel_id=1, source_target_pairs={{0,16},{1,3},{2,18},{3,1},{16,0},{17,19},{18,2},{19,17},{4,20},{5,... | collective-permute-start | bytes 7102472 | tf_op jit(solution)/shard_map/ppermute | solution.py:596
  223.9 29.8 %collective-permute-start.26 = (bf16[1088,1088]{1,0:T(8,128)(2,1)}, bf16[1088,1088]{1,0:T(8,128)(2,1)}, u32[]{:S(2)}, u32[]{:S(2)}) collective-permute-start(bf16[1088,1088]{1,0:T(8,128)(2,1)} %all-gather.5.cloned.1.call-done.refs_2_.refs_4_), channel_id=1, source_target_pairs={{0,1},{1,0},{2,3},{3,2},{16,17},{17,16},{18,19},{19,18},{4,5},{5,4... | collective-permute-start | bytes 7102472 | tf_op jit(solution)/shard_map/ppermute | solution.py:596
  234.9 32.8 %collective-permute-start.27 = (bf16[1088,1088]{1,0:T(8,128)(2,1)}, bf16[1088,1088]{1,0:T(8,128)(2,1)}, u32[]{:S(2)}, u32[]{:S(2)}) collective-permute-start(bf16[1088,1088]{1,0:T(8,128)(2,1)} %convolution_convert_fusion.11), channel_id=1, source_target_pairs={{0,1},{1,0},{2,3},{3,2},{16,17},{17,16},{18,19},{19,18},{4,5},{5,4... | collective-permute-start | bytes 7102472 | tf_op jit(solution)/shard_map/ppermute | solution.py:596
  253.1 20.6 %collective-permute-start.28 = (bf16[1088,1088]{1,0:T(8,128)(2,1)}, bf16[1088,1088]{1,0:T(8,128)(2,1)S(1)}, u32[]{:S(2)}, u32[]{:S(2)}) collective-permute-start(bf16[1088,1088]{1,0:T(8,128)(2,1)} %collective-permute-done.25.refs_2_.refs_5_), channel_id=1, source_target_pairs={{0,1},{1,0},{2,3},{3,2},{16,17},{17,16},{18,19},{19,18},{4,5},{5,4... | collective-permute-start | bytes 7102472 | tf_op jit(solution)/shard_map/ppermute | solution.py:596
  253.1 36.2 %collective-permute-start.24 = (bf16[1088,1088]{1,0:T(8,128)(2,1)}, bf16[1088,1088]{1,0:T(8,128)(2,1)}, u32[]{:S(2)}, u32[]{:S(2)}) collective-permute-start(bf16[1088,1088]{1,0:T(8,128)(2,1)} %convolution_convert_fusion.10), channel_id=1, source_target_pairs={{0,1},{1,0},{2,3},{3,2},{16,17},{17,16},{18,19},{19,18},{4,5},{5,4... | collective-permute-start | bytes 7102472 | tf_op jit(solution)/shard_map/ppermute | solution.py:596
  272.3 33.9 %collective-permute-start.31 = (bf16[1088,1088]{1,0:T(8,128)(2,1)}, bf16[1088,1088]{1,0:T(8,128)(2,1)}, u32[]{:S(2)}, u32[]{:S(2)}) collective-permute-start(bf16[1088,1088]{1,0:T(8,128)(2,1)} %add_convert_fusion.4), channel_id=1, source_target_pairs={{0,16},{1,3},{2,18},{3,1},{16,0},{17,19},{18,2},{19,17},{4,20},{5,... | collective-permute-start | bytes 7102472 | tf_op jit(solution)/shard_map/ppermute | solution.py:596
  301.1 17.3 %collective-permute-start.30 = (bf16[1088,1088]{1,0:T(8,128)(2,1)}, bf16[1088,1088]{1,0:T(8,128)(2,1)}, u32[]{:S(2)}, u32[]{:S(2)}) collective-permute-start(bf16[1088,1088]{1,0:T(8,128)(2,1)} %convolution_convert_fusion.6), channel_id=1, source_target_pairs={{0,1},{1,0},{2,3},{3,2},{16,17},{17,16},{18,19},{19,18},{4,5},{5,4... | collective-permute-start | bytes 7102472 | tf_op jit(solution)/shard_map/ppermute | solution.py:596
  318.4 264.9 %reduce-scatter.5.cloned.1.call-start = ((), (), s32[]{:S(2)}) async-start(), calls=%async_computation.5 | async-start | bytes 3133440 | tf_op jit(solution)/shard_map/reduce_scatter | solution.py:622
  318.5 39.2 %collective-permute-start.32 = (bf16[1088,1088]{1,0:T(8,128)(2,1)}, bf16[1088,1088]{1,0:T(8,128)(2,1)}, u32[]{:S(2)}, u32[]{:S(2)}) collective-permute-start(bf16[1088,1088]{1,0:T(8,128)(2,1)} %fusion.2), channel_id=1, source_target_pairs={{0,16},{1,3},{2,18},{3,1},{16,0},{17,19},{18,2},{19,17},{4,20},{5,... | collective-permute-start | bytes 7102472 | tf_op jit(solution)/shard_map/ppermute | solution.py:596
  390.2 32.7 %collective-permute-start.33 = (bf16[272,1088]{1,0:T(8,128)(2,1)}, bf16[272,1088]{1,0:T(8,128)(2,1)}, u32[]{:S(2)}, u32[]{:S(2)}) collective-permute-start(bf16[272,1088]{1,0:T(8,128)(2,1)} %reduce-scatter.3.cloned.1.call-done), channel_id=1, source_target_pairs={{0,2},{1,17},{2,0},{3,19},{16,18},{17,1},{18,16},{19,3},{4,6},{5,2... | collective-permute-start | bytes 1775624 | tf_op jit(solution)/shard_map/ppermute | solution.py:596
  394.6 43.8 %collective-permute-start.34 = (bf16[272,1088]{1,0:T(8,128)(2,1)}, bf16[272,1088]{1,0:T(8,128)(2,1)}, u32[]{:S(2)}, u32[]{:S(2)}) collective-permute-start(bf16[272,1088]{1,0:T(8,128)(2,1)} %get-tuple-element.389), channel_id=1, source_target_pairs={{0,4},{4,8},{8,12},{12,0},{1,5},{5,9},{9,13},{13,1},{2,6},{6,10},{... | collective-permute-start | bytes 1775624 | tf_op jit(solution)/shard_map/ppermute | solution.py:632
  396.7 53.5 %collective-permute-start.35 = (bf16[272,1088]{1,0:T(8,128)(2,1)}, bf16[272,1088]{1,0:T(8,128)(2,1)}, u32[]{:S(2)}, u32[]{:S(2)}) collective-permute-start(bf16[272,1088]{1,0:T(8,128)(2,1)} %get-tuple-element.388), channel_id=1, source_target_pairs={{0,8},{4,12},{8,0},{12,4},{1,9},{5,13},{9,1},{13,5},{2,10},{6,14},... | collective-permute-start | bytes 1775624 | tf_op jit(solution)/shard_map/ppermute | solution.py:632
  399.2 53.2 %collective-permute-start.36 = (bf16[272,1088]{1,0:T(8,128)(2,1)}, bf16[272,1088]{1,0:T(8,128)(2,1)}, u32[]{:S(2)}, u32[]{:S(2)}) collective-permute-start(bf16[272,1088]{1,0:T(8,128)(2,1)} %get-tuple-element.387), channel_id=1, source_target_pairs={{0,12},{4,0},{8,4},{12,8},{1,13},{5,1},{9,5},{13,9},{2,14},{6,2},{... | collective-permute-start | bytes 1775624 | tf_op jit(solution)/shard_map/ppermute | solution.py:632
  462.8 19.8 %collective-permute-start.37 = (bf16[1088,1088]{1,0:T(8,128)(2,1)S(1)}, bf16[1088,1088]{1,0:T(8,128)(2,1)S(1)}, u32[]{:S(2)}, u32[]{:S(2)}) collective-permute-start(bf16[1088,1088]{1,0:T(8,128)(2,1)S(1)} %get-tuple-element.386), channel_id=1, source_target_pairs={{0,1},{1,0},{2,3},{3,2},{16,17},{17,16},{18,19},{19,18},{4,5},{5,4... | collective-permute-start | bytes 7102472 | tf_op jit(solution)/shard_map/ppermute | solution.py:596
  465.5 16.9 %collective-permute-start.39 = (bf16[272,1088]{1,0:T(8,128)(2,1)S(1)}, bf16[272,1088]{1,0:T(8,128)(2,1)S(1)}, u32[]{:S(2)}, u32[]{:S(2)}) collective-permute-start(bf16[272,1088]{1,0:T(8,128)(2,1)S(1)} %add_convert_fusion.7), channel_id=1, source_target_pairs={{0,2},{1,17},{2,0},{3,19},{16,18},{17,1},{18,16},{19,3},{4,6},{5,2... | collective-permute-start | bytes 1775624 | tf_op jit(solution)/shard_map/ppermute | solution.py:596
  466.2 20.1 %collective-permute-start.38 = (bf16[1088,1088]{1,0:T(8,128)(2,1)S(1)}, bf16[1088,1088]{1,0:T(8,128)(2,1)}, u32[]{:S(2)}, u32[]{:S(2)}) collective-permute-start(bf16[1088,1088]{1,0:T(8,128)(2,1)S(1)} %get-tuple-element.385), channel_id=1, source_target_pairs={{0,1},{1,0},{2,3},{3,2},{16,17},{17,16},{18,19},{19,18},{4,5},{5,4... | collective-permute-start | bytes 7102472 | tf_op jit(solution)/shard_map/ppermute | solution.py:596
  466.2 20.1 %collective-permute-start.40 = (bf16[272,1088]{1,0:T(8,128)(2,1)S(1)}, bf16[272,1088]{1,0:T(8,128)(2,1)}, u32[]{:S(2)}, u32[]{:S(2)}) collective-permute-start(bf16[272,1088]{1,0:T(8,128)(2,1)S(1)} %add_convert_fusion.8.refs_0_), channel_id=1, source_target_pairs={{0,16},{1,3},{2,18},{3,1},{16,0},{17,19},{18,2},{19,17},{4,20},{5,... | collective-permute-start | bytes 1775624 | tf_op jit(solution)/shard_map/ppermute | solution.py:596
  486.3 30.7 %collective-permute-start.41 = (bf16[1088,1088]{1,0:T(8,128)(2,1)}, bf16[1088,1088]{1,0:T(8,128)(2,1)}, u32[]{:S(2)}, u32[]{:S(2)}) collective-permute-start(bf16[1088,1088]{1,0:T(8,128)(2,1)} %add_convert_fusion.1), channel_id=1, source_target_pairs={{0,16},{1,3},{2,18},{3,1},{16,0},{17,19},{18,2},{19,17},{4,20},{5,... | collective-permute-start | bytes 7102472 | tf_op jit(solution)/shard_map/ppermute | solution.py:596
  487.0 37.3 %collective-permute-start.42 = (bf16[272,1088]{1,0:T(8,128)(2,1)S(1)}, bf16[272,1088]{1,0:T(8,128)(2,1)S(1)}, u32[]{:S(2)}, u32[]{:S(2)}) collective-permute-start(bf16[272,1088]{1,0:T(8,128)(2,1)S(1)} %add_convert_fusion.6.refs_0_), channel_id=1, source_target_pairs={{0,16},{1,3},{2,18},{3,1},{16,0},{17,19},{18,2},{19,17},{4,20},{5,... | collective-permute-start | bytes 1775624 | tf_op jit(solution)/shard_map/ppermute | solution.py:596
  525.8 30.8 %collective-permute-start.52 = (bf16[272,1088]{1,0:T(8,128)(2,1)S(1)}, bf16[272,1088]{1,0:T(8,128)(2,1)S(1)}, u32[]{:S(2)}, u32[]{:S(2)}) collective-permute-start(bf16[272,1088]{1,0:T(8,128)(2,1)S(1)} %add_convert_fusion.6.refs_0_), channel_id=1, source_target_pairs={{0,1},{1,0},{2,3},{3,2},{16,17},{17,16},{18,19},{19,18},{4,5},{5,4... | collective-permute-start | bytes 1775624 | tf_op jit(solution)/shard_map/ppermute | solution.py:596
  525.9 30.8 %collective-permute-start.53 = (bf16[272,1088]{1,0:T(8,128)(2,1)S(1)}, bf16[272,1088]{1,0:T(8,128)(2,1)}, u32[]{:S(2)}, u32[]{:S(2)}) collective-permute-start(bf16[272,1088]{1,0:T(8,128)(2,1)S(1)} %collective-permute-done.42.refs_1_), channel_id=1, source_target_pairs={{0,1},{1,0},{2,3},{3,2},{16,17},{17,16},{18,19},{19,18},{4,5},{5,4... | collective-permute-start | bytes 1775624 | tf_op jit(solution)/shard_map/ppermute | solution.py:596
  526.3 30.3 %collective-permute-start.47 = (bf16[1088,256]{1,0:T(8,128)(2,1)}, bf16[1088,256]{1,0:T(8,128)(2,1)S(1)}, u32[]{:S(2)}, u32[]{:S(2)}) collective-permute-start(bf16[1088,256]{1,0:T(8,128)(2,1)} %get-tuple-element.329), channel_id=1, source_target_pairs={{0,1},{1,0},{2,3},{3,2},{4,5},{5,4},{6,7},{7,6},{8,9},{9,8},{10,11... | collective-permute-start | bytes 1671176 | tf_op jit(solution)/shard_map/ppermute | solution.py:602
  528.3 28.4 %collective-permute-start.48 = (bf16[1088,256]{1,0:T(8,128)(2,1)}, bf16[1088,256]{1,0:T(8,128)(2,1)}, u32[]{:S(2)}, u32[]{:S(2)}) collective-permute-start(bf16[1088,256]{1,0:T(8,128)(2,1)} %get-tuple-element.330), channel_id=1, source_target_pairs={{0,2},{1,3},{2,0},{3,1},{4,6},{5,7},{6,4},{7,5},{8,10},{9,11},{10,... | collective-permute-start | bytes 1671176 | tf_op jit(solution)/shard_map/ppermute | solution.py:602
  530.9 25.8 %collective-permute-start.49 = (bf16[1088,256]{1,0:T(8,128)(2,1)}, bf16[1088,256]{1,0:T(8,128)(2,1)}, u32[]{:S(2)}, u32[]{:S(2)}) collective-permute-start(bf16[1088,256]{1,0:T(8,128)(2,1)} %get-tuple-element.331), channel_id=1, source_target_pairs={{0,3},{1,2},{2,1},{3,0},{4,7},{5,6},{6,5},{7,4},{8,11},{9,10},{10,... | collective-permute-start | bytes 1671176 | tf_op jit(solution)/shard_map/ppermute | solution.py:602
  557.1 15.8 %collective-permute-start.55 = (bf16[1088,256]{1,0:T(8,128)(2,1)}, bf16[1088,256]{1,0:T(8,128)(2,1)}, u32[]{:S(2)}, u32[]{:S(2)}) collective-permute-start(bf16[1088,256]{1,0:T(8,128)(2,1)} %get-tuple-element.336), channel_id=1, source_target_pairs={{0,2},{1,3},{2,0},{3,1},{4,6},{5,7},{6,4},{7,5},{8,10},{9,11},{10,... | collective-permute-start | bytes 1671176 | tf_op jit(solution)/shard_map/ppermute | solution.py:602
  558.9 24.4 %collective-permute-start.56 = (bf16[1088,256]{1,0:T(8,128)(2,1)}, bf16[1088,256]{1,0:T(8,128)(2,1)}, u32[]{:S(2)}, u32[]{:S(2)}) collective-permute-start(bf16[1088,256]{1,0:T(8,128)(2,1)} %get-tuple-element.337), channel_id=1, source_target_pairs={{0,3},{1,2},{2,1},{3,0},{4,7},{5,6},{6,5},{7,4},{8,11},{9,10},{10,... | collective-permute-start | bytes 1671176 | tf_op jit(solution)/shard_map/ppermute | solution.py:602
  595.4 19.3 %collective-permute-start.59 = (bf16[272,1088]{1,0:T(8,128)(2,1)S(1)}, bf16[272,1088]{1,0:T(8,128)(2,1)S(1)}, u32[]{:S(2)}, u32[]{:S(2)}) collective-permute-start(bf16[272,1088]{1,0:T(8,128)(2,1)S(1)} %add_convert_fusion.5.refs_0_), channel_id=1, source_target_pairs={{0,16},{1,3},{2,18},{3,1},{16,0},{17,19},{18,2},{19,17},{4,20},{5,... | collective-permute-start | bytes 1775624 | tf_op jit(solution)/shard_map/ppermute | solution.py:596
  597.1 17.6 %collective-permute-start.60 = (bf16[272,1088]{1,0:T(8,128)(2,1)S(1)}, bf16[272,1088]{1,0:T(8,128)(2,1)S(1)}, u32[]{:S(2)}, u32[]{:S(2)}) collective-permute-start(bf16[272,1088]{1,0:T(8,128)(2,1)S(1)} %add_convert_fusion.5.refs_0_), channel_id=1, source_target_pairs={{0,1},{1,0},{2,3},{3,2},{16,17},{17,16},{18,19},{19,18},{4,5},{5,4... | collective-permute-start | bytes 1775624 | tf_op jit(solution)/shard_map/ppermute | solution.py:596
  597.1 17.6 %collective-permute-start.61 = (bf16[272,1088]{1,0:T(8,128)(2,1)S(1)}, bf16[272,1088]{1,0:T(8,128)(2,1)S(1)}, u32[]{:S(2)}, u32[]{:S(2)}) collective-permute-start(bf16[272,1088]{1,0:T(8,128)(2,1)S(1)} %add_convert_fusion.5.refs_0_), channel_id=1, source_target_pairs={{0,17},{1,2},{2,19},{3,0},{16,1},{17,18},{18,3},{19,16},{4,21},{5,... | collective-permute-start | bytes 1775624 | tf_op jit(solution)/shard_map/ppermute | solution.py:596
  597.7 17.0 %collective-permute-start.62 = (f32[3264]{0:T(1024)S(1)}, f32[3264]{0:T(1024)S(1)}, u32[]{:S(2)}, u32[]{:S(2)}) collective-permute-start(f32[3264]{0:T(1024)S(1)} %add.306), channel_id=1, source_target_pairs={{0,16},{1,17},{2,18},{3,19},{16,0},{17,1},{18,2},{19,3},{4,20},{5,... | collective-permute-start | bytes 39176 | tf_op jit(solution)/shard_map/ppermute | solution.py:667
  (77 other events, 843.0 us)
Sparse Core Ops, SparseCore 0:
  77.0 50.3 all-gather.2
  165.1 50.7 all-gather.4
  318.5 48.9 reduce-scatter.2
  524.4 49.9 reduce-scatter.4

commit v11 on v10

--- a/solution.py
+++ b/solution.py
@@ -622,15 +622,17 @@
     return lax.psum_scatter(values, "fsdp", scatter_dimension=0, tiled=True)
 
 
-def scatter_pieces(values, z):
+def cut_pieces(values, z):
     rows = values.reshape(4, values.shape[0] // 4, values.shape[1])
-
-    def share(step):
-        return lax.dynamic_index_in_dim(rows, (z + step) % 4, 0, keepdims=False)
-
-    return [share(0)] + [
+    return [
+        lax.dynamic_index_in_dim(rows, (z + step) % 4, 0, keepdims=False) for step in range(4)
+    ]
+
+
+def send_pieces(pieces):
+    return [pieces[0]] + [
         lax.ppermute(
-            share(step), "fsdp", [(device, (device + step) % 4) for device in range(4)]
+            pieces[step], "fsdp", [(device, (device + step) % 4) for device in range(4)]
         )
         for step in range(1, 4)
     ]
@@ -1274,12 +1276,13 @@
     )
     out_term = turned_product(attended, middle_low)
     up_first = low_sum(up_terms[0], up_far, up_close)
-    grad_low, out_term, up_first = pin((grad_low, out_term, up_first))
-    up_pieces = scatter_pieces(up_first, z)
+    up_pieces = cut_pieces(up_first, z)
+    grad_low, out_term, *up_pieces = pin((grad_low, out_term, *up_pieces))
+    up_pieces = send_pieces(up_pieces)
     in_grads = attend_back(
         place, queries, key_rows, value_rows, grad_low, attended, logs_one, seq_count, 0, 5, []
     )
-    down_shard, *in_grads = pin((down_shard, *in_grads))
+    down_shard, up_pieces[1], *in_grads = pin((down_shard, up_pieces[1], *in_grads))
     down_whole = low_sum(down_shard, plane_swap(down_shard, "other"))
     in_grads = attend_back(
         place,
@@ -1304,10 +1307,7 @@
     sections_mine = [chosen(kind, section_grads) for kind in classes]
     far, far_two = reduce_core(sections_mine)
     second = low_sum(sections_mine[1], far_two)
-    second, far, middle, up_whole, down_beside, *in_grads = pin(
-        (second, far, middle, up_whole, down_beside, *in_grads)
-    )
-    up_beside = plane_swap(up_whole, "near")
+    second, far, middle, *in_grads = pin((second, far, middle, *in_grads))
     query_low, key_low, value_low = in_grads
     close = plane_swap(second, "near")
     result_slots = by_rows(
@@ -1324,9 +1324,10 @@
         4,
     )
     first = low_sum(sections_mine[0], far, close)
-    first, up_beside, query_low, *result_slots = pin(
-        (first, up_beside, query_low, *result_slots)
-    )
+    first, up_whole, down_beside, query_low, *result_slots = pin(
+        (first, up_whole, down_beside, query_low, *result_slots)
+    )
+    up_beside = plane_swap(up_whole, "near")
     down_parts = share_by_core(down_whole, down_beside)
     up_parts = share_by_core(up_whole, up_beside)
     shard = scatter_rows(first)

time: 635 us -> 633 us (level)
    ppermute x3, waiting for transfers between devices: 27.7 us -> 14.2 us  [send_pieces(): lax.ppermute(pieces[step], 'fsdp', [(device, (device + step) % 4) for dev...]
    ppermute x36, waiting for transfers between devices: 50.8 us -> 60.5 us  [plane_swap(): lax.ppermute(values, ('dp', 'ctx'), [(device, plane_partner(device, kind)...]
  transfers between devices with their start and end apart: 67 -> 67, of which waited for: 25 -> 23; matrix products, arithmetic and copies ran while one was open for 15% -> 15% of each run, Pallas kernels for 43% -> 44%
where the time goes in v11:
time: 633 us; the launch traced here: 624 us
  Pallas kernels  275 us (43%)
  waiting for transfers between devices  155 us (24%)
  matrix products  61.7 us (10%)
  starting transfers between devices  46.6 us (7%)
  other arithmetic  37.5 us (6%)
  local copies, waits for them, and re-layouts  31.9 us (5%)
  between operations  15.3 us (2%)
    pallas_call x8, Pallas kernels, by_rows(): pl.pallas_call(kernel, grid=(rows // step,), in_specs=[tile] * len(tiled[...  155 us
    dot_general x12, matrix products, product(): lax.dot_general(left, right, ((dims[:1], dims[1:]), ((), ())), preferred_...  61.7 us
    ppermute x36, waiting for transfers between devices, plane_swap(): lax.ppermute(values, ('dp', 'ctx'), [(device, plane_partner(device, kind)...  60.5 us
    pallas_call x2, Pallas kernels, attend_back(): pl.pallas_call(functools.partial(attend_back_kernel, count=count, width=w...  47.8 us
    ppermute x12, waiting for transfers between devices, ctx_swap(): lax.ppermute(values, 'ctx', [(device, device ^ bits) for device in range(...  36.6 us
    pallas_call x1, Pallas kernels, attend(): pl.pallas_call(functools.partial(attend_kernel, count=count, width=width,...  32.2 us
    convert_element_type x9, other arithmetic, low_sum(): sum((term.astype(jnp.float32) for term in terms)).astype(jnp.bfloat16)  29.8 us
    ppermute x3, waiting for transfers between devices, per_device_exchanged(): lax.ppermute(section, 'fsdp', [(device, (device + step) % 4) for device i...  26.4 us
  transfers between devices with their start and end apart: 67, of which 23 were waited for; matrix products, arithmetic and copies ran while one was open for 15% of the time, Pallas kernels for 44%

profile of v11, /device:TPU:8, one launch (start us, length us, event | category | flops | bytes accessed | tf_op | source)
XLA Modules:
  0.0 623.9 jit_solution(8579466559033604770)
XLA Ops:
  7.3 3.6 fusion.11
  21.8 3.6 collective-permute-start.4
  27.2 14.1 %collective-permute-done.7.refs_2_ = bf16[1088,256]{1,0:T(8,128)(2,1)S(1)} collective-permute-done((bf16[1088,256]{1,0:T(8,128)(2,1)}, bf16[1088,256]{1,0:T(8,128)(2,1)S(1)}, u32[]{:S(2)}, u32[]{:S(2)}) %collective-permute-start.7) | collective-permute-done | bytes 557088 | tf_op jit(solution)/shard_map/ppermute | solution.py:602
  41.3 9.1 %collective-permute-done.8.refs_3_ = bf16[1088,256]{1,0:T(8,128)(2,1)S(1)} collective-permute-done((bf16[1088,256]{1,0:T(8,128)(2,1)}, bf16[1088,256]{1,0:T(8,128)(2,1)S(1)}, u32[]{:S(2)}, u32[]{:S(2)}) %collective-permute-start.8) | collective-permute-done | bytes 557088 | tf_op jit(solution)/shard_map/ppermute | solution.py:602
  50.4 22.8 %collective-permute-done.4.refs_9_ = bf16[272,1088]{1,0:T(8,128)(2,1)S(1)} collective-permute-done((bf16[272,1088]{1,0:T(8,128)(2,1)}, bf16[272,1088]{1,0:T(8,128)(2,1)S(1)}, u32[]{:S(2)}, u32[]{:S(2)}) %collective-permute-start.4) | collective-permute-done | bytes 591904 | tf_op jit(solution)/shard_map/ppermute | solution.py:1099
  73.2 3.6 collective-permute-done.5.refs_10_
  81.0 6.5 %collective-permute-done.9.refs_11_ = bf16[272,1088]{1,0:T(8,128)(2,1)} collective-permute-done((bf16[272,1088]{1,0:T(8,128)(2,1)}, bf16[272,1088]{1,0:T(8,128)(2,1)}, u32[]{:S(2)}, u32[]{:S(2)}) %collective-permute-start.9) | collective-permute-done | bytes 591904 | tf_op jit(solution)/shard_map/ppermute | solution.py:596
  87.6 6.7 %collective-permute-done.10.refs_12_ = bf16[272,1088]{1,0:T(8,128)(2,1)} collective-permute-done((bf16[272,1088]{1,0:T(8,128)(2,1)S(1)}, bf16[272,1088]{1,0:T(8,128)(2,1)}, u32[]{:S(2)}, u32[]{:S(2)}) %collective-permute-start.10) | collective-permute-done | bytes 591904 | tf_op jit(solution)/shard_map/ppermute | solution.py:596
  94.3 6.7 %collective-permute-done.11.refs_13_ = bf16[272,1088]{1,0:T(8,128)(2,1)} collective-permute-done((bf16[272,1088]{1,0:T(8,128)(2,1)}, bf16[272,1088]{1,0:T(8,128)(2,1)}, u32[]{:S(2)}, u32[]{:S(2)}) %collective-permute-start.11) | collective-permute-done | bytes 591904 | tf_op jit(solution)/shard_map/ppermute | solution.py:596
  105.2 21.7 %front.1 = (bf16[1024,1088]{1,0:T(8,128)(2,1)}, bf16[1024,1088]{1,0:T(8,128)(2,1)}, bf16[1024,1088]{1,0:T(8,128)(2,1)}, bf16[1024,1088]{1,0:T(8,128)(2,1)}, bf16...) custom-call(s32[16]{0:T(128)} %stack.120.places_ref, f32[4,1088]{1,0:T(4,128)} %pad_maximum_fusion.1.vectors_ref, ...), custom_call_target="tpu_custom_call" | custom-call | flops 1024 | bytes 1024 | tf_op jit(solution)/shard_map/front/pallas_call | solution.py:748
  131.4 32.2 %attend.1 = (bf16[1024,1088]{1,0:T(8,128)(2,1)S(1)}, f32[1024,128]{1,0:T(8,128)S(1)}) custom-call(s32[1]{0:T(128)} %bitcast.24.place_ref, bf16[1024,1088]{1,0:T(8,128)(2,1)S(1)} %copy-done.3, bf16[1024,1088]{1,0:T(8,128)(2,1)} %get-tuple-element.226.k_ref, bf16[1024,1088]{1,0:T(8,128)(2,1)} %get-tuple-element.227.v_ref), custom_call_target="tpu_custom_call" | custom-call | flops 1024 | bytes 1024 | tf_op jit(solution)/shard_map/attend/pallas_call | solution.py:507
  171.3 10.1 %middle.1 = (f32[1024,1088]{1,0:T(8,128)}, bf16[1024,1088]{1,0:T(8,128)(2,1)}) custom-call(bf16[1024,1088]{1,0:T(8,128)(2,1)} %get-tuple-element.220.x_ref, bf16[1024,1088]{1,0:T(8,128)(2,1)} %copy-done.4, f32[3,1088]{1,0:T(4,128)} %pad_maximum_fusion.2.vectors_ref, bf16[16,272,1088]{2,1,0:T(8,128)(2,1)} %get-tuple-element.230.all_ref.refs_8_), custom_call_target="tpu_custom_call" | custom-call | flops 1024 | bytes 1024 | tf_op jit(solution)/shard_map/middle/pallas_call | solution.py:1021
  181.4 17.4 %up.2 = (bf16[1024,1088]{1,0:T(8,128)(2,1)}, bf16[1024,1088]{1,0:T(8,128)(2,1)}, bf16[1024,1088]{1,0:T(8,128)(2,1)}, bf16[1024,1088]{1,0:T(8,128)(2,1)}) custom-call(bf16[1024,1088]{1,0:T(8,128)(2,1)} %get-tuple-element.268.h_ref, f32[2,1088]{1,0:T(2,128)} %pad_maximum_fusion.3.biases_ref, bf16[1088,1088]{1,0:T(8,128)(2,1)} %all-gather.3.cloned.1.call-done.refs_0_.refs_4_, ...), custom_call_target="tpu_custom_call" | custom-call | flops 1024 | bytes 1024 | tf_op jit(solution)/shard_map/up/pallas_call | solution.py:1021
  198.8 18.0 %up.3 = (bf16[1024,1088]{1,0:T(8,128)(2,1)}, bf16[1024,1088]{1,0:T(8,128)(2,1)}, bf16[1024,1088]{1,0:T(8,128)(2,1)}, bf16[1024,1088]{1,0:T(8,128)(2,1)}) custom-call(bf16[1024,1088]{1,0:T(8,128)(2,1)} %get-tuple-element.268.h_ref, f32[2,1088]{1,0:T(2,128)} %pad_maximum_fusion.4.biases_ref, bf16[1088,1088]{1,0:T(8,128)(2,1)} %collective-permute-done.19.refs_0_.refs_5_, ...), custom_call_target="tpu_custom_call" | custom-call | flops 1024 | bytes 1024 | tf_op jit(solution)/shard_map/up/pallas_call | solution.py:1021
  224.1 6.2 convolution_convert_fusion.11
  230.3 4.6 convolution_convert_fusion.10
  235.2 4.6 convolution_convert_fusion.9
  239.8 4.8 convolution_convert_fusion.8
  244.6 8.6 %collective-permute-done.25.refs_2_.refs_5_ = bf16[1088,1088]{1,0:T(8,128)(2,1)} collective-permute-done((bf16[1088,1088]{1,0:T(8,128)(2,1)}, bf16[1088,1088]{1,0:T(8,128)(2,1)}, u32[]{:S(2)}, u32[]{:S(2)}) %collective-permute-start.25) | collective-permute-done | bytes 2367520 | tf_op jit(solution)/shard_map/ppermute | solution.py:596
  253.7 14.0 %hidden.2 = (bf16[1024,1088]{1,0:T(8,128)(2,1)}, bf16[1024,1088]{1,0:T(8,128)(2,1)}, f32[3,8,1088]{2,1,0:T(8,128)}) custom-call(bf16[1024,1088]{1,0:T(8,128)(2,1)} %copy-done.2, bf16[1024,1088]{1,0:T(8,128)(2,1)} %get-tuple-element.254.refs_0_, bf16[1024,1088]{1,0:T(8,128)(2,1)} %get-tuple-element.255.refs_1_, ...), custom_call_target="tpu_custom_call" | custom-call | flops 1024 | bytes 1024 | tf_op jit(solution)/shard_map/hidden/pallas_call | solution.py:1021
  267.7 4.6 add_convert_fusion.4
  275.2 14.2 %hidden.3 = (bf16[1024,1088]{1,0:T(8,128)(2,1)}, bf16[1024,1088]{1,0:T(8,128)(2,1)}, f32[3,8,1088]{2,1,0:T(8,128)}) custom-call(bf16[1024,1088]{1,0:T(8,128)(2,1)} %copy-done.2, bf16[1024,1088]{1,0:T(8,128)(2,1)} %get-tuple-element.260.refs_0_, bf16[1024,1088]{1,0:T(8,128)(2,1)} %get-tuple-element.261.refs_1_, ...), custom_call_target="tpu_custom_call" | custom-call | flops 1024 | bytes 1024 | tf_op jit(solution)/shard_map/hidden/pallas_call | solution.py:1021
  289.4 7.1 %convolution_convert_fusion.7 = bf16[1088,1088]{1,0:T(8,128)(2,1)} fusion(bf16[1024,1088]{1,0:T(8,128)(2,1)} %get-tuple-element.268.h_ref, bf16[1024,1088]{1,0:T(8,128)(2,1)} %get-tuple-element.281.refs_3_), kind=kOutput, calls=%fused_computation.9 | convolution fusion | flops 2425491456 | bytes 6823936 | tf_op jit(solution)/shard_map/dot_general | solution.py:675
  296.5 4.6 convolution_convert_fusion.6
  301.6 4.6 convolution_convert_fusion.4
  306.2 4.9 add_convert_fusion.3
  311.1 7.4 %fusion.2 = bf16[1088,1088]{1,0:T(8,128)(2,1)} fusion(bf16[1024,1088]{1,0:T(8,128)(2,1)S(1)} %copy-done.27, bf16[1024,1088]{1,0:T(8,128)(2,1)} %get-tuple-element.279.refs_1_, bf16[1088,1088]{1,0:T(8,128)(2,1)} %collective-permute-done.29), kind=kOutput, calls=%fused_computation.14 | convolution fusion | flops 2430226432 | bytes 9191424 | tf_op jit(solution)/shard_map/dot_general | solution.py:675
  319.1 32.2 %back.1 = (f32[1024,1088]{1,0:T(8,128)}, bf16[1024,1088]{1,0:T(8,128)(2,1)}, bf16[1024,1088]{1,0:T(8,128)(2,1)}, f32[3,8,1088]{2,1,0:T(8,128)}) custom-call(bf16[1024,1088]{1,0:T(8,128)(2,1)} %copy-done.2, f32[1024,1088]{1,0:T(8,128)} %get-tuple-element.316.middle_ref, f32[1,1088]{1,0:T(1,128)} %copy-done.47, bf16[1024,1088]{1,0:T(8,128)(2,1)} %get-tuple-element.278.refs_0_, ...), custom_call_target="tpu_custom_call" | custom-call | flops 1024 | bytes 1024 | tf_op jit(solution)/shard_map/back/pallas_call | solution.py:1021
  351.3 6.4 %convolution_convert_fusion.3 = bf16[1088,1088]{1,0:T(8,128)(2,1)} fusion(bf16[1024,1088]{1,0:T(8,128)(2,1)S(1)} %copy-done.5, bf16[1024,1088]{1,0:T(8,128)(2,1)} %get-tuple-element.283), kind=kOutput, calls=%fused_computation.3 | convolution fusion | flops 2425491456 | bytes 6823936 | tf_op jit(solution)/shard_map/dot_general | solution.py:675
  357.7 3.4 add_convert_fusion.2
  364.8 26.1 %attend_back.2 = (bf16[1024,1088]{1,0:T(8,128)(2,1)S(1)}, bf16[1024,1088]{1,0:T(8,128)(2,1)S(1)}, bf16[1024,1088]{1,0:T(8,128)(2,1)}) custom-call(s32[1]{0:T(128)} %bitcast.24.place_ref, bf16[1024,1088]{1,0:T(8,128)(2,1)} %get-tuple-element.225.q_ref, bf16[1024,1088]{1,0:T(8,128)(2,1)} %get-tuple-element.226.k_ref, ...), custom_call_target="tpu_custom_call" | custom-call | flops 1024 | bytes 1024 | tf_op jit(solution)/shard_map/attend_back/pallas_call | solution.py:537
  398.3 21.6 %attend_back.3 = (bf16[1024,1088]{1,0:T(8,128)(2,1)S(1)}, bf16[1024,1088]{1,0:T(8,128)(2,1)S(1)}, bf16[1024,1088]{1,0:T(8,128)(2,1)}) custom-call(s32[1]{0:T(128)} %bitcast.24.place_ref, bf16[1024,1088]{1,0:T(8,128)(2,1)} %get-tuple-element.225.q_ref, ...), custom_call_target="tpu_custom_call", output_to_operand_aliasing={{0}: (7, {}), {1}: (8, {}), {2}: (9, {})} | custom-call | flops 1024 | bytes 1024 | tf_op jit(solution)/shard_map/attend_back/pallas_call | solution.py:537
  421.7 13.2 %collective-permute-done.35 = bf16[272,1088]{1,0:T(8,128)(2,1)} collective-permute-done((bf16[272,1088]{1,0:T(8,128)(2,1)}, bf16[272,1088]{1,0:T(8,128)(2,1)}, u32[]{:S(2)}, u32[]{:S(2)}) %collective-permute-start.35) | collective-permute-done | bytes 591904 | tf_op jit(solution)/shard_map/ppermute | solution.py:634
  442.3 5.3 select_select_fusion
  448.0 7.8 %collective-permute-done.37 = bf16[1088,1088]{1,0:T(8,128)(2,1)S(1)} collective-permute-done((bf16[1088,1088]{1,0:T(8,128)(2,1)S(1)}, bf16[1088,1088]{1,0:T(8,128)(2,1)S(1)}, u32[]{:S(2)}, u32[]{:S(2)}) %collective-permute-start.37) | collective-permute-done | bytes 2367520 | tf_op jit(solution)/shard_map/ppermute | solution.py:596
  466.0 14.3 %collective-permute-done.40 = bf16[272,1088]{1,0:T(8,128)(2,1)} collective-permute-done((bf16[272,1088]{1,0:T(8,128)(2,1)S(1)}, bf16[272,1088]{1,0:T(8,128)(2,1)}, u32[]{:S(2)}, u32[]{:S(2)}) %collective-permute-start.40) | collective-permute-done | bytes 591904 | tf_op jit(solution)/shard_map/ppermute | solution.py:596
  482.0 25.0 %down.1 = (bf16[1088,256]{1,0:T(8,128)(2,1)}, bf16[1088,256]{1,0:T(8,128)(2,1)}, bf16[1088,256]{1,0:T(8,128)(2,1)}, bf16[1088,256]{1,0:T(8,128)(2,1)}) custom-call(f32[1024,1088]{1,0:T(8,128)} %get-tuple-element.316.middle_ref, f32[1,1088]{1,0:T(1,128)} %reshape.450.vectors_ref, bf16[1024,1088]{1,0:T(8,128)(2,1)} %get-tuple-element.249.refs_0_, ...), custom_call_target="tpu_custom_call" | custom-call | flops 1024 | bytes 1024 | tf_op jit(solution)/shard_map/down/pallas_call | solution.py:1021
  507.0 7.3 %add_convert_fusion = bf16[1088,1088]{1,0:T(8,128)(2,1)} fusion(bf16[1088,1088]{1,0:T(8,128)(2,1)} %collective-permute-done.39, bf16[1088,1088]{1,0:T(8,128)(2,1)} %copy-done.31, bf16[1088,1088]{1,0:T(8,128)(2,1)} %copy-done.26, bf16[1088,1088]{1,0:T(8,128)(2,1)} %copy-done.24, bf16[1088,1088]{1,0:T(8,128)(2,1)} %copy-done.25, ...), kind=kLoop, calls=%fused_computation.15 | loop fusion | flops 10653696 | bytes 16572419 | tf_op jit(solution)/shard_map/convert_element_type | solution.py:606
  517.8 7.9 %collective-permute-done.51.refs_1_ = bf16[272,1088]{1,0:T(8,128)(2,1)S(1)} collective-permute-done((bf16[272,1088]{1,0:T(8,128)(2,1)S(1)}, bf16[272,1088]{1,0:T(8,128)(2,1)S(1)}, u32[]{:S(2)}, u32[]{:S(2)}) %collective-permute-start.51) | collective-permute-done | bytes 591904 | tf_op jit(solution)/shard_map/ppermute | solution.py:596
  530.2 23.8 %last.1 = (bf16[1088,256]{1,0:T(8,128)(2,1)}, bf16[1088,256]{1,0:T(8,128)(2,1)}, bf16[1088,256]{1,0:T(8,128)(2,1)}, bf16[1088,256]{1,0:T(8,128)(2,1)}, f32[4,8,1088]{2,1,0:T(8,128)}) custom-call(bf16[1024,1088]{1,0:T(8,128)(2,1)} %copy-done.6, bf16[1024,1088]{1,0:T(8,128)(2,1)} %copy-done.9, bf16[1024,1088]{1,0:T(8,128)(2,1)} %get-tuple-element.327.v_ref, ...), custom_call_target="tpu_custom_call" | custom-call | flops 1024 | bytes 1024 | tf_op jit(solution)/shard_map/last/pallas_call | solution.py:1021
  559.9 3.4 collective-permute-done.44
  563.4 3.7 collective-permute-done.42
  571.1 10.5 %collective-permute-done.56.refs_3_ = bf16[1088,256]{1,0:T(8,128)(2,1)} collective-permute-done((bf16[1088,256]{1,0:T(8,128)(2,1)}, bf16[1088,256]{1,0:T(8,128)(2,1)}, u32[]{:S(2)}, u32[]{:S(2)}) %collective-permute-start.56) | collective-permute-done | bytes 557088 | tf_op jit(solution)/shard_map/ppermute | solution.py:602
  583.7 8.8 %collective-permute-done.58 = f32[3264]{0:T(1024)S(1)} collective-permute-done((f32[3264]{0:T(1024)S(1)}, f32[3264]{0:T(1024)S(1)}, u32[]{:S(2)}, u32[]{:S(2)}) %collective-permute-start.58) | collective-permute-done | bytes 13088 | tf_op jit(solution)/shard_map/ppermute | solution.py:669
  597.2 4.7 assemble.2
  602.0 3.8 settle.5
  608.5 3.9 settle.4
  613.8 3.4 assemble.3
  (322 shorter events, 105.9 us)
Async XLA Ops:
  7.2 120.1 %all-gather.3.cloned.1.call-start = ((), (), s32[]{:S(2)}) async-start(), calls=%async_computation.2 | async-start | bytes 3133440 | tf_op jit(solution)/shard_map/all_gather | solution.py:1145
  14.0 13.0 %collective-permute-start.6 = (bf16[1088,256]{1,0:T(8,128)(2,1)}, bf16[1088,256]{1,0:T(8,128)(2,1)}, u32[]{:S(2)}, u32[]{:S(2)}) collective-permute-start(bf16[1088,256]{1,0:T(8,128)(2,1)} %get-tuple-element.406), channel_id=1, source_target_pairs={{0,1},{1,0},{2,3},{3,2},{4,5},{5,4},{6,7},{7,6},{8,9},{9,8},{10,11... | collective-permute-start | bytes 1671176 | tf_op jit(solution)/shard_map/ppermute | solution.py:602
  18.8 31.6 %collective-permute-start.3 = (bf16[272,1088]{1,0:T(8,128)(2,1)}, bf16[272,1088]{1,0:T(8,128)(2,1)}, u32[]{:S(2)}, u32[]{:S(2)}) collective-permute-start(bf16[272,1088]{1,0:T(8,128)(2,1)} %get-tuple-element.206), channel_id=1, source_target_pairs={{0,4},{4,8},{8,12},{12,0},{1,5},{5,9},{9,13},{13,1},{2,6},{6,10},{... | collective-permute-start | bytes 1775624 | tf_op jit(solution)/shard_map/ppermute | solution.py:1099
  21.8 51.4 %collective-permute-start.4 = (bf16[272,1088]{1,0:T(8,128)(2,1)}, bf16[272,1088]{1,0:T(8,128)(2,1)S(1)}, u32[]{:S(2)}, u32[]{:S(2)}) collective-permute-start(bf16[272,1088]{1,0:T(8,128)(2,1)} %get-tuple-element.206), channel_id=1, source_target_pairs={{0,8},{4,12},{8,0},{12,4},{1,9},{5,13},{9,1},{13,5},{2,10},{6,14},... | collective-permute-start | bytes 1775624 | tf_op jit(solution)/shard_map/ppermute | solution.py:1099
  25.4 51.4 %collective-permute-start.5 = (bf16[272,1088]{1,0:T(8,128)(2,1)}, bf16[272,1088]{1,0:T(8,128)(2,1)}, u32[]{:S(2)}, u32[]{:S(2)}) collective-permute-start(bf16[272,1088]{1,0:T(8,128)(2,1)} %get-tuple-element.206), channel_id=1, source_target_pairs={{0,12},{4,0},{8,4},{12,8},{1,13},{5,1},{9,5},{13,9},{2,14},{6,2},{... | collective-permute-start | bytes 1775624 | tf_op jit(solution)/shard_map/ppermute | solution.py:1099
  25.4 15.8 %collective-permute-start.7 = (bf16[1088,256]{1,0:T(8,128)(2,1)}, bf16[1088,256]{1,0:T(8,128)(2,1)S(1)}, u32[]{:S(2)}, u32[]{:S(2)}) collective-permute-start(bf16[1088,256]{1,0:T(8,128)(2,1)} %get-tuple-element.405), channel_id=1, source_target_pairs={{0,2},{1,3},{2,0},{3,1},{4,6},{5,7},{6,4},{7,5},{8,10},{9,11},{10,... | collective-permute-start | bytes 1671176 | tf_op jit(solution)/shard_map/ppermute | solution.py:602
  27.0 23.4 %collective-permute-start.8 = (bf16[1088,256]{1,0:T(8,128)(2,1)}, bf16[1088,256]{1,0:T(8,128)(2,1)S(1)}, u32[]{:S(2)}, u32[]{:S(2)}) collective-permute-start(bf16[1088,256]{1,0:T(8,128)(2,1)} %get-tuple-element.207), channel_id=1, source_target_pairs={{0,3},{1,2},{2,1},{3,0},{4,7},{5,6},{6,5},{7,4},{8,11},{9,10},{10,... | collective-permute-start | bytes 1671176 | tf_op jit(solution)/shard_map/ppermute | solution.py:602
  76.8 145.5 %all-gather.5.cloned.1.call-start = ((), (), s32[]{:S(2)}) async-start(), calls=%async_computation.3 | async-start | bytes 3133440 | tf_op jit(solution)/shard_map/all_gather | solution.py:1169
  78.5 15.8 %collective-permute-start.10 = (bf16[272,1088]{1,0:T(8,128)(2,1)S(1)}, bf16[272,1088]{1,0:T(8,128)(2,1)}, u32[]{:S(2)}, u32[]{:S(2)}) collective-permute-start(bf16[272,1088]{1,0:T(8,128)(2,1)S(1)} %collective-permute-done.4.refs_9_), channel_id=1, source_target_pairs={{0,16},{1,3},{2,18},{3,1},{16,0},{17,19},{18,2},{19,17},{4,20},{5,... | collective-permute-start | bytes 1775624 | tf_op jit(solution)/shard_map/ppermute | solution.py:596
  79.0 22.0 %collective-permute-start.11 = (bf16[272,1088]{1,0:T(8,128)(2,1)}, bf16[272,1088]{1,0:T(8,128)(2,1)}, u32[]{:S(2)}, u32[]{:S(2)}) collective-permute-start(bf16[272,1088]{1,0:T(8,128)(2,1)} %collective-permute-done.5.refs_10_), channel_id=1, source_target_pairs={{0,16},{1,3},{2,18},{3,1},{16,0},{17,19},{18,2},{19,17},{4,20},{5,... | collective-permute-start | bytes 1775624 | tf_op jit(solution)/shard_map/ppermute | solution.py:596
  80.5 21.0 %collective-permute-start.12 = (bf16[272,1088]{1,0:T(8,128)(2,1)}, bf16[272,1088]{1,0:T(8,128)(2,1)}, u32[]{:S(2)}, u32[]{:S(2)}) collective-permute-start(bf16[272,1088]{1,0:T(8,128)(2,1)} %collective-permute-done.3.refs_8_), channel_id=1, source_target_pairs={{0,1},{1,0},{2,3},{3,2},{16,17},{17,16},{18,19},{19,18},{4,5},{5,4... | collective-permute-start | bytes 1775624 | tf_op jit(solution)/shard_map/ppermute | solution.py:596
  80.5 22.8 %collective-permute-start.13 = (bf16[272,1088]{1,0:T(8,128)(2,1)S(1)}, bf16[272,1088]{1,0:T(8,128)(2,1)}, u32[]{:S(2)}, u32[]{:S(2)}) collective-permute-start(bf16[272,1088]{1,0:T(8,128)(2,1)S(1)} %collective-permute-done.4.refs_9_), channel_id=1, source_target_pairs={{0,1},{1,0},{2,3},{3,2},{16,17},{17,16},{18,19},{19,18},{4,5},{5,4... | collective-permute-start | bytes 1775624 | tf_op jit(solution)/shard_map/ppermute | solution.py:596
  87.5 15.7 %collective-permute-start.14 = (bf16[272,1088]{1,0:T(8,128)(2,1)}, bf16[272,1088]{1,0:T(8,128)(2,1)}, u32[]{:S(2)}, u32[]{:S(2)}) collective-permute-start(bf16[272,1088]{1,0:T(8,128)(2,1)} %collective-permute-done.5.refs_10_), channel_id=1, source_target_pairs={{0,1},{1,0},{2,3},{3,2},{16,17},{17,16},{18,19},{19,18},{4,5},{5,4... | collective-permute-start | bytes 1775624 | tf_op jit(solution)/shard_map/ppermute | solution.py:596
  127.3 37.6 %collective-permute-start.18 = (bf16[1088,1088]{1,0:T(8,128)(2,1)}, bf16[1088,1088]{1,0:T(8,128)(2,1)}, u32[]{:S(2)}, u32[]{:S(2)}) collective-permute-start(bf16[1088,1088]{1,0:T(8,128)(2,1)} %all-gather.3.cloned.1.call-done.refs_0_.refs_4_), channel_id=1, source_target_pairs={{0,1},{1,0},{2,3},{3,2},{16,17},{17,16},{18,19},{19,18},{4,5},{5,4... | collective-permute-start | bytes 7102472 | tf_op jit(solution)/shard_map/ppermute | solution.py:596
  127.3 37.6 %collective-permute-start.19 = (bf16[1088,1088]{1,0:T(8,128)(2,1)}, bf16[1088,1088]{1,0:T(8,128)(2,1)}, u32[]{:S(2)}, u32[]{:S(2)}) collective-permute-start(bf16[1088,1088]{1,0:T(8,128)(2,1)} %all-gather.3.cloned.1.call-done.refs_0_.refs_4_), channel_id=1, source_target_pairs={{0,16},{1,3},{2,18},{3,1},{16,0},{17,19},{18,2},{19,17},{4,20},{5,... | collective-permute-start | bytes 7102472 | tf_op jit(solution)/shard_map/ppermute | solution.py:596
  165.0 227.5 %reduce-scatter.3.cloned.1.call-start = ((), (), s32[]{:S(2)}) async-start(), calls=%async_computation.4 | async-start | bytes 3133440 | tf_op jit(solution)/shard_map/reduce_scatter | solution.py:622
  165.3 33.6 %collective-permute-start.22 = (bf16[1088,1088]{1,0:T(8,128)(2,1)}, bf16[1088,1088]{1,0:T(8,128)(2,1)}, u32[]{:S(2)}, u32[]{:S(2)}) collective-permute-start(bf16[1088,1088]{1,0:T(8,128)(2,1)} %collective-permute-done.19.refs_0_.refs_5_), channel_id=1, source_target_pairs={{0,1},{1,0},{2,3},{3,2},{16,17},{17,16},{18,19},{19,18},{4,5},{5,4... | collective-permute-start | bytes 7102472 | tf_op jit(solution)/shard_map/ppermute | solution.py:596
  167.1 49.7 %collective-permute-start.20 = (bf16[1088,256]{1,0:T(8,128)(2,1)}, bf16[1088,256]{1,0:T(8,128)(2,1)S(1)}, u32[]{:S(2)}, u32[]{:S(2)}) collective-permute-start(bf16[1088,256]{1,0:T(8,128)(2,1)} %get-tuple-element.403), channel_id=1, source_target_pairs={{0,1},{1,0},{2,3},{3,2},{4,5},{5,4},{6,7},{7,6},{8,9},{9,8},{10,11... | collective-permute-start | bytes 1671176 | tf_op jit(solution)/shard_map/ppermute | solution.py:602
  167.4 50.3 %collective-permute-start.21 = (bf16[1088,256]{1,0:T(8,128)(2,1)}, bf16[1088,256]{1,0:T(8,128)(2,1)S(1)}, u32[]{:S(2)}, u32[]{:S(2)}) collective-permute-start(bf16[1088,256]{1,0:T(8,128)(2,1)} %get-tuple-element.402), channel_id=1, source_target_pairs={{0,2},{1,3},{2,0},{3,1},{4,6},{5,7},{6,4},{7,5},{8,10},{9,11},{10,... | collective-permute-start | bytes 1671176 | tf_op jit(solution)/shard_map/ppermute | solution.py:602
  168.9 29.9 %collective-permute-start.23 = (bf16[1088,256]{1,0:T(8,128)(2,1)}, bf16[1088,256]{1,0:T(8,128)(2,1)S(1)}, u32[]{:S(2)}, u32[]{:S(2)}) collective-permute-start(bf16[1088,256]{1,0:T(8,128)(2,1)} %get-tuple-element.401), channel_id=1, source_target_pairs={{0,3},{1,2},{2,1},{3,0},{4,7},{5,6},{6,5},{7,4},{8,11},{9,10},{10,... | collective-permute-start | bytes 1671176 | tf_op jit(solution)/shard_map/ppermute | solution.py:602
  222.4 30.8 %collective-permute-start.25 = (bf16[1088,1088]{1,0:T(8,128)(2,1)}, bf16[1088,1088]{1,0:T(8,128)(2,1)}, u32[]{:S(2)}, u32[]{:S(2)}) collective-permute-start(bf16[1088,1088]{1,0:T(8,128)(2,1)} %all-gather.5.cloned.1.call-done.refs_2_.refs_4_), channel_id=1, source_target_pairs={{0,16},{1,3},{2,18},{3,1},{16,0},{17,19},{18,2},{19,17},{4,20},{5,... | collective-permute-start | bytes 7102472 | tf_op jit(solution)/shard_map/ppermute | solution.py:596
  223.9 29.8 %collective-permute-start.26 = (bf16[1088,1088]{1,0:T(8,128)(2,1)}, bf16[1088,1088]{1,0:T(8,128)(2,1)}, u32[]{:S(2)}, u32[]{:S(2)}) collective-permute-start(bf16[1088,1088]{1,0:T(8,128)(2,1)} %all-gather.5.cloned.1.call-done.refs_2_.refs_4_), channel_id=1, source_target_pairs={{0,1},{1,0},{2,3},{3,2},{16,17},{17,16},{18,19},{19,18},{4,5},{5,4... | collective-permute-start | bytes 7102472 | tf_op jit(solution)/shard_map/ppermute | solution.py:596
  234.9 32.8 %collective-permute-start.27 = (bf16[1088,1088]{1,0:T(8,128)(2,1)}, bf16[1088,1088]{1,0:T(8,128)(2,1)}, u32[]{:S(2)}, u32[]{:S(2)}) collective-permute-start(bf16[1088,1088]{1,0:T(8,128)(2,1)} %convolution_convert_fusion.11), channel_id=1, source_target_pairs={{0,1},{1,0},{2,3},{3,2},{16,17},{17,16},{18,19},{19,18},{4,5},{5,4... | collective-permute-start | bytes 7102472 | tf_op jit(solution)/shard_map/ppermute | solution.py:596
  253.2 20.6 %collective-permute-start.28 = (bf16[1088,1088]{1,0:T(8,128)(2,1)}, bf16[1088,1088]{1,0:T(8,128)(2,1)S(1)}, u32[]{:S(2)}, u32[]{:S(2)}) collective-permute-start(bf16[1088,1088]{1,0:T(8,128)(2,1)} %collective-permute-done.25.refs_2_.refs_5_), channel_id=1, source_target_pairs={{0,1},{1,0},{2,3},{3,2},{16,17},{17,16},{18,19},{19,18},{4,5},{5,4... | collective-permute-start | bytes 7102472 | tf_op jit(solution)/shard_map/ppermute | solution.py:596
  253.2 36.2 %collective-permute-start.24 = (bf16[1088,1088]{1,0:T(8,128)(2,1)}, bf16[1088,1088]{1,0:T(8,128)(2,1)}, u32[]{:S(2)}, u32[]{:S(2)}) collective-permute-start(bf16[1088,1088]{1,0:T(8,128)(2,1)} %convolution_convert_fusion.10), channel_id=1, source_target_pairs={{0,1},{1,0},{2,3},{3,2},{16,17},{17,16},{18,19},{19,18},{4,5},{5,4... | collective-permute-start | bytes 7102472 | tf_op jit(solution)/shard_map/ppermute | solution.py:596
  272.3 33.9 %collective-permute-start.31 = (bf16[1088,1088]{1,0:T(8,128)(2,1)}, bf16[1088,1088]{1,0:T(8,128)(2,1)}, u32[]{:S(2)}, u32[]{:S(2)}) collective-permute-start(bf16[1088,1088]{1,0:T(8,128)(2,1)} %add_convert_fusion.4), channel_id=1, source_target_pairs={{0,16},{1,3},{2,18},{3,1},{16,0},{17,19},{18,2},{19,17},{4,20},{5,... | collective-permute-start | bytes 7102472 | tf_op jit(solution)/shard_map/ppermute | solution.py:596
  301.1 17.3 %collective-permute-start.30 = (bf16[1088,1088]{1,0:T(8,128)(2,1)}, bf16[1088,1088]{1,0:T(8,128)(2,1)}, u32[]{:S(2)}, u32[]{:S(2)}) collective-permute-start(bf16[1088,1088]{1,0:T(8,128)(2,1)} %convolution_convert_fusion.6), channel_id=1, source_target_pairs={{0,1},{1,0},{2,3},{3,2},{16,17},{17,16},{18,19},{19,18},{4,5},{5,4... | collective-permute-start | bytes 7102472 | tf_op jit(solution)/shard_map/ppermute | solution.py:596
  318.4 39.3 %collective-permute-start.32 = (bf16[1088,1088]{1,0:T(8,128)(2,1)}, bf16[1088,1088]{1,0:T(8,128)(2,1)}, u32[]{:S(2)}, u32[]{:S(2)}) collective-permute-start(bf16[1088,1088]{1,0:T(8,128)(2,1)} %fusion.2), channel_id=1, source_target_pairs={{0,16},{1,3},{2,18},{3,1},{16,0},{17,19},{18,2},{19,17},{4,20},{5,... | collective-permute-start | bytes 7102472 | tf_op jit(solution)/shard_map/ppermute | solution.py:596
  319.0 262.6 %reduce-scatter.5.cloned.1.call-start = ((), (), s32[]{:S(2)}) async-start(), calls=%async_computation.5 | async-start | bytes 3133440 | tf_op jit(solution)/shard_map/reduce_scatter | solution.py:622
  362.7 29.8 %collective-permute-start.33 = (bf16[272,1088]{1,0:T(8,128)(2,1)}, bf16[272,1088]{1,0:T(8,128)(2,1)}, u32[]{:S(2)}, u32[]{:S(2)}) collective-permute-start(bf16[272,1088]{1,0:T(8,128)(2,1)} %get-tuple-element.287), channel_id=1, source_target_pairs={{0,4},{4,8},{8,12},{12,0},{1,5},{5,9},{9,13},{13,1},{2,6},{6,10},{... | collective-permute-start | bytes 1775624 | tf_op jit(solution)/shard_map/ppermute | solution.py:634
  392.5 27.5 %collective-permute-start.34 = (bf16[272,1088]{1,0:T(8,128)(2,1)}, bf16[272,1088]{1,0:T(8,128)(2,1)}, u32[]{:S(2)}, u32[]{:S(2)}) collective-permute-start(bf16[272,1088]{1,0:T(8,128)(2,1)} %reduce-scatter.3.cloned.1.call-done), channel_id=1, source_target_pairs={{0,2},{1,17},{2,0},{3,19},{16,18},{17,1},{18,16},{19,3},{4,6},{5,2... | collective-permute-start | bytes 1775624 | tf_op jit(solution)/shard_map/ppermute | solution.py:596
  393.9 41.0 %collective-permute-start.35 = (bf16[272,1088]{1,0:T(8,128)(2,1)}, bf16[272,1088]{1,0:T(8,128)(2,1)}, u32[]{:S(2)}, u32[]{:S(2)}) collective-permute-start(bf16[272,1088]{1,0:T(8,128)(2,1)} %get-tuple-element.296), channel_id=1, source_target_pairs={{0,8},{4,12},{8,0},{12,4},{1,9},{5,13},{9,1},{13,5},{2,10},{6,14},... | collective-permute-start | bytes 1775624 | tf_op jit(solution)/shard_map/ppermute | solution.py:634
  396.2 39.7 %collective-permute-start.36 = (bf16[272,1088]{1,0:T(8,128)(2,1)}, bf16[272,1088]{1,0:T(8,128)(2,1)}, u32[]{:S(2)}, u32[]{:S(2)}) collective-permute-start(bf16[272,1088]{1,0:T(8,128)(2,1)} %get-tuple-element.297), channel_id=1, source_target_pairs={{0,12},{4,0},{8,4},{12,8},{1,13},{5,1},{9,5},{13,9},{2,14},{6,2},{... | collective-permute-start | bytes 1775624 | tf_op jit(solution)/shard_map/ppermute | solution.py:634
  460.6 46.5 %collective-permute-start.39 = (bf16[1088,1088]{1,0:T(8,128)(2,1)}, bf16[1088,1088]{1,0:T(8,128)(2,1)}, u32[]{:S(2)}, u32[]{:S(2)}) collective-permute-start(bf16[1088,1088]{1,0:T(8,128)(2,1)} %add_convert_fusion.1), channel_id=1, source_target_pairs={{0,16},{1,3},{2,18},{3,1},{16,0},{17,19},{18,2},{19,17},{4,20},{5,... | collective-permute-start | bytes 7102472 | tf_op jit(solution)/shard_map/ppermute | solution.py:596
  463.1 17.2 %collective-permute-start.40 = (bf16[272,1088]{1,0:T(8,128)(2,1)S(1)}, bf16[272,1088]{1,0:T(8,128)(2,1)}, u32[]{:S(2)}, u32[]{:S(2)}) collective-permute-start(bf16[272,1088]{1,0:T(8,128)(2,1)S(1)} %add_convert_fusion.7), channel_id=1, source_target_pairs={{0,2},{1,17},{2,0},{3,19},{16,18},{17,1},{18,16},{19,3},{4,6},{5,2... | collective-permute-start | bytes 1775624 | tf_op jit(solution)/shard_map/ppermute | solution.py:596
  465.3 49.0 %collective-permute-start.41 = (bf16[272,1088]{1,0:T(8,128)(2,1)S(1)}, bf16[272,1088]{1,0:T(8,128)(2,1)S(1)}, u32[]{:S(2)}, u32[]{:S(2)}) collective-permute-start(bf16[272,1088]{1,0:T(8,128)(2,1)S(1)} %add_convert_fusion.8.refs_0_), channel_id=1, source_target_pairs={{0,16},{1,3},{2,18},{3,1},{16,0},{17,19},{18,2},{19,17},{4,20},{5,... | collective-permute-start | bytes 1775624 | tf_op jit(solution)/shard_map/ppermute | solution.py:596
  517.3 37.7 %collective-permute-start.52 = (bf16[272,1088]{1,0:T(8,128)(2,1)S(1)}, bf16[272,1088]{1,0:T(8,128)(2,1)S(1)}, u32[]{:S(2)}, u32[]{:S(2)}) collective-permute-start(bf16[272,1088]{1,0:T(8,128)(2,1)S(1)} %add_convert_fusion.6.refs_0_), channel_id=1, source_target_pairs={{0,1},{1,0},{2,3},{3,2},{16,17},{17,16},{18,19},{19,18},{4,5},{5,4... | collective-permute-start | bytes 1775624 | tf_op jit(solution)/shard_map/ppermute | solution.py:596
  517.3 37.7 %collective-permute-start.50 = (bf16[272,1088]{1,0:T(8,128)(2,1)}, bf16[272,1088]{1,0:T(8,128)(2,1)}, u32[]{:S(2)}, u32[]{:S(2)}) collective-permute-start(bf16[272,1088]{1,0:T(8,128)(2,1)} %copy-done.10), channel_id=1, source_target_pairs={{0,1},{1,0},{2,3},{3,2},{16,17},{17,16},{18,19},{19,18},{4,5},{5,4... | collective-permute-start | bytes 1775624 | tf_op jit(solution)/shard_map/ppermute | solution.py:596
  525.7 29.3 %collective-permute-start.53 = (bf16[272,1088]{1,0:T(8,128)(2,1)S(1)}, bf16[272,1088]{1,0:T(8,128)(2,1)}, u32[]{:S(2)}, u32[]{:S(2)}) collective-permute-start(bf16[272,1088]{1,0:T(8,128)(2,1)S(1)} %collective-permute-done.51.refs_1_), channel_id=1, source_target_pairs={{0,1},{1,0},{2,3},{3,2},{16,17},{17,16},{18,19},{19,18},{4,5},{5,4... | collective-permute-start | bytes 1775624 | tf_op jit(solution)/shard_map/ppermute | solution.py:596
  527.3 27.6 %collective-permute-start.47 = (bf16[1088,256]{1,0:T(8,128)(2,1)}, bf16[1088,256]{1,0:T(8,128)(2,1)}, u32[]{:S(2)}, u32[]{:S(2)}) collective-permute-start(bf16[1088,256]{1,0:T(8,128)(2,1)} %get-tuple-element.336), channel_id=1, source_target_pairs={{0,2},{1,3},{2,0},{3,1},{4,6},{5,7},{6,4},{7,5},{8,10},{9,11},{10,... | collective-permute-start | bytes 1671176 | tf_op jit(solution)/shard_map/ppermute | solution.py:602
  528.7 26.2 %collective-permute-start.48 = (bf16[1088,256]{1,0:T(8,128)(2,1)}, bf16[1088,256]{1,0:T(8,128)(2,1)}, u32[]{:S(2)}, u32[]{:S(2)}) collective-permute-start(bf16[1088,256]{1,0:T(8,128)(2,1)} %get-tuple-element.337), channel_id=1, source_target_pairs={{0,3},{1,2},{2,1},{3,0},{4,7},{5,6},{6,5},{7,4},{8,11},{9,10},{10,... | collective-permute-start | bytes 1671176 | tf_op jit(solution)/shard_map/ppermute | solution.py:602
  555.0 13.3 %collective-permute-start.54 = (bf16[1088,256]{1,0:T(8,128)(2,1)}, bf16[1088,256]{1,0:T(8,128)(2,1)}, u32[]{:S(2)}, u32[]{:S(2)}) collective-permute-start(bf16[1088,256]{1,0:T(8,128)(2,1)} %get-tuple-element.341), channel_id=1, source_target_pairs={{0,1},{1,0},{2,3},{3,2},{4,5},{5,4},{6,7},{7,6},{8,9},{9,8},{10,11... | collective-permute-start | bytes 1671176 | tf_op jit(solution)/shard_map/ppermute | solution.py:602
  555.3 15.8 %collective-permute-start.55 = (bf16[1088,256]{1,0:T(8,128)(2,1)}, bf16[1088,256]{1,0:T(8,128)(2,1)}, u32[]{:S(2)}, u32[]{:S(2)}) collective-permute-start(bf16[1088,256]{1,0:T(8,128)(2,1)} %get-tuple-element.342), channel_id=1, source_target_pairs={{0,2},{1,3},{2,0},{3,1},{4,6},{5,7},{6,4},{7,5},{8,10},{9,11},{10,... | collective-permute-start | bytes 1671176 | tf_op jit(solution)/shard_map/ppermute | solution.py:602
  556.8 24.9 %collective-permute-start.56 = (bf16[1088,256]{1,0:T(8,128)(2,1)}, bf16[1088,256]{1,0:T(8,128)(2,1)}, u32[]{:S(2)}, u32[]{:S(2)}) collective-permute-start(bf16[1088,256]{1,0:T(8,128)(2,1)} %get-tuple-element.343), channel_id=1, source_target_pairs={{0,3},{1,2},{2,1},{3,0},{4,7},{5,6},{6,5},{7,4},{8,11},{9,10},{10,... | collective-permute-start | bytes 1671176 | tf_op jit(solution)/shard_map/ppermute | solution.py:602
  593.7 18.8 %collective-permute-start.59 = (bf16[272,1088]{1,0:T(8,128)(2,1)S(1)}, bf16[272,1088]{1,0:T(8,128)(2,1)S(1)}, u32[]{:S(2)}, u32[]{:S(2)}) collective-permute-start(bf16[272,1088]{1,0:T(8,128)(2,1)S(1)} %add_convert_fusion.5.refs_0_), channel_id=1, source_target_pairs={{0,16},{1,3},{2,18},{3,1},{16,0},{17,19},{18,2},{19,17},{4,20},{5,... | collective-permute-start | bytes 1775624 | tf_op jit(solution)/shard_map/ppermute | solution.py:596
  594.9 17.6 %collective-permute-start.60 = (bf16[272,1088]{1,0:T(8,128)(2,1)S(1)}, bf16[272,1088]{1,0:T(8,128)(2,1)S(1)}, u32[]{:S(2)}, u32[]{:S(2)}) collective-permute-start(bf16[272,1088]{1,0:T(8,128)(2,1)S(1)} %add_convert_fusion.5.refs_0_), channel_id=1, source_target_pairs={{0,1},{1,0},{2,3},{3,2},{16,17},{17,16},{18,19},{19,18},{4,5},{5,4... | collective-permute-start | bytes 1775624 | tf_op jit(solution)/shard_map/ppermute | solution.py:596
  595.0 17.6 %collective-permute-start.61 = (bf16[272,1088]{1,0:T(8,128)(2,1)S(1)}, bf16[272,1088]{1,0:T(8,128)(2,1)S(1)}, u32[]{:S(2)}, u32[]{:S(2)}) collective-permute-start(bf16[272,1088]{1,0:T(8,128)(2,1)S(1)} %add_convert_fusion.5.refs_0_), channel_id=1, source_target_pairs={{0,17},{1,2},{2,19},{3,0},{16,1},{17,18},{18,3},{19,16},{4,21},{5,... | collective-permute-start | bytes 1775624 | tf_op jit(solution)/shard_map/ppermute | solution.py:596
  596.0 16.5 %collective-permute-start.62 = (f32[3264]{0:T(1024)S(1)}, f32[3264]{0:T(1024)S(1)}, u32[]{:S(2)}, u32[]{:S(2)}) collective-permute-start(f32[3264]{0:T(1024)S(1)} %add.306), channel_id=1, source_target_pairs={{0,16},{1,17},{2,18},{3,19},{16,0},{17,1},{18,2},{19,3},{4,20},{5,... | collective-permute-start | bytes 39176 | tf_op jit(solution)/shard_map/ppermute | solution.py:669
  (77 other events, 782.8 us)
Sparse Core Ops, SparseCore 0:
  77.0 50.3 all-gather.2
  165.1 50.7 all-gather.4
  319.2 49.1 reduce-scatter.2
  514.5 50.0 reduce-scatter.4

commit v12 on v11

--- a/solution.py
+++ b/solution.py
@@ -1301,7 +1301,7 @@
     up_pieces, in_grads = moved[:4], moved[4:]
     down_beside = plane_swap(down_whole, "near")
     up_shard = low_sum(*up_pieces)
-    up_whole = low_sum(up_shard, plane_swap(up_shard, "other"))
+    up_other = plane_swap(up_shard, "other")
     in_terms = [turned_product(normed_low, grad) for grad in in_grads]
     section_grads = in_terms + [out_term]
     sections_mine = [chosen(kind, section_grads) for kind in classes]
@@ -1324,12 +1324,12 @@
         4,
     )
     first = low_sum(sections_mine[0], far, close)
-    first, up_whole, down_beside, query_low, *result_slots = pin(
-        (first, up_whole, down_beside, query_low, *result_slots)
-    )
+    first, up_other, down_beside, query_low, *result_slots = pin(
+        (first, up_other, down_beside, query_low, *result_slots)
+    )
+    up_whole = low_sum(up_shard, up_other)
     up_beside = plane_swap(up_whole, "near")
     down_parts = share_by_core(down_whole, down_beside)
-    up_parts = share_by_core(up_whole, up_beside)
     shard = scatter_rows(first)
     outputs = exchange(result_slots)
     *input_slots, last_sums = by_rows(
@@ -1345,9 +1345,10 @@
         [(12,) + section.shape],
         3,
     )
-    moved = pin((*input_slots, *outputs, *down_parts, *up_parts))
+    moved = pin((*input_slots, *outputs, *down_parts, up_beside))
     input_slots, outputs = exchange(moved[:4]), moved[4:8]
-    down_parts, up_parts = moved[8:12], moved[12:]
+    down_parts, up_beside = moved[8:12], moved[12]
+    up_parts = share_by_core(up_whole, up_beside)
 
     back_sums = jnp.concatenate([hidden_sums, back_sums], axis=0)
     back_sums = jnp.sum(back_sums, axis=1)

time: 633 us -> 619 us (0.978)
  waiting for transfers between devices: 155 us -> 141 us
    ppermute x36, waiting for transfers between devices: 60.5 us -> 44.8 us  [plane_swap(): lax.ppermute(values, ('dp', 'ctx'), [(device, plane_partner(device, kind)...]
    unnamed x121 -> x127, local copies, waits for them, and re-layouts: 16.7 us -> 16.8 us
  transfers between devices with their start and end apart: 67 -> 67, of which waited for: 23 -> 24; matrix products, arithmetic and copies ran while one was open for 15% -> 16% of each run, Pallas kernels for 44% -> 45%
where the time goes in v12:
time: 619 us; the launch traced here: 610 us
  Pallas kernels  275 us (44%)
  waiting for transfers between devices  141 us (23%)
  matrix products  61.7 us (10%)
  starting transfers between devices  47.4 us (8%)
  other arithmetic  37.1 us (6%)
  local copies, waits for them, and re-layouts  32 us (5%)
  between operations  15.3 us (2%)
    pallas_call x8, Pallas kernels, by_rows(): pl.pallas_call(kernel, grid=(rows // step,), in_specs=[tile] * len(tiled[...  155 us
    dot_general x12, matrix products, product(): lax.dot_general(left, right, ((dims[:1], dims[1:]), ((), ())), preferred_...  61.7 us
    pallas_call x2, Pallas kernels, attend_back(): pl.pallas_call(functools.partial(attend_back_kernel, count=count, width=w...  47.8 us
    ppermute x36, waiting for transfers between devices, plane_swap(): lax.ppermute(values, ('dp', 'ctx'), [(device, plane_partner(device, kind)...  44.8 us
    ppermute x12, waiting for transfers between devices, ctx_swap(): lax.ppermute(values, 'ctx', [(device, device ^ bits) for device in range(...  41.1 us
    pallas_call x1, Pallas kernels, attend(): pl.pallas_call(functools.partial(attend_kernel, count=count, width=width,...  32.2 us
    convert_element_type x9, other arithmetic, low_sum(): sum((term.astype(jnp.float32) for term in terms)).astype(jnp.bfloat16)  29.4 us
    ppermute x3, waiting for transfers between devices, per_device_exchanged(): lax.ppermute(section, 'fsdp', [(device, (device + step) % 4) for device i...  26.4 us
  transfers between devices with their start and end apart: 67, of which 24 were waited for; matrix products, arithmetic and copies ran while one was open for 16% of the time, Pallas kernels for 45%

profile of v12, /device:TPU:8, one launch (start us, length us, event | category | flops | bytes accessed | tf_op | source)
XLA Modules:
  0.0 609.9 jit_solution(10216062759189564827)
XLA Ops:
  7.3 3.6 fusion.11
  21.8 3.6 collective-permute-start.4
  27.2 14.1 %collective-permute-done.7.refs_2_ = bf16[1088,256]{1,0:T(8,128)(2,1)S(1)} collective-permute-done((bf16[1088,256]{1,0:T(8,128)(2,1)}, bf16[1088,256]{1,0:T(8,128)(2,1)S(1)}, u32[]{:S(2)}, u32[]{:S(2)}) %collective-permute-start.7) | collective-permute-done | bytes 557088 | tf_op jit(solution)/shard_map/ppermute | solution.py:602
  41.3 9.1 %collective-permute-done.8.refs_3_ = bf16[1088,256]{1,0:T(8,128)(2,1)S(1)} collective-permute-done((bf16[1088,256]{1,0:T(8,128)(2,1)}, bf16[1088,256]{1,0:T(8,128)(2,1)S(1)}, u32[]{:S(2)}, u32[]{:S(2)}) %collective-permute-start.8) | collective-permute-done | bytes 557088 | tf_op jit(solution)/shard_map/ppermute | solution.py:602
  50.4 22.8 %collective-permute-done.4.refs_9_ = bf16[272,1088]{1,0:T(8,128)(2,1)S(1)} collective-permute-done((bf16[272,1088]{1,0:T(8,128)(2,1)}, bf16[272,1088]{1,0:T(8,128)(2,1)S(1)}, u32[]{:S(2)}, u32[]{:S(2)}) %collective-permute-start.4) | collective-permute-done | bytes 591904 | tf_op jit(solution)/shard_map/ppermute | solution.py:1099
  73.2 3.6 collective-permute-done.5.refs_10_
  81.0 6.5 %collective-permute-done.9.refs_11_ = bf16[272,1088]{1,0:T(8,128)(2,1)} collective-permute-done((bf16[272,1088]{1,0:T(8,128)(2,1)}, bf16[272,1088]{1,0:T(8,128)(2,1)}, u32[]{:S(2)}, u32[]{:S(2)}) %collective-permute-start.9) | collective-permute-done | bytes 591904 | tf_op jit(solution)/shard_map/ppermute | solution.py:596
  87.5 6.7 %collective-permute-done.10.refs_12_ = bf16[272,1088]{1,0:T(8,128)(2,1)} collective-permute-done((bf16[272,1088]{1,0:T(8,128)(2,1)S(1)}, bf16[272,1088]{1,0:T(8,128)(2,1)}, u32[]{:S(2)}, u32[]{:S(2)}) %collective-permute-start.10) | collective-permute-done | bytes 591904 | tf_op jit(solution)/shard_map/ppermute | solution.py:596
  94.3 6.7 %collective-permute-done.11.refs_13_ = bf16[272,1088]{1,0:T(8,128)(2,1)} collective-permute-done((bf16[272,1088]{1,0:T(8,128)(2,1)}, bf16[272,1088]{1,0:T(8,128)(2,1)}, u32[]{:S(2)}, u32[]{:S(2)}) %collective-permute-start.11) | collective-permute-done | bytes 591904 | tf_op jit(solution)/shard_map/ppermute | solution.py:596
  105.2 21.8 %front.1 = (bf16[1024,1088]{1,0:T(8,128)(2,1)}, bf16[1024,1088]{1,0:T(8,128)(2,1)}, bf16[1024,1088]{1,0:T(8,128)(2,1)}, bf16[1024,1088]{1,0:T(8,128)(2,1)}, bf16...) custom-call(s32[16]{0:T(128)} %stack.120.places_ref, f32[4,1088]{1,0:T(4,128)} %pad_maximum_fusion.1.vectors_ref, ...), custom_call_target="tpu_custom_call" | custom-call | flops 1024 | bytes 1024 | tf_op jit(solution)/shard_map/front/pallas_call | solution.py:748
  131.3 32.2 %attend.1 = (bf16[1024,1088]{1,0:T(8,128)(2,1)S(1)}, f32[1024,128]{1,0:T(8,128)S(1)}) custom-call(s32[1]{0:T(128)} %bitcast.24.place_ref, bf16[1024,1088]{1,0:T(8,128)(2,1)S(1)} %copy-done.3, bf16[1024,1088]{1,0:T(8,128)(2,1)} %get-tuple-element.223.k_ref, bf16[1024,1088]{1,0:T(8,128)(2,1)} %get-tuple-element.224.v_ref), custom_call_target="tpu_custom_call" | custom-call | flops 1024 | bytes 1024 | tf_op jit(solution)/shard_map/attend/pallas_call | solution.py:507
  171.3 10.1 %middle.1 = (f32[1024,1088]{1,0:T(8,128)}, bf16[1024,1088]{1,0:T(8,128)(2,1)}) custom-call(bf16[1024,1088]{1,0:T(8,128)(2,1)} %get-tuple-element.217.x_ref, bf16[1024,1088]{1,0:T(8,128)(2,1)} %copy-done.4, f32[3,1088]{1,0:T(4,128)} %pad_maximum_fusion.2.vectors_ref, bf16[16,272,1088]{2,1,0:T(8,128)(2,1)} %get-tuple-element.227.all_ref.refs_8_), custom_call_target="tpu_custom_call" | custom-call | flops 1024 | bytes 1024 | tf_op jit(solution)/shard_map/middle/pallas_call | solution.py:1021
  181.4 17.4 %up.2 = (bf16[1024,1088]{1,0:T(8,128)(2,1)}, bf16[1024,1088]{1,0:T(8,128)(2,1)}, bf16[1024,1088]{1,0:T(8,128)(2,1)}, bf16[1024,1088]{1,0:T(8,128)(2,1)}) custom-call(bf16[1024,1088]{1,0:T(8,128)(2,1)} %get-tuple-element.265.h_ref, f32[2,1088]{1,0:T(2,128)} %pad_maximum_fusion.3.biases_ref, bf16[1088,1088]{1,0:T(8,128)(2,1)} %all-gather.3.cloned.1.call-done.refs_0_.refs_4_, ...), custom_call_target="tpu_custom_call" | custom-call | flops 1024 | bytes 1024 | tf_op jit(solution)/shard_map/up/pallas_call | solution.py:1021
  198.8 18.0 %up.3 = (bf16[1024,1088]{1,0:T(8,128)(2,1)}, bf16[1024,1088]{1,0:T(8,128)(2,1)}, bf16[1024,1088]{1,0:T(8,128)(2,1)}, bf16[1024,1088]{1,0:T(8,128)(2,1)}) custom-call(bf16[1024,1088]{1,0:T(8,128)(2,1)} %get-tuple-element.265.h_ref, f32[2,1088]{1,0:T(2,128)} %pad_maximum_fusion.4.biases_ref, bf16[1088,1088]{1,0:T(8,128)(2,1)} %collective-permute-done.19.refs_0_.refs_5_, ...), custom_call_target="tpu_custom_call" | custom-call | flops 1024 | bytes 1024 | tf_op jit(solution)/shard_map/up/pallas_call | solution.py:1021
  224.1 6.2 %convolution_convert_fusion.11 = bf16[1088,1088]{1,0:T(8,128)(2,1)} fusion(bf16[1024,1088]{1,0:T(8,128)(2,1)} %get-tuple-element.241.refs_3_, bf16[1024,1088]{1,0:T(8,128)(2,1)S(1)} %turn.1.g_ref), kind=kOutput, calls=%fused_computation.13 | convolution fusion | flops 2425491456 | bytes 6823936 | tf_op jit(solution)/shard_map/dot_general | solution.py:675
  230.3 4.6 convolution_convert_fusion.10
  235.2 4.6 convolution_convert_fusion.9
  239.8 4.8 convolution_convert_fusion.8
  244.6 8.6 %collective-permute-done.25.refs_2_.refs_5_ = bf16[1088,1088]{1,0:T(8,128)(2,1)} collective-permute-done((bf16[1088,1088]{1,0:T(8,128)(2,1)}, bf16[1088,1088]{1,0:T(8,128)(2,1)}, u32[]{:S(2)}, u32[]{:S(2)}) %collective-permute-start.25) | collective-permute-done | bytes 2367520 | tf_op jit(solution)/shard_map/ppermute | solution.py:596
  253.7 14.0 %hidden.2 = (bf16[1024,1088]{1,0:T(8,128)(2,1)}, bf16[1024,1088]{1,0:T(8,128)(2,1)}, f32[3,8,1088]{2,1,0:T(8,128)}) custom-call(bf16[1024,1088]{1,0:T(8,128)(2,1)} %copy-done.2, bf16[1024,1088]{1,0:T(8,128)(2,1)} %get-tuple-element.251.refs_0_, bf16[1024,1088]{1,0:T(8,128)(2,1)} %get-tuple-element.252.refs_1_, ...), custom_call_target="tpu_custom_call" | custom-call | flops 1024 | bytes 1024 | tf_op jit(solution)/shard_map/hidden/pallas_call | solution.py:1021
  267.7 4.6 add_convert_fusion.4
  275.2 14.2 %hidden.3 = (bf16[1024,1088]{1,0:T(8,128)(2,1)}, bf16[1024,1088]{1,0:T(8,128)(2,1)}, f32[3,8,1088]{2,1,0:T(8,128)}) custom-call(bf16[1024,1088]{1,0:T(8,128)(2,1)} %copy-done.2, bf16[1024,1088]{1,0:T(8,128)(2,1)} %get-tuple-element.257.refs_0_, bf16[1024,1088]{1,0:T(8,128)(2,1)} %get-tuple-element.258.refs_1_, ...), custom_call_target="tpu_custom_call" | custom-call | flops 1024 | bytes 1024 | tf_op jit(solution)/shard_map/hidden/pallas_call | solution.py:1021
  289.5 7.1 %convolution_convert_fusion.7 = bf16[1088,1088]{1,0:T(8,128)(2,1)} fusion(bf16[1024,1088]{1,0:T(8,128)(2,1)} %get-tuple-element.265.h_ref, bf16[1024,1088]{1,0:T(8,128)(2,1)} %get-tuple-element.278.refs_3_), kind=kOutput, calls=%fused_computation.9 | convolution fusion | flops 2425491456 | bytes 6823936 | tf_op jit(solution)/shard_map/dot_general | solution.py:675
  296.5 4.6 convolution_convert_fusion.6
  301.6 4.6 convolution_convert_fusion.4
  306.2 4.9 add_convert_fusion.3
  311.1 7.4 %fusion.2 = bf16[1088,1088]{1,0:T(8,128)(2,1)} fusion(bf16[1024,1088]{1,0:T(8,128)(2,1)S(1)} %copy-done.29, bf16[1024,1088]{1,0:T(8,128)(2,1)} %get-tuple-element.276.refs_1_, bf16[1088,1088]{1,0:T(8,128)(2,1)} %collective-permute-done.29), kind=kOutput, calls=%fused_computation.14 | convolution fusion | flops 2430226432 | bytes 9191424 | tf_op jit(solution)/shard_map/dot_general | solution.py:675
  319.2 32.2 %back.1 = (f32[1024,1088]{1,0:T(8,128)}, bf16[1024,1088]{1,0:T(8,128)(2,1)}, bf16[1024,1088]{1,0:T(8,128)(2,1)}, f32[3,8,1088]{2,1,0:T(8,128)}) custom-call(bf16[1024,1088]{1,0:T(8,128)(2,1)} %copy-done.2, f32[1024,1088]{1,0:T(8,128)} %get-tuple-element.313.middle_ref, f32[1,1088]{1,0:T(1,128)} %copy-done.50, bf16[1024,1088]{1,0:T(8,128)(2,1)} %get-tuple-element.275.refs_0_, ...), custom_call_target="tpu_custom_call" | custom-call | flops 1024 | bytes 1024 | tf_op jit(solution)/shard_map/back/pallas_call | solution.py:1021
  351.4 6.4 %convolution_convert_fusion.3 = bf16[1088,1088]{1,0:T(8,128)(2,1)} fusion(bf16[1024,1088]{1,0:T(8,128)(2,1)S(1)} %copy-done.5, bf16[1024,1088]{1,0:T(8,128)(2,1)} %get-tuple-element.280), kind=kOutput, calls=%fused_computation.3 | convolution fusion | flops 2425491456 | bytes 6823936 | tf_op jit(solution)/shard_map/dot_general | solution.py:675
  357.8 3.4 add_convert_fusion.2
  364.9 26.1 %attend_back.2 = (bf16[1024,1088]{1,0:T(8,128)(2,1)S(1)}, bf16[1024,1088]{1,0:T(8,128)(2,1)S(1)}, bf16[1024,1088]{1,0:T(8,128)(2,1)}) custom-call(s32[1]{0:T(128)} %bitcast.24.place_ref, bf16[1024,1088]{1,0:T(8,128)(2,1)} %get-tuple-element.222.q_ref, bf16[1024,1088]{1,0:T(8,128)(2,1)} %get-tuple-element.223.k_ref, ...), custom_call_target="tpu_custom_call" | custom-call | flops 1024 | bytes 1024 | tf_op jit(solution)/shard_map/attend_back/pallas_call | solution.py:537
  398.4 21.6 %attend_back.3 = (bf16[1024,1088]{1,0:T(8,128)(2,1)S(1)}, bf16[1024,1088]{1,0:T(8,128)(2,1)S(1)}, bf16[1024,1088]{1,0:T(8,128)(2,1)}) custom-call(s32[1]{0:T(128)} %bitcast.24.place_ref, bf16[1024,1088]{1,0:T(8,128)(2,1)} %get-tuple-element.222.q_ref, ...), custom_call_target="tpu_custom_call", output_to_operand_aliasing={{0}: (7, {}), {1}: (8, {}), {2}: (9, {})} | custom-call | flops 1024 | bytes 1024 | tf_op jit(solution)/shard_map/attend_back/pallas_call | solution.py:537
  421.7 13.2 %collective-permute-done.35 = bf16[272,1088]{1,0:T(8,128)(2,1)} collective-permute-done((bf16[272,1088]{1,0:T(8,128)(2,1)}, bf16[272,1088]{1,0:T(8,128)(2,1)}, u32[]{:S(2)}, u32[]{:S(2)}) %collective-permute-start.35) | collective-permute-done | bytes 591904 | tf_op jit(solution)/shard_map/ppermute | solution.py:634
  435.9 3.1 convolution_convert_fusion.1
  442.3 5.3 select_select_fusion
  448.1 7.8 %collective-permute-done.37 = bf16[1088,1088]{1,0:T(8,128)(2,1)S(1)} collective-permute-done((bf16[1088,1088]{1,0:T(8,128)(2,1)S(1)}, bf16[1088,1088]{1,0:T(8,128)(2,1)S(1)}, u32[]{:S(2)}, u32[]{:S(2)}) %collective-permute-start.37) | collective-permute-done | bytes 2367520 | tf_op jit(solution)/shard_map/ppermute | solution.py:596
  455.9 3.2 add_convert_fusion.1
  466.1 25.4 %down.1 = (bf16[1088,256]{1,0:T(8,128)(2,1)}, bf16[1088,256]{1,0:T(8,128)(2,1)}, bf16[1088,256]{1,0:T(8,128)(2,1)}, bf16[1088,256]{1,0:T(8,128)(2,1)}) custom-call(f32[1024,1088]{1,0:T(8,128)} %get-tuple-element.313.middle_ref, f32[1,1088]{1,0:T(1,128)} %reshape.450.vectors_ref, bf16[1024,1088]{1,0:T(8,128)(2,1)} %get-tuple-element.246.refs_0_, ...), custom_call_target="tpu_custom_call" | custom-call | flops 1024 | bytes 1024 | tf_op jit(solution)/shard_map/down/pallas_call | solution.py:1021
  491.5 6.5 %collective-permute-done.39 = bf16[1088,1088]{1,0:T(8,128)(2,1)} collective-permute-done((bf16[1088,1088]{1,0:T(8,128)(2,1)}, bf16[1088,1088]{1,0:T(8,128)(2,1)}, u32[]{:S(2)}, u32[]{:S(2)}) %collective-permute-start.39) | collective-permute-done | bytes 2367520 | tf_op jit(solution)/shard_map/ppermute | solution.py:596
  498.1 7.3 %add_convert_fusion = bf16[1088,1088]{1,0:T(8,128)(2,1)} fusion(bf16[1088,1088]{1,0:T(8,128)(2,1)} %collective-permute-done.39, bf16[1088,1088]{1,0:T(8,128)(2,1)} %copy-done.33, bf16[1088,1088]{1,0:T(8,128)(2,1)} %copy-done.28, bf16[1088,1088]{1,0:T(8,128)(2,1)} %copy-done.26, bf16[1088,1088]{1,0:T(8,128)(2,1)} %copy-done.27, ...), kind=kLoop, calls=%fused_computation.15 | loop fusion | flops 10653696 | bytes 16572419 | tf_op jit(solution)/shard_map/convert_element_type | solution.py:606
  513.0 23.8 %last.1 = (bf16[1088,256]{1,0:T(8,128)(2,1)}, bf16[1088,256]{1,0:T(8,128)(2,1)}, bf16[1088,256]{1,0:T(8,128)(2,1)}, bf16[1088,256]{1,0:T(8,128)(2,1)}, f32[4,8,1088]{2,1,0:T(8,128)}) custom-call(bf16[1024,1088]{1,0:T(8,128)(2,1)} %copy-done.6, bf16[1024,1088]{1,0:T(8,128)(2,1)} %copy-done.9, bf16[1024,1088]{1,0:T(8,128)(2,1)} %get-tuple-element.324.v_ref, ...), custom_call_target="tpu_custom_call" | custom-call | flops 1024 | bytes 1024 | tf_op jit(solution)/shard_map/last/pallas_call | solution.py:1021
  537.8 3.9 collective-permute-done.48.refs_3_
  557.6 11.0 %collective-permute-done.54.refs_3_ = bf16[1088,256]{1,0:T(8,128)(2,1)} collective-permute-done((bf16[1088,256]{1,0:T(8,128)(2,1)}, bf16[1088,256]{1,0:T(8,128)(2,1)}, u32[]{:S(2)}, u32[]{:S(2)}) %collective-permute-start.54) | collective-permute-done | bytes 557088 | tf_op jit(solution)/shard_map/ppermute | solution.py:602
  571.1 8.1 %collective-permute-done.56 = f32[3264]{0:T(1024)S(1)} collective-permute-done((f32[3264]{0:T(1024)S(1)}, f32[3264]{0:T(1024)S(1)}, u32[]{:S(2)}, u32[]{:S(2)}) %collective-permute-start.56) | collective-permute-done | bytes 13088 | tf_op jit(solution)/shard_map/ppermute | solution.py:669
  586.9 3.7 settle.5
  590.6 4.1 assemble.2
  594.6 3.8 settle.4
  599.7 3.4 assemble.3
  (328 shorter events, 104.9 us)
Async XLA Ops:
  7.2 120.1 %all-gather.3.cloned.1.call-start = ((), (), s32[]{:S(2)}) async-start(), calls=%async_computation.2 | async-start | bytes 3133440 | tf_op jit(solution)/shard_map/all_gather | solution.py:1145
  13.9 13.0 %collective-permute-start.6 = (bf16[1088,256]{1,0:T(8,128)(2,1)}, bf16[1088,256]{1,0:T(8,128)(2,1)}, u32[]{:S(2)}, u32[]{:S(2)}) collective-permute-start(bf16[1088,256]{1,0:T(8,128)(2,1)} %get-tuple-element.400), channel_id=1, source_target_pairs={{0,1},{1,0},{2,3},{3,2},{4,5},{5,4},{6,7},{7,6},{8,9},{9,8},{10,11... | collective-permute-start | bytes 1671176 | tf_op jit(solution)/shard_map/ppermute | solution.py:602
  18.8 31.6 %collective-permute-start.3 = (bf16[272,1088]{1,0:T(8,128)(2,1)}, bf16[272,1088]{1,0:T(8,128)(2,1)}, u32[]{:S(2)}, u32[]{:S(2)}) collective-permute-start(bf16[272,1088]{1,0:T(8,128)(2,1)} %get-tuple-element.203), channel_id=1, source_target_pairs={{0,4},{4,8},{8,12},{12,0},{1,5},{5,9},{9,13},{13,1},{2,6},{6,10},{... | collective-permute-start | bytes 1775624 | tf_op jit(solution)/shard_map/ppermute | solution.py:1099
  21.8 51.4 %collective-permute-start.4 = (bf16[272,1088]{1,0:T(8,128)(2,1)}, bf16[272,1088]{1,0:T(8,128)(2,1)S(1)}, u32[]{:S(2)}, u32[]{:S(2)}) collective-permute-start(bf16[272,1088]{1,0:T(8,128)(2,1)} %get-tuple-element.203), channel_id=1, source_target_pairs={{0,8},{4,12},{8,0},{12,4},{1,9},{5,13},{9,1},{13,5},{2,10},{6,14},... | collective-permute-start | bytes 1775624 | tf_op jit(solution)/shard_map/ppermute | solution.py:1099
  25.4 51.4 %collective-permute-start.5 = (bf16[272,1088]{1,0:T(8,128)(2,1)}, bf16[272,1088]{1,0:T(8,128)(2,1)}, u32[]{:S(2)}, u32[]{:S(2)}) collective-permute-start(bf16[272,1088]{1,0:T(8,128)(2,1)} %get-tuple-element.203), channel_id=1, source_target_pairs={{0,12},{4,0},{8,4},{12,8},{1,13},{5,1},{9,5},{13,9},{2,14},{6,2},{... | collective-permute-start | bytes 1775624 | tf_op jit(solution)/shard_map/ppermute | solution.py:1099
  25.4 15.8 %collective-permute-start.7 = (bf16[1088,256]{1,0:T(8,128)(2,1)}, bf16[1088,256]{1,0:T(8,128)(2,1)S(1)}, u32[]{:S(2)}, u32[]{:S(2)}) collective-permute-start(bf16[1088,256]{1,0:T(8,128)(2,1)} %get-tuple-element.399), channel_id=1, source_target_pairs={{0,2},{1,3},{2,0},{3,1},{4,6},{5,7},{6,4},{7,5},{8,10},{9,11},{10,... | collective-permute-start | bytes 1671176 | tf_op jit(solution)/shard_map/ppermute | solution.py:602
  27.0 23.4 %collective-permute-start.8 = (bf16[1088,256]{1,0:T(8,128)(2,1)}, bf16[1088,256]{1,0:T(8,128)(2,1)S(1)}, u32[]{:S(2)}, u32[]{:S(2)}) collective-permute-start(bf16[1088,256]{1,0:T(8,128)(2,1)} %get-tuple-element.204), channel_id=1, source_target_pairs={{0,3},{1,2},{2,1},{3,0},{4,7},{5,6},{6,5},{7,4},{8,11},{9,10},{10,... | collective-permute-start | bytes 1671176 | tf_op jit(solution)/shard_map/ppermute | solution.py:602
  76.8 145.5 %all-gather.5.cloned.1.call-start = ((), (), s32[]{:S(2)}) async-start(), calls=%async_computation.3 | async-start | bytes 3133440 | tf_op jit(solution)/shard_map/all_gather | solution.py:1169
  78.5 15.8 %collective-permute-start.10 = (bf16[272,1088]{1,0:T(8,128)(2,1)S(1)}, bf16[272,1088]{1,0:T(8,128)(2,1)}, u32[]{:S(2)}, u32[]{:S(2)}) collective-permute-start(bf16[272,1088]{1,0:T(8,128)(2,1)S(1)} %collective-permute-done.4.refs_9_), channel_id=1, source_target_pairs={{0,16},{1,3},{2,18},{3,1},{16,0},{17,19},{18,2},{19,17},{4,20},{5,... | collective-permute-start | bytes 1775624 | tf_op jit(solution)/shard_map/ppermute | solution.py:596
  79.0 22.0 %collective-permute-start.11 = (bf16[272,1088]{1,0:T(8,128)(2,1)}, bf16[272,1088]{1,0:T(8,128)(2,1)}, u32[]{:S(2)}, u32[]{:S(2)}) collective-permute-start(bf16[272,1088]{1,0:T(8,128)(2,1)} %collective-permute-done.5.refs_10_), channel_id=1, source_target_pairs={{0,16},{1,3},{2,18},{3,1},{16,0},{17,19},{18,2},{19,17},{4,20},{5,... | collective-permute-start | bytes 1775624 | tf_op jit(solution)/shard_map/ppermute | solution.py:596
  80.5 21.0 %collective-permute-start.12 = (bf16[272,1088]{1,0:T(8,128)(2,1)}, bf16[272,1088]{1,0:T(8,128)(2,1)}, u32[]{:S(2)}, u32[]{:S(2)}) collective-permute-start(bf16[272,1088]{1,0:T(8,128)(2,1)} %collective-permute-done.3.refs_8_), channel_id=1, source_target_pairs={{0,1},{1,0},{2,3},{3,2},{16,17},{17,16},{18,19},{19,18},{4,5},{5,4... | collective-permute-start | bytes 1775624 | tf_op jit(solution)/shard_map/ppermute | solution.py:596
  80.5 22.8 %collective-permute-start.13 = (bf16[272,1088]{1,0:T(8,128)(2,1)S(1)}, bf16[272,1088]{1,0:T(8,128)(2,1)}, u32[]{:S(2)}, u32[]{:S(2)}) collective-permute-start(bf16[272,1088]{1,0:T(8,128)(2,1)S(1)} %collective-permute-done.4.refs_9_), channel_id=1, source_target_pairs={{0,1},{1,0},{2,3},{3,2},{16,17},{17,16},{18,19},{19,18},{4,5},{5,4... | collective-permute-start | bytes 1775624 | tf_op jit(solution)/shard_map/ppermute | solution.py:596
  87.5 15.7 %collective-permute-start.14 = (bf16[272,1088]{1,0:T(8,128)(2,1)}, bf16[272,1088]{1,0:T(8,128)(2,1)}, u32[]{:S(2)}, u32[]{:S(2)}) collective-permute-start(bf16[272,1088]{1,0:T(8,128)(2,1)} %collective-permute-done.5.refs_10_), channel_id=1, source_target_pairs={{0,1},{1,0},{2,3},{3,2},{16,17},{17,16},{18,19},{19,18},{4,5},{5,4... | collective-permute-start | bytes 1775624 | tf_op jit(solution)/shard_map/ppermute | solution.py:596
  127.3 37.7 %collective-permute-start.18 = (bf16[1088,1088]{1,0:T(8,128)(2,1)}, bf16[1088,1088]{1,0:T(8,128)(2,1)}, u32[]{:S(2)}, u32[]{:S(2)}) collective-permute-start(bf16[1088,1088]{1,0:T(8,128)(2,1)} %all-gather.3.cloned.1.call-done.refs_0_.refs_4_), channel_id=1, source_target_pairs={{0,1},{1,0},{2,3},{3,2},{16,17},{17,16},{18,19},{19,18},{4,5},{5,4... | collective-permute-start | bytes 7102472 | tf_op jit(solution)/shard_map/ppermute | solution.py:596
  127.3 37.7 %collective-permute-start.19 = (bf16[1088,1088]{1,0:T(8,128)(2,1)}, bf16[1088,1088]{1,0:T(8,128)(2,1)}, u32[]{:S(2)}, u32[]{:S(2)}) collective-permute-start(bf16[1088,1088]{1,0:T(8,128)(2,1)} %all-gather.3.cloned.1.call-done.refs_0_.refs_4_), channel_id=1, source_target_pairs={{0,16},{1,3},{2,18},{3,1},{16,0},{17,19},{18,2},{19,17},{4,20},{5,... | collective-permute-start | bytes 7102472 | tf_op jit(solution)/shard_map/ppermute | solution.py:596
  165.0 227.5 %reduce-scatter.3.cloned.1.call-start = ((), (), s32[]{:S(2)}) async-start(), calls=%async_computation.4 | async-start | bytes 3133440 | tf_op jit(solution)/shard_map/reduce_scatter | solution.py:622
  165.3 33.5 %collective-permute-start.22 = (bf16[1088,1088]{1,0:T(8,128)(2,1)}, bf16[1088,1088]{1,0:T(8,128)(2,1)}, u32[]{:S(2)}, u32[]{:S(2)}) collective-permute-start(bf16[1088,1088]{1,0:T(8,128)(2,1)} %collective-permute-done.19.refs_0_.refs_5_), channel_id=1, source_target_pairs={{0,1},{1,0},{2,3},{3,2},{16,17},{17,16},{18,19},{19,18},{4,5},{5,4... | collective-permute-start | bytes 7102472 | tf_op jit(solution)/shard_map/ppermute | solution.py:596
  167.1 49.7 %collective-permute-start.20 = (bf16[1088,256]{1,0:T(8,128)(2,1)}, bf16[1088,256]{1,0:T(8,128)(2,1)S(1)}, u32[]{:S(2)}, u32[]{:S(2)}) collective-permute-start(bf16[1088,256]{1,0:T(8,128)(2,1)} %get-tuple-element.397), channel_id=1, source_target_pairs={{0,1},{1,0},{2,3},{3,2},{4,5},{5,4},{6,7},{7,6},{8,9},{9,8},{10,11... | collective-permute-start | bytes 1671176 | tf_op jit(solution)/shard_map/ppermute | solution.py:602
  167.4 50.2 %collective-permute-start.21 = (bf16[1088,256]{1,0:T(8,128)(2,1)}, bf16[1088,256]{1,0:T(8,128)(2,1)S(1)}, u32[]{:S(2)}, u32[]{:S(2)}) collective-permute-start(bf16[1088,256]{1,0:T(8,128)(2,1)} %get-tuple-element.396), channel_id=1, source_target_pairs={{0,2},{1,3},{2,0},{3,1},{4,6},{5,7},{6,4},{7,5},{8,10},{9,11},{10,... | collective-permute-start | bytes 1671176 | tf_op jit(solution)/shard_map/ppermute | solution.py:602
  168.9 29.9 %collective-permute-start.23 = (bf16[1088,256]{1,0:T(8,128)(2,1)}, bf16[1088,256]{1,0:T(8,128)(2,1)S(1)}, u32[]{:S(2)}, u32[]{:S(2)}) collective-permute-start(bf16[1088,256]{1,0:T(8,128)(2,1)} %get-tuple-element.395), channel_id=1, source_target_pairs={{0,3},{1,2},{2,1},{3,0},{4,7},{5,6},{6,5},{7,4},{8,11},{9,10},{10,... | collective-permute-start | bytes 1671176 | tf_op jit(solution)/shard_map/ppermute | solution.py:602
  222.4 30.8 %collective-permute-start.25 = (bf16[1088,1088]{1,0:T(8,128)(2,1)}, bf16[1088,1088]{1,0:T(8,128)(2,1)}, u32[]{:S(2)}, u32[]{:S(2)}) collective-permute-start(bf16[1088,1088]{1,0:T(8,128)(2,1)} %all-gather.5.cloned.1.call-done.refs_2_.refs_4_), channel_id=1, source_target_pairs={{0,16},{1,3},{2,18},{3,1},{16,0},{17,19},{18,2},{19,17},{4,20},{5,... | collective-permute-start | bytes 7102472 | tf_op jit(solution)/shard_map/ppermute | solution.py:596
  223.9 29.8 %collective-permute-start.26 = (bf16[1088,1088]{1,0:T(8,128)(2,1)}, bf16[1088,1088]{1,0:T(8,128)(2,1)}, u32[]{:S(2)}, u32[]{:S(2)}) collective-permute-start(bf16[1088,1088]{1,0:T(8,128)(2,1)} %all-gather.5.cloned.1.call-done.refs_2_.refs_4_), channel_id=1, source_target_pairs={{0,1},{1,0},{2,3},{3,2},{16,17},{17,16},{18,19},{19,18},{4,5},{5,4... | collective-permute-start | bytes 7102472 | tf_op jit(solution)/shard_map/ppermute | solution.py:596
  234.9 32.8 %collective-permute-start.27 = (bf16[1088,1088]{1,0:T(8,128)(2,1)}, bf16[1088,1088]{1,0:T(8,128)(2,1)}, u32[]{:S(2)}, u32[]{:S(2)}) collective-permute-start(bf16[1088,1088]{1,0:T(8,128)(2,1)} %convolution_convert_fusion.11), channel_id=1, source_target_pairs={{0,1},{1,0},{2,3},{3,2},{16,17},{17,16},{18,19},{19,18},{4,5},{5,4... | collective-permute-start | bytes 7102472 | tf_op jit(solution)/shard_map/ppermute | solution.py:596
  253.2 20.6 %collective-permute-start.28 = (bf16[1088,1088]{1,0:T(8,128)(2,1)}, bf16[1088,1088]{1,0:T(8,128)(2,1)S(1)}, u32[]{:S(2)}, u32[]{:S(2)}) collective-permute-start(bf16[1088,1088]{1,0:T(8,128)(2,1)} %collective-permute-done.25.refs_2_.refs_5_), channel_id=1, source_target_pairs={{0,1},{1,0},{2,3},{3,2},{16,17},{17,16},{18,19},{19,18},{4,5},{5,4... | collective-permute-start | bytes 7102472 | tf_op jit(solution)/shard_map/ppermute | solution.py:596
  253.2 36.3 %collective-permute-start.24 = (bf16[1088,1088]{1,0:T(8,128)(2,1)}, bf16[1088,1088]{1,0:T(8,128)(2,1)}, u32[]{:S(2)}, u32[]{:S(2)}) collective-permute-start(bf16[1088,1088]{1,0:T(8,128)(2,1)} %convolution_convert_fusion.10), channel_id=1, source_target_pairs={{0,1},{1,0},{2,3},{3,2},{16,17},{17,16},{18,19},{19,18},{4,5},{5,4... | collective-permute-start | bytes 7102472 | tf_op jit(solution)/shard_map/ppermute | solution.py:596
  272.3 33.9 %collective-permute-start.31 = (bf16[1088,1088]{1,0:T(8,128)(2,1)}, bf16[1088,1088]{1,0:T(8,128)(2,1)}, u32[]{:S(2)}, u32[]{:S(2)}) collective-permute-start(bf16[1088,1088]{1,0:T(8,128)(2,1)} %add_convert_fusion.4), channel_id=1, source_target_pairs={{0,16},{1,3},{2,18},{3,1},{16,0},{17,19},{18,2},{19,17},{4,20},{5,... | collective-permute-start | bytes 7102472 | tf_op jit(solution)/shard_map/ppermute | solution.py:596
  301.1 17.3 %collective-permute-start.30 = (bf16[1088,1088]{1,0:T(8,128)(2,1)}, bf16[1088,1088]{1,0:T(8,128)(2,1)}, u32[]{:S(2)}, u32[]{:S(2)}) collective-permute-start(bf16[1088,1088]{1,0:T(8,128)(2,1)} %convolution_convert_fusion.6), channel_id=1, source_target_pairs={{0,1},{1,0},{2,3},{3,2},{16,17},{17,16},{18,19},{19,18},{4,5},{5,4... | collective-permute-start | bytes 7102472 | tf_op jit(solution)/shard_map/ppermute | solution.py:596
  318.5 39.3 %collective-permute-start.32 = (bf16[1088,1088]{1,0:T(8,128)(2,1)}, bf16[1088,1088]{1,0:T(8,128)(2,1)}, u32[]{:S(2)}, u32[]{:S(2)}) collective-permute-start(bf16[1088,1088]{1,0:T(8,128)(2,1)} %fusion.2), channel_id=1, source_target_pairs={{0,16},{1,3},{2,18},{3,1},{16,0},{17,19},{18,2},{19,17},{4,20},{5,... | collective-permute-start | bytes 7102472 | tf_op jit(solution)/shard_map/ppermute | solution.py:596
  319.1 249.5 %reduce-scatter.5.cloned.1.call-start = ((), (), s32[]{:S(2)}) async-start(), calls=%async_computation.5 | async-start | bytes 3133440 | tf_op jit(solution)/shard_map/reduce_scatter | solution.py:622
  362.8 29.8 %collective-permute-start.33 = (bf16[272,1088]{1,0:T(8,128)(2,1)}, bf16[272,1088]{1,0:T(8,128)(2,1)}, u32[]{:S(2)}, u32[]{:S(2)}) collective-permute-start(bf16[272,1088]{1,0:T(8,128)(2,1)} %get-tuple-element.284), channel_id=1, source_target_pairs={{0,4},{4,8},{8,12},{12,0},{1,5},{5,9},{9,13},{13,1},{2,6},{6,10},{... | collective-permute-start | bytes 1775624 | tf_op jit(solution)/shard_map/ppermute | solution.py:634
  392.6 27.5 %collective-permute-start.34 = (bf16[272,1088]{1,0:T(8,128)(2,1)}, bf16[272,1088]{1,0:T(8,128)(2,1)}, u32[]{:S(2)}, u32[]{:S(2)}) collective-permute-start(bf16[272,1088]{1,0:T(8,128)(2,1)} %reduce-scatter.3.cloned.1.call-done), channel_id=1, source_target_pairs={{0,2},{1,17},{2,0},{3,19},{16,18},{17,1},{18,16},{19,3},{4,6},{5,2... | collective-permute-start | bytes 1775624 | tf_op jit(solution)/shard_map/ppermute | solution.py:596
  393.9 41.0 %collective-permute-start.35 = (bf16[272,1088]{1,0:T(8,128)(2,1)}, bf16[272,1088]{1,0:T(8,128)(2,1)}, u32[]{:S(2)}, u32[]{:S(2)}) collective-permute-start(bf16[272,1088]{1,0:T(8,128)(2,1)} %get-tuple-element.293), channel_id=1, source_target_pairs={{0,8},{4,12},{8,0},{12,4},{1,9},{5,13},{9,1},{13,5},{2,10},{6,14},... | collective-permute-start | bytes 1775624 | tf_op jit(solution)/shard_map/ppermute | solution.py:634
  396.3 39.6 %collective-permute-start.36 = (bf16[272,1088]{1,0:T(8,128)(2,1)}, bf16[272,1088]{1,0:T(8,128)(2,1)}, u32[]{:S(2)}, u32[]{:S(2)}) collective-permute-start(bf16[272,1088]{1,0:T(8,128)(2,1)} %get-tuple-element.294), channel_id=1, source_target_pairs={{0,12},{4,0},{8,4},{12,8},{1,13},{5,1},{9,5},{13,9},{2,14},{6,2},{... | collective-permute-start | bytes 1775624 | tf_op jit(solution)/shard_map/ppermute | solution.py:634
  460.6 37.5 %collective-permute-start.39 = (bf16[1088,1088]{1,0:T(8,128)(2,1)}, bf16[1088,1088]{1,0:T(8,128)(2,1)}, u32[]{:S(2)}, u32[]{:S(2)}) collective-permute-start(bf16[1088,1088]{1,0:T(8,128)(2,1)} %add_convert_fusion.1), channel_id=1, source_target_pairs={{0,16},{1,3},{2,18},{3,1},{16,0},{17,19},{18,2},{19,17},{4,20},{5,... | collective-permute-start | bytes 7102472 | tf_op jit(solution)/shard_map/ppermute | solution.py:596
  463.9 41.5 %collective-permute-start.40 = (bf16[272,1088]{1,0:T(8,128)(2,1)S(1)}, bf16[272,1088]{1,0:T(8,128)(2,1)S(1)}, u32[]{:S(2)}, u32[]{:S(2)}) collective-permute-start(bf16[272,1088]{1,0:T(8,128)(2,1)S(1)} %add_convert_fusion.7), channel_id=1, source_target_pairs={{0,2},{1,17},{2,0},{3,19},{16,18},{17,1},{18,16},{19,3},{4,6},{5,2... | collective-permute-start | bytes 1775624 | tf_op jit(solution)/shard_map/ppermute | solution.py:596
  465.4 40.0 %collective-permute-start.41 = (bf16[272,1088]{1,0:T(8,128)(2,1)S(1)}, bf16[272,1088]{1,0:T(8,128)(2,1)S(1)}, u32[]{:S(2)}, u32[]{:S(2)}) collective-permute-start(bf16[272,1088]{1,0:T(8,128)(2,1)S(1)} %add_convert_fusion.8.refs_0_), channel_id=1, source_target_pairs={{0,16},{1,3},{2,18},{3,1},{16,0},{17,19},{18,2},{19,17},{4,20},{5,... | collective-permute-start | bytes 1775624 | tf_op jit(solution)/shard_map/ppermute | solution.py:596
  506.6 35.2 %collective-permute-start.50 = (bf16[272,1088]{1,0:T(8,128)(2,1)S(1)}, bf16[272,1088]{1,0:T(8,128)(2,1)}, u32[]{:S(2)}, u32[]{:S(2)}) collective-permute-start(bf16[272,1088]{1,0:T(8,128)(2,1)S(1)} %collective-permute-done.41.refs_1_), channel_id=1, source_target_pairs={{0,1},{1,0},{2,3},{3,2},{16,17},{17,16},{18,19},{19,18},{4,5},{5,4... | collective-permute-start | bytes 1775624 | tf_op jit(solution)/shard_map/ppermute | solution.py:596
  508.3 33.4 %collective-permute-start.51 = (bf16[272,1088]{1,0:T(8,128)(2,1)S(1)}, bf16[272,1088]{1,0:T(8,128)(2,1)S(1)}, u32[]{:S(2)}, u32[]{:S(2)}) collective-permute-start(bf16[272,1088]{1,0:T(8,128)(2,1)S(1)} %add_convert_fusion.6.refs_0_), channel_id=1, source_target_pairs={{0,16},{1,3},{2,18},{3,1},{16,0},{17,19},{18,2},{19,17},{4,20},{5,... | collective-permute-start | bytes 1775624 | tf_op jit(solution)/shard_map/ppermute | solution.py:596
  509.3 28.5 %collective-permute-start.46 = (bf16[1088,256]{1,0:T(8,128)(2,1)}, bf16[1088,256]{1,0:T(8,128)(2,1)}, u32[]{:S(2)}, u32[]{:S(2)}) collective-permute-start(bf16[1088,256]{1,0:T(8,128)(2,1)} %get-tuple-element.332), channel_id=1, source_target_pairs={{0,1},{1,0},{2,3},{3,2},{4,5},{5,4},{6,7},{7,6},{8,9},{9,8},{10,11... | collective-permute-start | bytes 1671176 | tf_op jit(solution)/shard_map/ppermute | solution.py:602
  509.3 28.6 %collective-permute-start.47 = (bf16[1088,256]{1,0:T(8,128)(2,1)}, bf16[1088,256]{1,0:T(8,128)(2,1)}, u32[]{:S(2)}, u32[]{:S(2)}) collective-permute-start(bf16[1088,256]{1,0:T(8,128)(2,1)} %get-tuple-element.333), channel_id=1, source_target_pairs={{0,2},{1,3},{2,0},{3,1},{4,6},{5,7},{6,4},{7,5},{8,10},{9,11},{10,... | collective-permute-start | bytes 1671176 | tf_op jit(solution)/shard_map/ppermute | solution.py:602
  511.5 30.2 %collective-permute-start.48 = (bf16[1088,256]{1,0:T(8,128)(2,1)}, bf16[1088,256]{1,0:T(8,128)(2,1)}, u32[]{:S(2)}, u32[]{:S(2)}) collective-permute-start(bf16[1088,256]{1,0:T(8,128)(2,1)} %get-tuple-element.334), channel_id=1, source_target_pairs={{0,3},{1,2},{2,1},{3,0},{4,7},{5,6},{6,5},{7,4},{8,11},{9,10},{10,... | collective-permute-start | bytes 1671176 | tf_op jit(solution)/shard_map/ppermute | solution.py:602
  541.8 15.8 %collective-permute-start.53 = (bf16[1088,256]{1,0:T(8,128)(2,1)}, bf16[1088,256]{1,0:T(8,128)(2,1)}, u32[]{:S(2)}, u32[]{:S(2)}) collective-permute-start(bf16[1088,256]{1,0:T(8,128)(2,1)} %get-tuple-element.339), channel_id=1, source_target_pairs={{0,2},{1,3},{2,0},{3,1},{4,6},{5,7},{6,4},{7,5},{8,10},{9,11},{10,... | collective-permute-start | bytes 1671176 | tf_op jit(solution)/shard_map/ppermute | solution.py:602
  542.8 25.8 %collective-permute-start.54 = (bf16[1088,256]{1,0:T(8,128)(2,1)}, bf16[1088,256]{1,0:T(8,128)(2,1)}, u32[]{:S(2)}, u32[]{:S(2)}) collective-permute-start(bf16[1088,256]{1,0:T(8,128)(2,1)} %get-tuple-element.340), channel_id=1, source_target_pairs={{0,3},{1,2},{2,1},{3,0},{4,7},{5,6},{6,5},{7,4},{8,11},{9,10},{10,... | collective-permute-start | bytes 1671176 | tf_op jit(solution)/shard_map/ppermute | solution.py:602
  570.6 19.9 %collective-permute-start.62 = (bf16[272,1088]{1,0:T(8,128)(2,1)S(1)}, bf16[272,1088]{1,0:T(8,128)(2,1)S(1)}, u32[]{:S(2)}, u32[]{:S(2)}) collective-permute-start(bf16[272,1088]{1,0:T(8,128)(2,1)S(1)} %collective-permute-done.51.refs_1_), channel_id=1, source_target_pairs={{0,1},{1,0},{2,3},{3,2},{16,17},{17,16},{18,19},{19,18},{4,5},{5,4... | collective-permute-start | bytes 1775624 | tf_op jit(solution)/shard_map/ppermute | solution.py:596
  580.5 17.9 %collective-permute-start.57 = (bf16[272,1088]{1,0:T(8,128)(2,1)S(1)}, bf16[272,1088]{1,0:T(8,128)(2,1)S(1)}, u32[]{:S(2)}, u32[]{:S(2)}) collective-permute-start(bf16[272,1088]{1,0:T(8,128)(2,1)S(1)} %add_convert_fusion.5.refs_0_), channel_id=1, source_target_pairs={{0,16},{1,3},{2,18},{3,1},{16,0},{17,19},{18,2},{19,17},{4,20},{5,... | collective-permute-start | bytes 1775624 | tf_op jit(solution)/shard_map/ppermute | solution.py:596
  581.6 16.8 %collective-permute-start.58 = (bf16[272,1088]{1,0:T(8,128)(2,1)S(1)}, bf16[272,1088]{1,0:T(8,128)(2,1)S(1)}, u32[]{:S(2)}, u32[]{:S(2)}) collective-permute-start(bf16[272,1088]{1,0:T(8,128)(2,1)S(1)} %add_convert_fusion.5.refs_0_), channel_id=1, source_target_pairs={{0,1},{1,0},{2,3},{3,2},{16,17},{17,16},{18,19},{19,18},{4,5},{5,4... | collective-permute-start | bytes 1775624 | tf_op jit(solution)/shard_map/ppermute | solution.py:596
  581.6 16.8 %collective-permute-start.59 = (bf16[272,1088]{1,0:T(8,128)(2,1)S(1)}, bf16[272,1088]{1,0:T(8,128)(2,1)S(1)}, u32[]{:S(2)}, u32[]{:S(2)}) collective-permute-start(bf16[272,1088]{1,0:T(8,128)(2,1)S(1)} %add_convert_fusion.5.refs_0_), channel_id=1, source_target_pairs={{0,17},{1,2},{2,19},{3,0},{16,1},{17,18},{18,3},{19,16},{4,21},{5,... | collective-permute-start | bytes 1775624 | tf_op jit(solution)/shard_map/ppermute | solution.py:596
  582.8 15.6 %collective-permute-start.60 = (f32[3264]{0:T(1024)S(1)}, f32[3264]{0:T(1024)S(1)}, u32[]{:S(2)}, u32[]{:S(2)}) collective-permute-start(f32[3264]{0:T(1024)S(1)} %add.306), channel_id=1, source_target_pairs={{0,16},{1,17},{2,18},{3,19},{16,0},{17,1},{18,2},{19,3},{4,20},{5,... | collective-permute-start | bytes 39176 | tf_op jit(solution)/shard_map/ppermute | solution.py:669
  (80 other events, 827.0 us)
Sparse Core Ops, SparseCore 0:
  77.0 50.3 all-gather.2
  165.1 50.7 all-gather.4
  319.2 49.1 reduce-scatter.2
  505.5 51.0 reduce-scatter.4
